TPU v7x, 32 devices: a whole 2x2x4 slice. The times are simulated.
32 devices in a mesh: lat: 8 (over y, x, core), lon: 4 (over z).
Axes of the slice: x: 2, y: 2, z: 4, core: 2. Of those that a mesh axis runs over, the one named last changes fastest.
Arguments:
- spectral: bfloat16 [6, 32, 640, 1280], P(None, 'lon', 'lat'), may hold values from -6 to 6
- legendre: bfloat16 [640, 1280, 128], P('lat'), may hold values from -0.15625 to 0.15625
- wave_ids: int32 [640], replicated, may hold values from 0 to 639, each once
- points: int32 [128], P('lat'), may hold values from 512 to 1024
- tracers: bfloat16 [16, 32, 128, 1024], P(None, None, 'lat', 'lon'), may hold values from -6 to 6
- react_base: float32 [16, 16], replicated, may hold values from -0.75 to 0.75
- react_temp: float32 [16, 16], replicated, may hold values from -0.75 to 0.75
- active_ids: int32 [4], replicated, may hold values from 0 to 15, as said below
Outputs:
- tracers_new: bfloat16 [16, 32, 128, 1024], P(None, None, 'lat', 'lon')
- active: float32 [4, 32, 128, 1024], P(None, 'lon', 'lat')
Inputs may be any that keep to these rules, and one draw needn't show every extreme that they name: `active_ids`: distinct tracer indices. `wave_ids`: each slot a different wavenumber.
All inputs are finite; a program needn't handle non-finite values.
Results may differ from a plain program's by a relative error of at most 0.0042.
Values may be sent and summed in bfloat16 or wider, within the bound.
No kernel may reach another device: no remote copies, remote signals or barrier semaphores. Data moves between devices by JAX's collectives and lax.ppermute only.
A program may use at most 256 MiB of HBM per device.

v0:
```python
import functools

import jax
import jax.numpy as jnp
import numpy as np
from jax import lax
from jax.experimental import pallas as pl
from jax.experimental.pallas import tpu as pltpu
from jax.sharding import PartitionSpec as P

F32 = jnp.float32
BF16 = jnp.bfloat16
LANES = 128
LOW = 16
VMEM = 56 * 1024 * 1024

COS = (
    0.9999999890590228,
    -19.739204499454026,
    64.93911745990036,
    -85.45013953095037,
    60.16763095136588,
    -25.96759924965491,
    6.528658162567069,
)
SIN = (
    6.283185302511503,
    -41.34170040531769,
    81.60513138580204,
    -76.7030153539128,
    42.02592698618416,
    -14.899846668691637,
    3.238137510515757,
)


def dot(a, b, dims):
    return lax.dot_general(a, b, (dims, ((), ())), preferred_element_type=F32)


def unit_circle(step, rows, waves, count):
    index = lax.broadcasted_iota(jnp.int32, (rows, waves.shape[1]), 0) * step
    product = index.astype(F32) * waves
    inverse = 1.0 / count
    turns = (product - jnp.floor(product * inverse) * count) * inverse
    y = turns - jnp.floor(turns + 0.5)
    z = y * y
    cosine = jnp.full_like(z, COS[-1])
    sine = jnp.full_like(z, SIN[-1])
    for c, s in zip(COS[-2::-1], SIN[-2::-1]):
        cosine = cosine * z + c
        sine = sine * z + s
    return cosine, sine * y


def table_kernel(points, waves_ref, table_ref, twiddle_ref):
    count = jnp.full(waves_ref.shape, points[pl.program_id(0)], jnp.int32).astype(F32)
    waves = waves_ref[...]
    size = waves.shape[1]
    cos_low, sin_low = unit_circle(1, LOW, waves, count)
    cos_high, sin_high = unit_circle(LOW, LANES // LOW, waves, count)
    for a in range(LANES // LOW):
        ch, sh = cos_high[a : a + 1], sin_high[a : a + 1]
        rows = slice(a * LOW, (a + 1) * LOW)
        table_ref[0, rows, :size] = (ch * cos_low - sh * sin_low).astype(BF16)
        table_ref[0, rows, size:] = (-sh * cos_low - ch * sin_low).astype(BF16)
    turns = twiddle_ref.shape[2]
    cos_turn, sin_turn = unit_circle(LANES, turns, waves, count)
    twiddle_ref[0, 0] = cos_turn
    twiddle_ref[0, 1] = sin_turn


def tables(points, wave_ids, turns):
    rows, waves = points.shape[0], wave_ids.shape[0]
    return pl.pallas_call(
        table_kernel,
        grid_spec=pltpu.PrefetchScalarGridSpec(
            num_scalar_prefetch=1,
            grid=(rows,),
            in_specs=[pl.BlockSpec((1, waves), lambda j, p: (0, 0))],
            out_specs=[
                pl.BlockSpec((1, LANES, 2 * waves), lambda j, p: (j, 0, 0)),
                pl.BlockSpec((1, 2, turns, waves), lambda j, p: (j, 0, 0, 0)),
            ],
        ),
        out_shape=[
            jax.ShapeDtypeStruct((rows, LANES, 2 * waves), BF16),
            jax.ShapeDtypeStruct((rows, 2, turns, waves), F32),
        ],
        compiler_params=pltpu.CompilerParams(vmem_limit_bytes=VMEM),
        name="tables",
    )(points, wave_ids.astype(F32)[None, :])


def place(pieces, width):
    out = [None] * (width // LANES)
    lane = lax.broadcasted_iota(jnp.int32, (pieces[0][0].shape[0], LANES), 1)
    for value, start, count, here in pieces:
        shift = (here - start) % LANES
        for a in range(start // LANES, (start + count - 1) // LANES + 1):
            part = value[:, a * LANES : (a + 1) * LANES]
            if shift:
                part = pltpu.roll(part, shift, 1)
            first = max(start, a * LANES) - start + here
            last = min(start + count, (a + 1) * LANES) - start + here
            for v in range(first // LANES, (last - 1) // LANES + 1):
                low, high = max(first - v * LANES, 0), min(last - v * LANES, LANES)
                if out[v] is None:
                    out[v] = part
                else:
                    out[v] = jnp.where((lane >= low) & (lane < high), part, out[v])
    return out


def synth_kernel(recv_ref, table_ref, twiddle_ref, out_ref, coef, grid):
    sources, levels, rows, _ = recv_ref.shape
    fields, waves = coef.shape[0] // 2, coef.shape[1] * LANES
    share = waves // sources
    turns = twiddle_ref.shape[2]
    j = pl.program_id(0)

    @pl.when(j == 0)
    def _():
        def level(l, carry):
            values = [recv_ref[s, l].astype(F32) for s in range(sources)]
            for r in range(2 * fields):
                windows = [
                    (values[s], r * share, share, s * share) for s in range(sources)
                ]
                for v, part in enumerate(place(windows, waves)):
                    coef[r, v, pl.ds(l * rows, rows), :] = part
            return carry

        lax.fori_loop(0, levels, level, 0)

    def own_row(r):
        parts = [coef[r, v, pl.ds(j, levels, stride=rows), :] for v in range(waves // LANES)]
        return jnp.concatenate(parts, axis=1)

    values = [own_row(r) for r in range(2 * fields)]
    real, imag = [], []
    for t in range(turns):
        c, s = twiddle_ref[0, 0, t : t + 1], twiddle_ref[0, 1, t : t + 1]
        for f in range(fields):
            re, im = values[2 * f], values[2 * f + 1]
            real.append(re * c - im * s)
            imag.append(re * s + im * c)
    real = jnp.concatenate(real, axis=0).astype(BF16)
    imag = jnp.concatenate(imag, axis=0).astype(BF16)
    nt = ((1,), (1,))
    values = dot(real, table_ref[0, :, :waves], nt) + dot(imag, table_ref[0, :, waves:], nt)
    grid[pl.ds(j, turns * fields * levels, stride=rows), :] = values

    @pl.when(j == rows - 1)
    def _():
        dests = out_ref.shape[0]
        each = turns // dests
        size = levels * rows
        for t in range(turns):
            lanes = slice((t % each) * LANES, (t % each + 1) * LANES)
            for f in range(fields):
                block = grid[(t * fields + f) * size : (t * fields + f + 1) * size, :]
                out_ref[t // each, f, :, :, lanes] = block.reshape(levels, rows, LANES).astype(BF16)


def synthesis(recv, table, twiddle, dests, tile):
    sources, levels, rows, lanes = recv.shape
    turns, waves = twiddle.shape[2:]
    fields = 3
    return pl.pallas_call(
        synth_kernel,
        grid=(rows,),
        in_specs=[
            pl.BlockSpec(recv.shape, lambda j: (0, 0, 0, 0)),
            pl.BlockSpec((1, LANES, 2 * waves), lambda j: (j, 0, 0)),
            pl.BlockSpec((1, 2, turns, waves), lambda j: (j, 0, 0, 0)),
        ],
        out_specs=pl.BlockSpec((dests, fields, levels, rows, tile), lambda j: (0, 0, 0, 0, 0)),
        out_shape=jax.ShapeDtypeStruct((dests, fields, levels, rows, tile), BF16),
        scratch_shapes=[
            pltpu.VMEM((2 * fields, waves // LANES, levels * rows, LANES), F32),
            pltpu.VMEM((turns * fields * levels * rows, LANES), F32),
        ],
        compiler_params=pltpu.CompilerParams(vmem_limit_bytes=VMEM),
        name="synthesis",
    )(recv, table, twiddle)


def edge_kernel(state_ref, pick_ref, first_ref, last_ref, west_ref, east_ref):
    tracers, levels, rows, tile = state_ref.shape
    ends = lax.broadcasted_iota(jnp.int32, (2 * levels, tile), 1)
    row = lax.broadcasted_iota(jnp.int32, (2 * levels, tile), 0)
    columns = jnp.zeros((2 * levels, tracers * rows), F32)
    for l in range(levels):
        x = state_ref[:, l].reshape(tracers * rows, tile)
        picked = dot(pick_ref[...], x, ((1,), (0,)))
        first_ref[l] = picked[:tracers].astype(BF16)
        last_ref[l] = picked[tracers:].astype(BF16)
        mark = ((row == l) & (ends == 0)) | ((row == levels + l) & (ends == tile - 1))
        columns = columns + dot(jnp.where(mark, 1.0, 0.0).astype(BF16), x, ((1,), (1,)))
    west_ref[...] = columns[:levels].astype(BF16)
    east_ref[...] = columns[levels:].astype(BF16)


def edges(state):
    tracers, levels, rows, tile = state.shape
    block = 16
    pick = np.zeros((2 * tracers, tracers * rows), np.float32)
    for t in range(tracers):
        pick[t, t * rows] = 1
        pick[tracers + t, t * rows + rows - 1] = 1
    rowed = jax.ShapeDtypeStruct((levels, tracers, tile), BF16)
    columned = jax.ShapeDtypeStruct((levels, tracers * rows), BF16)
    row_spec = pl.BlockSpec((block, tracers, tile), lambda i: (i, 0, 0))
    col_spec = pl.BlockSpec((block, tracers * rows), lambda i: (i, 0))
    return pl.pallas_call(
        edge_kernel,
        grid=(levels // block,),
        in_specs=[
            pl.BlockSpec((tracers, block, rows, tile), lambda i: (0, i, 0, 0)),
            pl.BlockSpec(pick.shape, lambda i: (0, 0)),
        ],
        out_specs=[row_spec, row_spec, col_spec, col_spec],
        out_shape=[rowed, rowed, columned, columned],
        compiler_params=pltpu.CompilerParams(vmem_limit_bytes=VMEM),
        name="edges",
    )(state, jnp.asarray(pick, BF16))


def chem_kernel(
    ids, state_ref, south_ref, north_ref, west_ref, east_ref, grid_ref, mask_ref, react_ref,
    along_ref, across_ref, new_ref, active_ref, react, scale,
):
    tracers, levels, rows, tile = state_ref.shape
    cells = tracers * rows

    @pl.when(pl.program_id(0) == 0)
    def _():
        value = react_ref[...]
        high = value.astype(BF16)
        react[:, :cells] = high
        react[:, cells : 2 * cells] = (value - high.astype(F32)).astype(BF16)
        react[:, 2 * cells :] = high

    outside = jnp.concatenate([west_ref[...], east_ref[...]], axis=0).astype(F32)
    outside = outside.T.astype(BF16)
    row = lax.broadcasted_iota(jnp.int32, (2 * levels, 2 * tile), 0)
    lane = lax.broadcasted_iota(jnp.int32, (2 * levels, 2 * tile), 1)
    mask = mask_ref[...]
    nn = ((1,), (0,))
    for l in range(levels):
        x = state_ref[:, l].reshape(cells, tile)
        west = (row == l) & ((lane == 0) | (lane == tile))
        east = (row == levels + l) & ((lane == tile - 1) | (lane == 2 * tile - 1))
        mark = jnp.where(east, 1.0, jnp.where(west, jnp.where(lane == 0, -1.0, 1.0), 0.0))
        lon = dot(x, along_ref[...], nn) + dot(outside, mark.astype(BF16), nn)
        stacked = jnp.concatenate([x, south_ref[l], north_ref[l]], axis=0)
        lat = dot(across_ref[...], stacked, nn)

        def three(v):
            return v.reshape(tracers, rows, tile)

        wind_u = grid_ref[0, 0, l].astype(F32) * (scale * 0.1)
        wind_v = grid_ref[0, 1, l].astype(F32) * (scale * 0.1)
        temper = grid_ref[0, 2, l].astype(F32) * scale
        moved = (
            three(x.astype(F32))
            - wind_u * three(lon[:, :tile])
            - wind_v * three(lat[:cells])
            + 0.05 * three(lon[:, tile:] + lat[cells:])
        )
        flat = moved.reshape(cells, tile)
        high = flat.astype(BF16)
        low = (flat - high.astype(F32)).astype(BF16)
        terms = dot(react[...], jnp.concatenate([high, high, low], axis=0), nn)
        reacted = (moved + three(terms[:cells]) + temper * three(terms[cells:])) * mask
        new_ref[:, l] = reacted.astype(BF16)
        for a in range(active_ref.shape[1]):
            active_ref[0, a, l] = new_ref[ids[a], l]


def chemistry(state, halos, grid, mask, react, active_ids, waves):
    tracers, levels, rows, tile = state.shape
    sources, fields, own = grid.shape[:3]
    south, north, west, east = halos
    actives = active_ids.shape[0]
    cells = tracers * rows
    block = own
    eye, one = np.eye(tracers), np.eye(tile)
    along = np.concatenate(
        [np.eye(tile, k=-1) - np.eye(tile, k=1), np.eye(tile, k=-1) + np.eye(tile, k=1) - 4 * one], 1
    )
    down, up = np.eye(rows, k=-1), np.eye(rows, k=1)
    at_first, at_last = np.eye(rows)[:, :1], np.eye(rows)[:, -1:]
    across = np.block(
        [
            [np.kron(eye, up - down), np.kron(eye, -at_first), np.kron(eye, at_last)],
            [np.kron(eye, up + down), np.kron(eye, at_first), np.kron(eye, at_last)],
        ]
    )
    kernel = functools.partial(chem_kernel)
    body = lambda *refs: kernel(*refs, 1.0 / float(np.sqrt(np.float32(waves))))
    whole = lambda shape: pl.BlockSpec(shape, lambda i, ids: (0,) * len(shape))
    return pl.pallas_call(
        body,
        grid_spec=pltpu.PrefetchScalarGridSpec(
            num_scalar_prefetch=1,
            grid=(levels // block,),
            in_specs=[
                pl.BlockSpec((tracers, block, rows, tile), lambda i, ids: (0, i, 0, 0)),
                pl.BlockSpec((block, tracers, tile), lambda i, ids: (i, 0, 0)),
                pl.BlockSpec((block, tracers, tile), lambda i, ids: (i, 0, 0)),
                pl.BlockSpec((block, cells), lambda i, ids: (i, 0)),
                pl.BlockSpec((block, cells), lambda i, ids: (i, 0)),
                pl.BlockSpec((1, fields, own, rows, tile), lambda i, ids: (i, 0, 0, 0, 0)),
                whole((rows, tile)),
                whole((2 * cells, cells)),
                whole(along.shape),
                whole(across.shape),
            ],
            out_specs=[
                pl.BlockSpec((tracers, block, rows, tile), lambda i, ids: (0, i, 0, 0)),
                pl.BlockSpec((1, actives, own, rows, tile), lambda i, ids: (i, 0, 0, 0, 0)),
            ],
            scratch_shapes=[pltpu.VMEM((2 * cells, 3 * cells), BF16)],
        ),
        out_shape=[
            jax.ShapeDtypeStruct(state.shape, BF16),
            jax.ShapeDtypeStruct((sources, actives, own, rows, tile), BF16),
        ],
        compiler_params=pltpu.CompilerParams(vmem_limit_bytes=VMEM),
        name="chemistry",
    )(
        active_ids, state, south, north, west, east, grid, mask, react,
        jnp.asarray(along, BF16), jnp.asarray(across, BF16),
    )


def spread_kernel(recv_ref, out_ref):
    tile = recv_ref.shape[4]
    for s in range(recv_ref.shape[0]):
        out_ref[0, :, :, s * tile : (s + 1) * tile] = recv_ref[s, 0].astype(F32)


def spread(recv):
    sources, actives, own, rows, tile = recv.shape
    return pl.pallas_call(
        spread_kernel,
        grid=(actives,),
        in_specs=[pl.BlockSpec((sources, 1, own, rows, tile), lambda a: (0, a, 0, 0, 0))],
        out_specs=pl.BlockSpec((1, own, rows, sources * tile), lambda a: (a, 0, 0, 0)),
        out_shape=jax.ShapeDtypeStruct((actives, own, rows, sources * tile), F32),
        compiler_params=pltpu.CompilerParams(vmem_limit_bytes=VMEM),
        name="spread",
    )(recv)


def to_next(value, axis):
    size = lax.axis_size(axis)
    return lax.ppermute(value, axis, [(i, i + 1) for i in range(size - 1)])


def to_previous(value, axis):
    size = lax.axis_size(axis)
    return lax.ppermute(value, axis, [(i + 1, i) for i in range(size - 1)])


def body(spectral, legendre, wave_ids, points, tracers, react_base, react_temp, active_ids):
    bands, tiles = lax.axis_size("lat"), lax.axis_size("lon")
    count, levels, rows, tile = tracers.shape
    own, share = spectral.shape[1:3]
    waves = wave_ids.shape[0]

    fourier = lax.dot_general(
        spectral, legendre, (((3,), (1,)), ((2,), (0,))), preferred_element_type=F32
    ).astype(BF16)
    fourier = fourier.reshape(share, 6, own, bands, rows)
    sent = jnp.transpose(fourier, (3, 2, 4, 1, 0)).reshape(bands, own, rows, 6 * share)
    sent = jnp.pad(sent, ((0, 0), (0, 0), (0, 0), (0, -(6 * share) % LANES)))
    recv = lax.all_to_all(sent, "lat", split_axis=0, concat_axis=0, tiled=True)

    first, last, west, east = edges(tracers)
    halos = (
        to_next(last, "lat"),
        to_previous(first, "lat"),
        to_next(east, "lon"),
        to_previous(west, "lon"),
    )
    table, twiddle = tables(points, wave_ids, tiles * tile // LANES)

    grid = synthesis(recv, table, twiddle, tiles, tile)
    grid = lax.all_to_all(grid, "lon", split_axis=0, concat_axis=0, tiled=True)

    columns = lax.axis_index("lon") * tile + jnp.arange(tile)
    mask = (columns[None, :] < points[:, None]).astype(F32)
    react = jnp.concatenate([react_base, react_temp], axis=0)
    eye = jnp.eye(rows, dtype=F32)
    react = (react[:, None, :, None] * eye[None, :, None, :]).reshape(2 * count * rows, count * rows)
    new, active = chemistry(tracers, halos, grid, mask, react, active_ids, waves)
    active = lax.all_to_all(active, "lon", split_axis=0, concat_axis=0, tiled=True)
    return new, spread(active)


def solution(mesh):
    return jax.shard_map(
        body,
        mesh=mesh,
        in_specs=(
            P(None, "lon", "lat", None),
            P("lat", None, None),
            P(),
            P("lat"),
            P(None, None, "lat", "lon"),
            P(),
            P(),
            P(),
        ),
        out_specs=(P(None, None, "lat", "lon"), P(None, "lon", "lat", None)),
        check_vma=False,
    )
```

profile of v0, /device:TPU:0, one launch (start us, length us, event | category | flops | bytes accessed | tf_op | source)
XLA Modules:
  0.0 143.5 jit_solution(4741225587659318691)
XLA Ops:
  0.6 13.9 %fusion.3 = bf16[80,6,8,128]{3,2,1,0:T(8,128)(2,1)S(1)} fusion(bf16[80,1280,128]{2,1,0:T(8,128)(2,1)} %param.12, bf16[6,8,80,1280]{3,2,1,0:T(8,128)(2,1)} %param.11), kind=kOutput, calls=%fused_computation.4 | convolution fusion | flops 1258782720 | bytes 37027840 | tf_op jit(solution)/shard_map/dot_general | solution.py:374
  14.5 1.6 %copy.16 = bf16[80,6,8,128]{0,3,2,1:T(8,128)(2,1)} copy(bf16[80,6,8,128]{3,2,1,0:T(8,128)(2,1)S(1)} %fusion.3) | data formatting | bytes 1966080 | tf_op jit(solution)/shard_map/convert_element_type | solution.py:376
  16.2 0.0 copy-start.8
  16.2 3.3 %copy.17 = bf16[8,8,16,6,80]{4,3,2,1,0:T(8,128)(2,1)S(1)} copy(bf16[8,8,16,6,80]{4,2,0,1,3:T(8,128)(2,1)} %bitcast.12) | data formatting | bytes 1966080 | tf_op jit(solution)/shard_map/transpose | solution.py:378
  19.5 1.2 reshape.29
  20.7 1.2 pad.4
  21.9 5.2 %all-to-all-start = ((bf16[8,8,16,512]{3,2,1,0:T(8,128)(2,1)}), bf16[8,8,16,512]{3,2,1,0:T(8,128)(2,1)S(1)}, u32[]{:S(2)}, u32[]{:S(2)}) async-start(bf16[8,8,16,512]{3,2,1,0:T(8,128)(2,1)} %pad.4), calls=%async_computation | async-start | bytes 2097152 | tf_op jit(solution)/shard_map/all_to_all | solution.py:380
  27.1 0.0 copy-done.8
  27.1 0.6 broadcast_in_dim.2.waves_ref
  27.7 9.1 %tables.1 = (bf16[16,128,1280]{2,1,0:T(8,128)(2,1)}, f32[16,2,8,640]{3,2,1,0:T(8,128)}) custom-call(s32[16]{0:T(128)} %points.1, f32[1,640]{1,0:T(1,128)} %broadcast_in_dim.2.waves_ref), custom_call_target="tpu_custom_call" | custom-call | tf_op jit(solution)/shard_map/tables/pallas_call | solution.py:75
  36.7 5.7 %all-to-all-done.recv_ref = bf16[8,8,16,512]{3,2,1,0:T(8,128)(2,1)S(1)} async-done(((bf16[8,8,16,512]{3,2,1,0:T(8,128)(2,1)}), bf16[8,8,16,512]{3,2,1,0:T(8,128)(2,1)S(1)}, u32[]{:S(2)}, u32[]{:S(2)}) %all-to-all-start) | async-done | bytes 1048608 | tf_op jit(solution)/shard_map/all_to_all | solution.py:380
  42.5 0.0 copy-start
  42.5 1.0 copy-done
  43.4 0.0 copy-start.6
  43.4 0.0 copy-start.7
  43.4 13.6 %synthesis.1 = bf16[4,3,8,16,256]{4,3,2,1,0:T(8,128)(2,1)} custom-call(bf16[8,8,16,512]{3,2,1,0:T(8,128)(2,1)} %copy-done, bf16[16,128,1280]{2,1,0:T(8,128)(2,1)} %get-tuple-element.14.table_ref, f32[16,2,8,640]{3,2,1,0:T(8,128)} %get-tuple-element.15.twiddle_ref), custom_call_target="tpu_custom_call" | custom-call | tf_op jit(solution)/shard_map/synthesis/pallas_call | solution.py:170
  57.1 0.0 copy-start.9
  57.1 5.0 %all-to-all-start.1 = ((bf16[4,3,8,16,256]{4,3,2,1,0:T(8,128)(2,1)}), bf16[4,3,8,16,256]{4,3,2,1,0:T(8,128)(2,1)S(1)}, u32[]{:S(2)}, u32[]{:S(2)}) async-start(bf16[4,3,8,16,256]{4,3,2,1,0:T(8,128)(2,1)} %synthesis.1), calls=%async_computation.1 | async-start | bytes 1572864 | tf_op jit(solution)/shard_map/all_to_all | solution.py:392
  62.1 4.3 %edges.1 = (bf16[32,16,256]{2,1,0:T(8,128)(2,1)}, bf16[32,16,256]{2,1,0:T(8,128)(2,1)}, bf16[32,256]{1,0:T(8,128)(2,1)}, bf16[32,256]{1,0:T(8,128)(2,1)}) custom-call(bf16[16,32,16,256]{3,2,1,0:T(8,128)(2,1)} %refs_1_.1, bf16[32,256]{1,0:T(8,128)(2,1)} %constant.15.clone.pick_ref), custom_call_target="tpu_custom_call" | custom-call | tf_op jit(solution)/shard_map/edges/pallas_call | solution.py:216
  66.4 1.3 collective-permute-start
  67.7 1.3 collective-permute-start.1
  69.0 3.9 %collective-permute-start.2 = (bf16[32,256]{1,0:T(8,128)(2,1)}, bf16[32,256]{1,0:T(8,128)(2,1)S(1)}, u32[]{:S(2)}, u32[]{:S(2)}) collective-permute-start(bf16[32,256]{1,0:T(8,128)(2,1)} %get-tuple-element.12), channel_id=1, source_target_pairs={{0,1},{1,2},{2,3},{4,5},{5,6},{6,7},{8,9},{9,10},{10,11},{12,13},{... | collective-permute-start | bytes 49160 | tf_op jit(solution)/shard_map/ppermute | solution.py:360
  73.0 1.5 %collective-permute-start.3 = (bf16[32,256]{1,0:T(8,128)(2,1)}, bf16[32,256]{1,0:T(8,128)(2,1)S(1)}, u32[]{:S(2)}, u32[]{:S(2)}) collective-permute-start(bf16[32,256]{1,0:T(8,128)(2,1)} %get-tuple-element.13), channel_id=1, source_target_pairs={{1,0},{2,1},{3,2},{5,4},{6,5},{7,6},{9,8},{10,9},{11,10},{13,12},{... | collective-permute-start | bytes 49160 | tf_op jit(solution)/shard_map/ppermute | solution.py:365
  74.5 0.0 copy-done.6
  74.5 0.0 copy-done.7
  74.5 2.4 %broadcast_multiply_fusion = f32[32,16,16,16]{3,2,1,0:T(8,128)} fusion(f32[16,16]{1,0:T(8,128)S(1)} %fusion.8, f32[32,16]{1,0:T(8,128)S(1)} %pad_maximum_fusion), kind=kLoop, calls=%fused_computation.3 | loop fusion | flops 131072 | bytes 527360 | tf_op jit(solution)/shard_map/mul | solution.py:398
  76.8 0.0 copy-done.9
  76.8 0.7 compare_convert_fusion.refs_7_
  77.5 4.2 %mul.24.refs_8_ = f32[512,256]{1,0:T(8,128)} reshape(f32[32,16,16,16]{3,2,1,0:T(8,128)} %broadcast_multiply_fusion) | data formatting | bytes 1048576 | tf_op jit(solution)/shard_map/mul | solution.py:398
  81.7 0.0 collective-permute-done.2.refs_4_
  81.7 0.0 copy-start.4
  81.7 0.0 collective-permute-done.3.refs_5_
  81.7 0.0 copy-start.5
  81.7 0.0 collective-permute-done.refs_2_
  81.7 0.0 copy-start.2
  81.8 0.0 collective-permute-done.1.refs_3_
  81.8 0.0 copy-start.3
  81.8 0.0 all-to-all-done.1.refs_6_
  81.8 0.5 copy-done.4
  82.3 0.0 copy-done.5
  82.3 0.1 copy-done.2
  82.4 0.1 copy-done.3
  82.5 0.0 copy-start.1
  82.5 0.9 copy-done.1
  83.4 23.5 %chemistry.1 = (bf16[16,32,16,256]{3,2,1,0:T(8,128)(2,1)}, bf16[4,4,8,16,256]{4,3,2,1,0:T(8,128)(2,1)}) custom-call(s32[4]{0:T(128)} %refs_0_.1, bf16[16,32,16,256]{3,2,1,0:T(8,128)(2,1)} %refs_1_.1, bf16[32,16,256]{2,1,0:T(8,128)(2,1)} %copy-done.2, bf16[32,16,256]{2,1,0:T(8,128)(2,1)} %copy-done.3, bf16[32,256]{1,0:T(8,128)(2,1)} %copy-done.4, ...), custom_call_target="tpu_custom_call" | custom-call | tf_op jit(solution)/shard_map/chemistry/pallas_call | solution.py:304
  106.9 33.0 %all_to_all.15.recv_ref = bf16[4,4,8,16,256]{4,3,2,1,0:T(8,128)(2,1)} all-to-all(bf16[4,4,8,16,256]{4,3,2,1,0:T(8,128)(2,1)} %get-tuple-element.17), channel_id=1, replica_groups=mesh['lat'=8,'lon'=4] {'lon'}, dimensions={0} | all-to-all | bytes 2097152 | tf_op jit(solution)/shard_map/all_to_all | solution.py:400
  139.9 3.6 %spread.1 = f32[4,8,16,1024]{3,2,1,0:T(8,128)} custom-call(bf16[4,4,8,16,256]{4,3,2,1,0:T(8,128)(2,1)} %all_to_all.15.recv_ref), custom_call_target="tpu_custom_call" | custom-call | tf_op jit(solution)/shard_map/spread/pallas_call | solution.py:347
  (4 shorter events, 0.0 us)
Async XLA Ops:
  16.2 10.9 %copy-start.8 = (s32[640]{0:T(1024)S(1)}, s32[640]{0:T(1024)}, u32[]{:S(2)}) copy-start(s32[640]{0:T(1024)} %param.13) | copy-start | bytes 7684
  21.9 20.6 %all-to-all-start = ((bf16[8,8,16,512]{3,2,1,0:T(8,128)(2,1)}), bf16[8,8,16,512]{3,2,1,0:T(8,128)(2,1)S(1)}, u32[]{:S(2)}, u32[]{:S(2)}) async-start(bf16[8,8,16,512]{3,2,1,0:T(8,128)(2,1)} %pad.4), calls=%async_computation | async-start | bytes 2097152 | tf_op jit(solution)/shard_map/all_to_all | solution.py:380
  42.5 1.0 copy-start
  43.4 31.0 %copy-start.6 = (f32[16,16]{1,0:T(8,128)S(1)}, f32[16,16]{1,0:T(8,128)}, u32[]{:S(2)}) copy-start(f32[16,16]{1,0:T(8,128)} %param.17) | copy-start | bytes 3076
  43.4 31.0 %copy-start.7 = (f32[16,16]{1,0:T(8,128)S(1)}, f32[16,16]{1,0:T(8,128)}, u32[]{:S(2)}) copy-start(f32[16,16]{1,0:T(8,128)} %param.16) | copy-start | bytes 3076
  57.1 19.8 %copy-start.9 = (s32[16]{0:T(128)S(1)}, s32[16]{0:T(128)}, u32[]{:S(2)}) copy-start(s32[16]{0:T(128)} %points.1) | copy-start | bytes 196
  57.1 24.7 %all-to-all-start.1 = ((bf16[4,3,8,16,256]{4,3,2,1,0:T(8,128)(2,1)}), bf16[4,3,8,16,256]{4,3,2,1,0:T(8,128)(2,1)S(1)}, u32[]{:S(2)}, u32[]{:S(2)}) async-start(bf16[4,3,8,16,256]{4,3,2,1,0:T(8,128)(2,1)} %synthesis.1), calls=%async_computation.1 | async-start | bytes 1572864 | tf_op jit(solution)/shard_map/all_to_all | solution.py:392
  66.4 15.3 %collective-permute-start = (bf16[32,16,256]{2,1,0:T(8,128)(2,1)}, bf16[32,16,256]{2,1,0:T(8,128)(2,1)S(1)}, u32[]{:S(2)}, u32[]{:S(2)}) collective-permute-start(bf16[32,16,256]{2,1,0:T(8,128)(2,1)} %get-tuple-element.10), channel_id=1, source_target_pairs={{0,4},{4,8},{8,12},{12,16},{16,20},{20,24},{24,28},{1,5},{5,9},{9,... | collective-permute-start | bytes 786440 | tf_op jit(solution)/shard_map/ppermute | solution.py:360
  67.7 14.0 %collective-permute-start.1 = (bf16[32,16,256]{2,1,0:T(8,128)(2,1)}, bf16[32,16,256]{2,1,0:T(8,128)(2,1)S(1)}, u32[]{:S(2)}, u32[]{:S(2)}) collective-permute-start(bf16[32,16,256]{2,1,0:T(8,128)(2,1)} %get-tuple-element.11), channel_id=1, source_target_pairs={{4,0},{8,4},{12,8},{16,12},{20,16},{24,20},{28,24},{5,1},{9,5},{13... | collective-permute-start | bytes 786440 | tf_op jit(solution)/shard_map/ppermute | solution.py:365
  69.0 12.7 %collective-permute-start.2 = (bf16[32,256]{1,0:T(8,128)(2,1)}, bf16[32,256]{1,0:T(8,128)(2,1)S(1)}, u32[]{:S(2)}, u32[]{:S(2)}) collective-permute-start(bf16[32,256]{1,0:T(8,128)(2,1)} %get-tuple-element.12), channel_id=1, source_target_pairs={{0,1},{1,2},{2,3},{4,5},{5,6},{6,7},{8,9},{9,10},{10,11},{12,13},{... | collective-permute-start | bytes 49160 | tf_op jit(solution)/shard_map/ppermute | solution.py:360
  73.0 8.8 %collective-permute-start.3 = (bf16[32,256]{1,0:T(8,128)(2,1)}, bf16[32,256]{1,0:T(8,128)(2,1)S(1)}, u32[]{:S(2)}, u32[]{:S(2)}) collective-permute-start(bf16[32,256]{1,0:T(8,128)(2,1)} %get-tuple-element.13), channel_id=1, source_target_pairs={{1,0},{2,1},{3,2},{5,4},{6,5},{7,6},{9,8},{10,9},{11,10},{13,12},{... | collective-permute-start | bytes 49160 | tf_op jit(solution)/shard_map/ppermute | solution.py:365
  81.7 0.6 copy-start.4
  81.7 0.6 copy-start.5
  81.7 0.7 copy-start.2
  81.8 0.8 copy-start.3
  82.5 0.9 copy-start.1
where the time goes:
time: 144 us; the launch traced here: 143 us
  Pallas kernels  54.1 us (38%)
  blocking collectives  33 us (23%)
  starting transfers between devices  18.2 us (13%)
  local copies, waits for them, and re-layouts  14.7 us (10%)
  matrix products  13.9 us (10%)
  waiting for transfers between devices  5.73 us (4%)
  other arithmetic  3.04 us (2%)
    all_to_all x1, blocking collectives, body(): lax.all_to_all(active, 'lon', split_axis=0, concat_axis=0, tiled=True)  33 us
    pallas_call x1, Pallas kernels, chemistry(): pl.pallas_call(body, grid_spec=pltpu.PrefetchScalarGridSpec(num_scalar_pr...  23.5 us
    dot_general x1, matrix products, body(): lax.dot_general(spectral, legendre, (((3,), (1,)), ((2,), (0,))), preferr...  13.9 us
    pallas_call x1, Pallas kernels, synthesis(): pl.pallas_call(synth_kernel, grid=(rows,), in_specs=[pl.BlockSpec(recv.sh...  13.6 us
    pallas_call x1, Pallas kernels, tables(): pl.pallas_call(table_kernel, grid_spec=pltpu.PrefetchScalarGridSpec(num_s...  9.08 us
    all_to_all x1, waiting for transfers between devices, body(): recv = lax.all_to_all(sent, 'lat', split_axis=0, concat_axis=0, tiled=True)  5.72 us
    ppermute x2, starting transfers between devices, to_next(): return lax.ppermute(value, axis, [(i, i + 1) for i in range(size - 1)])  5.22 us
    all_to_all x1, starting transfers between devices, body(): recv = lax.all_to_all(sent, 'lat', split_axis=0, concat_axis=0, tiled=True)  5.17 us
  transfers between devices with their start and end apart: 6, of which 1 were waited for; matrix products, arithmetic and copies ran while one was open for 5% of the time, Pallas kernels for 9%

commit v1 on v0

v1 whole, which is shorter than its diff:
```python
import functools

import jax
import jax.numpy as jnp
import numpy as np
from jax import lax
from jax.experimental import pallas as pl
from jax.experimental.pallas import tpu as pltpu
from jax.sharding import PartitionSpec as P

F32 = jnp.float32
BF16 = jnp.bfloat16
LANES = 128
LOW = 16
STEP = 4
PARTS = 2
VMEM = 56 * 1024 * 1024

COS = (
    0.9999999890590228,
    -19.739204499454026,
    64.93911745990036,
    -85.45013953095037,
    60.16763095136588,
    -25.96759924965491,
    6.528658162567069,
)
SIN = (
    6.283185302511503,
    -41.34170040531769,
    81.60513138580204,
    -76.7030153539128,
    42.02592698618416,
    -14.899846668691637,
    3.238137510515757,
)


def dot(a, b, dims):
    return lax.dot_general(a, b, (dims, ((), ())), preferred_element_type=F32)


def cost(flops, moved):
    return pl.CostEstimate(flops=int(flops), bytes_accessed=int(moved), transcendentals=0)


def unit_circle(step, rows, waves, count):
    index = lax.broadcasted_iota(jnp.int32, (rows, waves.shape[1]), 0) * step
    product = index.astype(F32) * waves
    inverse = 1.0 / count
    turns = (product - jnp.floor(product * inverse) * count) * inverse
    y = turns - jnp.floor(turns + 0.5)
    z = y * y
    cosine = jnp.full_like(z, COS[-1])
    sine = jnp.full_like(z, SIN[-1])
    for c, s in zip(COS[-2::-1], SIN[-2::-1]):
        cosine = cosine * z + c
        sine = sine * z + s
    return cosine, sine * y


def table_kernel(points, waves_ref, table_ref, twiddle_ref):
    size, turns = waves_ref.shape[1], twiddle_ref.shape[2]
    waves = waves_ref[...]
    for k in range(table_ref.shape[0]):
        row = pl.program_id(0) * table_ref.shape[0] + k
        count = jnp.full(waves.shape, points[row], jnp.int32).astype(F32)
        cos_low, sin_low = unit_circle(1, LOW, waves, count)
        cos_high, sin_high = unit_circle(LOW, LANES // LOW, waves, count)
        cosine, sine = [], []
        for a in range(LANES // LOW):
            ch, sh = cos_high[a : a + 1], sin_high[a : a + 1]
            cosine.append(ch * cos_low - sh * sin_low)
            sine.append(-sh * cos_low - ch * sin_low)
        table_ref[k, :size, :] = jnp.concatenate(cosine, axis=0).T.astype(BF16)
        table_ref[k, size:, :] = jnp.concatenate(sine, axis=0).T.astype(BF16)
        cos_turn, sin_turn = unit_circle(LANES, turns, waves, count)
        twiddle_ref[k, 0] = cos_turn
        twiddle_ref[k, 1] = sin_turn


def tables(points, wave_ids, turns):
    rows, waves = points.shape[0], wave_ids.shape[0]
    each = STEP if rows % STEP == 0 else 1
    return pl.pallas_call(
        table_kernel,
        grid_spec=pltpu.PrefetchScalarGridSpec(
            num_scalar_prefetch=1,
            grid=(rows // each,),
            in_specs=[pl.BlockSpec((1, waves), lambda j, p: (0, 0))],
            out_specs=[
                pl.BlockSpec((each, 2 * waves, LANES), lambda j, p: (j, 0, 0)),
                pl.BlockSpec((each, 2, turns, waves), lambda j, p: (j, 0, 0, 0)),
            ],
        ),
        out_shape=[
            jax.ShapeDtypeStruct((rows, 2 * waves, LANES), BF16),
            jax.ShapeDtypeStruct((rows, 2, turns, waves), F32),
        ],
        compiler_params=pltpu.CompilerParams(vmem_limit_bytes=VMEM),
        cost_estimate=cost(rows * waves * LANES * 8, rows * waves * LANES * 4),
        name="tables",
    )(points, wave_ids.astype(F32)[None, :])


def place(pieces, width):
    out = [None] * (width // LANES)
    lane = lax.broadcasted_iota(jnp.int32, (pieces[0][0].shape[0], LANES), 1)
    for value, start, count, here in pieces:
        shift = (here - start) % LANES
        for a in range(start // LANES, (start + count - 1) // LANES + 1):
            part = value[:, a * LANES : (a + 1) * LANES]
            if shift:
                part = pltpu.roll(part, shift, 1)
            first = max(start, a * LANES) - start + here
            last = min(start + count, (a + 1) * LANES) - start + here
            for v in range(first // LANES, (last - 1) // LANES + 1):
                low, high = max(first - v * LANES, 0), min(last - v * LANES, LANES)
                if out[v] is None:
                    out[v] = part
                else:
                    out[v] = jnp.where((lane >= low) & (lane < high), part, out[v])
    return out


def synth_kernel(recv_ref, table_ref, twiddle_ref, *refs):
    *out_refs, coef, grid = refs
    sources, levels, rows, _ = recv_ref.shape
    fields, waves = coef.shape[0] // 2, coef.shape[1] * LANES
    share = waves // sources
    each, _, turns = twiddle_ref.shape[:3]
    step = pl.program_id(0)

    @pl.when(step == 0)
    def _():
        def level(l, carry):
            values = [recv_ref[s, l].astype(F32) for s in range(sources)]
            for r in range(2 * fields):
                windows = [
                    (values[s], r * share, share, s * share) for s in range(sources)
                ]
                for v, part in enumerate(place(windows, waves)):
                    coef[r, v, pl.ds(l * rows, rows), :] = part
            return carry

        lax.fori_loop(0, levels, level, 0)

    for k in range(each):
        j = step * each + k

        def own_row(r):
            parts = [coef[r, v, pl.ds(j, levels, stride=rows), :] for v in range(waves // LANES)]
            return jnp.concatenate(parts, axis=1)

        values = [own_row(r) for r in range(2 * fields)]
        real, imag = [], []
        for t in range(turns):
            c, s = twiddle_ref[k, 0, t : t + 1], twiddle_ref[k, 1, t : t + 1]
            for f in range(fields):
                re, im = values[2 * f], values[2 * f + 1]
                real.append(re * c - im * s)
                imag.append(re * s + im * c)
        both = [jnp.concatenate(part, axis=0).astype(BF16) for part in (real, imag)]
        result = dot(jnp.concatenate(both, axis=1), table_ref[k], ((1,), (0,)))
        grid[pl.ds(j, turns * fields * levels, stride=rows), :] = result

    @pl.when(step == pl.num_programs(0) - 1)
    def _():
        dests = out_refs[0].shape[0]
        tiles = turns // dests
        size = levels * rows
        some = levels // len(out_refs)
        for t in range(turns):
            lanes = slice((t % tiles) * LANES, (t % tiles + 1) * LANES)
            for f in range(fields):
                block = grid[(t * fields + f) * size : (t * fields + f + 1) * size, :]
                block = block.reshape(levels, rows, LANES).astype(BF16)
                for p, out_ref in enumerate(out_refs):
                    out_ref[t // tiles, f, :, :, lanes] = block[p * some : (p + 1) * some]


def synthesis(recv, table, twiddle, dests, tile, parts):
    sources, levels, rows, lanes = recv.shape
    turns, waves = twiddle.shape[2:]
    fields = 3
    each = STEP if rows % STEP == 0 else 1
    shape = (dests, fields, levels // parts, rows, tile)
    return pl.pallas_call(
        synth_kernel,
        grid=(rows // each,),
        in_specs=[
            pl.BlockSpec(recv.shape, lambda j: (0, 0, 0, 0)),
            pl.BlockSpec((each, 2 * waves, LANES), lambda j: (j, 0, 0)),
            pl.BlockSpec((each, 2, turns, waves), lambda j: (j, 0, 0, 0)),
        ],
        out_specs=[pl.BlockSpec(shape, lambda j: (0, 0, 0, 0, 0))] * parts,
        out_shape=[jax.ShapeDtypeStruct(shape, BF16)] * parts,
        scratch_shapes=[
            pltpu.VMEM((2 * fields, waves // LANES, levels * rows, LANES), F32),
            pltpu.VMEM((turns * fields * levels * rows, LANES), F32),
        ],
        compiler_params=pltpu.CompilerParams(vmem_limit_bytes=VMEM),
        cost_estimate=cost(4 * rows * waves * fields * levels * turns * LANES, 4 * rows * waves * LANES),
        name="synthesis",
    )(recv, table, twiddle)


def edge_kernel(
    state_ref, pick_ref, base_ref, temp_ref, first_ref, last_ref, west_ref, east_ref, react_ref
):
    tracers, levels, rows, tile = state_ref.shape
    cells = tracers * rows

    @pl.when(pl.program_id(0) == 0)
    def _():
        rates = jnp.concatenate([base_ref[...], temp_ref[...]], axis=0)
        high = rates.astype(BF16)
        low = (rates - high.astype(F32)).astype(BF16)

        def iota(shape, axis):
            return lax.broadcasted_iota(jnp.int32, shape, axis)

        shape = (2 * cells, 2 * tracers)
        down = jnp.where(iota(shape, 0) // rows == iota(shape, 1), 1.0, 0.0).astype(BF16)
        shape = (tracers, cells)
        over = jnp.where(iota(shape, 0) == iota(shape, 1) // rows, 1.0, 0.0).astype(BF16)
        shape = (2 * cells, cells)
        same = iota(shape, 0) % rows == iota(shape, 1) % rows
        for k, part in enumerate((high, low)):
            wide = dot(dot(down, part, ((1,), (0,))).astype(BF16), over, ((1,), (0,)))
            react_ref[:, k * cells : (k + 1) * cells] = jnp.where(same, wide, 0.0).astype(BF16)

    ends = lax.broadcasted_iota(jnp.int32, (2 * levels, tile), 1)
    row = lax.broadcasted_iota(jnp.int32, (2 * levels, tile), 0)
    columns = jnp.zeros((2 * levels, tracers * rows), F32)
    for l in range(levels):
        x = state_ref[:, l].reshape(tracers * rows, tile)
        picked = dot(pick_ref[...], x, ((1,), (0,)))
        first_ref[l] = picked[:tracers].astype(BF16)
        last_ref[l] = picked[tracers:].astype(BF16)
        mark = ((row == l) & (ends == 0)) | ((row == levels + l) & (ends == tile - 1))
        columns = columns + dot(jnp.where(mark, 1.0, 0.0).astype(BF16), x, ((1,), (1,)))
    west_ref[...] = columns[:levels].astype(BF16)
    east_ref[...] = columns[levels:].astype(BF16)


def edges(state, react_base, react_temp):
    tracers, levels, rows, tile = state.shape
    block = 16
    pick = np.zeros((2 * tracers, tracers * rows), np.float32)
    for t in range(tracers):
        pick[t, t * rows] = 1
        pick[tracers + t, t * rows + rows - 1] = 1
    rowed = jax.ShapeDtypeStruct((levels, tracers, tile), BF16)
    columned = jax.ShapeDtypeStruct((levels, tracers * rows), BF16)
    row_spec = pl.BlockSpec((block, tracers, tile), lambda i: (i, 0, 0))
    col_spec = pl.BlockSpec((block, tracers * rows), lambda i: (i, 0))
    wide = (2 * tracers * rows, 2 * tracers * rows)
    return pl.pallas_call(
        edge_kernel,
        grid=(levels // block,),
        in_specs=[
            pl.BlockSpec((tracers, block, rows, tile), lambda i: (0, i, 0, 0)),
            pl.BlockSpec(pick.shape, lambda i: (0, 0)),
            pl.BlockSpec(react_base.shape, lambda i: (0, 0)),
            pl.BlockSpec(react_temp.shape, lambda i: (0, 0)),
        ],
        out_specs=[row_spec, row_spec, col_spec, col_spec, pl.BlockSpec(wide, lambda i: (0, 0))],
        out_shape=[rowed, rowed, columned, columned, jax.ShapeDtypeStruct(wide, BF16)],
        cost_estimate=cost(4 * state.size * 32, 2 * state.size),
        compiler_params=pltpu.CompilerParams(vmem_limit_bytes=VMEM),
        name="edges",
    )(state, jnp.asarray(pick, BF16), react_base, react_temp)


def chem_kernel(scale, part, parts, ids, *refs):
    (state_ref, south_ref, north_ref, west_ref, east_ref, grid_ref, mask_ref, react_ref) = refs[:8]
    along_ref, across_ref = refs[8:10]
    new_ref, active_ref, south, north = refs[-4:]
    tracers, levels, rows, tile = state_ref.shape
    cells = tracers * rows
    half, side = rows // 2, tile // 2
    first = (pl.program_id(0) * parts + part) * levels

    def column(ref):
        value = ref[...].astype(F32)
        pad = jnp.zeros((LANES - value.shape[0], cells), F32)
        return pltpu.roll(jnp.concatenate([value, pad], axis=0).T, lax.rem(LANES - first, LANES), 1)

    west, east = column(west_ref), column(east_ref)
    row = lax.broadcasted_iota(jnp.int32, (rows, tile), 0)
    lane = lax.broadcasted_iota(jnp.int32, (rows, tile), 1)
    mask = mask_ref[...]
    nn = ((1,), (0,))

    def three(v):
        return v.reshape(tracers, rows, tile)

    for l in range(levels):
        x = state_ref[:, l].reshape(cells, tile)
        lon = dot(x, along_ref[...], nn)
        lat = dot(across_ref[...], x, nn)
        wind_u = grid_ref[0, 0, l].astype(F32) * (scale * 0.1)
        wind_v = grid_ref[0, 1, l].astype(F32) * (scale * 0.1)
        temper = grid_ref[0, 2, l].astype(F32) * scale
        moved = (
            three(x.astype(F32))
            - wind_u * three(lon[:, :tile])
            - wind_v * three(lat[:cells])
            + 0.05 * three(lon[:, tile:] + lat[cells:])
        )
        south[...] = south_ref[l].astype(F32)
        north[...] = north_ref[l].astype(F32)
        in_row = jnp.where(row == 0, 0.05 + wind_v, jnp.where(row == rows - 1, 0.05 - wind_v, 0.0))
        in_col = jnp.where(lane == 0, 0.05 + wind_u, jnp.where(lane == tile - 1, 0.05 - wind_u, 0.0))
        outer = []
        for t in range(tracers):
            up = [jnp.broadcast_to(ref[t : t + 1], (half, tile)) for ref in (south, north)]
            cell = slice(t * rows, (t + 1) * rows)
            across = [
                jnp.broadcast_to(col[cell, l : l + 1], (rows, side)) for col in (west, east)
            ]
            outer.append(
                in_row * jnp.concatenate(up, axis=0) + in_col * jnp.concatenate(across, axis=1)
            )
        moved = moved + jnp.stack(outer, axis=0)
        high = moved.reshape(cells, tile).astype(BF16)
        terms = dot(react_ref[...], jnp.concatenate([high, high], axis=0), nn)
        reacted = (moved + three(terms[:cells]) + temper * three(terms[cells:])) * mask
        new_ref[:, l] = reacted.astype(BF16)
        for a in range(active_ref.shape[1]):
            active_ref[0, a, l] = new_ref[ids[a], l]


def chemistry(state, halos, grid, mask, react, active_ids, waves, part, parts, before):
    tracers, levels, rows, tile = state.shape
    sources, fields, some = grid.shape[:3]
    south, north, west, east = halos
    actives = active_ids.shape[0]
    cells = tracers * rows
    eye, one = np.eye(tracers), np.eye(tile)
    along = np.concatenate(
        [np.eye(tile, k=-1) - np.eye(tile, k=1), np.eye(tile, k=-1) + np.eye(tile, k=1) - 4 * one], 1
    )
    down, up = np.eye(rows, k=-1), np.eye(rows, k=1)
    across = np.concatenate([np.kron(eye, up - down), np.kron(eye, up + down)], 0)
    scale = 1.0 / float(np.sqrt(np.float32(waves)))

    def whole(shape):
        return pl.BlockSpec(shape, lambda i, ids: (0,) * len(shape))

    def leveled(*shape):
        return pl.BlockSpec((some,) + shape, lambda i, ids: (i * parts + part, 0, 0))

    state_spec = pl.BlockSpec((tracers, some, rows, tile), lambda i, ids: (0, i * parts + part, 0, 0))
    operands = [
        state, south, north, west, east, grid, mask, react,
        jnp.asarray(along, BF16), jnp.asarray(across, BF16),
    ]
    in_specs = [
        state_spec,
        leveled(tracers, tile),
        leveled(tracers, tile),
        whole(west.shape),
        whole(east.shape),
        pl.BlockSpec((1, fields, some, rows, tile), lambda i, ids: (i, 0, 0, 0, 0)),
        whole(mask.shape),
        whole(react.shape),
        whole(along.shape),
        whole(across.shape),
    ]
    aliases = {}
    if before is not None:
        aliases = {1 + len(operands): 0}
        operands.append(before)
        in_specs.append(pl.BlockSpec(memory_space=pl.ANY))
    return pl.pallas_call(
        functools.partial(chem_kernel, scale, part, parts),
        grid_spec=pltpu.PrefetchScalarGridSpec(
            num_scalar_prefetch=1,
            grid=(sources,),
            in_specs=in_specs,
            out_specs=[
                state_spec,
                pl.BlockSpec((1, actives, some, rows, tile), lambda i, ids: (i, 0, 0, 0, 0)),
            ],
            scratch_shapes=[pltpu.VMEM((tracers, tile), F32)] * 2,
        ),
        out_shape=[
            jax.ShapeDtypeStruct(state.shape, BF16),
            jax.ShapeDtypeStruct((sources, actives, some, rows, tile), BF16),
        ],
        input_output_aliases=aliases,
        compiler_params=pltpu.CompilerParams(vmem_limit_bytes=VMEM),
        cost_estimate=cost(state.size // parts * 2 * 2048, state.size // parts * 4),
        name="chemistry",
    )(active_ids, *operands)


def spread_kernel(recv_ref, *refs):
    out_ref = refs[-1]
    tile = recv_ref.shape[4]
    for s in range(recv_ref.shape[0]):
        out_ref[:, :, :, s * tile : (s + 1) * tile] = recv_ref[s].astype(F32)


def spread(recv, part, parts, before):
    sources, actives, some, rows, tile = recv.shape
    each = 2 if actives % 2 == 0 else 1
    operands = [recv]
    in_specs = [pl.BlockSpec((sources, each, some, rows, tile), lambda a: (0, a, 0, 0, 0))]
    aliases = {}
    if before is not None:
        operands.append(before)
        in_specs.append(pl.BlockSpec(memory_space=pl.ANY))
        aliases = {1: 0}
    return pl.pallas_call(
        spread_kernel,
        grid=(actives // each,),
        in_specs=in_specs,
        out_specs=pl.BlockSpec((each, some, rows, sources * tile), lambda a: (a, part, 0, 0)),
        out_shape=jax.ShapeDtypeStruct((actives, some * parts, rows, sources * tile), F32),
        input_output_aliases=aliases,
        compiler_params=pltpu.CompilerParams(vmem_limit_bytes=VMEM),
        cost_estimate=cost(recv.size, recv.size * 6),
        name="spread",
    )(*operands)


def to_next(value, axis):
    size = lax.axis_size(axis)
    return lax.ppermute(value, axis, [(i, i + 1) for i in range(size - 1)])


def to_previous(value, axis):
    size = lax.axis_size(axis)
    return lax.ppermute(value, axis, [(i + 1, i) for i in range(size - 1)])


def body(spectral, legendre, wave_ids, points, tracers, react_base, react_temp, active_ids):
    bands, tiles = lax.axis_size("lat"), lax.axis_size("lon")
    count, levels, rows, tile = tracers.shape
    own, share = spectral.shape[1:3]
    waves = wave_ids.shape[0]

    fourier = lax.dot_general(
        spectral, legendre, (((3,), (1,)), ((2,), (0,))), preferred_element_type=F32
    ).astype(BF16)
    fourier = fourier.reshape(share, 6, own, bands, rows)
    sent = jnp.transpose(fourier, (3, 2, 4, 1, 0)).reshape(bands, own, rows, 6 * share)
    sent = jnp.pad(sent, ((0, 0), (0, 0), (0, 0), (0, -(6 * share) % LANES)))
    recv = lax.all_to_all(sent, "lat", split_axis=0, concat_axis=0, tiled=True)

    first, last, west, east, react = edges(tracers, react_base, react_temp)
    halos = (
        to_next(last, "lat"),
        to_previous(first, "lat"),
        to_next(east, "lon"),
        to_previous(west, "lon"),
    )
    table, twiddle = tables(points, wave_ids, tiles * tile // LANES)
    columns = lax.axis_index("lon") * tile + jnp.arange(tile)
    mask = (columns[None, :] < points[:, None]).astype(F32)
    recv, table, twiddle, halos, mask = lax.optimization_barrier(
        (recv, table, twiddle, halos, mask)
    )

    parts = PARTS if own % PARTS == 0 else 1
    grids = synthesis(recv, table, twiddle, tiles, tile, parts)
    grids = [lax.all_to_all(g, "lon", split_axis=0, concat_axis=0, tiled=True) for g in grids]
    new, sent = None, []
    for p, grid in enumerate(grids):
        new, active = chemistry(
            tracers, halos, grid, mask, react, active_ids, waves, p, parts, new
        )
        sent.append(lax.all_to_all(active, "lon", split_axis=0, concat_axis=0, tiled=True))
    spreaded = None
    for p, active in enumerate(sent):
        spreaded = spread(active, p, parts, spreaded)
    return new, spreaded


def solution(mesh):
    return jax.shard_map(
        body,
        mesh=mesh,
        in_specs=(
            P(None, "lon", "lat", None),
            P("lat", None, None),
            P(),
            P("lat"),
            P(None, None, "lat", "lon"),
            P(),
            P(),
            P(),
        ),
        out_specs=(P(None, None, "lat", "lon"), P(None, "lon", "lat", None)),
        check_vma=False,
    )
```

time: 144 us -> 131 us (0.910)
  blocking collectives: 33 us -> 17.2 us
  waiting for transfers between devices: 5.73 us -> 20.1 us
  Pallas kernels: 54.1 us -> 43.7 us
  starting transfers between devices: 18.2 us -> 23.9 us
  local copies, waits for them, and re-layouts: 14.7 us -> 9.75 us
  other arithmetic: 3.04 us -> 0.68 us
    all_to_all x1 -> x3, waiting for transfers between devices: 0.01 us -> 20.1 us  [the longest x2 17.3 us: body(): lax.all_to_all(active, 'lon', split_axis=0, concat_axis=0, tiled=True)]
    all_to_all x1, blocking collectives: 33 us -> 17.2 us  [body(): lax.all_to_all(g, 'lon', split_axis=0, concat_axis=0, tiled=True)]
    pallas_call x3 -> x5, Pallas kernels: 40.7 us -> 32.2 us  [the longest x2 19.9 us: chemistry(): pl.pallas_call(functools.partial(chem_kernel, scale, part, parts), grid_s...]
    all_to_all x1, waiting for transfers between devices: 5.72 us -> 0.01 us  [body(): recv = lax.all_to_all(sent, 'lat', split_axis=0, concat_axis=0, tiled=True)]
    all_to_all x1 -> x3, starting transfers between devices: 5.01 us -> 10.6 us  [the longest x2 6.94 us: body(): lax.all_to_all(active, 'lon', split_axis=0, concat_axis=0, tiled=True)]
    mul x1 -> x0, local copies, waits for them, and re-layouts: 4.2 us -> none  [body(): react[:, None, :, None] * eye[None, :, None, :]]
    pallas_call x1, Pallas kernels: 9.08 us -> 6.53 us  [tables(): pl.pallas_call(table_kernel, grid_spec=pltpu.PrefetchScalarGridSpec(num_s...]
    mul x1 -> x0, other arithmetic: 2.35 us -> none  [body(): react[:, None, :, None] * eye[None, :, None, :]]
  transfers between devices with their start and end apart: 6 -> 8, of which waited for: 1 -> 3; matrix products, arithmetic and copies ran while one was open for 5% -> 1% of each run, Pallas kernels for 9% -> 26%
where the time goes in v1:
time: 131 us; the launch traced here: 130 us
  Pallas kernels  43.7 us (33%)
  starting transfers between devices  23.9 us (18%)
  waiting for transfers between devices  20.1 us (15%)
  blocking collectives  17.2 us (13%)
  matrix products  13.9 us (11%)
  local copies, waits for them, and re-layouts  9.75 us (7%)
    pallas_call x2, Pallas kernels, chemistry(): pl.pallas_call(functools.partial(chem_kernel, scale, part, parts), grid_s...  19.9 us
    all_to_all x2, waiting for transfers between devices, body(): lax.all_to_all(active, 'lon', split_axis=0, concat_axis=0, tiled=True)  17.3 us
    all_to_all x1, blocking collectives, body(): lax.all_to_all(g, 'lon', split_axis=0, concat_axis=0, tiled=True)  17.2 us
    dot_general x1, matrix products, body(): lax.dot_general(spectral, legendre, (((3,), (1,)), ((2,), (0,))), preferr...  13.9 us
    pallas_call x1, Pallas kernels, synthesis(): pl.pallas_call(synth_kernel, grid=(rows // each,), in_specs=[pl.BlockSpec...  8.41 us
    all_to_all x2, starting transfers between devices, body(): lax.all_to_all(active, 'lon', split_axis=0, concat_axis=0, tiled=True)  6.94 us
    pallas_call x1, Pallas kernels, tables(): pl.pallas_call(table_kernel, grid_spec=pltpu.PrefetchScalarGridSpec(num_s...  6.53 us
    ppermute x2, starting transfers between devices, to_next(): return lax.ppermute(value, axis, [(i, i + 1) for i in range(size - 1)])  5.61 us
  transfers between devices with their start and end apart: 8, of which 3 were waited for; matrix products, arithmetic and copies ran while one was open for 1% of the time, Pallas kernels for 26%

profile of v1, /device:TPU:0, one launch (start us, length us, event | category | flops | bytes accessed | tf_op | source)
XLA Modules:
  0.0 130.1 jit_solution(16213043515319077652)
XLA Ops:
  0.6 13.9 %fusion.3 = bf16[80,6,8,128]{3,2,1,0:T(8,128)(2,1)S(1)} fusion(bf16[80,1280,128]{2,1,0:T(8,128)(2,1)} %param.14, bf16[6,8,80,1280]{3,2,1,0:T(8,128)(2,1)} %param.13), kind=kOutput, calls=%fused_computation.3 | convolution fusion | flops 1258782720 | bytes 37027840 | tf_op jit(solution)/shard_map/dot_general | solution.py:446
  14.5 0.0 copy-start.5
  14.6 0.0 copy-start.4
  14.6 1.6 %copy.20 = bf16[80,6,8,128]{0,3,2,1:T(8,128)(2,1)} copy(bf16[80,6,8,128]{3,2,1,0:T(8,128)(2,1)S(1)} %fusion.3) | data formatting | bytes 1966080 | tf_op jit(solution)/shard_map/convert_element_type | solution.py:448
  16.2 3.3 %copy.21 = bf16[8,8,16,6,80]{4,3,2,1,0:T(8,128)(2,1)S(1)} copy(bf16[8,8,16,6,80]{4,2,0,1,3:T(8,128)(2,1)} %bitcast.10) | data formatting | bytes 1966080 | tf_op jit(solution)/shard_map/transpose | solution.py:450
  19.5 1.2 reshape.16
  20.7 1.2 pad.4
  21.9 5.2 %all-to-all-start = ((bf16[8,8,16,512]{3,2,1,0:T(8,128)(2,1)}), bf16[8,8,16,512]{3,2,1,0:T(8,128)(2,1)S(1)}, u32[]{:S(2)}, u32[]{:S(2)}) async-start(bf16[8,8,16,512]{3,2,1,0:T(8,128)(2,1)} %pad.4), calls=%async_computation | async-start | bytes 2097152 | tf_op jit(solution)/shard_map/all_to_all | solution.py:452
  27.1 4.9 %edges.1 = (bf16[32,16,256]{2,1,0:T(8,128)(2,1)}, bf16[32,16,256]{2,1,0:T(8,128)(2,1)}, bf16[32,256]{1,0:T(8,128)(2,1)}, bf16[32,256]{1,0:T(8,128)(2,1)}, bf16[512,512]{1,0:T(8,128)(2,1)}) custom-call(bf16[16,32,16,256]{3,2,1,0:T(8,128)(2,1)} %refs_0_.3, bf16[32,256]{1,0:T(8,128)(2,1)} %constant.15.clone.pick_ref, f32[16,16]{1,0:T(8,128)} %base_ref.1, ...), custom_call_target="tpu_custom_call" | custom-call | flops 268435456 | bytes 4194304 | tf_op jit(solution)/shard_map/edges/pallas_call | solution.py:259
  32.0 3.5 %collective-permute-start.2 = (bf16[32,256]{1,0:T(8,128)(2,1)}, bf16[32,256]{1,0:T(8,128)(2,1)S(1)}, u32[]{:S(2)}, u32[]{:S(2)}) collective-permute-start(bf16[32,256]{1,0:T(8,128)(2,1)} %get-tuple-element.27), channel_id=1, source_target_pairs={{0,1},{1,2},{2,3},{4,5},{5,6},{6,7},{8,9},{9,10},{10,11},{12,13},{... | collective-permute-start | bytes 49160 | tf_op jit(solution)/shard_map/ppermute | solution.py:432
  35.5 1.3 collective-permute-start.3
  36.8 2.1 %collective-permute-start = (bf16[32,16,256]{2,1,0:T(8,128)(2,1)}, bf16[32,16,256]{2,1,0:T(8,128)(2,1)S(1)}, u32[]{:S(2)}, u32[]{:S(2)}) collective-permute-start(bf16[32,16,256]{2,1,0:T(8,128)(2,1)} %get-tuple-element.25), channel_id=1, source_target_pairs={{0,4},{4,8},{8,12},{12,16},{16,20},{20,24},{24,28},{1,5},{5,9},{9,... | collective-permute-start | bytes 786440 | tf_op jit(solution)/shard_map/ppermute | solution.py:432
  38.9 1.3 collective-permute-start.1
  40.3 0.0 copy-done.5
  40.3 0.7 compare_convert_fusion.refs_6_
  40.9 0.0 copy-done.4
  40.9 0.6 broadcast_in_dim.2.waves_ref
  41.5 6.5 %tables.1 = (bf16[16,1280,128]{2,1,0:T(8,128)(2,1)}, f32[16,2,8,640]{3,2,1,0:T(8,128)}) custom-call(s32[16]{0:T(128)} %points.1, f32[1,640]{1,0:T(1,128)} %broadcast_in_dim.2.waves_ref), custom_call_target="tpu_custom_call" | custom-call | flops 10485760 | bytes 5242880 | tf_op jit(solution)/shard_map/tables/pallas_call | solution.py:85
  48.1 0.0 collective-permute-done.2.refs_3_
  48.1 0.0 copy-start.8
  48.1 0.0 collective-permute-done.3.refs_4_
  48.1 0.0 copy-start.9
  48.1 0.0 collective-permute-done.refs_1_
  48.1 0.0 copy-start.6
  48.1 0.0 collective-permute-done.1.refs_2_
  48.1 0.0 copy-start.7
  48.1 0.0 all-to-all-done.recv_ref
  48.1 0.0 copy-start
  48.1 1.0 copy-done
  49.2 8.4 %synthesis.1 = (bf16[4,3,4,16,256]{4,3,2,1,0:T(8,128)(2,1)}, bf16[4,3,4,16,256]{4,3,2,1,0:T(8,128)(2,1)}) custom-call(bf16[8,8,16,512]{3,2,1,0:T(8,128)(2,1)} %copy-done, bf16[16,1280,128]{2,1,0:T(8,128)(2,1)} %get-tuple-element.34.table_ref, f32[16,2,8,640]{3,2,1,0:T(8,128)} %get-tuple-element.35.twiddle_ref), custom_call_target="tpu_custom_call" | custom-call | flops 1006632960 | bytes 5242880 | tf_op jit(solution)/shard_map/synthesis/pallas_call | solution.py:188
  57.6 17.2 %all_to_all.25.refs_5_ = bf16[4,3,4,16,256]{4,3,2,1,0:T(8,128)(2,1)} all-to-all(bf16[4,3,4,16,256]{4,3,2,1,0:T(8,128)(2,1)} %get-tuple-element.39), channel_id=1, replica_groups=mesh['lat'=8,'lon'=4] {'lon'}, dimensions={0} | all-to-all | bytes 786432 | tf_op jit(solution)/shard_map/all_to_all | solution.py:470
  74.8 3.6 %all-to-all-start.1 = ((bf16[4,3,4,16,256]{4,3,2,1,0:T(8,128)(2,1)}), bf16[4,3,4,16,256]{4,3,2,1,0:T(8,128)(2,1)S(1)}, u32[]{:S(2)}, u32[]{:S(2)}) async-start(bf16[4,3,4,16,256]{4,3,2,1,0:T(8,128)(2,1)} %get-tuple-element.36), calls=%async_computation.1 | async-start | bytes 786432 | tf_op jit(solution)/shard_map/all_to_all | solution.py:470
  78.4 0.0 copy-done.8
  78.4 0.0 copy-done.9
  78.4 0.0 copy-done.6
  78.4 0.0 copy-done.7
  78.4 9.9 %chemistry.2 = (bf16[16,32,16,256]{3,2,1,0:T(8,128)(2,1)}, bf16[4,4,4,16,256]{4,3,2,1,0:T(8,128)(2,1)}) custom-call(s32[4]{0:T(128)} %ids.3, bf16[16,32,16,256]{3,2,1,0:T(8,128)(2,1)} %refs_0_.3, bf16[32,16,256]{2,1,0:T(8,128)(2,1)} %copy-done.6, bf16[32,16,256]{2,1,0:T(8,128)(2,1)} %copy-done.7, bf16[32,256]{1,0:T(8,128)(2,1)} %copy-done.8, ...), custom_call_target="tpu_custom_call" | custom-call | flops 4294967296 | bytes 4194304 | tf_op jit(solution)/shard_map/chemistry/pallas_call | solution.py:377
  88.4 2.8 %all-to-all-done.1.refs_5_ = bf16[4,3,4,16,256]{4,3,2,1,0:T(8,128)(2,1)S(1)} async-done(((bf16[4,3,4,16,256]{4,3,2,1,0:T(8,128)(2,1)}), bf16[4,3,4,16,256]{4,3,2,1,0:T(8,128)(2,1)S(1)}, u32[]{:S(2)}, u32[]{:S(2)}) %all-to-all-start.1) | async-done | bytes 393248 | tf_op jit(solution)/shard_map/all_to_all | solution.py:470
  91.2 0.0 copy-start.3
  91.2 3.5 %all-to-all-start.4 = ((bf16[4,4,4,16,256]{4,3,2,1,0:T(8,128)(2,1)}), bf16[4,4,4,16,256]{4,3,2,1,0:T(8,128)(2,1)S(1)}, u32[]{:S(2)}, u32[]{:S(2)}) async-start(bf16[4,4,4,16,256]{4,3,2,1,0:T(8,128)(2,1)} %get-tuple-element.43), calls=%async_computation.4 | async-start | bytes 1048576 | tf_op jit(solution)/shard_map/all_to_all | solution.py:476
  94.7 0.0 copy-done.3
  94.7 9.9 %chemistry.3 = (bf16[16,32,16,256]{3,2,1,0:T(8,128)(2,1)}, bf16[4,4,4,16,256]{4,3,2,1,0:T(8,128)(2,1)}) custom-call(s32[4]{0:T(128)} %ids.3, bf16[16,32,16,256]{3,2,1,0:T(8,128)(2,1)} %refs_0_.3, bf16[32,16,256]{2,1,0:T(8,128)(2,1)} %copy-done.6, bf16[32,16,256]{2,1,0:T(8,128)(2,1)} %copy-done.7, ...), custom_call_target="tpu_custom_call", output_to_operand_aliasing={{0}: (11, {})} | custom-call | flops 4294967296 | bytes 4194304 | tf_op jit(solution)/shard_map/chemistry/pallas_call | solution.py:377
  104.6 5.1 %all-to-all-done.4.recv_ref = bf16[4,4,4,16,256]{4,3,2,1,0:T(8,128)(2,1)S(1)} async-done(((bf16[4,4,4,16,256]{4,3,2,1,0:T(8,128)(2,1)}), bf16[4,4,4,16,256]{4,3,2,1,0:T(8,128)(2,1)S(1)}, u32[]{:S(2)}, u32[]{:S(2)}) %all-to-all-start.4) | async-done | bytes 524320 | tf_op jit(solution)/shard_map/all_to_all | solution.py:476
  109.7 0.0 copy-start.1
  109.7 3.5 %all-to-all-start.3 = ((bf16[4,4,4,16,256]{4,3,2,1,0:T(8,128)(2,1)}), bf16[4,4,4,16,256]{4,3,2,1,0:T(8,128)(2,1)S(1)}, u32[]{:S(2)}, u32[]{:S(2)}) async-start(bf16[4,4,4,16,256]{4,3,2,1,0:T(8,128)(2,1)} %get-tuple-element.42), calls=%async_computation.3 | async-start | bytes 1048576 | tf_op jit(solution)/shard_map/all_to_all | solution.py:476
  113.2 0.0 copy-done.1
  113.2 2.0 %spread.2.refs_0_ = f32[4,8,16,1024]{3,2,1,0:T(8,128)} custom-call(bf16[4,4,4,16,256]{4,3,2,1,0:T(8,128)(2,1)} %copy-done.1), custom_call_target="tpu_custom_call" | custom-call | flops 262144 | bytes 1572864 | tf_op jit(solution)/shard_map/spread/pallas_call | solution.py:417
  115.2 12.2 %all-to-all-done.3.recv_ref = bf16[4,4,4,16,256]{4,3,2,1,0:T(8,128)(2,1)S(1)} async-done(((bf16[4,4,4,16,256]{4,3,2,1,0:T(8,128)(2,1)}), bf16[4,4,4,16,256]{4,3,2,1,0:T(8,128)(2,1)S(1)}, u32[]{:S(2)}, u32[]{:S(2)}) %all-to-all-start.3) | async-done | bytes 524320 | tf_op jit(solution)/shard_map/all_to_all | solution.py:476
  127.4 0.0 copy-start.2
  127.4 0.8 copy-done.2
  128.2 2.0 %spread.3 = f32[4,8,16,1024]{3,2,1,0:T(8,128)} custom-call(bf16[4,4,4,16,256]{4,3,2,1,0:T(8,128)(2,1)} %copy-done.2, f32[4,8,16,1024]{3,2,1,0:T(8,128)} %spread.2.refs_0_), custom_call_target="tpu_custom_call", output_to_operand_aliasing={{}: (1, {})} | custom-call | flops 262144 | bytes 1572864 | tf_op jit(solution)/shard_map/spread/pallas_call | solution.py:417
  (2 shorter events, 0.0 us)
Async XLA Ops:
  14.5 25.7 %copy-start.5 = (s32[16]{0:T(128)S(1)}, s32[16]{0:T(128)}, u32[]{:S(2)}) copy-start(s32[16]{0:T(128)} %points.1) | copy-start | bytes 196
  14.6 26.4 %copy-start.4 = (s32[640]{0:T(1024)S(1)}, s32[640]{0:T(1024)}, u32[]{:S(2)}) copy-start(s32[640]{0:T(1024)} %param.15) | copy-start | bytes 7684
  21.9 26.2 %all-to-all-start = ((bf16[8,8,16,512]{3,2,1,0:T(8,128)(2,1)}), bf16[8,8,16,512]{3,2,1,0:T(8,128)(2,1)S(1)}, u32[]{:S(2)}, u32[]{:S(2)}) async-start(bf16[8,8,16,512]{3,2,1,0:T(8,128)(2,1)} %pad.4), calls=%async_computation | async-start | bytes 2097152 | tf_op jit(solution)/shard_map/all_to_all | solution.py:452
  32.0 16.0 %collective-permute-start.2 = (bf16[32,256]{1,0:T(8,128)(2,1)}, bf16[32,256]{1,0:T(8,128)(2,1)S(1)}, u32[]{:S(2)}, u32[]{:S(2)}) collective-permute-start(bf16[32,256]{1,0:T(8,128)(2,1)} %get-tuple-element.27), channel_id=1, source_target_pairs={{0,1},{1,2},{2,3},{4,5},{5,6},{6,7},{8,9},{9,10},{10,11},{12,13},{... | collective-permute-start | bytes 49160 | tf_op jit(solution)/shard_map/ppermute | solution.py:432
  35.5 12.6 %collective-permute-start.3 = (bf16[32,256]{1,0:T(8,128)(2,1)}, bf16[32,256]{1,0:T(8,128)(2,1)S(1)}, u32[]{:S(2)}, u32[]{:S(2)}) collective-permute-start(bf16[32,256]{1,0:T(8,128)(2,1)} %get-tuple-element.28), channel_id=1, source_target_pairs={{1,0},{2,1},{3,2},{5,4},{6,5},{7,6},{9,8},{10,9},{11,10},{13,12},{... | collective-permute-start | bytes 49160 | tf_op jit(solution)/shard_map/ppermute | solution.py:437
  36.8 11.3 %collective-permute-start = (bf16[32,16,256]{2,1,0:T(8,128)(2,1)}, bf16[32,16,256]{2,1,0:T(8,128)(2,1)S(1)}, u32[]{:S(2)}, u32[]{:S(2)}) collective-permute-start(bf16[32,16,256]{2,1,0:T(8,128)(2,1)} %get-tuple-element.25), channel_id=1, source_target_pairs={{0,4},{4,8},{8,12},{12,16},{16,20},{20,24},{24,28},{1,5},{5,9},{9,... | collective-permute-start | bytes 786440 | tf_op jit(solution)/shard_map/ppermute | solution.py:432
  38.9 9.2 %collective-permute-start.1 = (bf16[32,16,256]{2,1,0:T(8,128)(2,1)}, bf16[32,16,256]{2,1,0:T(8,128)(2,1)S(1)}, u32[]{:S(2)}, u32[]{:S(2)}) collective-permute-start(bf16[32,16,256]{2,1,0:T(8,128)(2,1)} %get-tuple-element.26), channel_id=1, source_target_pairs={{4,0},{8,4},{12,8},{16,12},{20,16},{24,20},{28,24},{5,1},{9,5},{13... | collective-permute-start | bytes 786440 | tf_op jit(solution)/shard_map/ppermute | solution.py:437
  48.1 30.4 %copy-start.8 = (bf16[32,256]{1,0:T(8,128)(2,1)}, bf16[32,256]{1,0:T(8,128)(2,1)S(1)}, u32[]{:S(2)}) copy-start(bf16[32,256]{1,0:T(8,128)(2,1)S(1)} %collective-permute-done.2.refs_3_) | copy-start | bytes 49156
  48.1 30.4 %copy-start.9 = (bf16[32,256]{1,0:T(8,128)(2,1)}, bf16[32,256]{1,0:T(8,128)(2,1)S(1)}, u32[]{:S(2)}) copy-start(bf16[32,256]{1,0:T(8,128)(2,1)S(1)} %collective-permute-done.3.refs_4_) | copy-start | bytes 49156
  48.1 30.3 %copy-start.6 = (bf16[32,16,256]{2,1,0:T(8,128)(2,1)}, bf16[32,16,256]{2,1,0:T(8,128)(2,1)S(1)}, u32[]{:S(2)}) copy-start(bf16[32,16,256]{2,1,0:T(8,128)(2,1)S(1)} %collective-permute-done.refs_1_) | copy-start | bytes 786436
  48.1 30.3 %copy-start.7 = (bf16[32,16,256]{2,1,0:T(8,128)(2,1)}, bf16[32,16,256]{2,1,0:T(8,128)(2,1)S(1)}, u32[]{:S(2)}) copy-start(bf16[32,16,256]{2,1,0:T(8,128)(2,1)S(1)} %collective-permute-done.1.refs_2_) | copy-start | bytes 786436
  48.1 1.0 copy-start
  74.8 16.4 %all-to-all-start.1 = ((bf16[4,3,4,16,256]{4,3,2,1,0:T(8,128)(2,1)}), bf16[4,3,4,16,256]{4,3,2,1,0:T(8,128)(2,1)S(1)}, u32[]{:S(2)}, u32[]{:S(2)}) async-start(bf16[4,3,4,16,256]{4,3,2,1,0:T(8,128)(2,1)} %get-tuple-element.36), calls=%async_computation.1 | async-start | bytes 786432 | tf_op jit(solution)/shard_map/all_to_all | solution.py:470
  91.2 3.5 %copy-start.3 = (bf16[4,3,4,16,256]{4,3,2,1,0:T(8,128)(2,1)}, bf16[4,3,4,16,256]{4,3,2,1,0:T(8,128)(2,1)S(1)}, u32[]{:S(2)}) copy-start(bf16[4,3,4,16,256]{4,3,2,1,0:T(8,128)(2,1)S(1)} %all-to-all-done.1.refs_5_) | copy-start | bytes 1179652
  91.2 18.5 %all-to-all-start.4 = ((bf16[4,4,4,16,256]{4,3,2,1,0:T(8,128)(2,1)}), bf16[4,4,4,16,256]{4,3,2,1,0:T(8,128)(2,1)S(1)}, u32[]{:S(2)}, u32[]{:S(2)}) async-start(bf16[4,4,4,16,256]{4,3,2,1,0:T(8,128)(2,1)} %get-tuple-element.43), calls=%async_computation.4 | async-start | bytes 1048576 | tf_op jit(solution)/shard_map/all_to_all | solution.py:476
  109.7 3.5 %copy-start.1 = (bf16[4,4,4,16,256]{4,3,2,1,0:T(8,128)(2,1)}, bf16[4,4,4,16,256]{4,3,2,1,0:T(8,128)(2,1)S(1)}, u32[]{:S(2)}) copy-start(bf16[4,4,4,16,256]{4,3,2,1,0:T(8,128)(2,1)S(1)} %all-to-all-done.4.recv_ref) | copy-start | bytes 1572868
  109.7 17.7 %all-to-all-start.3 = ((bf16[4,4,4,16,256]{4,3,2,1,0:T(8,128)(2,1)}), bf16[4,4,4,16,256]{4,3,2,1,0:T(8,128)(2,1)S(1)}, u32[]{:S(2)}, u32[]{:S(2)}) async-start(bf16[4,4,4,16,256]{4,3,2,1,0:T(8,128)(2,1)} %get-tuple-element.42), calls=%async_computation.3 | async-start | bytes 1048576 | tf_op jit(solution)/shard_map/all_to_all | solution.py:476
  127.4 0.8 copy-start.2

commit v2 on v1

v2 whole, which is shorter than its diff:
```python
import functools

import jax
import jax.numpy as jnp
import numpy as np
from jax import lax
from jax.experimental import pallas as pl
from jax.experimental.pallas import tpu as pltpu
from jax.sharding import PartitionSpec as P

F32 = jnp.float32
BF16 = jnp.bfloat16
LANES = 128
LOW = 16
STEP = 4
VMEM = 56 * 1024 * 1024

COS = (
    0.9999999890590228,
    -19.739204499454026,
    64.93911745990036,
    -85.45013953095037,
    60.16763095136588,
    -25.96759924965491,
    6.528658162567069,
)
SIN = (
    6.283185302511503,
    -41.34170040531769,
    81.60513138580204,
    -76.7030153539128,
    42.02592698618416,
    -14.899846668691637,
    3.238137510515757,
)


def dot(a, b, dims):
    return lax.dot_general(a, b, (dims, ((), ())), preferred_element_type=F32)


def cost(flops, moved):
    return pl.CostEstimate(flops=int(flops), bytes_accessed=int(moved), transcendentals=0)


def unit_circle(step, rows, waves, count):
    index = lax.broadcasted_iota(jnp.int32, (rows, waves.shape[1]), 0) * step
    product = index.astype(F32) * waves
    inverse = 1.0 / count
    turns = (product - jnp.floor(product * inverse) * count) * inverse
    y = turns - jnp.floor(turns + 0.5)
    z = y * y
    cosine = jnp.full_like(z, COS[-1])
    sine = jnp.full_like(z, SIN[-1])
    for c, s in zip(COS[-2::-1], SIN[-2::-1]):
        cosine = cosine * z + c
        sine = sine * z + s
    return cosine, sine * y


def table_kernel(points, waves_ref, table_ref, twiddle_ref):
    size, turns = waves_ref.shape[1], twiddle_ref.shape[2]
    waves = waves_ref[...]
    for k in range(table_ref.shape[0]):
        row = pl.program_id(0) * table_ref.shape[0] + k
        count = jnp.full(waves.shape, points[row], jnp.int32).astype(F32)
        cos_low, sin_low = unit_circle(1, LOW, waves, count)
        cos_high, sin_high = unit_circle(LOW, LANES // LOW, waves, count)
        cosine, sine = [], []
        for a in range(LANES // LOW):
            ch, sh = cos_high[a : a + 1], sin_high[a : a + 1]
            cosine.append(ch * cos_low - sh * sin_low)
            sine.append(-sh * cos_low - ch * sin_low)
        table_ref[k, :size, :] = jnp.concatenate(cosine, axis=0).T.astype(BF16)
        table_ref[k, size:, :] = jnp.concatenate(sine, axis=0).T.astype(BF16)
        cos_turn, sin_turn = unit_circle(LANES, turns, waves, count)
        twiddle_ref[k, 0] = cos_turn
        twiddle_ref[k, 1] = sin_turn


def tables(points, wave_ids, turns):
    rows, waves = points.shape[0], wave_ids.shape[0]
    each = STEP if rows % STEP == 0 else 1
    return pl.pallas_call(
        table_kernel,
        grid_spec=pltpu.PrefetchScalarGridSpec(
            num_scalar_prefetch=1,
            grid=(rows // each,),
            in_specs=[pl.BlockSpec((1, waves), lambda j, p: (0, 0))],
            out_specs=[
                pl.BlockSpec((each, 2 * waves, LANES), lambda j, p: (j, 0, 0)),
                pl.BlockSpec((each, 2, turns, waves), lambda j, p: (j, 0, 0, 0)),
            ],
        ),
        out_shape=[
            jax.ShapeDtypeStruct((rows, 2 * waves, LANES), BF16),
            jax.ShapeDtypeStruct((rows, 2, turns, waves), F32),
        ],
        compiler_params=pltpu.CompilerParams(vmem_limit_bytes=VMEM),
        cost_estimate=cost(rows * waves * LANES * 8, rows * waves * LANES * 4),
        name="tables",
    )(points, wave_ids.astype(F32)[None, :])


def place(pieces, width):
    out = [None] * (width // LANES)
    lane = lax.broadcasted_iota(jnp.int32, (pieces[0][0].shape[0], LANES), 1)
    for value, start, count, here in pieces:
        shift = (here - start) % LANES
        for a in range(start // LANES, (start + count - 1) // LANES + 1):
            part = value[:, a * LANES : (a + 1) * LANES]
            if shift:
                part = pltpu.roll(part, shift, 1)
            first = max(start, a * LANES) - start + here
            last = min(start + count, (a + 1) * LANES) - start + here
            for v in range(first // LANES, (last - 1) // LANES + 1):
                low, high = max(first - v * LANES, 0), min(last - v * LANES, LANES)
                if out[v] is None:
                    out[v] = part
                else:
                    out[v] = jnp.where((lane >= low) & (lane < high), part, out[v])
    return out


def synth_kernel(me, recv_ref, table_ref, twiddle_ref, *refs):
    *out_refs, coef, grid = refs
    sources, levels, rows, _ = recv_ref.shape
    fields, waves = coef.shape[0] // 2, coef.shape[1] * LANES
    share = waves // sources
    each, _, turns = twiddle_ref.shape[:3]
    step = pl.program_id(0)

    @pl.when(step == 0)
    def _():
        def level(l, carry):
            values = [recv_ref[s, l].astype(F32) for s in range(sources)]
            for r in range(2 * fields):
                windows = [
                    (values[s], r * share, share, s * share) for s in range(sources)
                ]
                for v, part in enumerate(place(windows, waves)):
                    coef[r, v, pl.ds(l * rows, rows), :] = part
            return carry

        lax.fori_loop(0, levels, level, 0)

    for k in range(each):
        j = step * each + k

        def own_row(r):
            parts = [coef[r, v, pl.ds(j, levels, stride=rows), :] for v in range(waves // LANES)]
            return jnp.concatenate(parts, axis=1)

        values = [own_row(r) for r in range(2 * fields)]
        real, imag = [], []
        for t in range(turns):
            c, s = twiddle_ref[k, 0, t : t + 1], twiddle_ref[k, 1, t : t + 1]
            for f in range(fields):
                re, im = values[2 * f], values[2 * f + 1]
                real.append(re * c - im * s)
                imag.append(re * s + im * c)
        both = [jnp.concatenate(part, axis=0).astype(BF16) for part in (real, imag)]
        result = dot(jnp.concatenate(both, axis=1), table_ref[k], ((1,), (0,)))
        grid[pl.ds(j, turns * fields * levels, stride=rows), :] = result

    @pl.when(step == pl.num_programs(0) - 1)
    def _():
        tiles = turns // len(out_refs)
        size = levels * rows
        for k, out_ref in enumerate(out_refs):
            for t in range(tiles):
                for f in range(fields):
                    start = (((me[0] ^ k) * tiles + t) * fields + f) * size
                    block = grid[pl.ds(pl.multiple_of(start, size), size), :]
                    block = block.reshape(levels, rows, LANES).astype(BF16)
                    out_ref[f, :, :, t * LANES : (t + 1) * LANES] = block


def synthesis(recv, table, twiddle, me, dests, tile):
    sources, levels, rows, lanes = recv.shape
    turns, waves = twiddle.shape[2:]
    fields = 3
    each = STEP if rows % STEP == 0 else 1
    shape = (fields, levels, rows, tile)
    return pl.pallas_call(
        synth_kernel,
        grid_spec=pltpu.PrefetchScalarGridSpec(
            num_scalar_prefetch=1,
            grid=(rows // each,),
            in_specs=[
                pl.BlockSpec(recv.shape, lambda j, me: (0, 0, 0, 0)),
                pl.BlockSpec((each, 2 * waves, LANES), lambda j, me: (j, 0, 0)),
                pl.BlockSpec((each, 2, turns, waves), lambda j, me: (j, 0, 0, 0)),
            ],
            out_specs=[pl.BlockSpec(shape, lambda j, me: (0, 0, 0, 0))] * dests,
            scratch_shapes=[
                pltpu.VMEM((2 * fields, waves // LANES, levels * rows, LANES), F32),
                pltpu.VMEM((turns * fields * levels * rows, LANES), F32),
            ],
        ),
        out_shape=[jax.ShapeDtypeStruct(shape, BF16)] * dests,
        compiler_params=pltpu.CompilerParams(vmem_limit_bytes=VMEM),
        cost_estimate=cost(4 * rows * waves * fields * levels * turns * LANES, 4 * rows * waves * LANES),
        name="synthesis",
    )(me, recv, table, twiddle)


def edge_kernel(
    odd, state_ref, base_ref, temp_ref, row_a_ref, row_b_ref, col_a_ref, col_b_ref, react_ref
):
    tracers, levels, rows, tile = state_ref.shape
    cells = tracers * rows

    @pl.when(pl.program_id(0) == 0)
    def _():
        rates = jnp.concatenate([base_ref[...], temp_ref[...]], axis=0)
        high = rates.astype(BF16)
        low = (rates - high.astype(F32)).astype(BF16)

        def iota(shape, axis):
            return lax.broadcasted_iota(jnp.int32, shape, axis)

        shape = (2 * cells, 2 * tracers)
        down = jnp.where(iota(shape, 0) // rows == iota(shape, 1), 1.0, 0.0).astype(BF16)
        shape = (tracers, cells)
        over = jnp.where(iota(shape, 0) == iota(shape, 1) // rows, 1.0, 0.0).astype(BF16)
        shape = (2 * cells, cells)
        same = iota(shape, 0) % rows == iota(shape, 1) % rows
        for k, part in enumerate((high, low)):
            wide = dot(dot(down, part, ((1,), (0,))).astype(BF16), over, ((1,), (0,)))
            react_ref[:, k * cells : (k + 1) * cells] = jnp.where(same, wide, 0.0).astype(BF16)

    def iota(shape, axis):
        return lax.broadcasted_iota(jnp.int32, shape, axis)

    far, near = (1 - odd[0]) * (rows - 1), odd[0] * (rows - 1)
    shape = (2 * tracers, cells)
    end = jnp.where(iota(shape, 0) < tracers, far, near)
    pick = iota(shape, 1) == (iota(shape, 0) % tracers) * rows + end
    pick = jnp.where(pick, 1.0, 0.0).astype(BF16)
    shape = (2 * levels, tile)
    far, near = (1 - odd[1]) * (tile - 1), odd[1] * (tile - 1)
    is_end = iota(shape, 1) == jnp.where(iota(shape, 0) < levels, far, near)
    row = iota(shape, 0) % levels
    columns = jnp.zeros((2 * levels, cells), F32)
    for l in range(levels):
        x = state_ref[:, l].reshape(cells, tile)
        picked = dot(pick, x, ((1,), (0,)))
        row_a_ref[l] = picked[:tracers].astype(BF16)
        row_b_ref[l] = picked[tracers:].astype(BF16)
        mark = jnp.where(is_end & (row == l), 1.0, 0.0).astype(BF16)
        columns = columns + dot(mark, x, ((1,), (1,)))
    col_a_ref[...] = columns[:levels].astype(BF16)
    col_b_ref[...] = columns[levels:].astype(BF16)


def edges(state, react_base, react_temp, odd):
    tracers, levels, rows, tile = state.shape
    block = 16
    cells = tracers * rows
    rowed = jax.ShapeDtypeStruct((levels, tracers, tile), BF16)
    columned = jax.ShapeDtypeStruct((levels, cells), BF16)
    row_spec = pl.BlockSpec((block, tracers, tile), lambda i, odd: (i, 0, 0))
    col_spec = pl.BlockSpec((block, cells), lambda i, odd: (i, 0))
    wide = (2 * cells, 2 * cells)
    return pl.pallas_call(
        edge_kernel,
        grid_spec=pltpu.PrefetchScalarGridSpec(
            num_scalar_prefetch=1,
            grid=(levels // block,),
            in_specs=[
                pl.BlockSpec((tracers, block, rows, tile), lambda i, odd: (0, i, 0, 0)),
                pl.BlockSpec(react_base.shape, lambda i, odd: (0, 0)),
                pl.BlockSpec(react_temp.shape, lambda i, odd: (0, 0)),
            ],
            out_specs=[
                row_spec, row_spec, col_spec, col_spec, pl.BlockSpec(wide, lambda i, odd: (0, 0)),
            ],
        ),
        out_shape=[rowed, rowed, columned, columned, jax.ShapeDtypeStruct(wide, BF16)],
        compiler_params=pltpu.CompilerParams(vmem_limit_bytes=VMEM),
        cost_estimate=cost(4 * state.size * 32, 2 * state.size),
        name="edges",
    )(odd, state, react_base, react_temp)


def chem_kernel(scale, info, *refs):
    state_ref, row_a_ref, row_b_ref, col_a_ref, col_b_ref, grid_ref, mask_ref, react_ref = refs[:8]
    along_ref, across_ref = refs[8:10]
    new_ref, active_ref, south, north = refs[-4:]
    tracers, levels, rows, tile = state_ref.shape
    cells = tracers * rows
    half, side = rows // 2, tile // 2
    group, odd_band, odd_tile = info[0], info[1] == 1, info[2] == 1
    first = (group * pl.num_programs(0) + pl.program_id(0)) * levels

    def column(value):
        pad = jnp.zeros((LANES - value.shape[0], cells), F32)
        turn = lax.rem(LANES - first, LANES)
        return pltpu.roll(jnp.concatenate([value, pad], axis=0).T, turn, 1)

    a, b = col_a_ref[...].astype(F32), col_b_ref[...].astype(F32)
    west, east = column(jnp.where(odd_tile, a, b)), column(jnp.where(odd_tile, b, a))
    row = lax.broadcasted_iota(jnp.int32, (rows, tile), 0)
    lane = lax.broadcasted_iota(jnp.int32, (rows, tile), 1)
    mask = mask_ref[...]
    nn = ((1,), (0,))

    def three(v):
        return v.reshape(tracers, rows, tile)

    for l in range(levels):
        x = state_ref[:, l].reshape(cells, tile)
        lon = dot(x, along_ref[...], nn)
        lat = dot(across_ref[...], x, nn)
        wind_u = grid_ref[0, l].astype(F32) * (scale * 0.1)
        wind_v = grid_ref[1, l].astype(F32) * (scale * 0.1)
        temper = grid_ref[2, l].astype(F32) * scale
        moved = (
            three(x.astype(F32))
            - wind_u * three(lon[:, :tile])
            - wind_v * three(lat[:cells])
            + 0.05 * three(lon[:, tile:] + lat[cells:])
        )
        a, b = row_a_ref[l].astype(F32), row_b_ref[l].astype(F32)
        south[l] = jnp.where(odd_band, a, b)
        north[l] = jnp.where(odd_band, b, a)
        in_row = jnp.where(row == 0, 0.05 + wind_v, jnp.where(row == rows - 1, 0.05 - wind_v, 0.0))
        in_col = jnp.where(lane == 0, 0.05 + wind_u, jnp.where(lane == tile - 1, 0.05 - wind_u, 0.0))
        outer = []
        for t in range(tracers):
            up = [jnp.broadcast_to(ref[l, t : t + 1], (half, tile)) for ref in (south, north)]
            cell = slice(t * rows, (t + 1) * rows)
            across = [
                jnp.broadcast_to(col[cell, l : l + 1], (rows, side)) for col in (west, east)
            ]
            outer.append(
                in_row * jnp.concatenate(up, axis=0) + in_col * jnp.concatenate(across, axis=1)
            )
        moved = moved + jnp.stack(outer, axis=0)
        high = moved.reshape(cells, tile).astype(BF16)
        terms = dot(react_ref[...], jnp.concatenate([high, high], axis=0), nn)
        reacted = (moved + three(terms[:cells]) + temper * three(terms[cells:])) * mask
        new_ref[:, l] = reacted.astype(BF16)
    for a in range(active_ref.shape[0]):
        active_ref[a] = new_ref[info[3 + a]]


def chemistry(state, halos, grid, mask, react, info, actives, waves, before):
    tracers, levels, rows, tile = state.shape
    fields, own = grid.shape[:2]
    some = 4 if own % 4 == 0 else own
    steps = own // some
    cells = tracers * rows
    eye, one = np.eye(tracers), np.eye(tile)
    along = np.concatenate(
        [np.eye(tile, k=-1) - np.eye(tile, k=1), np.eye(tile, k=-1) + np.eye(tile, k=1) - 4 * one], 1
    )
    down, up = np.eye(rows, k=-1), np.eye(rows, k=1)
    across = np.concatenate([np.kron(eye, up - down), np.kron(eye, up + down)], 0)
    scale = 1.0 / float(np.sqrt(np.float32(waves)))

    def whole(shape):
        return pl.BlockSpec(shape, lambda i, info: (0,) * len(shape))

    row_spec = pl.BlockSpec((some, tracers, tile), lambda i, info: (info[0] * steps + i, 0, 0))
    state_spec = pl.BlockSpec(
        (tracers, some, rows, tile), lambda i, info: (0, info[0] * steps + i, 0, 0)
    )
    operands = [
        state, *halos, grid, mask, react, jnp.asarray(along, BF16), jnp.asarray(across, BF16),
    ]
    in_specs = [
        state_spec,
        row_spec,
        row_spec,
        whole(halos[2].shape),
        whole(halos[3].shape),
        pl.BlockSpec((fields, some, rows, tile), lambda i, info: (0, i, 0, 0)),
        whole(mask.shape),
        whole(react.shape),
        whole(along.shape),
        whole(across.shape),
    ]
    aliases = {}
    if before is not None:
        aliases = {1 + len(operands): 0}
        operands.append(before)
        in_specs.append(pl.BlockSpec(memory_space=pl.ANY))
    return pl.pallas_call(
        functools.partial(chem_kernel, scale),
        grid_spec=pltpu.PrefetchScalarGridSpec(
            num_scalar_prefetch=1,
            grid=(steps,),
            in_specs=in_specs,
            out_specs=[
                state_spec,
                pl.BlockSpec((actives, some, rows, tile), lambda i, info: (0, i, 0, 0)),
            ],
            scratch_shapes=[pltpu.VMEM((some, tracers, tile), F32)] * 2,
        ),
        out_shape=[
            jax.ShapeDtypeStruct(state.shape, BF16),
            jax.ShapeDtypeStruct((actives, own, rows, tile), BF16),
        ],
        input_output_aliases=aliases,
        compiler_params=pltpu.CompilerParams(vmem_limit_bytes=VMEM),
        cost_estimate=cost(own * cells * tile * 2 * 2048, own * cells * tile * 4),
        name="chemistry",
    )(info, *operands)


def spread_kernel(info, recv_ref, *refs):
    refs[-1][...] = recv_ref[...].astype(F32)


def spread(recv, info, sources, before):
    actives, own, rows, tile = recv.shape
    each = 2 if actives % 2 == 0 else 1
    operands = [recv]
    in_specs = [pl.BlockSpec((each, own, rows, tile), lambda a, info: (a, 0, 0, 0))]
    aliases = {}
    if before is not None:
        operands.append(before)
        in_specs.append(pl.BlockSpec(memory_space=pl.ANY))
        aliases = {2: 0}
    return pl.pallas_call(
        spread_kernel,
        grid_spec=pltpu.PrefetchScalarGridSpec(
            num_scalar_prefetch=1,
            grid=(actives // each,),
            in_specs=in_specs,
            out_specs=pl.BlockSpec((each, own, rows, tile), lambda a, info: (a, 0, 0, info[0])),
        ),
        out_shape=jax.ShapeDtypeStruct((actives, own, rows, sources * tile), F32),
        input_output_aliases=aliases,
        compiler_params=pltpu.CompilerParams(vmem_limit_bytes=VMEM),
        cost_estimate=cost(recv.size, recv.size * 6),
        name="spread",
    )(info, *operands)


def legendre_kernel(spectral_ref, legendre_ref, out_ref, rows_of, sums):
    parts, own, block, size = spectral_ref.shape
    bands, _, rows, pitch = out_ref.shape
    share = block * pl.num_programs(0)
    step = pl.program_id(0)
    lines = parts * own

    @pl.when(step == 0)
    def _():
        for h in range(sums.shape[0]):
            for l in range(own):
                tail = slice(l * pitch + parts * share, (l + 1) * pitch)
                sums[h, tail, :] = jnp.zeros((pitch - parts * share, LANES), F32)

    for v in range(size // LANES):
        part = spectral_ref[:, :, :, v * LANES : (v + 1) * LANES].astype(F32)
        rows_of[v] = part.reshape(lines * block, LANES)
    for m in range(block):
        x = [rows_of[v, pl.ds(m, lines, stride=block), :] for v in range(size // LANES)]
        x = jnp.concatenate(x, axis=1).astype(BF16)
        result = dot(x, legendre_ref[m], ((1,), (0,)))
        for r in range(parts):
            at = r * share + step * block + m
            for h in range(sums.shape[0]):
                piece = result[r * own : (r + 1) * own, h * LANES : (h + 1) * LANES]
                sums[h, pl.ds(at, own, stride=pitch), :] = piece

    @pl.when(step == pl.num_programs(0) - 1)
    def _():
        some = LANES // rows
        for l in range(own):
            for h in range(sums.shape[0]):
                turned = sums[h, l * pitch : (l + 1) * pitch, :].T.astype(BF16)
                out_ref[h * some : (h + 1) * some, l] = turned.reshape(some, rows, pitch)


def legendre_sums(spectral, legendre, bands):
    parts, own, share, size = spectral.shape
    rows = legendre.shape[2] // bands
    pitch = -(-parts * share // LANES) * LANES
    block = 16 if share % 16 == 0 else 8
    shape = (bands, own, rows, pitch)
    return pl.pallas_call(
        legendre_kernel,
        grid=(share // block,),
        in_specs=[
            pl.BlockSpec((parts, own, block, size), lambda i: (0, 0, i, 0)),
            pl.BlockSpec((block,) + legendre.shape[1:], lambda i: (i, 0, 0)),
        ],
        out_specs=pl.BlockSpec(shape, lambda i: (0, 0, 0, 0)),
        out_shape=jax.ShapeDtypeStruct(shape, BF16),
        scratch_shapes=[
            pltpu.VMEM((size // LANES, parts * own * block, LANES), F32),
            pltpu.VMEM((legendre.shape[2] // LANES, own * pitch, LANES), F32),
        ],
        compiler_params=pltpu.CompilerParams(vmem_limit_bytes=VMEM),
        cost_estimate=cost(2 * parts * own * legendre.size, 2 * (spectral.size + legendre.size)),
        name="legendre",
    )(spectral, legendre)


def exchange(value, axis, pairs):
    return lax.ppermute(value, axis, [p for a, b in pairs for p in ((a, b), (b, a))])


def neighbours(axis, first):
    size = lax.axis_size(axis)
    return [(i, i + 1) for i in range(first, size - 1, 2)]


def partners(axis, k):
    return [(i, i ^ k) for i in range(lax.axis_size(axis)) if i < i ^ k]


def body(spectral, legendre, wave_ids, points, tracers, react_base, react_temp, active_ids):
    bands, tiles = lax.axis_size("lat"), lax.axis_size("lon")
    tile = tracers.shape[3]
    waves = wave_ids.shape[0]
    band, me = lax.axis_index("lat"), lax.axis_index("lon")

    sent = legendre_sums(spectral, legendre, bands)
    recv = lax.all_to_all(sent, "lat", split_axis=0, concat_axis=0, tiled=True)

    table, twiddle = tables(points, wave_ids, tiles * tile // LANES)
    odd = jnp.stack([band % 2, me % 2]).astype(jnp.int32)
    row_a, row_b, col_a, col_b, react = edges(tracers, react_base, react_temp, odd)
    columns = me * tile + jnp.arange(tile)
    mask = (columns[None, :] < points[:, None]).astype(F32)
    infos = [
        jnp.concatenate([jnp.stack([me ^ k, odd[0], odd[1]]), active_ids]).astype(jnp.int32)
        for k in range(tiles)
    ]
    recv, table, twiddle, row_a, row_b, col_a, col_b, react, mask, infos = lax.optimization_barrier(
        (recv, table, twiddle, row_a, row_b, col_a, col_b, react, mask, infos)
    )

    grids = synthesis(recv, table, twiddle, infos[0][:1], tiles, tile)
    row_a, row_b, col_a, col_b, grids = lax.optimization_barrier((row_a, row_b, col_a, col_b, grids))
    order = list(range(2, tiles)) + [1]
    grids = {0: grids[0]} | {k: exchange(grids[k], "lon", partners("lon", k)) for k in order}
    halos = (
        exchange(row_a, "lat", neighbours("lat", 0)),
        exchange(row_b, "lat", neighbours("lat", 1)),
        exchange(col_a, "lon", neighbours("lon", 0)),
        exchange(col_b, "lon", neighbours("lon", 1)),
    )
    new, active = None, {}
    for k in [0] + order:
        new, active[k] = chemistry(
            tracers, halos, grids[k], mask, react, infos[k], active_ids.shape[0], waves, new
        )
        if k:
            active[k] = exchange(active[k], "lon", partners("lon", k))
    spreaded = None
    for k in [0] + order:
        spreaded = spread(active[k], infos[k], tiles, spreaded)
    return new, spreaded


def solution(mesh):
    return jax.shard_map(
        body,
        mesh=mesh,
        in_specs=(
            P(None, "lon", "lat", None),
            P("lat", None, None),
            P(),
            P("lat"),
            P(None, None, "lat", "lon"),
            P(),
            P(),
            P(),
        ),
        out_specs=(P(None, None, "lat", "lon"), P(None, "lon", "lat", None)),
        check_vma=False,
    )
```

time: 131 us -> 126 us (0.962)
  Pallas kernels: 43.7 us -> 74.9 us
  blocking collectives: 17.2 us -> 0 us
  matrix products: 13.9 us -> 0 us
  starting transfers between devices: 23.9 us -> 20.8 us
  local copies, waits for them, and re-layouts: 9.75 us -> 7.07 us
  other arithmetic: 0.68 us -> 2.6 us
    pallas_call x6 -> x11, Pallas kernels: 37.1 us -> 68.4 us  [the longest x4 25.8 us: chemistry(): pl.pallas_call(functools.partial(chem_kernel, scale), grid_spec=pltpu.Pre...]
    all_to_all x3 -> x0, waiting for transfers between devices: 20.1 us -> none  [the longest x2 17.3 us: body(): lax.all_to_all(active, 'lon', split_axis=0, concat_axis=0, tiled=True)]
    ppermute x4 -> x10, waiting for transfers between devices: 0.01 us -> 18.8 us  [exchange(): lax.ppermute(value, axis, [p for a, b in pairs for p in ((a, b), (b, a))])]
    all_to_all x1 -> x0, blocking collectives: 17.2 us -> none  [body(): lax.all_to_all(g, 'lon', split_axis=0, concat_axis=0, tiled=True)]
    dot_general x1 -> x0, matrix products: 13.9 us -> none  [body(): lax.dot_general(spectral, legendre, (((3,), (1,)), ((2,), (0,))), preferr...]
    all_to_all x3 -> x0, starting transfers between devices: 10.6 us -> none  [the longest x2 6.94 us: body(): lax.all_to_all(active, 'lon', split_axis=0, concat_axis=0, tiled=True)]
    ppermute x4 -> x10, starting transfers between devices: 8.2 us -> 15.5 us  [exchange(): lax.ppermute(value, axis, [p for a, b in pairs for p in ((a, b), (b, a))])]
    unnamed x20 -> x38, local copies, waits for them, and re-layouts: 1.85 us -> 6.48 us
  transfers between devices with their start and end apart: 8 -> 11, of which waited for: 3 -> 2; matrix products, arithmetic and copies ran while one was open for 1% -> 3% of each run, Pallas kernels for 26% -> 36%
where the time goes in v2:
time: 126 us; the launch traced here: 125 us
  Pallas kernels  74.9 us (59%)
  starting transfers between devices  20.8 us (17%)
  waiting for transfers between devices  18.8 us (15%)
  local copies, waits for them, and re-layouts  7.07 us (6%)
  other arithmetic  2.6 us (2%)
    pallas_call x4, Pallas kernels, chemistry(): pl.pallas_call(functools.partial(chem_kernel, scale), grid_spec=pltpu.Pre...  25.8 us
    ppermute x10, waiting for transfers between devices, exchange(): lax.ppermute(value, axis, [p for a, b in pairs for p in ((a, b), (b, a))])  18.8 us
    pallas_call x1, Pallas kernels, legendre_sums(): pl.pallas_call(legendre_kernel, grid=(share // block,), in_specs=[pl.Bloc...  18 us
    ppermute x10, starting transfers between devices, exchange(): lax.ppermute(value, axis, [p for a, b in pairs for p in ((a, b), (b, a))])  15.5 us
    pallas_call x4, Pallas kernels, spread(): pl.pallas_call(spread_kernel, grid_spec=pltpu.PrefetchScalarGridSpec(num_...  9.53 us
    pallas_call x1, Pallas kernels, synthesis(): pl.pallas_call(synth_kernel, grid_spec=pltpu.PrefetchScalarGridSpec(num_s...  9.4 us
    pallas_call x1, Pallas kernels, tables(): pl.pallas_call(table_kernel, grid_spec=pltpu.PrefetchScalarGridSpec(num_s...  6.57 us
    unnamed x38, local copies, waits for them, and re-layouts  6.48 us
  transfers between devices with their start and end apart: 11, of which 2 were waited for; matrix products, arithmetic and copies ran while one was open for 3% of the time, Pallas kernels for 36%

profile of v2, /device:TPU:0, one launch (start us, length us, event | category | flops | bytes accessed | tf_op | source)
XLA Modules:
  0.0 125.0 jit_solution(10705865800238790119)
XLA Ops:
  0.6 0.0 copy-start.11
  0.6 18.0 %legendre.1 = bf16[8,8,16,512]{3,2,1,0:T(8,128)(2,1)} custom-call(bf16[6,8,80,1280]{3,2,1,0:T(8,128)(2,1)} %spectral_ref.1, bf16[80,1280,128]{2,1,0:T(8,128)(2,1)} %legendre_ref.1), custom_call_target="tpu_custom_call" | custom-call | flops 1258291200 | bytes 36044800 | tf_op jit(solution)/shard_map/legendre/pallas_call | solution.py:485
  18.6 5.3 %all-to-all-start = ((bf16[8,8,16,512]{3,2,1,0:T(8,128)(2,1)}), bf16[8,8,16,512]{3,2,1,0:T(8,128)(2,1)S(1)}, u32[]{:S(2)}, u32[]{:S(2)}) async-start(bf16[8,8,16,512]{3,2,1,0:T(8,128)(2,1)} %legendre.1), calls=%async_computation | async-start | bytes 2097152 | tf_op jit(solution)/shard_map/all_to_all | solution.py:524
  23.9 0.0 copy-done.11
  23.9 0.6 broadcast_in_dim.2.waves_ref
  24.5 6.6 %tables.1 = (bf16[16,1280,128]{2,1,0:T(8,128)(2,1)}, f32[16,2,8,640]{3,2,1,0:T(8,128)}) custom-call(s32[16]{0:T(128)} %points.1, f32[1,640]{1,0:T(1,128)} %broadcast_in_dim.2.waves_ref), custom_call_target="tpu_custom_call" | custom-call | flops 10485760 | bytes 5242880 | tf_op jit(solution)/shard_map/tables/pallas_call | solution.py:84
  31.1 0.6 pad_add_fusion.odd
  31.7 5.6 %edges.1 = (bf16[32,16,256]{2,1,0:T(8,128)(2,1)}, bf16[32,16,256]{2,1,0:T(8,128)(2,1)}, bf16[32,256]{1,0:T(8,128)(2,1)}, bf16[32,256]{1,0:T(8,128)(2,1)}, bf16[512,512]{1,0:T(8,128)(2,1)}) custom-call(s32[2]{0:T(128)} %pad_add_fusion.odd, bf16[16,32,16,256]{3,2,1,0:T(8,128)(2,1)} %refs_0_.7, f32[16,16]{1,0:T(8,128)} %base_ref.1, f32[16,16]{1,0:T(8,128)} %temp_ref.1), custom_call_target="tpu_custom_call" | custom-call | flops 268435456 | bytes 4194304 | tf_op jit(solution)/shard_map/edges/pallas_call | solution.py:266
  37.4 0.0 copy-start.14
  37.4 0.0 copy-start.18
  37.4 0.0 copy-start.17
  37.4 0.0 copy-done.12
  37.4 0.7 add_add_fusion.3
  38.1 0.6 add_add_fusion.2
  38.7 0.0 copy-done.13
  38.7 0.7 compare_convert_fusion.refs_6_
  39.4 0.0 all-to-all-done.recv_ref
  39.4 1.0 copy-done
  40.4 9.4 %synthesis.1 = (bf16[3,8,16,256]{3,2,1,0:T(8,128)(2,1)}, bf16[3,8,16,256]{3,2,1,0:T(8,128)(2,1)}, bf16[3,8,16,256]{3,2,1,0:T(8,128)(2,1)}, bf16[3,8,16,256]{3,2,1,0:T(8,128)(2,1)}) custom-call(s32[1]{0:T(128)} %bitcast.7, bf16[8,8,16,512]{3,2,1,0:T(8,128)(2,1)} %copy-done, bf16[16,1280,128]{2,1,0:T(8,128)(2,1)} %get-tuple-element.56.table_ref, ...), custom_call_target="tpu_custom_call" | custom-call | flops 1006632960 | bytes 5242880 | tf_op jit(solution)/shard_map/synthesis/pallas_call | solution.py:185
  49.8 0.0 copy-done.15
  49.8 0.5 collective-permute-start
  50.3 0.0 copy-done.14
  50.3 0.7 collective-permute-start.1
  50.9 0.0 copy-done.18
  50.9 1.6 %collective-permute-start.2 = (bf16[32,256]{1,0:T(8,128)(2,1)S(1)}, bf16[32,256]{1,0:T(8,128)(2,1)S(1)}, u32[]{:S(2)}, u32[]{:S(2)}) collective-permute-start(bf16[32,256]{1,0:T(8,128)(2,1)S(1)} %copy-done.18), channel_id=1, source_target_pairs={{0,1},{1,0},{2,3},{3,2},{4,5},{5,4},{6,7},{7,6},{8,9},{9,8},{10,11... | collective-permute-start | bytes 49160 | tf_op jit(solution)/shard_map/ppermute | solution.py:505
  52.6 0.0 copy-done.17
  52.6 0.8 collective-permute-start.3
  53.4 4.5 %collective-permute-start.4 = (bf16[3,8,16,256]{3,2,1,0:T(8,128)(2,1)}, bf16[3,8,16,256]{3,2,1,0:T(8,128)(2,1)S(1)}, u32[]{:S(2)}, u32[]{:S(2)}) collective-permute-start(bf16[3,8,16,256]{3,2,1,0:T(8,128)(2,1)} %get-tuple-element.66), channel_id=1, source_target_pairs={{0,1},{1,0},{2,3},{3,2},{4,5},{5,4},{6,7},{7,6},{8,9},{9,8},{10,11... | collective-permute-start | bytes 589832 | tf_op jit(solution)/shard_map/ppermute | solution.py:505
  57.9 0.0 collective-permute-done.2.refs_3_
  57.9 0.9 collective-permute-start.5
  58.8 0.0 collective-permute-done.3.refs_4_
  58.8 2.0 %collective-permute-start.6 = (bf16[3,8,16,256]{3,2,1,0:T(8,128)(2,1)}, bf16[3,8,16,256]{3,2,1,0:T(8,128)(2,1)S(1)}, u32[]{:S(2)}, u32[]{:S(2)}) collective-permute-start(bf16[3,8,16,256]{3,2,1,0:T(8,128)(2,1)} %get-tuple-element.72), channel_id=1, source_target_pairs={{0,2},{2,0},{1,3},{3,1},{4,6},{6,4},{5,7},{7,5},{8,10},{10,8},{9,1... | collective-permute-start | bytes 589832 | tf_op jit(solution)/shard_map/ppermute | solution.py:505
  60.8 0.0 collective-permute-done.refs_1_
  60.8 0.0 collective-permute-done.1.refs_2_
  60.8 0.0 copy-done.9
  60.8 0.0 copy-done.10
  60.8 0.7 copy-done.1
  61.5 0.7 copy-done.2
  62.2 6.4 %chemistry.4 = (bf16[16,32,16,256]{3,2,1,0:T(8,128)(2,1)}, bf16[4,8,16,256]{3,2,1,0:T(8,128)(2,1)}) custom-call(s32[7]{0:T(128)} %get-tuple-element.54.info, bf16[16,32,16,256]{3,2,1,0:T(8,128)(2,1)} %refs_0_.7, bf16[32,16,256]{2,1,0:T(8,128)(2,1)} %copy-done.1, bf16[32,16,256]{2,1,0:T(8,128)(2,1)} %copy-done.2, bf16[32,256]{1,0:T(8,128)(2,1)} %copy-done.9, ...), custom_call_target="tpu_custom_call" | custom-call | flops 2147483648 | bytes 2097152 | tf_op jit(solution)/shard_map/chemistry/pallas_call | solution.py:390
  68.6 7.9 %collective-permute-done.6.refs_5_ = bf16[3,8,16,256]{3,2,1,0:T(8,128)(2,1)S(1)} collective-permute-done((bf16[3,8,16,256]{3,2,1,0:T(8,128)(2,1)}, bf16[3,8,16,256]{3,2,1,0:T(8,128)(2,1)S(1)}, u32[]{:S(2)}, u32[]{:S(2)}) %collective-permute-start.6) | collective-permute-done | bytes 196640 | tf_op jit(solution)/shard_map/ppermute | solution.py:505
  76.5 0.7 copy-done.8
  77.2 6.4 %chemistry.5 = (bf16[16,32,16,256]{3,2,1,0:T(8,128)(2,1)}, bf16[4,8,16,256]{3,2,1,0:T(8,128)(2,1)}) custom-call(s32[7]{0:T(128)} %get-tuple-element.71.info, bf16[16,32,16,256]{3,2,1,0:T(8,128)(2,1)} %refs_0_.7, bf16[32,16,256]{2,1,0:T(8,128)(2,1)} %copy-done.1, bf16[32,16,256]{2,1,0:T(8,128)(2,1)} %copy-done.2, ...), custom_call_target="tpu_custom_call", output_to_operand_aliasing={{0}: (11, {})} | custom-call | flops 2147483648 | bytes 2097152 | tf_op jit(solution)/shard_map/chemistry/pallas_call | solution.py:390
  83.6 0.0 collective-permute-done.5.refs_5_
  83.6 0.0 copy-start.7
  83.6 0.7 copy-done.7
  84.3 6.6 %chemistry.6 = (bf16[16,32,16,256]{3,2,1,0:T(8,128)(2,1)}, bf16[4,8,16,256]{3,2,1,0:T(8,128)(2,1)}) custom-call(s32[7]{0:T(128)} %get-tuple-element.69.info, bf16[16,32,16,256]{3,2,1,0:T(8,128)(2,1)} %refs_0_.7, bf16[32,16,256]{2,1,0:T(8,128)(2,1)} %copy-done.1, bf16[32,16,256]{2,1,0:T(8,128)(2,1)} %copy-done.2, ...), custom_call_target="tpu_custom_call", output_to_operand_aliasing={{0}: (11, {})} | custom-call | flops 2147483648 | bytes 2097152 | tf_op jit(solution)/shard_map/chemistry/pallas_call | solution.py:390
  90.8 2.5 %collective-permute-start.8 = (bf16[4,8,16,256]{3,2,1,0:T(8,128)(2,1)}, bf16[4,8,16,256]{3,2,1,0:T(8,128)(2,1)S(1)}, u32[]{:S(2)}, u32[]{:S(2)}) collective-permute-start(bf16[4,8,16,256]{3,2,1,0:T(8,128)(2,1)} %get-tuple-element.79), channel_id=1, source_target_pairs={{0,3},{3,0},{1,2},{2,1},{4,7},{7,4},{5,6},{6,5},{8,11},{11,8},{9,1... | collective-permute-start | bytes 786440 | tf_op jit(solution)/shard_map/ppermute | solution.py:505
  93.3 0.0 copy-done.16
  93.3 0.0 collective-permute-start.9
  93.3 0.0 collective-permute-done.4.refs_5_
  93.3 0.0 copy-start.6
  93.3 0.7 copy-done.6
  94.0 6.4 %chemistry.7 = (bf16[16,32,16,256]{3,2,1,0:T(8,128)(2,1)}, bf16[4,8,16,256]{3,2,1,0:T(8,128)(2,1)}) custom-call(s32[7]{0:T(128)} %get-tuple-element.49.info, bf16[16,32,16,256]{3,2,1,0:T(8,128)(2,1)} %refs_0_.7, bf16[32,16,256]{2,1,0:T(8,128)(2,1)} %copy-done.1, bf16[32,16,256]{2,1,0:T(8,128)(2,1)} %copy-done.2, ...), custom_call_target="tpu_custom_call", output_to_operand_aliasing={{0}: (11, {})} | custom-call | flops 2147483648 | bytes 2097152 | tf_op jit(solution)/shard_map/chemistry/pallas_call | solution.py:390
  100.4 2.0 %collective-permute-start.7 = (bf16[4,8,16,256]{3,2,1,0:T(8,128)(2,1)}, bf16[4,8,16,256]{3,2,1,0:T(8,128)(2,1)S(1)}, u32[]{:S(2)}, u32[]{:S(2)}) collective-permute-start(bf16[4,8,16,256]{3,2,1,0:T(8,128)(2,1)} %get-tuple-element.78), channel_id=1, source_target_pairs={{0,1},{1,0},{2,3},{3,2},{4,5},{5,4},{6,7},{7,6},{8,9},{9,8},{10,11... | collective-permute-start | bytes 786440 | tf_op jit(solution)/shard_map/ppermute | solution.py:505
  102.4 2.4 %spread.4.refs_0_ = f32[4,8,16,1024]{3,2,1,0:T(8,128)} custom-call(s32[7]{0:T(128)} %get-tuple-element.54.info, bf16[4,8,16,256]{3,2,1,0:T(8,128)(2,1)} %get-tuple-element.81.recv_ref), custom_call_target="tpu_custom_call" | custom-call | flops 131072 | bytes 786432 | tf_op jit(solution)/shard_map/spread/pallas_call | solution.py:427
  104.8 10.9 %collective-permute-done.9.recv_ref = bf16[4,8,16,256]{3,2,1,0:T(8,128)(2,1)S(1)} collective-permute-done((bf16[4,8,16,256]{3,2,1,0:T(8,128)(2,1)S(1)}, bf16[4,8,16,256]{3,2,1,0:T(8,128)(2,1)S(1)}, u32[]{:S(2)}, u32[]{:S(2)}) %collective-permute-start.9) | collective-permute-done | bytes 262176 | tf_op jit(solution)/shard_map/ppermute | solution.py:505
  115.7 0.7 copy-done.4
  116.4 2.4 %spread.5.refs_0_ = f32[4,8,16,1024]{3,2,1,0:T(8,128)} custom-call(s32[7]{0:T(128)} %get-tuple-element.71.info, bf16[4,8,16,256]{3,2,1,0:T(8,128)(2,1)} %copy-done.4, f32[4,8,16,1024]{3,2,1,0:T(8,128)} %spread.4.refs_0_), custom_call_target="tpu_custom_call", output_to_operand_aliasing={{}: (2, {})} | custom-call | flops 131072 | bytes 786432 | tf_op jit(solution)/shard_map/spread/pallas_call | solution.py:427
  118.8 0.0 collective-permute-done.8.recv_ref
  118.8 0.7 copy-done.3
  119.5 2.4 %spread.6.refs_0_ = f32[4,8,16,1024]{3,2,1,0:T(8,128)} custom-call(s32[7]{0:T(128)} %get-tuple-element.69.info, bf16[4,8,16,256]{3,2,1,0:T(8,128)(2,1)} %copy-done.3, f32[4,8,16,1024]{3,2,1,0:T(8,128)} %spread.5.refs_0_), custom_call_target="tpu_custom_call", output_to_operand_aliasing={{}: (2, {})} | custom-call | flops 131072 | bytes 786432 | tf_op jit(solution)/shard_map/spread/pallas_call | solution.py:427
  121.9 0.0 collective-permute-done.7.recv_ref
  121.9 0.7 copy-done.5
  122.6 2.4 %spread.7 = f32[4,8,16,1024]{3,2,1,0:T(8,128)} custom-call(s32[7]{0:T(128)} %get-tuple-element.49.info, bf16[4,8,16,256]{3,2,1,0:T(8,128)(2,1)} %copy-done.5, f32[4,8,16,1024]{3,2,1,0:T(8,128)} %spread.6.refs_0_), custom_call_target="tpu_custom_call", output_to_operand_aliasing={{}: (2, {})} | custom-call | flops 131072 | bytes 786432 | tf_op jit(solution)/shard_map/spread/pallas_call | solution.py:427
  (15 shorter events, 0.0 us)
Async XLA Ops:
  0.6 23.3 %copy-start.11 = (s32[640]{0:T(1024)S(1)}, s32[640]{0:T(1024)}, u32[]{:S(2)}) copy-start(s32[640]{0:T(1024)} %param.18) | copy-start | bytes 7684
  18.6 18.8 %copy-start.12 = (s32[4]{0:T(128)S(1)}, s32[4]{0:T(128)}, u32[]{:S(2)}) copy-start(s32[4]{0:T(128)} %param.23) | copy-start | bytes 52
  18.6 20.1 %copy-start.13 = (s32[16]{0:T(128)S(1)}, s32[16]{0:T(128)}, u32[]{:S(2)}) copy-start(s32[16]{0:T(128)} %points.1) | copy-start | bytes 196
  18.6 20.8 %all-to-all-start = ((bf16[8,8,16,512]{3,2,1,0:T(8,128)(2,1)}), bf16[8,8,16,512]{3,2,1,0:T(8,128)(2,1)S(1)}, u32[]{:S(2)}, u32[]{:S(2)}) async-start(bf16[8,8,16,512]{3,2,1,0:T(8,128)(2,1)} %legendre.1), calls=%async_computation | async-start | bytes 2097152 | tf_op jit(solution)/shard_map/all_to_all | solution.py:524
  37.4 12.4 %copy-start.15 = (bf16[32,16,256]{2,1,0:T(8,128)(2,1)S(1)}, bf16[32,16,256]{2,1,0:T(8,128)(2,1)}, u32[]{:S(2)}) copy-start(bf16[32,16,256]{2,1,0:T(8,128)(2,1)} %get-tuple-element.62) | copy-start | bytes 786436
  37.4 12.9 %copy-start.14 = (bf16[32,16,256]{2,1,0:T(8,128)(2,1)S(1)}, bf16[32,16,256]{2,1,0:T(8,128)(2,1)}, u32[]{:S(2)}) copy-start(bf16[32,16,256]{2,1,0:T(8,128)(2,1)} %get-tuple-element.63) | copy-start | bytes 786436
  37.4 13.6 %copy-start.18 = (bf16[32,256]{1,0:T(8,128)(2,1)S(1)}, bf16[32,256]{1,0:T(8,128)(2,1)}, u32[]{:S(2)}) copy-start(bf16[32,256]{1,0:T(8,128)(2,1)} %get-tuple-element.64) | copy-start | bytes 49156
  37.4 15.2 %copy-start.17 = (bf16[32,256]{1,0:T(8,128)(2,1)S(1)}, bf16[32,256]{1,0:T(8,128)(2,1)}, u32[]{:S(2)}) copy-start(bf16[32,256]{1,0:T(8,128)(2,1)} %get-tuple-element.65) | copy-start | bytes 49156
  39.4 1.0 copy-start
  49.8 11.0 %collective-permute-start = (bf16[32,16,256]{2,1,0:T(8,128)(2,1)S(1)}, bf16[32,16,256]{2,1,0:T(8,128)(2,1)S(1)}, u32[]{:S(2)}, u32[]{:S(2)}) collective-permute-start(bf16[32,16,256]{2,1,0:T(8,128)(2,1)S(1)} %copy-done.15), channel_id=1, source_target_pairs={{0,4},{4,0},{8,12},{12,8},{16,20},{20,16},{24,28},{28,24},{1,5},{5... | collective-permute-start | bytes 786440 | tf_op jit(solution)/shard_map/ppermute | solution.py:505
  50.3 10.6 %collective-permute-start.1 = (bf16[32,16,256]{2,1,0:T(8,128)(2,1)S(1)}, bf16[32,16,256]{2,1,0:T(8,128)(2,1)S(1)}, u32[]{:S(2)}, u32[]{:S(2)}) collective-permute-start(bf16[32,16,256]{2,1,0:T(8,128)(2,1)S(1)} %copy-done.14), channel_id=1, source_target_pairs={{4,8},{8,4},{12,16},{16,12},{20,24},{24,20},{5,9},{9,5},{13,17},{1... | collective-permute-start | bytes 786440 | tf_op jit(solution)/shard_map/ppermute | solution.py:505
  50.9 7.0 %collective-permute-start.2 = (bf16[32,256]{1,0:T(8,128)(2,1)S(1)}, bf16[32,256]{1,0:T(8,128)(2,1)S(1)}, u32[]{:S(2)}, u32[]{:S(2)}) collective-permute-start(bf16[32,256]{1,0:T(8,128)(2,1)S(1)} %copy-done.18), channel_id=1, source_target_pairs={{0,1},{1,0},{2,3},{3,2},{4,5},{5,4},{6,7},{7,6},{8,9},{9,8},{10,11... | collective-permute-start | bytes 49160 | tf_op jit(solution)/shard_map/ppermute | solution.py:505
  52.6 6.2 %collective-permute-start.3 = (bf16[32,256]{1,0:T(8,128)(2,1)S(1)}, bf16[32,256]{1,0:T(8,128)(2,1)S(1)}, u32[]{:S(2)}, u32[]{:S(2)}) collective-permute-start(bf16[32,256]{1,0:T(8,128)(2,1)S(1)} %copy-done.17), channel_id=1, source_target_pairs={{1,2},{2,1},{5,6},{6,5},{9,10},{10,9},{13,14},{14,13},{17,18},{18,... | collective-permute-start | bytes 49160 | tf_op jit(solution)/shard_map/ppermute | solution.py:505
  53.4 39.9 %collective-permute-start.4 = (bf16[3,8,16,256]{3,2,1,0:T(8,128)(2,1)}, bf16[3,8,16,256]{3,2,1,0:T(8,128)(2,1)S(1)}, u32[]{:S(2)}, u32[]{:S(2)}) collective-permute-start(bf16[3,8,16,256]{3,2,1,0:T(8,128)(2,1)} %get-tuple-element.66), channel_id=1, source_target_pairs={{0,1},{1,0},{2,3},{3,2},{4,5},{5,4},{6,7},{7,6},{8,9},{9,8},{10,11... | collective-permute-start | bytes 589832 | tf_op jit(solution)/shard_map/ppermute | solution.py:505
  57.9 2.9 %copy-start.9 = (bf16[32,256]{1,0:T(8,128)(2,1)}, bf16[32,256]{1,0:T(8,128)(2,1)S(1)}, u32[]{:S(2)}) copy-start(bf16[32,256]{1,0:T(8,128)(2,1)S(1)} %collective-permute-done.2.refs_3_) | copy-start | bytes 49156
  57.9 25.7 %collective-permute-start.5 = (bf16[3,8,16,256]{3,2,1,0:T(8,128)(2,1)}, bf16[3,8,16,256]{3,2,1,0:T(8,128)(2,1)S(1)}, u32[]{:S(2)}, u32[]{:S(2)}) collective-permute-start(bf16[3,8,16,256]{3,2,1,0:T(8,128)(2,1)} %get-tuple-element.70), channel_id=1, source_target_pairs={{0,3},{3,0},{1,2},{2,1},{4,7},{7,4},{5,6},{6,5},{8,11},{11,8},{9,1... | collective-permute-start | bytes 589832 | tf_op jit(solution)/shard_map/ppermute | solution.py:505
  58.8 2.0 %copy-start.10 = (bf16[32,256]{1,0:T(8,128)(2,1)}, bf16[32,256]{1,0:T(8,128)(2,1)S(1)}, u32[]{:S(2)}) copy-start(bf16[32,256]{1,0:T(8,128)(2,1)S(1)} %collective-permute-done.3.refs_4_) | copy-start | bytes 49156
  58.8 17.7 %collective-permute-start.6 = (bf16[3,8,16,256]{3,2,1,0:T(8,128)(2,1)}, bf16[3,8,16,256]{3,2,1,0:T(8,128)(2,1)S(1)}, u32[]{:S(2)}, u32[]{:S(2)}) collective-permute-start(bf16[3,8,16,256]{3,2,1,0:T(8,128)(2,1)} %get-tuple-element.72), channel_id=1, source_target_pairs={{0,2},{2,0},{1,3},{3,1},{4,6},{6,4},{5,7},{7,5},{8,10},{10,8},{9,1... | collective-permute-start | bytes 589832 | tf_op jit(solution)/shard_map/ppermute | solution.py:505
  60.8 0.7 copy-start.1
  61.5 0.7 copy-start.2
  76.5 0.7 copy-start.8
  83.6 0.7 copy-start.7
  84.3 9.0 %copy-start.16 = (bf16[4,8,16,256]{3,2,1,0:T(8,128)(2,1)S(1)}, bf16[4,8,16,256]{3,2,1,0:T(8,128)(2,1)}, u32[]{:S(2)}) copy-start(bf16[4,8,16,256]{3,2,1,0:T(8,128)(2,1)} %get-tuple-element.80) | copy-start | bytes 786436
  90.8 28.0 %collective-permute-start.8 = (bf16[4,8,16,256]{3,2,1,0:T(8,128)(2,1)}, bf16[4,8,16,256]{3,2,1,0:T(8,128)(2,1)S(1)}, u32[]{:S(2)}, u32[]{:S(2)}) collective-permute-start(bf16[4,8,16,256]{3,2,1,0:T(8,128)(2,1)} %get-tuple-element.79), channel_id=1, source_target_pairs={{0,3},{3,0},{1,2},{2,1},{4,7},{7,4},{5,6},{6,5},{8,11},{11,8},{9,1... | collective-permute-start | bytes 786440 | tf_op jit(solution)/shard_map/ppermute | solution.py:505
  93.3 22.4 %collective-permute-start.9 = (bf16[4,8,16,256]{3,2,1,0:T(8,128)(2,1)S(1)}, bf16[4,8,16,256]{3,2,1,0:T(8,128)(2,1)S(1)}, u32[]{:S(2)}, u32[]{:S(2)}) collective-permute-start(bf16[4,8,16,256]{3,2,1,0:T(8,128)(2,1)S(1)} %copy-done.16), channel_id=1, source_target_pairs={{0,2},{2,0},{1,3},{3,1},{4,6},{6,4},{5,7},{7,5},{8,10},{10,8},{9,1... | collective-permute-start | bytes 786440 | tf_op jit(solution)/shard_map/ppermute | solution.py:505
  93.3 0.7 copy-start.6
  100.4 21.5 %collective-permute-start.7 = (bf16[4,8,16,256]{3,2,1,0:T(8,128)(2,1)}, bf16[4,8,16,256]{3,2,1,0:T(8,128)(2,1)S(1)}, u32[]{:S(2)}, u32[]{:S(2)}) collective-permute-start(bf16[4,8,16,256]{3,2,1,0:T(8,128)(2,1)} %get-tuple-element.78), channel_id=1, source_target_pairs={{0,1},{1,0},{2,3},{3,2},{4,5},{5,4},{6,7},{7,6},{8,9},{9,8},{10,11... | collective-permute-start | bytes 786440 | tf_op jit(solution)/shard_map/ppermute | solution.py:505
  115.7 0.7 copy-start.4
  118.8 0.7 copy-start.3
  121.9 0.7 copy-start.5

commit v3 on v2

--- a/solution.py
+++ b/solution.py
@@ -13,7 +13,7 @@
 LANES = 128
 LOW = 16
 STEP = 4
-VMEM = 56 * 1024 * 1024
+MIB = 1024 * 1024
 
 COS = (
     0.9999999890590228,
@@ -39,6 +39,9 @@
     return lax.dot_general(a, b, (dims, ((), ())), preferred_element_type=F32)
 
 
+BAND, ME, IDS = 0, 1, 2
+
+
 def cost(flops, moved):
     return pl.CostEstimate(flops=int(flops), bytes_accessed=int(moved), transcendentals=0)
 
@@ -58,12 +61,12 @@
     return cosine, sine * y
 
 
-def table_kernel(points, waves_ref, table_ref, twiddle_ref):
+def table_kernel(first, info, waves_ref, table_ref, twiddle_ref):
     size, turns = waves_ref.shape[1], twiddle_ref.shape[2]
-    waves = waves_ref[...]
+    waves = waves_ref[...].astype(F32)
     for k in range(table_ref.shape[0]):
         row = pl.program_id(0) * table_ref.shape[0] + k
-        count = jnp.full(waves.shape, points[row], jnp.int32).astype(F32)
+        count = jnp.full(waves.shape, info[first + row], jnp.int32).astype(F32)
         cos_low, sin_low = unit_circle(1, LOW, waves, count)
         cos_high, sin_high = unit_circle(LOW, LANES // LOW, waves, count)
         cosine, sine = [], []
@@ -78,11 +81,11 @@
         twiddle_ref[k, 1] = sin_turn
 
 
-def tables(points, wave_ids, turns):
-    rows, waves = points.shape[0], wave_ids.shape[0]
+def tables(info, wave_ids, rows, turns):
+    waves = wave_ids.shape[0]
     each = STEP if rows % STEP == 0 else 1
     return pl.pallas_call(
-        table_kernel,
+        functools.partial(table_kernel, info.shape[0] - rows),
         grid_spec=pltpu.PrefetchScalarGridSpec(
             num_scalar_prefetch=1,
             grid=(rows // each,),
@@ -96,10 +99,10 @@
             jax.ShapeDtypeStruct((rows, 2 * waves, LANES), BF16),
             jax.ShapeDtypeStruct((rows, 2, turns, waves), F32),
         ],
-        compiler_params=pltpu.CompilerParams(vmem_limit_bytes=VMEM),
+        compiler_params=pltpu.CompilerParams(vmem_limit_bytes=20 * MIB),
         cost_estimate=cost(rows * waves * LANES * 8, rows * waves * LANES * 4),
         name="tables",
-    )(points, wave_ids.astype(F32)[None, :])
+    )(info, wave_ids[None, :])
 
 
 def place(pieces, width):
@@ -122,12 +125,13 @@
     return out
 
 
-def synth_kernel(me, recv_ref, table_ref, twiddle_ref, *refs):
+def synth_kernel(info, recv_ref, table_ref, twiddle_ref, *refs):
     *out_refs, coef, grid = refs
     sources, levels, rows, _ = recv_ref.shape
     fields, waves = coef.shape[0] // 2, coef.shape[1] * LANES
     share = waves // sources
     each, _, turns = twiddle_ref.shape[:3]
+    pitch = rows + 1
     step = pl.program_id(0)
 
     @pl.when(step == 0)
@@ -139,7 +143,7 @@
                     (values[s], r * share, share, s * share) for s in range(sources)
                 ]
                 for v, part in enumerate(place(windows, waves)):
-                    coef[r, v, pl.ds(l * rows, rows), :] = part
+                    coef[r, v, pl.ds(l * pitch, rows), :] = part
             return carry
 
         lax.fori_loop(0, levels, level, 0)
@@ -148,7 +152,7 @@
         j = step * each + k
 
         def own_row(r):
-            parts = [coef[r, v, pl.ds(j, levels, stride=rows), :] for v in range(waves // LANES)]
+            parts = [coef[r, v, pl.ds(j, levels, stride=pitch), :] for v in range(waves // LANES)]
             return jnp.concatenate(parts, axis=1)
 
         values = [own_row(r) for r in range(2 * fields)]
@@ -161,22 +165,21 @@
                 imag.append(re * s + im * c)
         both = [jnp.concatenate(part, axis=0).astype(BF16) for part in (real, imag)]
         result = dot(jnp.concatenate(both, axis=1), table_ref[k], ((1,), (0,)))
-        grid[pl.ds(j, turns * fields * levels, stride=rows), :] = result
+        grid[pl.ds(j, turns * fields * levels, stride=pitch), :] = result
 
     @pl.when(step == pl.num_programs(0) - 1)
     def _():
         tiles = turns // len(out_refs)
-        size = levels * rows
         for k, out_ref in enumerate(out_refs):
             for t in range(tiles):
                 for f in range(fields):
-                    start = (((me[0] ^ k) * tiles + t) * fields + f) * size
-                    block = grid[pl.ds(pl.multiple_of(start, size), size), :]
-                    block = block.reshape(levels, rows, LANES).astype(BF16)
-                    out_ref[f, :, :, t * LANES : (t + 1) * LANES] = block
-
-
-def synthesis(recv, table, twiddle, me, dests, tile):
+                    start = (((info[ME] ^ k) * tiles + t) * fields + f) * levels
+                    for l in range(levels):
+                        block = grid[pl.ds((start + l) * pitch, rows), :].astype(BF16)
+                        out_ref[f, l, :, t * LANES : (t + 1) * LANES] = block
+
+
+def synthesis(recv, table, twiddle, info, dests, tile):
     sources, levels, rows, lanes = recv.shape
     turns, waves = twiddle.shape[2:]
     fields = 3
@@ -188,25 +191,25 @@
             num_scalar_prefetch=1,
             grid=(rows // each,),
             in_specs=[
-                pl.BlockSpec(recv.shape, lambda j, me: (0, 0, 0, 0)),
-                pl.BlockSpec((each, 2 * waves, LANES), lambda j, me: (j, 0, 0)),
-                pl.BlockSpec((each, 2, turns, waves), lambda j, me: (j, 0, 0, 0)),
+                pl.BlockSpec(recv.shape, lambda j, info: (0, 0, 0, 0)),
+                pl.BlockSpec((each, 2 * waves, LANES), lambda j, info: (j, 0, 0)),
+                pl.BlockSpec((each, 2, turns, waves), lambda j, info: (j, 0, 0, 0)),
             ],
-            out_specs=[pl.BlockSpec(shape, lambda j, me: (0, 0, 0, 0))] * dests,
+            out_specs=[pl.BlockSpec(shape, lambda j, info: (0, 0, 0, 0))] * dests,
             scratch_shapes=[
-                pltpu.VMEM((2 * fields, waves // LANES, levels * rows, LANES), F32),
-                pltpu.VMEM((turns * fields * levels * rows, LANES), F32),
+                pltpu.VMEM((2 * fields, waves // LANES, levels * (rows + 1), LANES), F32),
+                pltpu.VMEM((turns * fields * levels * (rows + 1), LANES), F32),
             ],
         ),
         out_shape=[jax.ShapeDtypeStruct(shape, BF16)] * dests,
-        compiler_params=pltpu.CompilerParams(vmem_limit_bytes=VMEM),
+        compiler_params=pltpu.CompilerParams(vmem_limit_bytes=24 * MIB),
         cost_estimate=cost(4 * rows * waves * fields * levels * turns * LANES, 4 * rows * waves * LANES),
         name="synthesis",
-    )(me, recv, table, twiddle)
+    )(info, recv, table, twiddle)
 
 
 def edge_kernel(
-    odd, state_ref, base_ref, temp_ref, row_a_ref, row_b_ref, col_a_ref, col_b_ref, react_ref
+    info, state_ref, base_ref, temp_ref, row_a_ref, row_b_ref, col_a_ref, col_b_ref, react_ref
 ):
     tracers, levels, rows, tile = state_ref.shape
     cells = tracers * rows
@@ -233,6 +236,7 @@
     def iota(shape, axis):
         return lax.broadcasted_iota(jnp.int32, shape, axis)
 
+    odd = info[BAND] % 2, info[ME] % 2
     far, near = (1 - odd[0]) * (rows - 1), odd[0] * (rows - 1)
     shape = (2 * tracers, cells)
     end = jnp.where(iota(shape, 0) < tracers, far, near)
@@ -254,14 +258,14 @@
     col_b_ref[...] = columns[levels:].astype(BF16)
 
 
-def edges(state, react_base, react_temp, odd):
+def edges(state, react_base, react_temp, info):
     tracers, levels, rows, tile = state.shape
     block = 16
     cells = tracers * rows
     rowed = jax.ShapeDtypeStruct((levels, tracers, tile), BF16)
     columned = jax.ShapeDtypeStruct((levels, cells), BF16)
-    row_spec = pl.BlockSpec((block, tracers, tile), lambda i, odd: (i, 0, 0))
-    col_spec = pl.BlockSpec((block, cells), lambda i, odd: (i, 0))
+    row_spec = pl.BlockSpec((block, tracers, tile), lambda i, info: (i, 0, 0))
+    col_spec = pl.BlockSpec((block, cells), lambda i, info: (i, 0))
     wide = (2 * cells, 2 * cells)
     return pl.pallas_call(
         edge_kernel,
@@ -269,30 +273,30 @@
             num_scalar_prefetch=1,
             grid=(levels // block,),
             in_specs=[
-                pl.BlockSpec((tracers, block, rows, tile), lambda i, odd: (0, i, 0, 0)),
-                pl.BlockSpec(react_base.shape, lambda i, odd: (0, 0)),
-                pl.BlockSpec(react_temp.shape, lambda i, odd: (0, 0)),
+                pl.BlockSpec((tracers, block, rows, tile), lambda i, info: (0, i, 0, 0)),
+                pl.BlockSpec(react_base.shape, lambda i, info: (0, 0)),
+                pl.BlockSpec(react_temp.shape, lambda i, info: (0, 0)),
             ],
             out_specs=[
-                row_spec, row_spec, col_spec, col_spec, pl.BlockSpec(wide, lambda i, odd: (0, 0)),
+                row_spec, row_spec, col_spec, col_spec, pl.BlockSpec(wide, lambda i, info: (0, 0)),
             ],
         ),
         out_shape=[rowed, rowed, columned, columned, jax.ShapeDtypeStruct(wide, BF16)],
-        compiler_params=pltpu.CompilerParams(vmem_limit_bytes=VMEM),
+        compiler_params=pltpu.CompilerParams(vmem_limit_bytes=16 * MIB),
         cost_estimate=cost(4 * state.size * 32, 2 * state.size),
         name="edges",
-    )(odd, state, react_base, react_temp)
-
-
-def chem_kernel(scale, info, *refs):
-    state_ref, row_a_ref, row_b_ref, col_a_ref, col_b_ref, grid_ref, mask_ref, react_ref = refs[:8]
-    along_ref, across_ref = refs[8:10]
+    )(info, state, react_base, react_temp)
+
+
+def chem_kernel(scale, k, info, *refs):
+    state_ref, row_a_ref, row_b_ref, col_a_ref, col_b_ref, grid_ref, react_ref = refs[:7]
+    along_ref, across_ref = refs[7:9]
     new_ref, active_ref, south, north = refs[-4:]
     tracers, levels, rows, tile = state_ref.shape
     cells = tracers * rows
     half, side = rows // 2, tile // 2
-    group, odd_band, odd_tile = info[0], info[1] == 1, info[2] == 1
-    first = (group * pl.num_programs(0) + pl.program_id(0)) * levels
+    odd_band, odd_tile = info[BAND] % 2 == 1, info[ME] % 2 == 1
+    first = ((info[ME] ^ k) * pl.num_programs(0) + pl.program_id(0)) * levels
 
     def column(value):
         pad = jnp.zeros((LANES - value.shape[0], cells), F32)
@@ -303,7 +307,11 @@
     west, east = column(jnp.where(odd_tile, a, b)), column(jnp.where(odd_tile, b, a))
     row = lax.broadcasted_iota(jnp.int32, (rows, tile), 0)
     lane = lax.broadcasted_iota(jnp.int32, (rows, tile), 1)
-    mask = mask_ref[...]
+    ids, points = IDS, IDS + active_ref.shape[0]
+    count = jnp.full((rows, tile), info[points], jnp.int32)
+    for j in range(1, rows):
+        count = jnp.where(row == j, info[points + j], count)
+    mask = jnp.where(info[ME] * tile + lane < count, 1.0, 0.0)
     nn = ((1,), (0,))
 
     def three(v):
@@ -343,10 +351,10 @@
         reacted = (moved + three(terms[:cells]) + temper * three(terms[cells:])) * mask
         new_ref[:, l] = reacted.astype(BF16)
     for a in range(active_ref.shape[0]):
-        active_ref[a] = new_ref[info[3 + a]]
-
-
-def chemistry(state, halos, grid, mask, react, info, actives, waves, before):
+        active_ref[a] = new_ref[info[ids + a]]
+
+
+def chemistry(state, halos, grid, react, info, k, actives, waves, before):
     tracers, levels, rows, tile = state.shape
     fields, own = grid.shape[:2]
     some = 4 if own % 4 == 0 else own
@@ -363,12 +371,12 @@
     def whole(shape):
         return pl.BlockSpec(shape, lambda i, info: (0,) * len(shape))
 
-    row_spec = pl.BlockSpec((some, tracers, tile), lambda i, info: (info[0] * steps + i, 0, 0))
+    row_spec = pl.BlockSpec((some, tracers, tile), lambda i, info: ((info[ME] ^ k) * steps + i, 0, 0))
     state_spec = pl.BlockSpec(
-        (tracers, some, rows, tile), lambda i, info: (0, info[0] * steps + i, 0, 0)
+        (tracers, some, rows, tile), lambda i, info: (0, (info[ME] ^ k) * steps + i, 0, 0)
     )
     operands = [
-        state, *halos, grid, mask, react, jnp.asarray(along, BF16), jnp.asarray(across, BF16),
+        state, *halos, grid, react, jnp.asarray(along, BF16), jnp.asarray(across, BF16),
     ]
     in_specs = [
         state_spec,
@@ -377,7 +385,6 @@
         whole(halos[2].shape),
         whole(halos[3].shape),
         pl.BlockSpec((fields, some, rows, tile), lambda i, info: (0, i, 0, 0)),
-        whole(mask.shape),
         whole(react.shape),
         whole(along.shape),
         whole(across.shape),
@@ -388,7 +395,7 @@
         operands.append(before)
         in_specs.append(pl.BlockSpec(memory_space=pl.ANY))
     return pl.pallas_call(
-        functools.partial(chem_kernel, scale),
+        functools.partial(chem_kernel, scale, k),
         grid_spec=pltpu.PrefetchScalarGridSpec(
             num_scalar_prefetch=1,
             grid=(steps,),
@@ -404,8 +411,8 @@
             jax.ShapeDtypeStruct((actives, own, rows, tile), BF16),
         ],
         input_output_aliases=aliases,
-        compiler_params=pltpu.CompilerParams(vmem_limit_bytes=VMEM),
-        cost_estimate=cost(own * cells * tile * 2 * 2048, own * cells * tile * 4),
+        compiler_params=pltpu.CompilerParams(vmem_limit_bytes=16 * MIB),
+        cost_estimate=cost(own * cells * tile, own * tile),
         name="chemistry",
     )(info, *operands)
 
@@ -414,7 +421,7 @@
     refs[-1][...] = recv_ref[...].astype(F32)
 
 
-def spread(recv, info, sources, before):
+def spread(recv, info, k, sources, before):
     actives, own, rows, tile = recv.shape
     each = 2 if actives % 2 == 0 else 1
     operands = [recv]
@@ -430,12 +437,12 @@
             num_scalar_prefetch=1,
             grid=(actives // each,),
             in_specs=in_specs,
-            out_specs=pl.BlockSpec((each, own, rows, tile), lambda a, info: (a, 0, 0, info[0])),
+            out_specs=pl.BlockSpec((each, own, rows, tile), lambda a, info: (a, 0, 0, info[ME] ^ k)),
         ),
         out_shape=jax.ShapeDtypeStruct((actives, own, rows, sources * tile), F32),
         input_output_aliases=aliases,
-        compiler_params=pltpu.CompilerParams(vmem_limit_bytes=VMEM),
-        cost_estimate=cost(recv.size, recv.size * 6),
+        compiler_params=pltpu.CompilerParams(vmem_limit_bytes=8 * MIB),
+        cost_estimate=cost(recv.size, recv.shape[0]),
         name="spread",
     )(info, *operands)
 
@@ -446,33 +453,36 @@
     share = block * pl.num_programs(0)
     step = pl.program_id(0)
     lines = parts * own
+    apart, stretch = block + 1, pitch + 1
 
     @pl.when(step == 0)
     def _():
         for h in range(sums.shape[0]):
             for l in range(own):
-                tail = slice(l * pitch + parts * share, (l + 1) * pitch)
+                tail = pl.ds(l * stretch + parts * share, pitch - parts * share)
                 sums[h, tail, :] = jnp.zeros((pitch - parts * share, LANES), F32)
 
     for v in range(size // LANES):
         part = spectral_ref[:, :, :, v * LANES : (v + 1) * LANES].astype(F32)
-        rows_of[v] = part.reshape(lines * block, LANES)
+        part = part.reshape(lines, block, LANES)
+        for i in range(lines):
+            rows_of[v, pl.ds(i * apart, block), :] = part[i]
     for m in range(block):
-        x = [rows_of[v, pl.ds(m, lines, stride=block), :] for v in range(size // LANES)]
+        x = [rows_of[v, pl.ds(m, lines, stride=apart), :] for v in range(size // LANES)]
         x = jnp.concatenate(x, axis=1).astype(BF16)
         result = dot(x, legendre_ref[m], ((1,), (0,)))
         for r in range(parts):
             at = r * share + step * block + m
             for h in range(sums.shape[0]):
                 piece = result[r * own : (r + 1) * own, h * LANES : (h + 1) * LANES]
-                sums[h, pl.ds(at, own, stride=pitch), :] = piece
+                sums[h, pl.ds(at, own, stride=stretch), :] = piece
 
     @pl.when(step == pl.num_programs(0) - 1)
     def _():
         some = LANES // rows
         for l in range(own):
             for h in range(sums.shape[0]):
-                turned = sums[h, l * pitch : (l + 1) * pitch, :].T.astype(BF16)
+                turned = sums[h, pl.ds(l * stretch, pitch), :].T.astype(BF16)
                 out_ref[h * some : (h + 1) * some, l] = turned.reshape(some, rows, pitch)
 
 
@@ -492,10 +502,10 @@
         out_specs=pl.BlockSpec(shape, lambda i: (0, 0, 0, 0)),
         out_shape=jax.ShapeDtypeStruct(shape, BF16),
         scratch_shapes=[
-            pltpu.VMEM((size // LANES, parts * own * block, LANES), F32),
-            pltpu.VMEM((legendre.shape[2] // LANES, own * pitch, LANES), F32),
+            pltpu.VMEM((size // LANES, parts * own * (block + 1), LANES), F32),
+            pltpu.VMEM((legendre.shape[2] // LANES, own * (pitch + 1), LANES), F32),
         ],
-        compiler_params=pltpu.CompilerParams(vmem_limit_bytes=VMEM),
+        compiler_params=pltpu.CompilerParams(vmem_limit_bytes=56 * MIB),
         cost_estimate=cost(2 * parts * own * legendre.size, 2 * (spectral.size + legendre.size)),
         name="legendre",
     )(spectral, legendre)
@@ -523,39 +533,41 @@
     sent = legendre_sums(spectral, legendre, bands)
     recv = lax.all_to_all(sent, "lat", split_axis=0, concat_axis=0, tiled=True)
 
-    table, twiddle = tables(points, wave_ids, tiles * tile // LANES)
-    odd = jnp.stack([band % 2, me % 2]).astype(jnp.int32)
-    row_a, row_b, col_a, col_b, react = edges(tracers, react_base, react_temp, odd)
-    columns = me * tile + jnp.arange(tile)
-    mask = (columns[None, :] < points[:, None]).astype(F32)
-    infos = [
-        jnp.concatenate([jnp.stack([me ^ k, odd[0], odd[1]]), active_ids]).astype(jnp.int32)
-        for k in range(tiles)
-    ]
-    recv, table, twiddle, row_a, row_b, col_a, col_b, react, mask, infos = lax.optimization_barrier(
-        (recv, table, twiddle, row_a, row_b, col_a, col_b, react, mask, infos)
-    )
-
-    grids = synthesis(recv, table, twiddle, infos[0][:1], tiles, tile)
-    row_a, row_b, col_a, col_b, grids = lax.optimization_barrier((row_a, row_b, col_a, col_b, grids))
-    order = list(range(2, tiles)) + [1]
-    grids = {0: grids[0]} | {k: exchange(grids[k], "lon", partners("lon", k)) for k in order}
+    rows = points.shape[0]
+    info = jnp.concatenate([jnp.stack([band, me]), active_ids, points]).astype(jnp.int32)
+    table, twiddle = tables(info, wave_ids, rows, tiles * tile // LANES)
+    *ends, react = edges(tracers, react_base, react_temp, info)
+    recv, table, twiddle, ends, react = lax.optimization_barrier((recv, table, twiddle, ends, react))
+
+    grids = synthesis(recv, table, twiddle, info, tiles, tile)
+    ends, grids = lax.optimization_barrier((ends, grids))
+    middle = list(range(tiles // 2, tiles))
+    soon, late = middle[: tiles // 4], middle[tiles // 4 :]
+    inner = list(range(tiles // 2 - 1, 0, -1))
+
+    def send(value, k):
+        return exchange(value, "lon", partners("lon", k))
+
+    moved = {0: grids[0]} | {k: send(grids[k], k) for k in soon + inner}
     halos = (
-        exchange(row_a, "lat", neighbours("lat", 0)),
-        exchange(row_b, "lat", neighbours("lat", 1)),
-        exchange(col_a, "lon", neighbours("lon", 0)),
-        exchange(col_b, "lon", neighbours("lon", 1)),
+        exchange(ends[0], "lat", neighbours("lat", 0)),
+        exchange(ends[1], "lat", neighbours("lat", 1)),
+        exchange(ends[2], "lon", neighbours("lon", 0)),
+        exchange(ends[3], "lon", neighbours("lon", 1)),
     )
     new, active = None, {}
-    for k in [0] + order:
+    for k in [0] + soon + late + inner:
         new, active[k] = chemistry(
-            tracers, halos, grids[k], mask, react, infos[k], active_ids.shape[0], waves, new
+            tracers, halos, moved[k], react, info, k, active_ids.shape[0], waves, new
         )
         if k:
-            active[k] = exchange(active[k], "lon", partners("lon", k))
+            active[k] = send(active[k], k)
+        else:
+            held, active[0] = lax.optimization_barrier(([grids[i] for i in late], active[0]))
+            moved |= {i: send(value, i) for i, value in zip(late, held)}
     spreaded = None
-    for k in [0] + order:
-        spreaded = spread(active[k], infos[k], tiles, spreaded)
+    for k in [0] + soon + inner + late:
+        spreaded = spread(active[k], info, k, tiles, spreaded)
     return new, spreaded
 
 

time: 126 us -> 97.9 us (0.78)
  Pallas kernels: 74.9 us -> 53.2 us
  waiting for transfers between devices: 18.8 us -> 10.8 us
  starting transfers between devices: 20.8 us -> 24.6 us
  other arithmetic: 2.6 us -> 0.08 us
    ppermute x10, waiting for transfers between devices: 18.8 us -> 8.04 us  [exchange(): lax.ppermute(value, axis, [p for a, b in pairs for p in ((a, b), (b, a))])]
    pallas_call x5, Pallas kernels: 32.4 us -> 24.7 us  [the longest x4 20.1 us: chemistry(): pl.pallas_call(functools.partial(chem_kernel, scale, k), grid_spec=pltpu....]
    pallas_call x1, Pallas kernels: 9.4 us -> 5.01 us  [synthesis(): pl.pallas_call(synth_kernel, grid_spec=pltpu.PrefetchScalarGridSpec(num_s...]
    pallas_call x4, Pallas kernels: 9.53 us -> 5.49 us  [spread(): pl.pallas_call(spread_kernel, grid_spec=pltpu.PrefetchScalarGridSpec(num_...]
    ppermute x10, starting transfers between devices: 15.5 us -> 19.4 us  [exchange(): lax.ppermute(value, axis, [p for a, b in pairs for p in ((a, b), (b, a))])]
    pallas_call x1, Pallas kernels: 18 us -> 14.6 us  [legendre_sums(): pl.pallas_call(legendre_kernel, grid=(share // block,), in_specs=[pl.Bloc...]
    all_to_all x1, waiting for transfers between devices: 0.01 us -> 2.71 us  [body(): recv = lax.all_to_all(sent, 'lat', split_axis=0, concat_axis=0, tiled=True)]
    pallas_call x1, Pallas kernels: 5.63 us -> 3.44 us  [edges(): pl.pallas_call(edge_kernel, grid_spec=pltpu.PrefetchScalarGridSpec(num_sc...]
  transfers between devices with their start and end apart: 11 -> 11, of which waited for: 2 -> 3; matrix products, arithmetic and copies ran while one was open for 3% -> 0% of each run, Pallas kernels for 36% -> 33%
where the time goes in v3:
time: 97.9 us; the launch traced here: 96.6 us
  Pallas kernels  53.2 us (54%)
  starting transfers between devices  24.6 us (25%)
  waiting for transfers between devices  10.8 us (11%)
  local copies, waits for them, and re-layouts  7.18 us (7%)
    pallas_call x4, Pallas kernels, chemistry(): pl.pallas_call(functools.partial(chem_kernel, scale, k), grid_spec=pltpu....  20.1 us
    ppermute x10, starting transfers between devices, exchange(): lax.ppermute(value, axis, [p for a, b in pairs for p in ((a, b), (b, a))])  19.4 us
    pallas_call x1, Pallas kernels, legendre_sums(): pl.pallas_call(legendre_kernel, grid=(share // block,), in_specs=[pl.Bloc...  14.6 us
    ppermute x10, waiting for transfers between devices, exchange(): lax.ppermute(value, axis, [p for a, b in pairs for p in ((a, b), (b, a))])  8.04 us
    unnamed x22, local copies, waits for them, and re-layouts  7.18 us
    pallas_call x4, Pallas kernels, spread(): pl.pallas_call(spread_kernel, grid_spec=pltpu.PrefetchScalarGridSpec(num_...  5.49 us
    all_to_all x1, starting transfers between devices, body(): recv = lax.all_to_all(sent, 'lat', split_axis=0, concat_axis=0, tiled=True)  5.18 us
    pallas_call x1, Pallas kernels, synthesis(): pl.pallas_call(synth_kernel, grid_spec=pltpu.PrefetchScalarGridSpec(num_s...  5.01 us
  transfers between devices with their start and end apart: 11, of which 3 were waited for; matrix products, arithmetic and copies ran while one was open for 0% of the time, Pallas kernels for 33%

profile of v3, /device:TPU:0, one launch (start us, length us, event | category | flops | bytes accessed | tf_op | source)
XLA Modules:
  0.0 96.6 jit_solution(13011995232692663475)
XLA Ops:
  0.6 0.0 copy-start.8
  0.6 0.0 copy-start.9
  0.7 0.0 copy-start.10
  0.7 0.0 copy-start.6
  0.7 0.0 copy-start.7
  0.7 14.6 %legendre.1 = bf16[8,8,16,512]{3,2,1,0:T(8,128)(2,1)} custom-call(bf16[6,8,80,1280]{3,2,1,0:T(8,128)(2,1)} %spectral_ref.1, bf16[80,1280,128]{2,1,0:T(8,128)(2,1)} %legendre_ref.1), custom_call_target="tpu_custom_call" | custom-call | flops 1258291200 | bytes 36044800 | tf_op jit(solution)/shard_map/legendre/pallas_call | solution.py:495
  15.2 5.2 %all-to-all-start = ((bf16[8,8,16,512]{3,2,1,0:T(8,128)(2,1)}), bf16[8,8,16,512]{3,2,1,0:T(8,128)(2,1)S(1)}, u32[]{:S(2)}, u32[]{:S(2)}) async-start(bf16[8,8,16,512]{3,2,1,0:T(8,128)(2,1)} %legendre.1), calls=%async_computation | async-start | bytes 2097152 | tf_op jit(solution)/shard_map/all_to_all | solution.py:534
  20.4 0.0 copy-done.8
  20.4 0.0 copy-done.9
  20.5 0.0 copy-done.10
  20.5 0.1 pad_add_fusion.info
  20.5 4.6 %tables.1 = (bf16[16,1280,128]{2,1,0:T(8,128)(2,1)S(1)}, f32[16,2,8,640]{3,2,1,0:T(8,128)S(1)}) custom-call(s32[22]{0:T(128)S(1)} %pad_add_fusion.info, s32[1,640]{1,0:T(1,128)S(1)} %broadcast_in_dim.3.waves_ref), custom_call_target="tpu_custom_call" | custom-call | flops 10485760 | bytes 5242880 | tf_op jit(solution)/shard_map/tables/pallas_call | solution.py:87
  25.1 0.0 copy-start.2
  25.2 2.3 %copy-done.2 = bf16[16,1280,128]{2,1,0:T(8,128)(2,1)} copy-done((bf16[16,1280,128]{2,1,0:T(8,128)(2,1)}, bf16[16,1280,128]{2,1,0:T(8,128)(2,1)S(1)}, u32[]{:S(2)}) %copy-start.2) | copy-done | bytes 5242904
  27.5 0.0 copy-done.6
  27.5 0.0 copy-done.7
  27.5 0.0 copy-start
  27.5 2.2 %copy-done = bf16[16,32,16,256]{3,2,1,0:T(8,128)(2,1)S(1)} copy-done((bf16[16,32,16,256]{3,2,1,0:T(8,128)(2,1)S(1)}, bf16[16,32,16,256]{3,2,1,0:T(8,128)(2,1)}, u32[]{:S(2)}) %copy-start) | copy-done | bytes 4194328
  29.7 0.0 copy-start.4
  29.7 0.0 copy-start.5
  29.7 3.4 %edges.1 = (bf16[32,16,256]{2,1,0:T(8,128)(2,1)S(1)}, bf16[32,16,256]{2,1,0:T(8,128)(2,1)S(1)}, bf16[32,256]{1,0:T(8,128)(2,1)S(1)}, bf16[32,256]{1,0:T(8,128)(2,1)S(1)}, bf16[512,512]{1,0:T(8,128)(2,1)S(1)}) custom-call(s32[22]{0:T(128)S(1)} %pad_add_fusion.info, bf16[16,32,16,256]{3,2,1,0:T(8,128)(2,1)S(1)} %copy-done, f32[16,16]{1,0:T(8,128)S(1)} %copy-done.6, ...), custom_call_target="tpu_custom_call" | custom-call | flops 268435456 | bytes 4194304 | tf_op jit(solution)/shard_map/edges/pallas_call | solution.py:270
  33.1 2.7 %all-to-all-done.recv_ref = bf16[8,8,16,512]{3,2,1,0:T(8,128)(2,1)S(1)} async-done(((bf16[8,8,16,512]{3,2,1,0:T(8,128)(2,1)}), bf16[8,8,16,512]{3,2,1,0:T(8,128)(2,1)S(1)}, u32[]{:S(2)}, u32[]{:S(2)}) %all-to-all-start) | async-done | bytes 1048608 | tf_op jit(solution)/shard_map/all_to_all | solution.py:534
  35.8 0.0 copy-start.1
  35.8 0.0 copy-start.3
  35.8 2.6 %copy-done.3 = bf16[16,1280,128]{2,1,0:T(8,128)(2,1)S(1)} copy-done((bf16[16,1280,128]{2,1,0:T(8,128)(2,1)S(1)}, bf16[16,1280,128]{2,1,0:T(8,128)(2,1)}, u32[]{:S(2)}) %copy-start.3) | copy-done | bytes 5242904
  38.5 5.0 %synthesis.1 = (bf16[3,8,16,256]{3,2,1,0:T(8,128)(2,1)S(1)}, bf16[3,8,16,256]{3,2,1,0:T(8,128)(2,1)S(1)}, bf16[3,8,16,256]{3,2,1,0:T(8,128)(2,1)S(1)}, bf16[3,8,16,256]{3,2,1,0:T(8,128)(2,1)S(1)}) custom-call(s32[22]{0:T(128)S(1)} %pad_add_fusion.info, bf16[8,8,16,512]{3,2,1,0:T(8,128)(2,1)S(1)} %all-to-all-done.recv_ref, ...), custom_call_target="tpu_custom_call" | custom-call | flops 1006632960 | bytes 5242880 | tf_op jit(solution)/shard_map/synthesis/pallas_call | solution.py:188
  43.5 0.1 collective-permute-start
  43.6 0.7 collective-permute-start.1
  44.3 1.6 %collective-permute-start.2 = (bf16[32,256]{1,0:T(8,128)(2,1)S(1)}, bf16[32,256]{1,0:T(8,128)(2,1)S(1)}, u32[]{:S(2)}, u32[]{:S(2)}) collective-permute-start(bf16[32,256]{1,0:T(8,128)(2,1)S(1)} %get-tuple-element.59), channel_id=1, source_target_pairs={{0,1},{1,0},{2,3},{3,2},{4,5},{5,4},{6,7},{7,6},{8,9},{9,8},{10,11... | collective-permute-start | bytes 49160 | tf_op jit(solution)/shard_map/ppermute | solution.py:515
  45.9 0.8 collective-permute-start.3
  46.7 3.9 %collective-permute-start.6 = (bf16[3,8,16,256]{3,2,1,0:T(8,128)(2,1)S(1)}, bf16[3,8,16,256]{3,2,1,0:T(8,128)(2,1)S(1)}, u32[]{:S(2)}, u32[]{:S(2)}) collective-permute-start(bf16[3,8,16,256]{3,2,1,0:T(8,128)(2,1)S(1)} %get-tuple-element.67), channel_id=1, source_target_pairs={{0,2},{2,0},{1,3},{3,1},{4,6},{6,4},{5,7},{7,5},{8,10},{10,8},{9,1... | collective-permute-start | bytes 589832 | tf_op jit(solution)/shard_map/ppermute | solution.py:515
  50.6 0.0 collective-permute-done.2.refs_3_
  50.7 0.0 collective-permute-done.3.refs_4_
  50.7 0.0 collective-permute-done.refs_1_
  50.7 0.0 collective-permute-done.1.refs_2_
  50.7 0.0 copy-done.4
  50.7 0.0 copy-done.5
  50.7 0.0 copy-done.1
  50.7 5.0 %chemistry.4 = (bf16[16,32,16,256]{3,2,1,0:T(8,128)(2,1)}, bf16[4,8,16,256]{3,2,1,0:T(8,128)(2,1)S(1)}) custom-call(s32[22]{0:T(128)S(1)} %pad_add_fusion.info, bf16[16,32,16,256]{3,2,1,0:T(8,128)(2,1)S(1)} %copy-done.1, bf16[32,16,256]{2,1,0:T(8,128)(2,1)S(1)} %collective-permute-done.refs_1_, bf16[32,16,256]{2,1,0:T(8,128)(2,1)S(1)} %collective-permute-done.1.refs_2_, ...), custom_call_target="tpu_custom_call" | custom-call | flops 524288 | bytes 2048 | tf_op jit(solution)/shard_map/chemistry/pallas_call | solution.py:397
  55.7 2.9 %collective-permute-start.5 = (bf16[3,8,16,256]{3,2,1,0:T(8,128)(2,1)S(1)}, bf16[3,8,16,256]{3,2,1,0:T(8,128)(2,1)S(1)}, u32[]{:S(2)}, u32[]{:S(2)}) collective-permute-start(bf16[3,8,16,256]{3,2,1,0:T(8,128)(2,1)S(1)} %get-tuple-element.66), channel_id=1, source_target_pairs={{0,3},{3,0},{1,2},{2,1},{4,7},{7,4},{5,6},{6,5},{8,11},{11,8},{9,1... | collective-permute-start | bytes 589832 | tf_op jit(solution)/shard_map/ppermute | solution.py:515
  58.7 1.1 %collective-permute-start.4 = (bf16[3,8,16,256]{3,2,1,0:T(8,128)(2,1)S(1)}, bf16[3,8,16,256]{3,2,1,0:T(8,128)(2,1)S(1)}, u32[]{:S(2)}, u32[]{:S(2)}) collective-permute-start(bf16[3,8,16,256]{3,2,1,0:T(8,128)(2,1)S(1)} %get-tuple-element.61), channel_id=1, source_target_pairs={{0,1},{1,0},{2,3},{3,2},{4,5},{5,4},{6,7},{7,6},{8,9},{9,8},{10,11... | collective-permute-start | bytes 589832 | tf_op jit(solution)/shard_map/ppermute | solution.py:515
  59.7 0.3 collective-permute-done.6.refs_5_
  60.0 5.0 %chemistry.5 = (bf16[16,32,16,256]{3,2,1,0:T(8,128)(2,1)}, bf16[4,8,16,256]{3,2,1,0:T(8,128)(2,1)S(1)}) custom-call(s32[22]{0:T(128)S(1)} %pad_add_fusion.info, bf16[16,32,16,256]{3,2,1,0:T(8,128)(2,1)S(1)} %copy-done.1, bf16[32,16,256]{2,1,0:T(8,128)(2,1)S(1)} %collective-permute-done.refs_1_, ...), custom_call_target="tpu_custom_call", output_to_operand_aliasing={{0}: (10, {})} | custom-call | flops 524288 | bytes 2048 | tf_op jit(solution)/shard_map/chemistry/pallas_call | solution.py:397
  65.0 0.1 collective-permute-start.9
  65.1 0.0 collective-permute-done.5.refs_5_
  65.1 5.0 %chemistry.6 = (bf16[16,32,16,256]{3,2,1,0:T(8,128)(2,1)}, bf16[4,8,16,256]{3,2,1,0:T(8,128)(2,1)S(1)}) custom-call(s32[22]{0:T(128)S(1)} %pad_add_fusion.info, bf16[16,32,16,256]{3,2,1,0:T(8,128)(2,1)S(1)} %copy-done.1, bf16[32,16,256]{2,1,0:T(8,128)(2,1)S(1)} %collective-permute-done.refs_1_, ...), custom_call_target="tpu_custom_call", output_to_operand_aliasing={{0}: (10, {})} | custom-call | flops 524288 | bytes 2048 | tf_op jit(solution)/shard_map/chemistry/pallas_call | solution.py:397
  70.2 0.0 collective-permute-done.4.refs_5_
  70.2 5.0 %chemistry.7 = (bf16[16,32,16,256]{3,2,1,0:T(8,128)(2,1)}, bf16[4,8,16,256]{3,2,1,0:T(8,128)(2,1)S(1)}) custom-call(s32[22]{0:T(128)S(1)} %pad_add_fusion.info, bf16[16,32,16,256]{3,2,1,0:T(8,128)(2,1)S(1)} %copy-done.1, bf16[32,16,256]{2,1,0:T(8,128)(2,1)S(1)} %collective-permute-done.refs_1_, ...), custom_call_target="tpu_custom_call", output_to_operand_aliasing={{0}: (10, {})} | custom-call | flops 524288 | bytes 2048 | tf_op jit(solution)/shard_map/chemistry/pallas_call | solution.py:397
  75.2 4.3 %collective-permute-start.8 = (bf16[4,8,16,256]{3,2,1,0:T(8,128)(2,1)S(1)}, bf16[4,8,16,256]{3,2,1,0:T(8,128)(2,1)S(1)}, u32[]{:S(2)}, u32[]{:S(2)}) collective-permute-start(bf16[4,8,16,256]{3,2,1,0:T(8,128)(2,1)S(1)} %get-tuple-element.73), channel_id=1, source_target_pairs={{0,1},{1,0},{2,3},{3,2},{4,5},{5,4},{6,7},{7,6},{8,9},{9,8},{10,11... | collective-permute-start | bytes 786440 | tf_op jit(solution)/shard_map/ppermute | solution.py:515
  79.4 3.9 %collective-permute-start.7 = (bf16[4,8,16,256]{3,2,1,0:T(8,128)(2,1)S(1)}, bf16[4,8,16,256]{3,2,1,0:T(8,128)(2,1)S(1)}, u32[]{:S(2)}, u32[]{:S(2)}) collective-permute-start(bf16[4,8,16,256]{3,2,1,0:T(8,128)(2,1)S(1)} %get-tuple-element.72), channel_id=1, source_target_pairs={{0,3},{3,0},{1,2},{2,1},{4,7},{7,4},{5,6},{6,5},{8,11},{11,8},{9,1... | collective-permute-start | bytes 786440 | tf_op jit(solution)/shard_map/ppermute | solution.py:515
  83.3 1.4 %spread.4.refs_0_ = f32[4,8,16,1024]{3,2,1,0:T(8,128)} custom-call(s32[22]{0:T(128)S(1)} %pad_add_fusion.info, bf16[4,8,16,256]{3,2,1,0:T(8,128)(2,1)S(1)} %get-tuple-element.75.recv_ref), custom_call_target="tpu_custom_call" | custom-call | flops 131072 | bytes 4 | tf_op jit(solution)/shard_map/spread/pallas_call | solution.py:434
  84.7 0.0 collective-permute-done.9.recv_ref
  84.7 1.4 %spread.5.refs_0_ = f32[4,8,16,1024]{3,2,1,0:T(8,128)} custom-call(s32[22]{0:T(128)S(1)} %pad_add_fusion.info, bf16[4,8,16,256]{3,2,1,0:T(8,128)(2,1)S(1)} %collective-permute-done.9.recv_ref, f32[4,8,16,1024]{3,2,1,0:T(8,128)} %spread.4.refs_0_), custom_call_target="tpu_custom_call", output_to_operand_aliasing={{}: (2, {})} | custom-call | flops 131072 | bytes 4 | tf_op jit(solution)/shard_map/spread/pallas_call | solution.py:434
  86.1 0.0 collective-permute-done.8.recv_ref
  86.1 1.4 %spread.6.refs_0_ = f32[4,8,16,1024]{3,2,1,0:T(8,128)} custom-call(s32[22]{0:T(128)S(1)} %pad_add_fusion.info, bf16[4,8,16,256]{3,2,1,0:T(8,128)(2,1)S(1)} %collective-permute-done.8.recv_ref, f32[4,8,16,1024]{3,2,1,0:T(8,128)} %spread.5.refs_0_), custom_call_target="tpu_custom_call", output_to_operand_aliasing={{}: (2, {})} | custom-call | flops 131072 | bytes 4 | tf_op jit(solution)/shard_map/spread/pallas_call | solution.py:434
  87.4 7.8 %collective-permute-done.7.recv_ref = bf16[4,8,16,256]{3,2,1,0:T(8,128)(2,1)S(1)} collective-permute-done((bf16[4,8,16,256]{3,2,1,0:T(8,128)(2,1)S(1)}, bf16[4,8,16,256]{3,2,1,0:T(8,128)(2,1)S(1)}, u32[]{:S(2)}, u32[]{:S(2)}) %collective-permute-start.7) | collective-permute-done | bytes 262176 | tf_op jit(solution)/shard_map/ppermute | solution.py:515
  95.2 1.4 %spread.7 = f32[4,8,16,1024]{3,2,1,0:T(8,128)} custom-call(s32[22]{0:T(128)S(1)} %pad_add_fusion.info, bf16[4,8,16,256]{3,2,1,0:T(8,128)(2,1)S(1)} %collective-permute-done.7.recv_ref, f32[4,8,16,1024]{3,2,1,0:T(8,128)} %spread.6.refs_0_), custom_call_target="tpu_custom_call", output_to_operand_aliasing={{}: (2, {})} | custom-call | flops 131072 | bytes 4 | tf_op jit(solution)/shard_map/spread/pallas_call | solution.py:434
  (1 shorter events, 0.0 us)
Async XLA Ops:
  0.6 19.8 %copy-start.8 = (s32[640]{0:T(1024)S(1)}, s32[640]{0:T(1024)}, u32[]{:S(2)}) copy-start(s32[640]{0:T(1024)} %param.18) | copy-start | bytes 7684
  0.6 19.8 %copy-start.9 = (s32[16]{0:T(128)S(1)}, s32[16]{0:T(128)}, u32[]{:S(2)}) copy-start(s32[16]{0:T(128)} %param.19) | copy-start | bytes 196
  0.7 19.8 %copy-start.10 = (s32[4]{0:T(128)S(1)}, s32[4]{0:T(128)}, u32[]{:S(2)}) copy-start(s32[4]{0:T(128)} %param.23) | copy-start | bytes 52
  0.7 26.8 %copy-start.6 = (f32[16,16]{1,0:T(8,128)S(1)}, f32[16,16]{1,0:T(8,128)}, u32[]{:S(2)}) copy-start(f32[16,16]{1,0:T(8,128)} %base_ref.1) | copy-start | bytes 3076
  0.7 26.8 %copy-start.7 = (f32[16,16]{1,0:T(8,128)S(1)}, f32[16,16]{1,0:T(8,128)}, u32[]{:S(2)}) copy-start(f32[16,16]{1,0:T(8,128)} %temp_ref.1) | copy-start | bytes 3076
  15.2 20.6 %all-to-all-start = ((bf16[8,8,16,512]{3,2,1,0:T(8,128)(2,1)}), bf16[8,8,16,512]{3,2,1,0:T(8,128)(2,1)S(1)}, u32[]{:S(2)}, u32[]{:S(2)}) async-start(bf16[8,8,16,512]{3,2,1,0:T(8,128)(2,1)} %legendre.1), calls=%async_computation | async-start | bytes 2097152 | tf_op jit(solution)/shard_map/all_to_all | solution.py:534
  25.1 2.3 %copy-start.2 = (bf16[16,1280,128]{2,1,0:T(8,128)(2,1)}, bf16[16,1280,128]{2,1,0:T(8,128)(2,1)S(1)}, u32[]{:S(2)}) copy-start(bf16[16,1280,128]{2,1,0:T(8,128)(2,1)S(1)} %get-tuple-element.51.table_ref) | copy-start | bytes 15728644
  27.5 2.2 %copy-start = (bf16[16,32,16,256]{3,2,1,0:T(8,128)(2,1)S(1)}, bf16[16,32,16,256]{3,2,1,0:T(8,128)(2,1)}, u32[]{:S(2)}) copy-start(bf16[16,32,16,256]{3,2,1,0:T(8,128)(2,1)} %refs_0_.7) | copy-start | bytes 12582916
  29.7 21.0 %copy-start.4 = (bf16[256,512]{1,0:T(8,128)(2,1)S(1)}, bf16[256,512]{1,0:T(8,128)(2,1)}, u32[]{:S(2)}) copy-start(bf16[256,512]{1,0:T(8,128)(2,1)} %constant.13.clone.refs_7_) | copy-start | bytes 786436
  29.7 21.0 %copy-start.5 = (bf16[512,256]{1,0:T(8,128)(2,1)S(1)}, bf16[512,256]{1,0:T(8,128)(2,1)}, u32[]{:S(2)}) copy-start(bf16[512,256]{1,0:T(8,128)(2,1)} %constant.14.clone.refs_8_) | copy-start | bytes 786436
  35.8 14.9 %copy-start.1 = (bf16[16,32,16,256]{3,2,1,0:T(8,128)(2,1)S(1)}, bf16[16,32,16,256]{3,2,1,0:T(8,128)(2,1)}, u32[]{:S(2)}) copy-start(bf16[16,32,16,256]{3,2,1,0:T(8,128)(2,1)} %refs_0_.7) | copy-start | bytes 12582916
  35.8 2.6 %copy-start.3 = (bf16[16,1280,128]{2,1,0:T(8,128)(2,1)S(1)}, bf16[16,1280,128]{2,1,0:T(8,128)(2,1)}, u32[]{:S(2)}) copy-start(bf16[16,1280,128]{2,1,0:T(8,128)(2,1)} %copy-done.2) | copy-start | bytes 15728644
  43.5 7.2 %collective-permute-start = (bf16[32,16,256]{2,1,0:T(8,128)(2,1)S(1)}, bf16[32,16,256]{2,1,0:T(8,128)(2,1)S(1)}, u32[]{:S(2)}, u32[]{:S(2)}) collective-permute-start(bf16[32,16,256]{2,1,0:T(8,128)(2,1)S(1)} %get-tuple-element.57), channel_id=1, source_target_pairs={{0,4},{4,0},{8,12},{12,8},{16,20},{20,16},{24,28},{28,24},{1,5},{5... | collective-permute-start | bytes 786440 | tf_op jit(solution)/shard_map/ppermute | solution.py:515
  43.6 7.1 %collective-permute-start.1 = (bf16[32,16,256]{2,1,0:T(8,128)(2,1)S(1)}, bf16[32,16,256]{2,1,0:T(8,128)(2,1)S(1)}, u32[]{:S(2)}, u32[]{:S(2)}) collective-permute-start(bf16[32,16,256]{2,1,0:T(8,128)(2,1)S(1)} %get-tuple-element.58), channel_id=1, source_target_pairs={{4,8},{8,4},{12,16},{16,12},{20,24},{24,20},{5,9},{9,5},{13,17},{1... | collective-permute-start | bytes 786440 | tf_op jit(solution)/shard_map/ppermute | solution.py:515
  44.3 6.4 %collective-permute-start.2 = (bf16[32,256]{1,0:T(8,128)(2,1)S(1)}, bf16[32,256]{1,0:T(8,128)(2,1)S(1)}, u32[]{:S(2)}, u32[]{:S(2)}) collective-permute-start(bf16[32,256]{1,0:T(8,128)(2,1)S(1)} %get-tuple-element.59), channel_id=1, source_target_pairs={{0,1},{1,0},{2,3},{3,2},{4,5},{5,4},{6,7},{7,6},{8,9},{9,8},{10,11... | collective-permute-start | bytes 49160 | tf_op jit(solution)/shard_map/ppermute | solution.py:515
  45.9 4.8 %collective-permute-start.3 = (bf16[32,256]{1,0:T(8,128)(2,1)S(1)}, bf16[32,256]{1,0:T(8,128)(2,1)S(1)}, u32[]{:S(2)}, u32[]{:S(2)}) collective-permute-start(bf16[32,256]{1,0:T(8,128)(2,1)S(1)} %get-tuple-element.60), channel_id=1, source_target_pairs={{1,2},{2,1},{5,6},{6,5},{9,10},{10,9},{13,14},{14,13},{17,18},{18,... | collective-permute-start | bytes 49160 | tf_op jit(solution)/shard_map/ppermute | solution.py:515
  46.7 13.3 %collective-permute-start.6 = (bf16[3,8,16,256]{3,2,1,0:T(8,128)(2,1)S(1)}, bf16[3,8,16,256]{3,2,1,0:T(8,128)(2,1)S(1)}, u32[]{:S(2)}, u32[]{:S(2)}) collective-permute-start(bf16[3,8,16,256]{3,2,1,0:T(8,128)(2,1)S(1)} %get-tuple-element.67), channel_id=1, source_target_pairs={{0,2},{2,0},{1,3},{3,1},{4,6},{6,4},{5,7},{7,5},{8,10},{10,8},{9,1... | collective-permute-start | bytes 589832 | tf_op jit(solution)/shard_map/ppermute | solution.py:515
  55.7 9.4 %collective-permute-start.5 = (bf16[3,8,16,256]{3,2,1,0:T(8,128)(2,1)S(1)}, bf16[3,8,16,256]{3,2,1,0:T(8,128)(2,1)S(1)}, u32[]{:S(2)}, u32[]{:S(2)}) collective-permute-start(bf16[3,8,16,256]{3,2,1,0:T(8,128)(2,1)S(1)} %get-tuple-element.66), channel_id=1, source_target_pairs={{0,3},{3,0},{1,2},{2,1},{4,7},{7,4},{5,6},{6,5},{8,11},{11,8},{9,1... | collective-permute-start | bytes 589832 | tf_op jit(solution)/shard_map/ppermute | solution.py:515
  58.7 11.5 %collective-permute-start.4 = (bf16[3,8,16,256]{3,2,1,0:T(8,128)(2,1)S(1)}, bf16[3,8,16,256]{3,2,1,0:T(8,128)(2,1)S(1)}, u32[]{:S(2)}, u32[]{:S(2)}) collective-permute-start(bf16[3,8,16,256]{3,2,1,0:T(8,128)(2,1)S(1)} %get-tuple-element.61), channel_id=1, source_target_pairs={{0,1},{1,0},{2,3},{3,2},{4,5},{5,4},{6,7},{7,6},{8,9},{9,8},{10,11... | collective-permute-start | bytes 589832 | tf_op jit(solution)/shard_map/ppermute | solution.py:515
  65.0 19.7 %collective-permute-start.9 = (bf16[4,8,16,256]{3,2,1,0:T(8,128)(2,1)S(1)}, bf16[4,8,16,256]{3,2,1,0:T(8,128)(2,1)S(1)}, u32[]{:S(2)}, u32[]{:S(2)}) collective-permute-start(bf16[4,8,16,256]{3,2,1,0:T(8,128)(2,1)S(1)} %get-tuple-element.74), channel_id=1, source_target_pairs={{0,2},{2,0},{1,3},{3,1},{4,6},{6,4},{5,7},{7,5},{8,10},{10,8},{9,1... | collective-permute-start | bytes 786440 | tf_op jit(solution)/shard_map/ppermute | solution.py:515
  75.2 10.9 %collective-permute-start.8 = (bf16[4,8,16,256]{3,2,1,0:T(8,128)(2,1)S(1)}, bf16[4,8,16,256]{3,2,1,0:T(8,128)(2,1)S(1)}, u32[]{:S(2)}, u32[]{:S(2)}) collective-permute-start(bf16[4,8,16,256]{3,2,1,0:T(8,128)(2,1)S(1)} %get-tuple-element.73), channel_id=1, source_target_pairs={{0,1},{1,0},{2,3},{3,2},{4,5},{5,4},{6,7},{7,6},{8,9},{9,8},{10,11... | collective-permute-start | bytes 786440 | tf_op jit(solution)/shard_map/ppermute | solution.py:515
  79.4 15.8 %collective-permute-start.7 = (bf16[4,8,16,256]{3,2,1,0:T(8,128)(2,1)S(1)}, bf16[4,8,16,256]{3,2,1,0:T(8,128)(2,1)S(1)}, u32[]{:S(2)}, u32[]{:S(2)}) collective-permute-start(bf16[4,8,16,256]{3,2,1,0:T(8,128)(2,1)S(1)} %get-tuple-element.72), channel_id=1, source_target_pairs={{0,3},{3,0},{1,2},{2,1},{4,7},{7,4},{5,6},{6,5},{8,11},{11,8},{9,1... | collective-permute-start | bytes 786440 | tf_op jit(solution)/shard_map/ppermute | solution.py:515

commit v4 on v3

--- a/solution.py
+++ b/solution.py
@@ -282,7 +282,7 @@
             ],
         ),
         out_shape=[rowed, rowed, columned, columned, jax.ShapeDtypeStruct(wide, BF16)],
-        compiler_params=pltpu.CompilerParams(vmem_limit_bytes=16 * MIB),
+        compiler_params=pltpu.CompilerParams(vmem_limit_bytes=52 * MIB),
         cost_estimate=cost(4 * state.size * 32, 2 * state.size),
         name="edges",
     )(info, state, react_base, react_temp)
@@ -531,32 +531,36 @@
     band, me = lax.axis_index("lat"), lax.axis_index("lon")
 
     sent = legendre_sums(spectral, legendre, bands)
-    recv = lax.all_to_all(sent, "lat", split_axis=0, concat_axis=0, tiled=True)
 
     rows = points.shape[0]
     info = jnp.concatenate([jnp.stack([band, me]), active_ids, points]).astype(jnp.int32)
-    table, twiddle = tables(info, wave_ids, rows, tiles * tile // LANES)
+    sent, info = lax.optimization_barrier((sent, info))
+    recv = lax.all_to_all(sent, "lat", split_axis=0, concat_axis=0, tiled=True)
     *ends, react = edges(tracers, react_base, react_temp, info)
-    recv, table, twiddle, ends, react = lax.optimization_barrier((recv, table, twiddle, ends, react))
-
-    grids = synthesis(recv, table, twiddle, info, tiles, tile)
-    ends, grids = lax.optimization_barrier((ends, grids))
-    middle = list(range(tiles // 2, tiles))
-    soon, late = middle[: tiles // 4], middle[tiles // 4 :]
-    inner = list(range(tiles // 2 - 1, 0, -1))
-
-    def send(value, k):
-        return exchange(value, "lon", partners("lon", k))
-
-    moved = {0: grids[0]} | {k: send(grids[k], k) for k in soon + inner}
     halos = (
         exchange(ends[0], "lat", neighbours("lat", 0)),
         exchange(ends[1], "lat", neighbours("lat", 1)),
         exchange(ends[2], "lon", neighbours("lon", 0)),
         exchange(ends[3], "lon", neighbours("lon", 1)),
     )
+    react, wave_ids = lax.optimization_barrier((react, wave_ids))
+    table, twiddle = tables(info, wave_ids, rows, tiles * tile // LANES)
+    recv, table, twiddle, halos, react = lax.optimization_barrier(
+        (recv, table, twiddle, halos, react)
+    )
+    grids = synthesis(recv, table, twiddle, info, tiles, tile)
+
+    middle = list(range(tiles // 2, tiles))
+    soon, late = middle[: tiles // 4], middle[tiles // 4 :]
+    inner = list(range(1, tiles // 2))
+
+    def send(value, k):
+        return exchange(value, "lon", partners("lon", k))
+
+    moved = {0: grids[0]} | {k: send(grids[k], k) for k in soon + inner}
     new, active = None, {}
-    for k in [0] + soon + late + inner:
+    order = [0] + inner + soon + late
+    for k in order:
         new, active[k] = chemistry(
             tracers, halos, moved[k], react, info, k, active_ids.shape[0], waves, new
         )
@@ -566,7 +570,7 @@
             held, active[0] = lax.optimization_barrier(([grids[i] for i in late], active[0]))
             moved |= {i: send(value, i) for i, value in zip(late, held)}
     spreaded = None
-    for k in [0] + soon + inner + late:
+    for k in order:
         spreaded = spread(active[k], info, k, tiles, spreaded)
     return new, spreaded
 

time: 97.9 us -> 99.5 us (1.016)
  the two profiles are of different devices: /device:TPU:0 before, /device:TPU:19 now
where the time goes in v4:
time: 99.5 us; the launch traced here: 99.3 us
  Pallas kernels  54.5 us (55%)
  waiting for transfers between devices  21.1 us (21%)
  starting transfers between devices  17.8 us (18%)
  local copies, waits for them, and re-layouts  5.01 us (5%)
    ppermute x10, waiting for transfers between devices, exchange(): lax.ppermute(value, axis, [p for a, b in pairs for p in ((a, b), (b, a))])  21.1 us
    pallas_call x4, Pallas kernels, chemistry(): pl.pallas_call(functools.partial(chem_kernel, scale, k), grid_spec=pltpu....  20 us
    pallas_call x1, Pallas kernels, legendre_sums(): pl.pallas_call(legendre_kernel, grid=(share // block,), in_specs=[pl.Bloc...  14.6 us
    ppermute x10, starting transfers between devices, exchange(): lax.ppermute(value, axis, [p for a, b in pairs for p in ((a, b), (b, a))])  13.2 us
    pallas_call x4, Pallas kernels, spread(): pl.pallas_call(spread_kernel, grid_spec=pltpu.PrefetchScalarGridSpec(num_...  5.49 us
    pallas_call x1, Pallas kernels, synthesis(): pl.pallas_call(synth_kernel, grid_spec=pltpu.PrefetchScalarGridSpec(num_s...  5.12 us
    unnamed x20, local copies, waits for them, and re-layouts  5 us
    pallas_call x1, Pallas kernels, edges(): pl.pallas_call(edge_kernel, grid_spec=pltpu.PrefetchScalarGridSpec(num_sc...  4.76 us
  transfers between devices with their start and end apart: 11, of which 4 were waited for; matrix products, arithmetic and copies ran while one was open for 0% of the time, Pallas kernels for 34%

profile of v4, /device:TPU:19, one launch (start us, length us, event | category | flops | bytes accessed | tf_op | source)
XLA Modules:
  0.0 99.3 jit_solution(17130778520540077393)
XLA Ops:
  0.6 0.0 copy-start.8
  0.6 0.0 copy-start.9
  0.7 0.0 copy-start.5
  0.7 0.0 copy-start.6
  0.7 14.6 %legendre.1 = bf16[8,8,16,512]{3,2,1,0:T(8,128)(2,1)} custom-call(bf16[6,8,80,1280]{3,2,1,0:T(8,128)(2,1)} %spectral_ref.1, bf16[80,1280,128]{2,1,0:T(8,128)(2,1)} %legendre_ref.1), custom_call_target="tpu_custom_call" | custom-call | flops 1258291200 | bytes 36044800 | tf_op jit(solution)/shard_map/legendre/pallas_call | solution.py:495
  15.2 0.0 copy-start.7
  15.2 0.0 copy-done.8
  15.2 0.0 copy-done.9
  15.3 0.1 pad_add_fusion.info
  15.3 4.6 %all-to-all-start = ((bf16[8,8,16,512]{3,2,1,0:T(8,128)(2,1)}), bf16[8,8,16,512]{3,2,1,0:T(8,128)(2,1)S(1)}, u32[]{:S(2)}, u32[]{:S(2)}) async-start(bf16[8,8,16,512]{3,2,1,0:T(8,128)(2,1)} %legendre.1), calls=%async_computation | async-start | bytes 2097152 | tf_op jit(solution)/shard_map/all_to_all | solution.py:538
  19.9 0.0 copy-done.5
  19.9 0.0 copy-done.6
  19.9 0.0 copy-start.3
  19.9 0.0 copy-start.4
  19.9 4.8 %edges.1 = (bf16[32,16,256]{2,1,0:T(8,128)(2,1)S(1)}, bf16[32,16,256]{2,1,0:T(8,128)(2,1)S(1)}, bf16[32,256]{1,0:T(8,128)(2,1)S(1)}, bf16[32,256]{1,0:T(8,128)(2,1)S(1)}, bf16[512,512]{1,0:T(8,128)(2,1)S(1)}) custom-call(s32[22]{0:T(128)S(1)} %pad_add_fusion.info, bf16[16,32,16,256]{3,2,1,0:T(8,128)(2,1)} %refs_0_.7, f32[16,16]{1,0:T(8,128)S(1)} %copy-done.5, ...), custom_call_target="tpu_custom_call" | custom-call | flops 268435456 | bytes 4194304 | tf_op jit(solution)/shard_map/edges/pallas_call | solution.py:270
  24.7 0.4 collective-permute-start
  25.1 3.1 %collective-permute-start.1 = (bf16[32,16,256]{2,1,0:T(8,128)(2,1)S(1)}, bf16[32,16,256]{2,1,0:T(8,128)(2,1)S(1)}, u32[]{:S(2)}, u32[]{:S(2)}) collective-permute-start(bf16[32,16,256]{2,1,0:T(8,128)(2,1)S(1)} %get-tuple-element.42), channel_id=1, source_target_pairs={{4,8},{8,4},{12,16},{16,12},{20,24},{24,20},{5,9},{9,5},{13,17},{1... | collective-permute-start | bytes 786440 | tf_op jit(solution)/shard_map/ppermute | solution.py:515
  28.2 1.4 %collective-permute-start.2 = (bf16[32,256]{1,0:T(8,128)(2,1)S(1)}, bf16[32,256]{1,0:T(8,128)(2,1)S(1)}, u32[]{:S(2)}, u32[]{:S(2)}) collective-permute-start(bf16[32,256]{1,0:T(8,128)(2,1)S(1)} %get-tuple-element.43), channel_id=1, source_target_pairs={{0,1},{1,0},{2,3},{3,2},{4,5},{5,4},{6,7},{7,6},{8,9},{9,8},{10,11... | collective-permute-start | bytes 49160 | tf_op jit(solution)/shard_map/ppermute | solution.py:515
  29.6 2.1 %collective-permute-start.3 = (bf16[32,256]{1,0:T(8,128)(2,1)S(1)}, bf16[32,256]{1,0:T(8,128)(2,1)S(1)}, u32[]{:S(2)}, u32[]{:S(2)}) collective-permute-start(bf16[32,256]{1,0:T(8,128)(2,1)S(1)} %get-tuple-element.44), channel_id=1, source_target_pairs={{1,2},{2,1},{5,6},{6,5},{9,10},{10,9},{13,14},{14,13},{17,18},{18,... | collective-permute-start | bytes 49160 | tf_op jit(solution)/shard_map/ppermute | solution.py:515
  31.7 0.0 copy-done.7
  31.7 4.6 %tables.1 = (bf16[16,1280,128]{2,1,0:T(8,128)(2,1)S(1)}, f32[16,2,8,640]{3,2,1,0:T(8,128)S(1)}) custom-call(s32[22]{0:T(128)S(1)} %pad_add_fusion.info, s32[1,640]{1,0:T(1,128)S(1)} %broadcast_in_dim.3.waves_ref), custom_call_target="tpu_custom_call" | custom-call | flops 10485760 | bytes 5242880 | tf_op jit(solution)/shard_map/tables/pallas_call | solution.py:87
  36.3 0.0 copy-start.1
  36.3 2.3 %copy-done.1 = bf16[16,1280,128]{2,1,0:T(8,128)(2,1)} copy-done((bf16[16,1280,128]{2,1,0:T(8,128)(2,1)}, bf16[16,1280,128]{2,1,0:T(8,128)(2,1)S(1)}, u32[]{:S(2)}) %copy-start.1) | copy-done | bytes 5242904
  38.7 0.0 collective-permute-done.2.refs_3_
  38.7 0.0 collective-permute-done.3.refs_4_
  38.7 0.0 collective-permute-done.refs_1_
  38.7 0.5 collective-permute-done.1.refs_2_
  39.2 0.0 all-to-all-done.recv_ref
  39.2 0.0 copy-start
  39.2 0.0 copy-start.2
  39.2 2.6 %copy-done.2 = bf16[16,1280,128]{2,1,0:T(8,128)(2,1)S(1)} copy-done((bf16[16,1280,128]{2,1,0:T(8,128)(2,1)S(1)}, bf16[16,1280,128]{2,1,0:T(8,128)(2,1)}, u32[]{:S(2)}) %copy-start.2) | copy-done | bytes 5242904
  41.8 5.1 %synthesis.1 = (bf16[3,8,16,256]{3,2,1,0:T(8,128)(2,1)S(1)}, bf16[3,8,16,256]{3,2,1,0:T(8,128)(2,1)S(1)}, bf16[3,8,16,256]{3,2,1,0:T(8,128)(2,1)S(1)}, bf16[3,8,16,256]{3,2,1,0:T(8,128)(2,1)S(1)}) custom-call(s32[22]{0:T(128)S(1)} %pad_add_fusion.info, bf16[8,8,16,512]{3,2,1,0:T(8,128)(2,1)S(1)} %all-to-all-done.recv_ref, ...), custom_call_target="tpu_custom_call" | custom-call | flops 1006632960 | bytes 5242880 | tf_op jit(solution)/shard_map/synthesis/pallas_call | solution.py:188
  47.0 0.1 collective-permute-start.5
  47.1 2.1 %collective-permute-start.6 = (bf16[3,8,16,256]{3,2,1,0:T(8,128)(2,1)S(1)}, bf16[3,8,16,256]{3,2,1,0:T(8,128)(2,1)S(1)}, u32[]{:S(2)}, u32[]{:S(2)}) collective-permute-start(bf16[3,8,16,256]{3,2,1,0:T(8,128)(2,1)S(1)} %get-tuple-element.59), channel_id=1, source_target_pairs={{0,1},{1,0},{2,3},{3,2},{4,5},{5,4},{6,7},{7,6},{8,9},{9,8},{10,11... | collective-permute-start | bytes 589832 | tf_op jit(solution)/shard_map/ppermute | solution.py:515
  49.2 0.0 copy-done.3
  49.2 0.0 copy-done.4
  49.2 0.0 copy-done
  49.2 5.0 %chemistry.4 = (bf16[16,32,16,256]{3,2,1,0:T(8,128)(2,1)}, bf16[4,8,16,256]{3,2,1,0:T(8,128)(2,1)S(1)}) custom-call(s32[22]{0:T(128)S(1)} %pad_add_fusion.info, bf16[16,32,16,256]{3,2,1,0:T(8,128)(2,1)S(1)} %copy-done, bf16[32,16,256]{2,1,0:T(8,128)(2,1)S(1)} %collective-permute-done.refs_1_, bf16[32,16,256]{2,1,0:T(8,128)(2,1)S(1)} %collective-permute-done.1.refs_2_, ...), custom_call_target="tpu_custom_call" | custom-call | flops 524288 | bytes 2048 | tf_op jit(solution)/shard_map/chemistry/pallas_call | solution.py:397
  54.2 0.5 collective-permute-start.4
  54.7 7.2 %collective-permute-done.6.refs_5_ = bf16[3,8,16,256]{3,2,1,0:T(8,128)(2,1)S(1)} collective-permute-done((bf16[3,8,16,256]{3,2,1,0:T(8,128)(2,1)S(1)}, bf16[3,8,16,256]{3,2,1,0:T(8,128)(2,1)S(1)}, u32[]{:S(2)}, u32[]{:S(2)}) %collective-permute-start.6) | collective-permute-done | bytes 196640 | tf_op jit(solution)/shard_map/ppermute | solution.py:515
  61.9 5.0 %chemistry.5 = (bf16[16,32,16,256]{3,2,1,0:T(8,128)(2,1)}, bf16[4,8,16,256]{3,2,1,0:T(8,128)(2,1)S(1)}) custom-call(s32[22]{0:T(128)S(1)} %pad_add_fusion.info, bf16[16,32,16,256]{3,2,1,0:T(8,128)(2,1)S(1)} %copy-done, bf16[32,16,256]{2,1,0:T(8,128)(2,1)S(1)} %collective-permute-done.refs_1_, ...), custom_call_target="tpu_custom_call", output_to_operand_aliasing={{0}: (10, {})} | custom-call | flops 524288 | bytes 2048 | tf_op jit(solution)/shard_map/chemistry/pallas_call | solution.py:397
  66.9 0.0 collective-permute-done.5.refs_5_
  66.9 5.0 %chemistry.6 = (bf16[16,32,16,256]{3,2,1,0:T(8,128)(2,1)}, bf16[4,8,16,256]{3,2,1,0:T(8,128)(2,1)S(1)}) custom-call(s32[22]{0:T(128)S(1)} %pad_add_fusion.info, bf16[16,32,16,256]{3,2,1,0:T(8,128)(2,1)S(1)} %copy-done, bf16[32,16,256]{2,1,0:T(8,128)(2,1)S(1)} %collective-permute-done.refs_1_, ...), custom_call_target="tpu_custom_call", output_to_operand_aliasing={{0}: (10, {})} | custom-call | flops 524288 | bytes 2048 | tf_op jit(solution)/shard_map/chemistry/pallas_call | solution.py:397
  71.9 0.0 collective-permute-start.8
  71.9 2.3 %collective-permute-start.9 = (bf16[4,8,16,256]{3,2,1,0:T(8,128)(2,1)S(1)}, bf16[4,8,16,256]{3,2,1,0:T(8,128)(2,1)S(1)}, u32[]{:S(2)}, u32[]{:S(2)}) collective-permute-start(bf16[4,8,16,256]{3,2,1,0:T(8,128)(2,1)S(1)} %get-tuple-element.66), channel_id=1, source_target_pairs={{0,1},{1,0},{2,3},{3,2},{4,5},{5,4},{6,7},{7,6},{8,9},{9,8},{10,11... | collective-permute-start | bytes 786440 | tf_op jit(solution)/shard_map/ppermute | solution.py:515
  74.2 0.0 collective-permute-done.4.refs_5_
  74.2 5.0 %chemistry.7 = (bf16[16,32,16,256]{3,2,1,0:T(8,128)(2,1)}, bf16[4,8,16,256]{3,2,1,0:T(8,128)(2,1)S(1)}) custom-call(s32[22]{0:T(128)S(1)} %pad_add_fusion.info, bf16[16,32,16,256]{3,2,1,0:T(8,128)(2,1)S(1)} %copy-done, bf16[32,16,256]{2,1,0:T(8,128)(2,1)S(1)} %collective-permute-done.refs_1_, ...), custom_call_target="tpu_custom_call", output_to_operand_aliasing={{0}: (10, {})} | custom-call | flops 524288 | bytes 2048 | tf_op jit(solution)/shard_map/chemistry/pallas_call | solution.py:397
  79.2 1.2 %collective-permute-start.7 = (bf16[4,8,16,256]{3,2,1,0:T(8,128)(2,1)S(1)}, bf16[4,8,16,256]{3,2,1,0:T(8,128)(2,1)S(1)}, u32[]{:S(2)}, u32[]{:S(2)}) collective-permute-start(bf16[4,8,16,256]{3,2,1,0:T(8,128)(2,1)S(1)} %get-tuple-element.64), channel_id=1, source_target_pairs={{0,3},{3,0},{1,2},{2,1},{4,7},{7,4},{5,6},{6,5},{8,11},{11,8},{9,1... | collective-permute-start | bytes 786440 | tf_op jit(solution)/shard_map/ppermute | solution.py:515
  80.4 1.4 %spread.4.refs_0_ = f32[4,8,16,1024]{3,2,1,0:T(8,128)} custom-call(s32[22]{0:T(128)S(1)} %pad_add_fusion.info, bf16[4,8,16,256]{3,2,1,0:T(8,128)(2,1)S(1)} %get-tuple-element.67.recv_ref), custom_call_target="tpu_custom_call" | custom-call | flops 131072 | bytes 4 | tf_op jit(solution)/shard_map/spread/pallas_call | solution.py:434
  81.8 4.2 %collective-permute-done.9.recv_ref = bf16[4,8,16,256]{3,2,1,0:T(8,128)(2,1)S(1)} collective-permute-done((bf16[4,8,16,256]{3,2,1,0:T(8,128)(2,1)S(1)}, bf16[4,8,16,256]{3,2,1,0:T(8,128)(2,1)S(1)}, u32[]{:S(2)}, u32[]{:S(2)}) %collective-permute-start.9) | collective-permute-done | bytes 262176 | tf_op jit(solution)/shard_map/ppermute | solution.py:515
  86.0 1.4 %spread.5.refs_0_ = f32[4,8,16,1024]{3,2,1,0:T(8,128)} custom-call(s32[22]{0:T(128)S(1)} %pad_add_fusion.info, bf16[4,8,16,256]{3,2,1,0:T(8,128)(2,1)S(1)} %collective-permute-done.9.recv_ref, f32[4,8,16,1024]{3,2,1,0:T(8,128)} %spread.4.refs_0_), custom_call_target="tpu_custom_call", output_to_operand_aliasing={{}: (2, {})} | custom-call | flops 131072 | bytes 4 | tf_op jit(solution)/shard_map/spread/pallas_call | solution.py:434
  87.3 0.0 collective-permute-done.8.recv_ref
  87.3 1.4 %spread.6.refs_0_ = f32[4,8,16,1024]{3,2,1,0:T(8,128)} custom-call(s32[22]{0:T(128)S(1)} %pad_add_fusion.info, bf16[4,8,16,256]{3,2,1,0:T(8,128)(2,1)S(1)} %collective-permute-done.8.recv_ref, f32[4,8,16,1024]{3,2,1,0:T(8,128)} %spread.5.refs_0_), custom_call_target="tpu_custom_call", output_to_operand_aliasing={{}: (2, {})} | custom-call | flops 131072 | bytes 4 | tf_op jit(solution)/shard_map/spread/pallas_call | solution.py:434
  88.7 9.2 %collective-permute-done.7.recv_ref = bf16[4,8,16,256]{3,2,1,0:T(8,128)(2,1)S(1)} collective-permute-done((bf16[4,8,16,256]{3,2,1,0:T(8,128)(2,1)S(1)}, bf16[4,8,16,256]{3,2,1,0:T(8,128)(2,1)S(1)}, u32[]{:S(2)}, u32[]{:S(2)}) %collective-permute-start.7) | collective-permute-done | bytes 262176 | tf_op jit(solution)/shard_map/ppermute | solution.py:515
  97.9 1.4 %spread.7 = f32[4,8,16,1024]{3,2,1,0:T(8,128)} custom-call(s32[22]{0:T(128)S(1)} %pad_add_fusion.info, bf16[4,8,16,256]{3,2,1,0:T(8,128)(2,1)S(1)} %collective-permute-done.7.recv_ref, f32[4,8,16,1024]{3,2,1,0:T(8,128)} %spread.6.refs_0_), custom_call_target="tpu_custom_call", output_to_operand_aliasing={{}: (2, {})} | custom-call | flops 131072 | bytes 4 | tf_op jit(solution)/shard_map/spread/pallas_call | solution.py:434
  (1 shorter events, 0.0 us)
Async XLA Ops:
  0.6 14.6 %copy-start.8 = (s32[16]{0:T(128)S(1)}, s32[16]{0:T(128)}, u32[]{:S(2)}) copy-start(s32[16]{0:T(128)} %param.19) | copy-start | bytes 196
  0.6 14.6 %copy-start.9 = (s32[4]{0:T(128)S(1)}, s32[4]{0:T(128)}, u32[]{:S(2)}) copy-start(s32[4]{0:T(128)} %param.23) | copy-start | bytes 52
  0.7 19.2 %copy-start.5 = (f32[16,16]{1,0:T(8,128)S(1)}, f32[16,16]{1,0:T(8,128)}, u32[]{:S(2)}) copy-start(f32[16,16]{1,0:T(8,128)} %base_ref.1) | copy-start | bytes 3076
  0.7 19.2 %copy-start.6 = (f32[16,16]{1,0:T(8,128)S(1)}, f32[16,16]{1,0:T(8,128)}, u32[]{:S(2)}) copy-start(f32[16,16]{1,0:T(8,128)} %temp_ref.1) | copy-start | bytes 3076
  15.2 16.5 %copy-start.7 = (s32[640]{0:T(1024)S(1)}, s32[640]{0:T(1024)}, u32[]{:S(2)}) copy-start(s32[640]{0:T(1024)} %param.18) | copy-start | bytes 7684
  15.3 23.9 %all-to-all-start = ((bf16[8,8,16,512]{3,2,1,0:T(8,128)(2,1)}), bf16[8,8,16,512]{3,2,1,0:T(8,128)(2,1)S(1)}, u32[]{:S(2)}, u32[]{:S(2)}) async-start(bf16[8,8,16,512]{3,2,1,0:T(8,128)(2,1)} %legendre.1), calls=%async_computation | async-start | bytes 2097152 | tf_op jit(solution)/shard_map/all_to_all | solution.py:538
  19.9 29.3 %copy-start.3 = (bf16[256,512]{1,0:T(8,128)(2,1)S(1)}, bf16[256,512]{1,0:T(8,128)(2,1)}, u32[]{:S(2)}) copy-start(bf16[256,512]{1,0:T(8,128)(2,1)} %constant.13.clone.refs_7_) | copy-start | bytes 786436
  19.9 29.3 %copy-start.4 = (bf16[512,256]{1,0:T(8,128)(2,1)S(1)}, bf16[512,256]{1,0:T(8,128)(2,1)}, u32[]{:S(2)}) copy-start(bf16[512,256]{1,0:T(8,128)(2,1)} %constant.14.clone.refs_8_) | copy-start | bytes 786436
  24.7 14.0 %collective-permute-start = (bf16[32,16,256]{2,1,0:T(8,128)(2,1)S(1)}, bf16[32,16,256]{2,1,0:T(8,128)(2,1)S(1)}, u32[]{:S(2)}, u32[]{:S(2)}) collective-permute-start(bf16[32,16,256]{2,1,0:T(8,128)(2,1)S(1)} %get-tuple-element.41), channel_id=1, source_target_pairs={{0,4},{4,0},{8,12},{12,8},{16,20},{20,16},{24,28},{28,24},{1,5},{5... | collective-permute-start | bytes 786440 | tf_op jit(solution)/shard_map/ppermute | solution.py:515
  25.1 14.1 %collective-permute-start.1 = (bf16[32,16,256]{2,1,0:T(8,128)(2,1)S(1)}, bf16[32,16,256]{2,1,0:T(8,128)(2,1)S(1)}, u32[]{:S(2)}, u32[]{:S(2)}) collective-permute-start(bf16[32,16,256]{2,1,0:T(8,128)(2,1)S(1)} %get-tuple-element.42), channel_id=1, source_target_pairs={{4,8},{8,4},{12,16},{16,12},{20,24},{24,20},{5,9},{9,5},{13,17},{1... | collective-permute-start | bytes 786440 | tf_op jit(solution)/shard_map/ppermute | solution.py:515
  28.2 10.4 %collective-permute-start.2 = (bf16[32,256]{1,0:T(8,128)(2,1)S(1)}, bf16[32,256]{1,0:T(8,128)(2,1)S(1)}, u32[]{:S(2)}, u32[]{:S(2)}) collective-permute-start(bf16[32,256]{1,0:T(8,128)(2,1)S(1)} %get-tuple-element.43), channel_id=1, source_target_pairs={{0,1},{1,0},{2,3},{3,2},{4,5},{5,4},{6,7},{7,6},{8,9},{9,8},{10,11... | collective-permute-start | bytes 49160 | tf_op jit(solution)/shard_map/ppermute | solution.py:515
  29.6 9.1 %collective-permute-start.3 = (bf16[32,256]{1,0:T(8,128)(2,1)S(1)}, bf16[32,256]{1,0:T(8,128)(2,1)S(1)}, u32[]{:S(2)}, u32[]{:S(2)}) collective-permute-start(bf16[32,256]{1,0:T(8,128)(2,1)S(1)} %get-tuple-element.44), channel_id=1, source_target_pairs={{1,2},{2,1},{5,6},{6,5},{9,10},{10,9},{13,14},{14,13},{17,18},{18,... | collective-permute-start | bytes 49160 | tf_op jit(solution)/shard_map/ppermute | solution.py:515
  36.3 2.3 %copy-start.1 = (bf16[16,1280,128]{2,1,0:T(8,128)(2,1)}, bf16[16,1280,128]{2,1,0:T(8,128)(2,1)S(1)}, u32[]{:S(2)}) copy-start(bf16[16,1280,128]{2,1,0:T(8,128)(2,1)S(1)} %get-tuple-element.51.table_ref) | copy-start | bytes 15728644
  39.2 10.0 %copy-start = (bf16[16,32,16,256]{3,2,1,0:T(8,128)(2,1)S(1)}, bf16[16,32,16,256]{3,2,1,0:T(8,128)(2,1)}, u32[]{:S(2)}) copy-start(bf16[16,32,16,256]{3,2,1,0:T(8,128)(2,1)} %refs_0_.7) | copy-start | bytes 12582916
  39.2 2.6 %copy-start.2 = (bf16[16,1280,128]{2,1,0:T(8,128)(2,1)S(1)}, bf16[16,1280,128]{2,1,0:T(8,128)(2,1)}, u32[]{:S(2)}) copy-start(bf16[16,1280,128]{2,1,0:T(8,128)(2,1)} %copy-done.1) | copy-start | bytes 15728644
  47.0 19.9 %collective-permute-start.5 = (bf16[3,8,16,256]{3,2,1,0:T(8,128)(2,1)S(1)}, bf16[3,8,16,256]{3,2,1,0:T(8,128)(2,1)S(1)}, u32[]{:S(2)}, u32[]{:S(2)}) collective-permute-start(bf16[3,8,16,256]{3,2,1,0:T(8,128)(2,1)S(1)} %get-tuple-element.58), channel_id=1, source_target_pairs={{0,2},{2,0},{1,3},{3,1},{4,6},{6,4},{5,7},{7,5},{8,10},{10,8},{9,1... | collective-permute-start | bytes 589832 | tf_op jit(solution)/shard_map/ppermute | solution.py:515
  47.1 14.8 %collective-permute-start.6 = (bf16[3,8,16,256]{3,2,1,0:T(8,128)(2,1)S(1)}, bf16[3,8,16,256]{3,2,1,0:T(8,128)(2,1)S(1)}, u32[]{:S(2)}, u32[]{:S(2)}) collective-permute-start(bf16[3,8,16,256]{3,2,1,0:T(8,128)(2,1)S(1)} %get-tuple-element.59), channel_id=1, source_target_pairs={{0,1},{1,0},{2,3},{3,2},{4,5},{5,4},{6,7},{7,6},{8,9},{9,8},{10,11... | collective-permute-start | bytes 589832 | tf_op jit(solution)/shard_map/ppermute | solution.py:515
  54.2 20.0 %collective-permute-start.4 = (bf16[3,8,16,256]{3,2,1,0:T(8,128)(2,1)S(1)}, bf16[3,8,16,256]{3,2,1,0:T(8,128)(2,1)S(1)}, u32[]{:S(2)}, u32[]{:S(2)}) collective-permute-start(bf16[3,8,16,256]{3,2,1,0:T(8,128)(2,1)S(1)} %get-tuple-element.57), channel_id=1, source_target_pairs={{0,3},{3,0},{1,2},{2,1},{4,7},{7,4},{5,6},{6,5},{8,11},{11,8},{9,1... | collective-permute-start | bytes 589832 | tf_op jit(solution)/shard_map/ppermute | solution.py:515
  71.9 15.5 %collective-permute-start.8 = (bf16[4,8,16,256]{3,2,1,0:T(8,128)(2,1)S(1)}, bf16[4,8,16,256]{3,2,1,0:T(8,128)(2,1)S(1)}, u32[]{:S(2)}, u32[]{:S(2)}) collective-permute-start(bf16[4,8,16,256]{3,2,1,0:T(8,128)(2,1)S(1)} %get-tuple-element.65), channel_id=1, source_target_pairs={{0,2},{2,0},{1,3},{3,1},{4,6},{6,4},{5,7},{7,5},{8,10},{10,8},{9,1... | collective-permute-start | bytes 786440 | tf_op jit(solution)/shard_map/ppermute | solution.py:515
  71.9 14.1 %collective-permute-start.9 = (bf16[4,8,16,256]{3,2,1,0:T(8,128)(2,1)S(1)}, bf16[4,8,16,256]{3,2,1,0:T(8,128)(2,1)S(1)}, u32[]{:S(2)}, u32[]{:S(2)}) collective-permute-start(bf16[4,8,16,256]{3,2,1,0:T(8,128)(2,1)S(1)} %get-tuple-element.66), channel_id=1, source_target_pairs={{0,1},{1,0},{2,3},{3,2},{4,5},{5,4},{6,7},{7,6},{8,9},{9,8},{10,11... | collective-permute-start | bytes 786440 | tf_op jit(solution)/shard_map/ppermute | solution.py:515
  79.2 18.7 %collective-permute-start.7 = (bf16[4,8,16,256]{3,2,1,0:T(8,128)(2,1)S(1)}, bf16[4,8,16,256]{3,2,1,0:T(8,128)(2,1)S(1)}, u32[]{:S(2)}, u32[]{:S(2)}) collective-permute-start(bf16[4,8,16,256]{3,2,1,0:T(8,128)(2,1)S(1)} %get-tuple-element.64), channel_id=1, source_target_pairs={{0,3},{3,0},{1,2},{2,1},{4,7},{7,4},{5,6},{6,5},{8,11},{11,8},{9,1... | collective-permute-start | bytes 786440 | tf_op jit(solution)/shard_map/ppermute | solution.py:515

commit v5 on v4

--- a/solution.py
+++ b/solution.py
@@ -99,7 +99,7 @@
             jax.ShapeDtypeStruct((rows, 2 * waves, LANES), BF16),
             jax.ShapeDtypeStruct((rows, 2, turns, waves), F32),
         ],
-        compiler_params=pltpu.CompilerParams(vmem_limit_bytes=20 * MIB),
+        compiler_params=pltpu.CompilerParams(vmem_limit_bytes=55 * MIB),
         cost_estimate=cost(rows * waves * LANES * 8, rows * waves * LANES * 4),
         name="tables",
     )(info, wave_ids[None, :])
@@ -202,7 +202,7 @@
             ],
         ),
         out_shape=[jax.ShapeDtypeStruct(shape, BF16)] * dests,
-        compiler_params=pltpu.CompilerParams(vmem_limit_bytes=24 * MIB),
+        compiler_params=pltpu.CompilerParams(vmem_limit_bytes=50 * MIB),
         cost_estimate=cost(4 * rows * waves * fields * levels * turns * LANES, 4 * rows * waves * LANES),
         name="synthesis",
     )(info, recv, table, twiddle)
@@ -242,20 +242,28 @@
     end = jnp.where(iota(shape, 0) < tracers, far, near)
     pick = iota(shape, 1) == (iota(shape, 0) % tracers) * rows + end
     pick = jnp.where(pick, 1.0, 0.0).astype(BF16)
-    shape = (2 * levels, tile)
+    shape = (tile, 2 * LANES)
     far, near = (1 - odd[1]) * (tile - 1), odd[1] * (tile - 1)
-    is_end = iota(shape, 1) == jnp.where(iota(shape, 0) < levels, far, near)
-    row = iota(shape, 0) % levels
-    columns = jnp.zeros((2 * levels, cells), F32)
+    is_end = iota(shape, 0) == jnp.where(iota(shape, 1) < LANES, far, near)
+    level = iota(shape, 1) % LANES - pl.program_id(0) * levels
+    columns = jnp.zeros((cells, 2 * LANES), F32)
     for l in range(levels):
         x = state_ref[:, l].reshape(cells, tile)
         picked = dot(pick, x, ((1,), (0,)))
         row_a_ref[l] = picked[:tracers].astype(BF16)
         row_b_ref[l] = picked[tracers:].astype(BF16)
-        mark = jnp.where(is_end & (row == l), 1.0, 0.0).astype(BF16)
-        columns = columns + dot(mark, x, ((1,), (1,)))
-    col_a_ref[...] = columns[:levels].astype(BF16)
-    col_b_ref[...] = columns[levels:].astype(BF16)
+        mark = jnp.where(is_end & (level == l), 1.0, 0.0).astype(BF16)
+        columns = columns + dot(x, mark, ((1,), (0,)))
+
+    @pl.when(pl.program_id(0) == 0)
+    def _():
+        col_a_ref[...] = columns[:, :LANES].astype(BF16)
+        col_b_ref[...] = columns[:, LANES:].astype(BF16)
+
+    @pl.when(pl.program_id(0) > 0)
+    def _():
+        col_a_ref[...] = (col_a_ref[...].astype(F32) + columns[:, :LANES]).astype(BF16)
+        col_b_ref[...] = (col_b_ref[...].astype(F32) + columns[:, LANES:]).astype(BF16)
 
 
 def edges(state, react_base, react_temp, info):
@@ -263,9 +271,9 @@
     block = 16
     cells = tracers * rows
     rowed = jax.ShapeDtypeStruct((levels, tracers, tile), BF16)
-    columned = jax.ShapeDtypeStruct((levels, cells), BF16)
+    columned = jax.ShapeDtypeStruct((cells, LANES), BF16)
     row_spec = pl.BlockSpec((block, tracers, tile), lambda i, info: (i, 0, 0))
-    col_spec = pl.BlockSpec((block, cells), lambda i, info: (i, 0))
+    col_spec = pl.BlockSpec((cells, LANES), lambda i, info: (0, 0))
     wide = (2 * cells, 2 * cells)
     return pl.pallas_call(
         edge_kernel,
@@ -299,9 +307,7 @@
     first = ((info[ME] ^ k) * pl.num_programs(0) + pl.program_id(0)) * levels
 
     def column(value):
-        pad = jnp.zeros((LANES - value.shape[0], cells), F32)
-        turn = lax.rem(LANES - first, LANES)
-        return pltpu.roll(jnp.concatenate([value, pad], axis=0).T, turn, 1)
+        return pltpu.roll(value, lax.rem(LANES - first, LANES), 1)
 
     a, b = col_a_ref[...].astype(F32), col_b_ref[...].astype(F32)
     west, east = column(jnp.where(odd_tile, a, b)), column(jnp.where(odd_tile, b, a))
@@ -557,7 +563,7 @@
     def send(value, k):
         return exchange(value, "lon", partners("lon", k))
 
-    moved = {0: grids[0]} | {k: send(grids[k], k) for k in soon + inner}
+    moved = {0: grids[0]} | {k: send(grids[k], k) for k in inner + soon}
     new, active = None, {}
     order = [0] + inner + soon + late
     for k in order:

time: 99.5 us -> 97.5 us (0.980)
  the two profiles are of different devices: /device:TPU:19 before, /device:TPU:18 now
where the time goes in v5:
time: 97.5 us; the launch traced here: 97.1 us
  Pallas kernels  57.7 us (59%)
  waiting for transfers between devices  18.2 us (19%)
  starting transfers between devices  17.7 us (18%)
  local copies, waits for them, and re-layouts  2.71 us (3%)
    pallas_call x4, Pallas kernels, chemistry(): pl.pallas_call(functools.partial(chem_kernel, scale, k), grid_spec=pltpu....  19.4 us
    ppermute x10, waiting for transfers between devices, exchange(): lax.ppermute(value, axis, [p for a, b in pairs for p in ((a, b), (b, a))])  18.2 us
    pallas_call x1, Pallas kernels, legendre_sums(): pl.pallas_call(legendre_kernel, grid=(share // block,), in_specs=[pl.Bloc...  14.6 us
    ppermute x10, starting transfers between devices, exchange(): lax.ppermute(value, axis, [p for a, b in pairs for p in ((a, b), (b, a))])  13.4 us
    pallas_call x1, Pallas kernels, synthesis(): pl.pallas_call(synth_kernel, grid_spec=pltpu.PrefetchScalarGridSpec(num_s...  6.92 us
    pallas_call x1, Pallas kernels, tables(): pl.pallas_call(functools.partial(table_kernel, info.shape[0] - rows), gri...  6.56 us
    pallas_call x4, Pallas kernels, spread(): pl.pallas_call(spread_kernel, grid_spec=pltpu.PrefetchScalarGridSpec(num_...  5.49 us
    pallas_call x1, Pallas kernels, edges(): pl.pallas_call(edge_kernel, grid_spec=pltpu.PrefetchScalarGridSpec(num_sc...  4.76 us
  transfers between devices with their start and end apart: 11, of which 3 were waited for; matrix products, arithmetic and copies ran while one was open for 1% of the time, Pallas kernels for 36%

profile of v5, /device:TPU:18, one launch (start us, length us, event | category | flops | bytes accessed | tf_op | source)
XLA Modules:
  0.0 97.1 jit_solution(371761696292853689)
XLA Ops:
  0.6 0.0 copy-start.9
  0.6 0.0 copy-start.10
  0.7 0.0 copy-start.6
  0.7 0.0 copy-start.7
  0.7 14.6 %legendre.1 = bf16[8,8,16,512]{3,2,1,0:T(8,128)(2,1)} custom-call(bf16[6,8,80,1280]{3,2,1,0:T(8,128)(2,1)} %spectral_ref.1, bf16[80,1280,128]{2,1,0:T(8,128)(2,1)} %legendre_ref.1), custom_call_target="tpu_custom_call" | custom-call | flops 1258291200 | bytes 36044800 | tf_op jit(solution)/shard_map/legendre/pallas_call | solution.py:501
  15.2 0.0 copy-start.8
  15.2 0.0 copy-done.9
  15.2 0.0 copy-done.10
  15.3 0.1 pad_add_fusion.info
  15.3 0.0 copy-start.4
  15.3 4.3 %all-to-all-start = ((bf16[8,8,16,512]{3,2,1,0:T(8,128)(2,1)}), bf16[8,8,16,512]{3,2,1,0:T(8,128)(2,1)S(1)}, u32[]{:S(2)}, u32[]{:S(2)}) async-start(bf16[8,8,16,512]{3,2,1,0:T(8,128)(2,1)} %legendre.1), calls=%async_computation | async-start | bytes 2097152 | tf_op jit(solution)/shard_map/all_to_all | solution.py:544
  19.6 0.0 copy-done.6
  19.6 0.0 copy-done.7
  19.6 4.8 %edges.1 = (bf16[32,16,256]{2,1,0:T(8,128)(2,1)S(1)}, bf16[32,16,256]{2,1,0:T(8,128)(2,1)S(1)}, bf16[256,128]{1,0:T(8,128)(2,1)S(1)}, bf16[256,128]{1,0:T(8,128)(2,1)S(1)}, bf16[512,512]{1,0:T(8,128)(2,1)S(1)}) custom-call(s32[22]{0:T(128)S(1)} %pad_add_fusion.info, bf16[16,32,16,256]{3,2,1,0:T(8,128)(2,1)} %refs_0_.7, f32[16,16]{1,0:T(8,128)S(1)} %copy-done.6, ...), custom_call_target="tpu_custom_call" | custom-call | flops 268435456 | bytes 4194304 | tf_op jit(solution)/shard_map/edges/pallas_call | solution.py:278
  24.4 0.0 copy-start.1
  24.4 0.0 copy-start.2
  24.4 0.2 collective-permute-start
  24.6 2.0 %collective-permute-start.1 = (bf16[32,16,256]{2,1,0:T(8,128)(2,1)S(1)}, bf16[32,16,256]{2,1,0:T(8,128)(2,1)S(1)}, u32[]{:S(2)}, u32[]{:S(2)}) collective-permute-start(bf16[32,16,256]{2,1,0:T(8,128)(2,1)S(1)} %get-tuple-element.42), channel_id=1, source_target_pairs={{4,8},{8,4},{12,16},{16,12},{20,24},{24,20},{5,9},{9,5},{13,17},{1... | collective-permute-start | bytes 786440 | tf_op jit(solution)/shard_map/ppermute | solution.py:521
  26.6 1.6 %collective-permute-start.2 = (bf16[256,128]{1,0:T(8,128)(2,1)S(1)}, bf16[256,128]{1,0:T(8,128)(2,1)S(1)}, u32[]{:S(2)}, u32[]{:S(2)}) collective-permute-start(bf16[256,128]{1,0:T(8,128)(2,1)S(1)} %get-tuple-element.43), channel_id=1, source_target_pairs={{0,1},{1,0},{2,3},{3,2},{4,5},{5,4},{6,7},{7,6},{8,9},{9,8},{10,11... | collective-permute-start | bytes 196616 | tf_op jit(solution)/shard_map/ppermute | solution.py:521
  28.3 2.1 %collective-permute-start.3 = (bf16[256,128]{1,0:T(8,128)(2,1)S(1)}, bf16[256,128]{1,0:T(8,128)(2,1)S(1)}, u32[]{:S(2)}, u32[]{:S(2)}) collective-permute-start(bf16[256,128]{1,0:T(8,128)(2,1)S(1)} %get-tuple-element.44), channel_id=1, source_target_pairs={{1,2},{2,1},{5,6},{6,5},{9,10},{10,9},{13,14},{14,13},{17,18},{18,... | collective-permute-start | bytes 196616 | tf_op jit(solution)/shard_map/ppermute | solution.py:521
  30.4 0.0 copy-done.8
  30.4 0.6 broadcast_in_dim.3.waves_ref
  31.0 0.0 copy-done.4
  31.0 6.6 %tables.1 = (bf16[16,1280,128]{2,1,0:T(8,128)(2,1)}, f32[16,2,8,640]{3,2,1,0:T(8,128)}) custom-call(s32[22]{0:T(128)} %copy-done.4, s32[1,640]{1,0:T(1,128)} %broadcast_in_dim.3.waves_ref), custom_call_target="tpu_custom_call" | custom-call | flops 10485760 | bytes 5242880 | tf_op jit(solution)/shard_map/tables/pallas_call | solution.py:87
  37.5 0.0 collective-permute-done.2.refs_3_
  37.5 0.0 collective-permute-done.3.refs_4_
  37.5 0.0 collective-permute-done.refs_1_
  37.6 0.0 collective-permute-done.1.refs_2_
  37.6 0.0 all-to-all-done.recv_ref
  37.6 0.0 copy-start
  37.6 0.0 copy-start.3
  37.6 1.2 %copy-done.3 = f32[16,2,8,640]{3,2,1,0:T(8,128)S(1)} copy-done((f32[16,2,8,640]{3,2,1,0:T(8,128)S(1)}, f32[16,2,8,640]{3,2,1,0:T(8,128)}, u32[]{:S(2)}) %copy-start.3) | copy-done | bytes 655384
  38.8 0.0 copy-start.5
  38.8 0.8 copy-done.5
  39.7 6.9 %synthesis.1 = (bf16[3,8,16,256]{3,2,1,0:T(8,128)(2,1)S(1)}, bf16[3,8,16,256]{3,2,1,0:T(8,128)(2,1)S(1)}, bf16[3,8,16,256]{3,2,1,0:T(8,128)(2,1)S(1)}, bf16[3,8,16,256]{3,2,1,0:T(8,128)(2,1)S(1)}) custom-call(s32[22]{0:T(128)S(1)} %copy-done.5, bf16[8,8,16,512]{3,2,1,0:T(8,128)(2,1)S(1)} %all-to-all-done.recv_ref, ...), custom_call_target="tpu_custom_call" | custom-call | flops 1006632960 | bytes 5242880 | tf_op jit(solution)/shard_map/synthesis/pallas_call | solution.py:188
  46.6 0.1 collective-permute-start.5
  46.7 3.5 %collective-permute-start.6 = (bf16[3,8,16,256]{3,2,1,0:T(8,128)(2,1)S(1)}, bf16[3,8,16,256]{3,2,1,0:T(8,128)(2,1)S(1)}, u32[]{:S(2)}, u32[]{:S(2)}) collective-permute-start(bf16[3,8,16,256]{3,2,1,0:T(8,128)(2,1)S(1)} %get-tuple-element.59), channel_id=1, source_target_pairs={{0,1},{1,0},{2,3},{3,2},{4,5},{5,4},{6,7},{7,6},{8,9},{9,8},{10,11... | collective-permute-start | bytes 589832 | tf_op jit(solution)/shard_map/ppermute | solution.py:521
  50.1 0.0 copy-done.1
  50.1 0.0 copy-done.2
  50.2 0.0 copy-done
  50.2 4.8 %chemistry.4 = (bf16[16,32,16,256]{3,2,1,0:T(8,128)(2,1)}, bf16[4,8,16,256]{3,2,1,0:T(8,128)(2,1)S(1)}) custom-call(s32[22]{0:T(128)S(1)} %copy-done.5, bf16[16,32,16,256]{3,2,1,0:T(8,128)(2,1)S(1)} %copy-done, bf16[32,16,256]{2,1,0:T(8,128)(2,1)S(1)} %collective-permute-done.refs_1_, bf16[32,16,256]{2,1,0:T(8,128)(2,1)S(1)} %collective-permute-done.1.refs_2_, ...), custom_call_target="tpu_custom_call" | custom-call | flops 524288 | bytes 2048 | tf_op jit(solution)/shard_map/chemistry/pallas_call | solution.py:403
  55.0 0.0 collective-permute-start.4
  55.0 8.2 %collective-permute-done.6.refs_5_ = bf16[3,8,16,256]{3,2,1,0:T(8,128)(2,1)S(1)} collective-permute-done((bf16[3,8,16,256]{3,2,1,0:T(8,128)(2,1)S(1)}, bf16[3,8,16,256]{3,2,1,0:T(8,128)(2,1)S(1)}, u32[]{:S(2)}, u32[]{:S(2)}) %collective-permute-start.6) | collective-permute-done | bytes 196640 | tf_op jit(solution)/shard_map/ppermute | solution.py:521
  63.2 4.8 %chemistry.5 = (bf16[16,32,16,256]{3,2,1,0:T(8,128)(2,1)}, bf16[4,8,16,256]{3,2,1,0:T(8,128)(2,1)S(1)}) custom-call(s32[22]{0:T(128)S(1)} %copy-done.5, bf16[16,32,16,256]{3,2,1,0:T(8,128)(2,1)S(1)} %copy-done, bf16[32,16,256]{2,1,0:T(8,128)(2,1)S(1)} %collective-permute-done.refs_1_, ...), custom_call_target="tpu_custom_call", output_to_operand_aliasing={{0}: (10, {})} | custom-call | flops 524288 | bytes 2048 | tf_op jit(solution)/shard_map/chemistry/pallas_call | solution.py:403
  68.1 0.0 collective-permute-done.5.refs_5_
  68.1 4.8 %chemistry.6 = (bf16[16,32,16,256]{3,2,1,0:T(8,128)(2,1)}, bf16[4,8,16,256]{3,2,1,0:T(8,128)(2,1)S(1)}) custom-call(s32[22]{0:T(128)S(1)} %copy-done.5, bf16[16,32,16,256]{3,2,1,0:T(8,128)(2,1)S(1)} %copy-done, bf16[32,16,256]{2,1,0:T(8,128)(2,1)S(1)} %collective-permute-done.refs_1_, ...), custom_call_target="tpu_custom_call", output_to_operand_aliasing={{0}: (10, {})} | custom-call | flops 524288 | bytes 2048 | tf_op jit(solution)/shard_map/chemistry/pallas_call | solution.py:403
  72.9 0.0 collective-permute-start.8
  72.9 2.4 %collective-permute-start.9 = (bf16[4,8,16,256]{3,2,1,0:T(8,128)(2,1)S(1)}, bf16[4,8,16,256]{3,2,1,0:T(8,128)(2,1)S(1)}, u32[]{:S(2)}, u32[]{:S(2)}) collective-permute-start(bf16[4,8,16,256]{3,2,1,0:T(8,128)(2,1)S(1)} %get-tuple-element.66), channel_id=1, source_target_pairs={{0,1},{1,0},{2,3},{3,2},{4,5},{5,4},{6,7},{7,6},{8,9},{9,8},{10,11... | collective-permute-start | bytes 786440 | tf_op jit(solution)/shard_map/ppermute | solution.py:521
  75.4 0.0 collective-permute-done.4.refs_5_
  75.4 4.8 %chemistry.7 = (bf16[16,32,16,256]{3,2,1,0:T(8,128)(2,1)}, bf16[4,8,16,256]{3,2,1,0:T(8,128)(2,1)S(1)}) custom-call(s32[22]{0:T(128)S(1)} %copy-done.5, bf16[16,32,16,256]{3,2,1,0:T(8,128)(2,1)S(1)} %copy-done, bf16[32,16,256]{2,1,0:T(8,128)(2,1)S(1)} %collective-permute-done.refs_1_, ...), custom_call_target="tpu_custom_call", output_to_operand_aliasing={{0}: (10, {})} | custom-call | flops 524288 | bytes 2048 | tf_op jit(solution)/shard_map/chemistry/pallas_call | solution.py:403
  80.2 1.5 %collective-permute-start.7 = (bf16[4,8,16,256]{3,2,1,0:T(8,128)(2,1)S(1)}, bf16[4,8,16,256]{3,2,1,0:T(8,128)(2,1)S(1)}, u32[]{:S(2)}, u32[]{:S(2)}) collective-permute-start(bf16[4,8,16,256]{3,2,1,0:T(8,128)(2,1)S(1)} %get-tuple-element.64), channel_id=1, source_target_pairs={{0,3},{3,0},{1,2},{2,1},{4,7},{7,4},{5,6},{6,5},{8,11},{11,8},{9,1... | collective-permute-start | bytes 786440 | tf_op jit(solution)/shard_map/ppermute | solution.py:521
  81.7 1.4 %spread.4.refs_0_ = f32[4,8,16,1024]{3,2,1,0:T(8,128)} custom-call(s32[22]{0:T(128)S(1)} %copy-done.5, bf16[4,8,16,256]{3,2,1,0:T(8,128)(2,1)S(1)} %get-tuple-element.67.recv_ref), custom_call_target="tpu_custom_call" | custom-call | flops 131072 | bytes 4 | tf_op jit(solution)/shard_map/spread/pallas_call | solution.py:440
  83.0 3.6 %collective-permute-done.9.recv_ref = bf16[4,8,16,256]{3,2,1,0:T(8,128)(2,1)S(1)} collective-permute-done((bf16[4,8,16,256]{3,2,1,0:T(8,128)(2,1)S(1)}, bf16[4,8,16,256]{3,2,1,0:T(8,128)(2,1)S(1)}, u32[]{:S(2)}, u32[]{:S(2)}) %collective-permute-start.9) | collective-permute-done | bytes 262176 | tf_op jit(solution)/shard_map/ppermute | solution.py:521
  86.6 1.4 %spread.5.refs_0_ = f32[4,8,16,1024]{3,2,1,0:T(8,128)} custom-call(s32[22]{0:T(128)S(1)} %copy-done.5, bf16[4,8,16,256]{3,2,1,0:T(8,128)(2,1)S(1)} %collective-permute-done.9.recv_ref, f32[4,8,16,1024]{3,2,1,0:T(8,128)} %spread.4.refs_0_), custom_call_target="tpu_custom_call", output_to_operand_aliasing={{}: (2, {})} | custom-call | flops 131072 | bytes 4 | tf_op jit(solution)/shard_map/spread/pallas_call | solution.py:440
  88.0 0.0 collective-permute-done.8.recv_ref
  88.0 1.4 %spread.6.refs_0_ = f32[4,8,16,1024]{3,2,1,0:T(8,128)} custom-call(s32[22]{0:T(128)S(1)} %copy-done.5, bf16[4,8,16,256]{3,2,1,0:T(8,128)(2,1)S(1)} %collective-permute-done.8.recv_ref, f32[4,8,16,1024]{3,2,1,0:T(8,128)} %spread.5.refs_0_), custom_call_target="tpu_custom_call", output_to_operand_aliasing={{}: (2, {})} | custom-call | flops 131072 | bytes 4 | tf_op jit(solution)/shard_map/spread/pallas_call | solution.py:440
  89.4 6.4 %collective-permute-done.7.recv_ref = bf16[4,8,16,256]{3,2,1,0:T(8,128)(2,1)S(1)} collective-permute-done((bf16[4,8,16,256]{3,2,1,0:T(8,128)(2,1)S(1)}, bf16[4,8,16,256]{3,2,1,0:T(8,128)(2,1)S(1)}, u32[]{:S(2)}, u32[]{:S(2)}) %collective-permute-start.7) | collective-permute-done | bytes 262176 | tf_op jit(solution)/shard_map/ppermute | solution.py:521
  95.8 1.4 %spread.7 = f32[4,8,16,1024]{3,2,1,0:T(8,128)} custom-call(s32[22]{0:T(128)S(1)} %copy-done.5, bf16[4,8,16,256]{3,2,1,0:T(8,128)(2,1)S(1)} %collective-permute-done.7.recv_ref, f32[4,8,16,1024]{3,2,1,0:T(8,128)} %spread.6.refs_0_), custom_call_target="tpu_custom_call", output_to_operand_aliasing={{}: (2, {})} | custom-call | flops 131072 | bytes 4 | tf_op jit(solution)/shard_map/spread/pallas_call | solution.py:440
Async XLA Ops:
  0.6 14.6 %copy-start.9 = (s32[16]{0:T(128)S(1)}, s32[16]{0:T(128)}, u32[]{:S(2)}) copy-start(s32[16]{0:T(128)} %param.19) | copy-start | bytes 196
  0.6 14.6 %copy-start.10 = (s32[4]{0:T(128)S(1)}, s32[4]{0:T(128)}, u32[]{:S(2)}) copy-start(s32[4]{0:T(128)} %param.23) | copy-start | bytes 52
  0.7 18.9 %copy-start.6 = (f32[16,16]{1,0:T(8,128)S(1)}, f32[16,16]{1,0:T(8,128)}, u32[]{:S(2)}) copy-start(f32[16,16]{1,0:T(8,128)} %base_ref.1) | copy-start | bytes 3076
  0.7 18.9 %copy-start.7 = (f32[16,16]{1,0:T(8,128)S(1)}, f32[16,16]{1,0:T(8,128)}, u32[]{:S(2)}) copy-start(f32[16,16]{1,0:T(8,128)} %temp_ref.1) | copy-start | bytes 3076
  15.2 15.1 %copy-start.8 = (s32[640]{0:T(1024)S(1)}, s32[640]{0:T(1024)}, u32[]{:S(2)}) copy-start(s32[640]{0:T(1024)} %param.18) | copy-start | bytes 7684
  15.3 15.6 %copy-start.4 = (s32[22]{0:T(128)}, s32[22]{0:T(128)S(1)}, u32[]{:S(2)}) copy-start(s32[22]{0:T(128)S(1)} %pad_add_fusion.info) | copy-start | bytes 268
  15.3 22.2 %all-to-all-start = ((bf16[8,8,16,512]{3,2,1,0:T(8,128)(2,1)}), bf16[8,8,16,512]{3,2,1,0:T(8,128)(2,1)S(1)}, u32[]{:S(2)}, u32[]{:S(2)}) async-start(bf16[8,8,16,512]{3,2,1,0:T(8,128)(2,1)} %legendre.1), calls=%async_computation | async-start | bytes 2097152 | tf_op jit(solution)/shard_map/all_to_all | solution.py:544
  24.4 25.8 %copy-start.1 = (bf16[256,512]{1,0:T(8,128)(2,1)S(1)}, bf16[256,512]{1,0:T(8,128)(2,1)}, u32[]{:S(2)}) copy-start(bf16[256,512]{1,0:T(8,128)(2,1)} %constant.13.clone.refs_7_) | copy-start | bytes 786436
  24.4 25.8 %copy-start.2 = (bf16[512,256]{1,0:T(8,128)(2,1)S(1)}, bf16[512,256]{1,0:T(8,128)(2,1)}, u32[]{:S(2)}) copy-start(bf16[512,256]{1,0:T(8,128)(2,1)} %constant.14.clone.refs_8_) | copy-start | bytes 786436
  24.4 13.2 %collective-permute-start = (bf16[32,16,256]{2,1,0:T(8,128)(2,1)S(1)}, bf16[32,16,256]{2,1,0:T(8,128)(2,1)S(1)}, u32[]{:S(2)}, u32[]{:S(2)}) collective-permute-start(bf16[32,16,256]{2,1,0:T(8,128)(2,1)S(1)} %get-tuple-element.41), channel_id=1, source_target_pairs={{0,4},{4,0},{8,12},{12,8},{16,20},{20,16},{24,28},{28,24},{1,5},{5... | collective-permute-start | bytes 786440 | tf_op jit(solution)/shard_map/ppermute | solution.py:521
  24.6 13.0 %collective-permute-start.1 = (bf16[32,16,256]{2,1,0:T(8,128)(2,1)S(1)}, bf16[32,16,256]{2,1,0:T(8,128)(2,1)S(1)}, u32[]{:S(2)}, u32[]{:S(2)}) collective-permute-start(bf16[32,16,256]{2,1,0:T(8,128)(2,1)S(1)} %get-tuple-element.42), channel_id=1, source_target_pairs={{4,8},{8,4},{12,16},{16,12},{20,24},{24,20},{5,9},{9,5},{13,17},{1... | collective-permute-start | bytes 786440 | tf_op jit(solution)/shard_map/ppermute | solution.py:521
  26.6 10.9 %collective-permute-start.2 = (bf16[256,128]{1,0:T(8,128)(2,1)S(1)}, bf16[256,128]{1,0:T(8,128)(2,1)S(1)}, u32[]{:S(2)}, u32[]{:S(2)}) collective-permute-start(bf16[256,128]{1,0:T(8,128)(2,1)S(1)} %get-tuple-element.43), channel_id=1, source_target_pairs={{0,1},{1,0},{2,3},{3,2},{4,5},{5,4},{6,7},{7,6},{8,9},{9,8},{10,11... | collective-permute-start | bytes 196616 | tf_op jit(solution)/shard_map/ppermute | solution.py:521
  28.3 9.3 %collective-permute-start.3 = (bf16[256,128]{1,0:T(8,128)(2,1)S(1)}, bf16[256,128]{1,0:T(8,128)(2,1)S(1)}, u32[]{:S(2)}, u32[]{:S(2)}) collective-permute-start(bf16[256,128]{1,0:T(8,128)(2,1)S(1)} %get-tuple-element.44), channel_id=1, source_target_pairs={{1,2},{2,1},{5,6},{6,5},{9,10},{10,9},{13,14},{14,13},{17,18},{18,... | collective-permute-start | bytes 196616 | tf_op jit(solution)/shard_map/ppermute | solution.py:521
  37.6 12.6 %copy-start = (bf16[16,32,16,256]{3,2,1,0:T(8,128)(2,1)S(1)}, bf16[16,32,16,256]{3,2,1,0:T(8,128)(2,1)}, u32[]{:S(2)}) copy-start(bf16[16,32,16,256]{3,2,1,0:T(8,128)(2,1)} %refs_0_.7) | copy-start | bytes 12582916
  37.6 1.2 %copy-start.3 = (f32[16,2,8,640]{3,2,1,0:T(8,128)S(1)}, f32[16,2,8,640]{3,2,1,0:T(8,128)}, u32[]{:S(2)}) copy-start(f32[16,2,8,640]{3,2,1,0:T(8,128)} %get-tuple-element.52.twiddle_ref) | copy-start | bytes 1966084
  38.8 0.8 copy-start.5
  46.6 21.5 %collective-permute-start.5 = (bf16[3,8,16,256]{3,2,1,0:T(8,128)(2,1)S(1)}, bf16[3,8,16,256]{3,2,1,0:T(8,128)(2,1)S(1)}, u32[]{:S(2)}, u32[]{:S(2)}) collective-permute-start(bf16[3,8,16,256]{3,2,1,0:T(8,128)(2,1)S(1)} %get-tuple-element.58), channel_id=1, source_target_pairs={{0,2},{2,0},{1,3},{3,1},{4,6},{6,4},{5,7},{7,5},{8,10},{10,8},{9,1... | collective-permute-start | bytes 589832 | tf_op jit(solution)/shard_map/ppermute | solution.py:521
  46.7 16.5 %collective-permute-start.6 = (bf16[3,8,16,256]{3,2,1,0:T(8,128)(2,1)S(1)}, bf16[3,8,16,256]{3,2,1,0:T(8,128)(2,1)S(1)}, u32[]{:S(2)}, u32[]{:S(2)}) collective-permute-start(bf16[3,8,16,256]{3,2,1,0:T(8,128)(2,1)S(1)} %get-tuple-element.59), channel_id=1, source_target_pairs={{0,1},{1,0},{2,3},{3,2},{4,5},{5,4},{6,7},{7,6},{8,9},{9,8},{10,11... | collective-permute-start | bytes 589832 | tf_op jit(solution)/shard_map/ppermute | solution.py:521
  55.0 20.4 %collective-permute-start.4 = (bf16[3,8,16,256]{3,2,1,0:T(8,128)(2,1)S(1)}, bf16[3,8,16,256]{3,2,1,0:T(8,128)(2,1)S(1)}, u32[]{:S(2)}, u32[]{:S(2)}) collective-permute-start(bf16[3,8,16,256]{3,2,1,0:T(8,128)(2,1)S(1)} %get-tuple-element.57), channel_id=1, source_target_pairs={{0,3},{3,0},{1,2},{2,1},{4,7},{7,4},{5,6},{6,5},{8,11},{11,8},{9,1... | collective-permute-start | bytes 589832 | tf_op jit(solution)/shard_map/ppermute | solution.py:521
  72.9 15.1 %collective-permute-start.8 = (bf16[4,8,16,256]{3,2,1,0:T(8,128)(2,1)S(1)}, bf16[4,8,16,256]{3,2,1,0:T(8,128)(2,1)S(1)}, u32[]{:S(2)}, u32[]{:S(2)}) collective-permute-start(bf16[4,8,16,256]{3,2,1,0:T(8,128)(2,1)S(1)} %get-tuple-element.65), channel_id=1, source_target_pairs={{0,2},{2,0},{1,3},{3,1},{4,6},{6,4},{5,7},{7,5},{8,10},{10,8},{9,1... | collective-permute-start | bytes 786440 | tf_op jit(solution)/shard_map/ppermute | solution.py:521
  72.9 13.7 %collective-permute-start.9 = (bf16[4,8,16,256]{3,2,1,0:T(8,128)(2,1)S(1)}, bf16[4,8,16,256]{3,2,1,0:T(8,128)(2,1)S(1)}, u32[]{:S(2)}, u32[]{:S(2)}) collective-permute-start(bf16[4,8,16,256]{3,2,1,0:T(8,128)(2,1)S(1)} %get-tuple-element.66), channel_id=1, source_target_pairs={{0,1},{1,0},{2,3},{3,2},{4,5},{5,4},{6,7},{7,6},{8,9},{9,8},{10,11... | collective-permute-start | bytes 786440 | tf_op jit(solution)/shard_map/ppermute | solution.py:521
  80.2 15.6 %collective-permute-start.7 = (bf16[4,8,16,256]{3,2,1,0:T(8,128)(2,1)S(1)}, bf16[4,8,16,256]{3,2,1,0:T(8,128)(2,1)S(1)}, u32[]{:S(2)}, u32[]{:S(2)}) collective-permute-start(bf16[4,8,16,256]{3,2,1,0:T(8,128)(2,1)S(1)} %get-tuple-element.64), channel_id=1, source_target_pairs={{0,3},{3,0},{1,2},{2,1},{4,7},{7,4},{5,6},{6,5},{8,11},{11,8},{9,1... | collective-permute-start | bytes 786440 | tf_op jit(solution)/shard_map/ppermute | solution.py:521

commit v6 on v5

--- a/solution.py
+++ b/solution.py
@@ -11,6 +11,7 @@
 F32 = jnp.float32
 BF16 = jnp.bfloat16
 LANES = 128
+SUBLANES = 8
 LOW = 16
 STEP = 4
 MIB = 1024 * 1024
@@ -96,10 +97,10 @@
             ],
         ),
         out_shape=[
-            jax.ShapeDtypeStruct((rows, 2 * waves, LANES), BF16),
-            jax.ShapeDtypeStruct((rows, 2, turns, waves), F32),
+            pltpu.VMEM((rows, 2 * waves, LANES), BF16),
+            pltpu.VMEM((rows, 2, turns, waves), F32),
         ],
-        compiler_params=pltpu.CompilerParams(vmem_limit_bytes=55 * MIB),
+        compiler_params=pltpu.CompilerParams(vmem_limit_bytes=20 * MIB),
         cost_estimate=cost(rows * waves * LANES * 8, rows * waves * LANES * 4),
         name="tables",
     )(info, wave_ids[None, :])
@@ -202,7 +203,7 @@
             ],
         ),
         out_shape=[jax.ShapeDtypeStruct(shape, BF16)] * dests,
-        compiler_params=pltpu.CompilerParams(vmem_limit_bytes=50 * MIB),
+        compiler_params=pltpu.CompilerParams(vmem_limit_bytes=24 * MIB),
         cost_estimate=cost(4 * rows * waves * fields * levels * turns * LANES, 4 * rows * waves * LANES),
         name="synthesis",
     )(info, recv, table, twiddle)
@@ -296,13 +297,20 @@
     )(info, state, react_base, react_temp)
 
 
+def shifted(value, outer, axis, step):
+    size = value[0].shape[axis]
+    turned = [pltpu.roll(v, -step % size, axis) for v in value]
+    place = lax.broadcasted_iota(jnp.int32, value[0].shape, axis)
+    at_end = place == (size - 1 if step == 1 else 0)
+    following = turned[1:] + [outer] if step == 1 else [outer] + turned[:-1]
+    return [jnp.where(at_end, f, t) for f, t in zip(following, turned)]
+
+
 def chem_kernel(scale, k, info, *refs):
     state_ref, row_a_ref, row_b_ref, col_a_ref, col_b_ref, grid_ref, react_ref = refs[:7]
-    along_ref, across_ref = refs[7:9]
-    new_ref, active_ref, south, north = refs[-4:]
+    new_ref, active_ref, south, north, advected, rounded = refs[-6:]
     tracers, levels, rows, tile = state_ref.shape
     cells = tracers * rows
-    half, side = rows // 2, tile // 2
     odd_band, odd_tile = info[BAND] % 2 == 1, info[ME] % 2 == 1
     first = ((info[ME] ^ k) * pl.num_programs(0) + pl.program_id(0)) * levels
 
@@ -318,44 +326,41 @@
     for j in range(1, rows):
         count = jnp.where(row == j, info[points + j], count)
     mask = jnp.where(info[ME] * tile + lane < count, 1.0, 0.0)
-    nn = ((1,), (0,))
-
-    def three(v):
-        return v.reshape(tracers, rows, tile)
+    across = [slice(v * LANES, (v + 1) * LANES) for v in range(tile // LANES)]
+    along = [slice(v * SUBLANES, (v + 1) * SUBLANES) for v in range(rows // SUBLANES)]
 
     for l in range(levels):
-        x = state_ref[:, l].reshape(cells, tile)
-        lon = dot(x, along_ref[...], nn)
-        lat = dot(across_ref[...], x, nn)
         wind_u = grid_ref[0, l].astype(F32) * (scale * 0.1)
         wind_v = grid_ref[1, l].astype(F32) * (scale * 0.1)
-        temper = grid_ref[2, l].astype(F32) * scale
-        moved = (
-            three(x.astype(F32))
-            - wind_u * three(lon[:, :tile])
-            - wind_v * three(lat[:cells])
-            + 0.05 * three(lon[:, tile:] + lat[cells:])
-        )
+        from_east, from_west = 0.05 - wind_u, 0.05 + wind_u
+        from_north, from_south = 0.05 - wind_v, 0.05 + wind_v
         a, b = row_a_ref[l].astype(F32), row_b_ref[l].astype(F32)
         south[l] = jnp.where(odd_band, a, b)
         north[l] = jnp.where(odd_band, b, a)
-        in_row = jnp.where(row == 0, 0.05 + wind_v, jnp.where(row == rows - 1, 0.05 - wind_v, 0.0))
-        in_col = jnp.where(lane == 0, 0.05 + wind_u, jnp.where(lane == tile - 1, 0.05 - wind_u, 0.0))
-        outer = []
         for t in range(tracers):
-            up = [jnp.broadcast_to(ref[l, t : t + 1], (half, tile)) for ref in (south, north)]
             cell = slice(t * rows, (t + 1) * rows)
-            across = [
-                jnp.broadcast_to(col[cell, l : l + 1], (rows, side)) for col in (west, east)
-            ]
-            outer.append(
-                in_row * jnp.concatenate(up, axis=0) + in_col * jnp.concatenate(across, axis=1)
-            )
-        moved = moved + jnp.stack(outer, axis=0)
-        high = moved.reshape(cells, tile).astype(BF16)
-        terms = dot(react_ref[...], jnp.concatenate([high, high], axis=0), nn)
-        reacted = (moved + three(terms[:cells]) + temper * three(terms[cells:])) * mask
-        new_ref[:, l] = reacted.astype(BF16)
+            x = state_ref[t, l].astype(F32)
+            outer = [jnp.broadcast_to(col[cell, l : l + 1], (rows, LANES)) for col in (east, west)]
+            parts = [x[:, v] for v in across]
+            qe = jnp.concatenate(shifted(parts, outer[0], 1, 1), axis=1)
+            qw = jnp.concatenate(shifted(parts, outer[1], 1, -1), axis=1)
+            shape = (SUBLANES, tile)
+            outer = [jnp.broadcast_to(ref[l, t : t + 1], shape) for ref in (north, south)]
+            parts = [x[v] for v in along]
+            qn = jnp.concatenate(shifted(parts, outer[0], 0, 1), axis=0)
+            qs = jnp.concatenate(shifted(parts, outer[1], 0, -1), axis=0)
+            moved = 0.8 * x + from_east * qe + from_west * qw + from_north * qn + from_south * qs
+            advected[l, cell] = moved
+            rounded[l, cell] = moved.astype(BF16)
+    for l in range(levels):
+        temper = grid_ref[2, l].astype(F32) * scale
+        high = rounded[l]
+        terms = dot(react_ref[...], jnp.concatenate([high, high], axis=0), ((1,), (0,)))
+        for t in range(tracers):
+            cell = slice(t * rows, (t + 1) * rows)
+            warm = slice(cells + t * rows, cells + (t + 1) * rows)
+            reacted = (advected[l, cell] + terms[cell] + temper * terms[warm]) * mask
+            new_ref[t, l] = reacted.astype(BF16)
     for a in range(active_ref.shape[0]):
         active_ref[a] = new_ref[info[ids + a]]
 
@@ -366,12 +371,6 @@
     some = 4 if own % 4 == 0 else own
     steps = own // some
     cells = tracers * rows
-    eye, one = np.eye(tracers), np.eye(tile)
-    along = np.concatenate(
-        [np.eye(tile, k=-1) - np.eye(tile, k=1), np.eye(tile, k=-1) + np.eye(tile, k=1) - 4 * one], 1
-    )
-    down, up = np.eye(rows, k=-1), np.eye(rows, k=1)
-    across = np.concatenate([np.kron(eye, up - down), np.kron(eye, up + down)], 0)
     scale = 1.0 / float(np.sqrt(np.float32(waves)))
 
     def whole(shape):
@@ -381,9 +380,7 @@
     state_spec = pl.BlockSpec(
         (tracers, some, rows, tile), lambda i, info: (0, (info[ME] ^ k) * steps + i, 0, 0)
     )
-    operands = [
-        state, *halos, grid, react, jnp.asarray(along, BF16), jnp.asarray(across, BF16),
-    ]
+    operands = [state, *halos, grid, react]
     in_specs = [
         state_spec,
         row_spec,
@@ -392,8 +389,6 @@
         whole(halos[3].shape),
         pl.BlockSpec((fields, some, rows, tile), lambda i, info: (0, i, 0, 0)),
         whole(react.shape),
-        whole(along.shape),
-        whole(across.shape),
     ]
     aliases = {}
     if before is not None:
@@ -410,7 +405,12 @@
                 state_spec,
                 pl.BlockSpec((actives, some, rows, tile), lambda i, info: (0, i, 0, 0)),
             ],
-            scratch_shapes=[pltpu.VMEM((some, tracers, tile), F32)] * 2,
+            scratch_shapes=[
+                pltpu.VMEM((some, tracers, tile), F32),
+                pltpu.VMEM((some, tracers, tile), F32),
+                pltpu.VMEM((some, cells, tile), F32),
+                pltpu.VMEM((some, cells, tile), BF16),
+            ],
         ),
         out_shape=[
             jax.ShapeDtypeStruct(state.shape, BF16),

time: 97.5 us -> 96.3 us (0.988)
  the two profiles are of different devices: /device:TPU:18 before, /device:TPU:19 now
where the time goes in v6:
time: 96.3 us; the launch traced here: 96.1 us
  Pallas kernels  52 us (54%)
  starting transfers between devices  20.7 us (21%)
  waiting for transfers between devices  17.6 us (18%)
  local copies, waits for them, and re-layouts  5 us (5%)
    ppermute x10, waiting for transfers between devices, exchange(): lax.ppermute(value, axis, [p for a, b in pairs for p in ((a, b), (b, a))])  17.6 us
    pallas_call x4, Pallas kernels, chemistry(): pl.pallas_call(functools.partial(chem_kernel, scale, k), grid_spec=pltpu....  17.4 us
    ppermute x10, starting transfers between devices, exchange(): lax.ppermute(value, axis, [p for a, b in pairs for p in ((a, b), (b, a))])  16.1 us
    pallas_call x1, Pallas kernels, legendre_sums(): pl.pallas_call(legendre_kernel, grid=(share // block,), in_specs=[pl.Bloc...  14.6 us
    pallas_call x4, Pallas kernels, spread(): pl.pallas_call(spread_kernel, grid_spec=pltpu.PrefetchScalarGridSpec(num_...  5.49 us
    pallas_call x1, Pallas kernels, synthesis(): pl.pallas_call(synth_kernel, grid_spec=pltpu.PrefetchScalarGridSpec(num_s...  5.12 us
    unnamed x16, local copies, waits for them, and re-layouts  5 us
    pallas_call x1, Pallas kernels, edges(): pl.pallas_call(edge_kernel, grid_spec=pltpu.PrefetchScalarGridSpec(num_sc...  4.76 us
  transfers between devices with their start and end apart: 11, of which 4 were waited for; matrix products, arithmetic and copies ran while one was open for 0% of the time, Pallas kernels for 32%

profile of v6, /device:TPU:19, one launch (start us, length us, event | category | flops | bytes accessed | tf_op | source)
XLA Modules:
  0.0 96.1 jit_solution(1047635799702529751)
XLA Ops:
  0.6 0.0 copy-start.6
  0.6 0.0 copy-start.7
  0.7 0.0 copy-start.3
  0.7 0.0 copy-start.4
  0.7 14.6 %legendre.1 = bf16[8,8,16,512]{3,2,1,0:T(8,128)(2,1)} custom-call(bf16[6,8,80,1280]{3,2,1,0:T(8,128)(2,1)} %spectral_ref.1, bf16[80,1280,128]{2,1,0:T(8,128)(2,1)} %legendre_ref.1), custom_call_target="tpu_custom_call" | custom-call | flops 1258291200 | bytes 36044800 | tf_op jit(solution)/shard_map/legendre/pallas_call | solution.py:501
  15.2 0.0 copy-start.5
  15.2 0.0 copy-done.6
  15.2 0.0 copy-done.7
  15.3 0.1 pad_add_fusion.info
  15.3 4.6 %all-to-all-start = ((bf16[8,8,16,512]{3,2,1,0:T(8,128)(2,1)}), bf16[8,8,16,512]{3,2,1,0:T(8,128)(2,1)S(1)}, u32[]{:S(2)}, u32[]{:S(2)}) async-start(bf16[8,8,16,512]{3,2,1,0:T(8,128)(2,1)} %legendre.1), calls=%async_computation | async-start | bytes 2097152 | tf_op jit(solution)/shard_map/all_to_all | solution.py:544
  19.9 0.0 copy-done.3
  19.9 0.0 copy-done.4
  19.9 4.8 %edges.1 = (bf16[32,16,256]{2,1,0:T(8,128)(2,1)S(1)}, bf16[32,16,256]{2,1,0:T(8,128)(2,1)S(1)}, bf16[256,128]{1,0:T(8,128)(2,1)S(1)}, bf16[256,128]{1,0:T(8,128)(2,1)S(1)}, bf16[512,512]{1,0:T(8,128)(2,1)S(1)}) custom-call(s32[22]{0:T(128)S(1)} %pad_add_fusion.info, bf16[16,32,16,256]{3,2,1,0:T(8,128)(2,1)} %refs_0_.7, f32[16,16]{1,0:T(8,128)S(1)} %copy-done.3, ...), custom_call_target="tpu_custom_call" | custom-call | flops 268435456 | bytes 4194304 | tf_op jit(solution)/shard_map/edges/pallas_call | solution.py:279
  24.7 0.4 collective-permute-start
  25.1 3.1 %collective-permute-start.1 = (bf16[32,16,256]{2,1,0:T(8,128)(2,1)S(1)}, bf16[32,16,256]{2,1,0:T(8,128)(2,1)S(1)}, u32[]{:S(2)}, u32[]{:S(2)}) collective-permute-start(bf16[32,16,256]{2,1,0:T(8,128)(2,1)S(1)} %get-tuple-element.42), channel_id=1, source_target_pairs={{4,8},{8,4},{12,16},{16,12},{20,24},{24,20},{5,9},{9,5},{13,17},{1... | collective-permute-start | bytes 786440 | tf_op jit(solution)/shard_map/ppermute | solution.py:521
  28.2 1.4 %collective-permute-start.2 = (bf16[256,128]{1,0:T(8,128)(2,1)S(1)}, bf16[256,128]{1,0:T(8,128)(2,1)S(1)}, u32[]{:S(2)}, u32[]{:S(2)}) collective-permute-start(bf16[256,128]{1,0:T(8,128)(2,1)S(1)} %get-tuple-element.43), channel_id=1, source_target_pairs={{0,1},{1,0},{2,3},{3,2},{4,5},{5,4},{6,7},{7,6},{8,9},{9,8},{10,11... | collective-permute-start | bytes 196616 | tf_op jit(solution)/shard_map/ppermute | solution.py:521
  29.6 1.9 %collective-permute-start.3 = (bf16[256,128]{1,0:T(8,128)(2,1)S(1)}, bf16[256,128]{1,0:T(8,128)(2,1)S(1)}, u32[]{:S(2)}, u32[]{:S(2)}) collective-permute-start(bf16[256,128]{1,0:T(8,128)(2,1)S(1)} %get-tuple-element.44), channel_id=1, source_target_pairs={{1,2},{2,1},{5,6},{6,5},{9,10},{10,9},{13,14},{14,13},{17,18},{18,... | collective-permute-start | bytes 196616 | tf_op jit(solution)/shard_map/ppermute | solution.py:521
  31.5 0.0 copy-done.5
  31.5 4.6 %tables.1 = (bf16[16,1280,128]{2,1,0:T(8,128)(2,1)S(1)}, f32[16,2,8,640]{3,2,1,0:T(8,128)S(1)}) custom-call(s32[22]{0:T(128)S(1)} %pad_add_fusion.info, s32[1,640]{1,0:T(1,128)S(1)} %broadcast_in_dim.3.waves_ref), custom_call_target="tpu_custom_call" | custom-call | flops 10485760 | bytes 5242880 | tf_op jit(solution)/shard_map/tables/pallas_call | solution.py:88
  36.1 0.0 copy-start.1
  36.1 2.3 %copy-done.1 = bf16[16,1280,128]{2,1,0:T(8,128)(2,1)} copy-done((bf16[16,1280,128]{2,1,0:T(8,128)(2,1)}, bf16[16,1280,128]{2,1,0:T(8,128)(2,1)S(1)}, u32[]{:S(2)}) %copy-start.1) | copy-done | bytes 5242904
  38.5 0.0 collective-permute-done.2.refs_3_
  38.5 0.0 collective-permute-done.3.refs_4_
  38.5 0.0 collective-permute-done.refs_1_
  38.5 0.7 collective-permute-done.1.refs_2_
  39.2 0.0 all-to-all-done.recv_ref
  39.2 0.0 copy-start
  39.2 0.0 copy-start.2
  39.2 2.6 %copy-done.2 = bf16[16,1280,128]{2,1,0:T(8,128)(2,1)S(1)} copy-done((bf16[16,1280,128]{2,1,0:T(8,128)(2,1)S(1)}, bf16[16,1280,128]{2,1,0:T(8,128)(2,1)}, u32[]{:S(2)}) %copy-start.2) | copy-done | bytes 5242904
  41.8 5.1 %synthesis.1 = (bf16[3,8,16,256]{3,2,1,0:T(8,128)(2,1)S(1)}, bf16[3,8,16,256]{3,2,1,0:T(8,128)(2,1)S(1)}, bf16[3,8,16,256]{3,2,1,0:T(8,128)(2,1)S(1)}, bf16[3,8,16,256]{3,2,1,0:T(8,128)(2,1)S(1)}) custom-call(s32[22]{0:T(128)S(1)} %pad_add_fusion.info, bf16[8,8,16,512]{3,2,1,0:T(8,128)(2,1)S(1)} %all-to-all-done.recv_ref, ...), custom_call_target="tpu_custom_call" | custom-call | flops 1006632960 | bytes 5242880 | tf_op jit(solution)/shard_map/synthesis/pallas_call | solution.py:189
  47.0 0.1 collective-permute-start.5
  47.1 1.9 %collective-permute-start.6 = (bf16[3,8,16,256]{3,2,1,0:T(8,128)(2,1)S(1)}, bf16[3,8,16,256]{3,2,1,0:T(8,128)(2,1)S(1)}, u32[]{:S(2)}, u32[]{:S(2)}) collective-permute-start(bf16[3,8,16,256]{3,2,1,0:T(8,128)(2,1)S(1)} %get-tuple-element.59), channel_id=1, source_target_pairs={{0,1},{1,0},{2,3},{3,2},{4,5},{5,4},{6,7},{7,6},{8,9},{9,8},{10,11... | collective-permute-start | bytes 589832 | tf_op jit(solution)/shard_map/ppermute | solution.py:521
  49.0 0.0 copy-done
  49.0 4.4 %chemistry.4 = (bf16[16,32,16,256]{3,2,1,0:T(8,128)(2,1)}, bf16[4,8,16,256]{3,2,1,0:T(8,128)(2,1)S(1)}) custom-call(s32[22]{0:T(128)S(1)} %pad_add_fusion.info, bf16[16,32,16,256]{3,2,1,0:T(8,128)(2,1)S(1)} %copy-done, bf16[32,16,256]{2,1,0:T(8,128)(2,1)S(1)} %collective-permute-done.refs_1_, bf16[32,16,256]{2,1,0:T(8,128)(2,1)S(1)} %collective-permute-done.1.refs_2_, ...), custom_call_target="tpu_custom_call" | custom-call | flops 524288 | bytes 2048 | tf_op jit(solution)/shard_map/chemistry/pallas_call | solution.py:398
  53.3 0.7 collective-permute-start.4
  54.0 4.6 %collective-permute-done.6.refs_5_ = bf16[3,8,16,256]{3,2,1,0:T(8,128)(2,1)S(1)} collective-permute-done((bf16[3,8,16,256]{3,2,1,0:T(8,128)(2,1)S(1)}, bf16[3,8,16,256]{3,2,1,0:T(8,128)(2,1)S(1)}, u32[]{:S(2)}, u32[]{:S(2)}) %collective-permute-start.6) | collective-permute-done | bytes 196640 | tf_op jit(solution)/shard_map/ppermute | solution.py:521
  58.6 4.4 %chemistry.5 = (bf16[16,32,16,256]{3,2,1,0:T(8,128)(2,1)}, bf16[4,8,16,256]{3,2,1,0:T(8,128)(2,1)S(1)}) custom-call(s32[22]{0:T(128)S(1)} %pad_add_fusion.info, bf16[16,32,16,256]{3,2,1,0:T(8,128)(2,1)S(1)} %copy-done, bf16[32,16,256]{2,1,0:T(8,128)(2,1)S(1)} %collective-permute-done.refs_1_, ...), custom_call_target="tpu_custom_call", output_to_operand_aliasing={{0}: (8, {})} | custom-call | flops 524288 | bytes 2048 | tf_op jit(solution)/shard_map/chemistry/pallas_call | solution.py:398
  63.0 0.0 collective-permute-done.5.refs_5_
  63.0 4.4 %chemistry.6 = (bf16[16,32,16,256]{3,2,1,0:T(8,128)(2,1)}, bf16[4,8,16,256]{3,2,1,0:T(8,128)(2,1)S(1)}) custom-call(s32[22]{0:T(128)S(1)} %pad_add_fusion.info, bf16[16,32,16,256]{3,2,1,0:T(8,128)(2,1)S(1)} %copy-done, bf16[32,16,256]{2,1,0:T(8,128)(2,1)S(1)} %collective-permute-done.refs_1_, ...), custom_call_target="tpu_custom_call", output_to_operand_aliasing={{0}: (8, {})} | custom-call | flops 524288 | bytes 2048 | tf_op jit(solution)/shard_map/chemistry/pallas_call | solution.py:398
  67.4 0.0 collective-permute-start.8
  67.4 5.4 %collective-permute-start.9 = (bf16[4,8,16,256]{3,2,1,0:T(8,128)(2,1)S(1)}, bf16[4,8,16,256]{3,2,1,0:T(8,128)(2,1)S(1)}, u32[]{:S(2)}, u32[]{:S(2)}) collective-permute-start(bf16[4,8,16,256]{3,2,1,0:T(8,128)(2,1)S(1)} %get-tuple-element.66), channel_id=1, source_target_pairs={{0,1},{1,0},{2,3},{3,2},{4,5},{5,4},{6,7},{7,6},{8,9},{9,8},{10,11... | collective-permute-start | bytes 786440 | tf_op jit(solution)/shard_map/ppermute | solution.py:521
  72.8 0.0 collective-permute-done.4.refs_5_
  72.8 4.4 %chemistry.7 = (bf16[16,32,16,256]{3,2,1,0:T(8,128)(2,1)}, bf16[4,8,16,256]{3,2,1,0:T(8,128)(2,1)S(1)}) custom-call(s32[22]{0:T(128)S(1)} %pad_add_fusion.info, bf16[16,32,16,256]{3,2,1,0:T(8,128)(2,1)S(1)} %copy-done, bf16[32,16,256]{2,1,0:T(8,128)(2,1)S(1)} %collective-permute-done.refs_1_, ...), custom_call_target="tpu_custom_call", output_to_operand_aliasing={{0}: (8, {})} | custom-call | flops 524288 | bytes 2048 | tf_op jit(solution)/shard_map/chemistry/pallas_call | solution.py:398
  77.1 1.2 %collective-permute-start.7 = (bf16[4,8,16,256]{3,2,1,0:T(8,128)(2,1)S(1)}, bf16[4,8,16,256]{3,2,1,0:T(8,128)(2,1)S(1)}, u32[]{:S(2)}, u32[]{:S(2)}) collective-permute-start(bf16[4,8,16,256]{3,2,1,0:T(8,128)(2,1)S(1)} %get-tuple-element.64), channel_id=1, source_target_pairs={{0,3},{3,0},{1,2},{2,1},{4,7},{7,4},{5,6},{6,5},{8,11},{11,8},{9,1... | collective-permute-start | bytes 786440 | tf_op jit(solution)/shard_map/ppermute | solution.py:521
  78.3 1.4 %spread.4.refs_0_ = f32[4,8,16,1024]{3,2,1,0:T(8,128)} custom-call(s32[22]{0:T(128)S(1)} %pad_add_fusion.info, bf16[4,8,16,256]{3,2,1,0:T(8,128)(2,1)S(1)} %get-tuple-element.67.recv_ref), custom_call_target="tpu_custom_call" | custom-call | flops 131072 | bytes 4 | tf_op jit(solution)/shard_map/spread/pallas_call | solution.py:440
  79.7 9.3 %collective-permute-done.9.recv_ref = bf16[4,8,16,256]{3,2,1,0:T(8,128)(2,1)S(1)} collective-permute-done((bf16[4,8,16,256]{3,2,1,0:T(8,128)(2,1)S(1)}, bf16[4,8,16,256]{3,2,1,0:T(8,128)(2,1)S(1)}, u32[]{:S(2)}, u32[]{:S(2)}) %collective-permute-start.9) | collective-permute-done | bytes 262176 | tf_op jit(solution)/shard_map/ppermute | solution.py:521
  89.0 1.4 %spread.5.refs_0_ = f32[4,8,16,1024]{3,2,1,0:T(8,128)} custom-call(s32[22]{0:T(128)S(1)} %pad_add_fusion.info, bf16[4,8,16,256]{3,2,1,0:T(8,128)(2,1)S(1)} %collective-permute-done.9.recv_ref, f32[4,8,16,1024]{3,2,1,0:T(8,128)} %spread.4.refs_0_), custom_call_target="tpu_custom_call", output_to_operand_aliasing={{}: (2, {})} | custom-call | flops 131072 | bytes 4 | tf_op jit(solution)/shard_map/spread/pallas_call | solution.py:440
  90.4 0.0 collective-permute-done.8.recv_ref
  90.4 1.4 %spread.6.refs_0_ = f32[4,8,16,1024]{3,2,1,0:T(8,128)} custom-call(s32[22]{0:T(128)S(1)} %pad_add_fusion.info, bf16[4,8,16,256]{3,2,1,0:T(8,128)(2,1)S(1)} %collective-permute-done.8.recv_ref, f32[4,8,16,1024]{3,2,1,0:T(8,128)} %spread.5.refs_0_), custom_call_target="tpu_custom_call", output_to_operand_aliasing={{}: (2, {})} | custom-call | flops 131072 | bytes 4 | tf_op jit(solution)/shard_map/spread/pallas_call | solution.py:440
  91.7 3.0 %collective-permute-done.7.recv_ref = bf16[4,8,16,256]{3,2,1,0:T(8,128)(2,1)S(1)} collective-permute-done((bf16[4,8,16,256]{3,2,1,0:T(8,128)(2,1)S(1)}, bf16[4,8,16,256]{3,2,1,0:T(8,128)(2,1)S(1)}, u32[]{:S(2)}, u32[]{:S(2)}) %collective-permute-start.7) | collective-permute-done | bytes 262176 | tf_op jit(solution)/shard_map/ppermute | solution.py:521
  94.7 1.4 %spread.7 = f32[4,8,16,1024]{3,2,1,0:T(8,128)} custom-call(s32[22]{0:T(128)S(1)} %pad_add_fusion.info, bf16[4,8,16,256]{3,2,1,0:T(8,128)(2,1)S(1)} %collective-permute-done.7.recv_ref, f32[4,8,16,1024]{3,2,1,0:T(8,128)} %spread.6.refs_0_), custom_call_target="tpu_custom_call", output_to_operand_aliasing={{}: (2, {})} | custom-call | flops 131072 | bytes 4 | tf_op jit(solution)/shard_map/spread/pallas_call | solution.py:440
  (1 shorter events, 0.0 us)
Async XLA Ops:
  0.6 14.6 %copy-start.6 = (s32[16]{0:T(128)S(1)}, s32[16]{0:T(128)}, u32[]{:S(2)}) copy-start(s32[16]{0:T(128)} %param.11) | copy-start | bytes 196
  0.6 14.6 %copy-start.7 = (s32[4]{0:T(128)S(1)}, s32[4]{0:T(128)}, u32[]{:S(2)}) copy-start(s32[4]{0:T(128)} %param.15) | copy-start | bytes 52
  0.7 19.2 %copy-start.3 = (f32[16,16]{1,0:T(8,128)S(1)}, f32[16,16]{1,0:T(8,128)}, u32[]{:S(2)}) copy-start(f32[16,16]{1,0:T(8,128)} %base_ref.1) | copy-start | bytes 3076
  0.7 19.2 %copy-start.4 = (f32[16,16]{1,0:T(8,128)S(1)}, f32[16,16]{1,0:T(8,128)}, u32[]{:S(2)}) copy-start(f32[16,16]{1,0:T(8,128)} %temp_ref.1) | copy-start | bytes 3076
  15.2 16.3 %copy-start.5 = (s32[640]{0:T(1024)S(1)}, s32[640]{0:T(1024)}, u32[]{:S(2)}) copy-start(s32[640]{0:T(1024)} %param.10) | copy-start | bytes 7684
  15.3 23.9 %all-to-all-start = ((bf16[8,8,16,512]{3,2,1,0:T(8,128)(2,1)}), bf16[8,8,16,512]{3,2,1,0:T(8,128)(2,1)S(1)}, u32[]{:S(2)}, u32[]{:S(2)}) async-start(bf16[8,8,16,512]{3,2,1,0:T(8,128)(2,1)} %legendre.1), calls=%async_computation | async-start | bytes 2097152 | tf_op jit(solution)/shard_map/all_to_all | solution.py:544
  24.7 13.8 %collective-permute-start = (bf16[32,16,256]{2,1,0:T(8,128)(2,1)S(1)}, bf16[32,16,256]{2,1,0:T(8,128)(2,1)S(1)}, u32[]{:S(2)}, u32[]{:S(2)}) collective-permute-start(bf16[32,16,256]{2,1,0:T(8,128)(2,1)S(1)} %get-tuple-element.41), channel_id=1, source_target_pairs={{0,4},{4,0},{8,12},{12,8},{16,20},{20,16},{24,28},{28,24},{1,5},{5... | collective-permute-start | bytes 786440 | tf_op jit(solution)/shard_map/ppermute | solution.py:521
  25.1 14.1 %collective-permute-start.1 = (bf16[32,16,256]{2,1,0:T(8,128)(2,1)S(1)}, bf16[32,16,256]{2,1,0:T(8,128)(2,1)S(1)}, u32[]{:S(2)}, u32[]{:S(2)}) collective-permute-start(bf16[32,16,256]{2,1,0:T(8,128)(2,1)S(1)} %get-tuple-element.42), channel_id=1, source_target_pairs={{4,8},{8,4},{12,16},{16,12},{20,24},{24,20},{5,9},{9,5},{13,17},{1... | collective-permute-start | bytes 786440 | tf_op jit(solution)/shard_map/ppermute | solution.py:521
  28.2 10.3 %collective-permute-start.2 = (bf16[256,128]{1,0:T(8,128)(2,1)S(1)}, bf16[256,128]{1,0:T(8,128)(2,1)S(1)}, u32[]{:S(2)}, u32[]{:S(2)}) collective-permute-start(bf16[256,128]{1,0:T(8,128)(2,1)S(1)} %get-tuple-element.43), channel_id=1, source_target_pairs={{0,1},{1,0},{2,3},{3,2},{4,5},{5,4},{6,7},{7,6},{8,9},{9,8},{10,11... | collective-permute-start | bytes 196616 | tf_op jit(solution)/shard_map/ppermute | solution.py:521
  29.6 8.9 %collective-permute-start.3 = (bf16[256,128]{1,0:T(8,128)(2,1)S(1)}, bf16[256,128]{1,0:T(8,128)(2,1)S(1)}, u32[]{:S(2)}, u32[]{:S(2)}) collective-permute-start(bf16[256,128]{1,0:T(8,128)(2,1)S(1)} %get-tuple-element.44), channel_id=1, source_target_pairs={{1,2},{2,1},{5,6},{6,5},{9,10},{10,9},{13,14},{14,13},{17,18},{18,... | collective-permute-start | bytes 196616 | tf_op jit(solution)/shard_map/ppermute | solution.py:521
  36.1 2.3 %copy-start.1 = (bf16[16,1280,128]{2,1,0:T(8,128)(2,1)}, bf16[16,1280,128]{2,1,0:T(8,128)(2,1)S(1)}, u32[]{:S(2)}) copy-start(bf16[16,1280,128]{2,1,0:T(8,128)(2,1)S(1)} %get-tuple-element.51.table_ref) | copy-start | bytes 15728644
  39.2 9.8 %copy-start = (bf16[16,32,16,256]{3,2,1,0:T(8,128)(2,1)S(1)}, bf16[16,32,16,256]{3,2,1,0:T(8,128)(2,1)}, u32[]{:S(2)}) copy-start(bf16[16,32,16,256]{3,2,1,0:T(8,128)(2,1)} %refs_0_.7) | copy-start | bytes 12582916
  39.2 2.6 %copy-start.2 = (bf16[16,1280,128]{2,1,0:T(8,128)(2,1)S(1)}, bf16[16,1280,128]{2,1,0:T(8,128)(2,1)}, u32[]{:S(2)}) copy-start(bf16[16,1280,128]{2,1,0:T(8,128)(2,1)} %copy-done.1) | copy-start | bytes 15728644
  47.0 16.0 %collective-permute-start.5 = (bf16[3,8,16,256]{3,2,1,0:T(8,128)(2,1)S(1)}, bf16[3,8,16,256]{3,2,1,0:T(8,128)(2,1)S(1)}, u32[]{:S(2)}, u32[]{:S(2)}) collective-permute-start(bf16[3,8,16,256]{3,2,1,0:T(8,128)(2,1)S(1)} %get-tuple-element.58), channel_id=1, source_target_pairs={{0,2},{2,0},{1,3},{3,1},{4,6},{6,4},{5,7},{7,5},{8,10},{10,8},{9,1... | collective-permute-start | bytes 589832 | tf_op jit(solution)/shard_map/ppermute | solution.py:521
  47.1 11.6 %collective-permute-start.6 = (bf16[3,8,16,256]{3,2,1,0:T(8,128)(2,1)S(1)}, bf16[3,8,16,256]{3,2,1,0:T(8,128)(2,1)S(1)}, u32[]{:S(2)}, u32[]{:S(2)}) collective-permute-start(bf16[3,8,16,256]{3,2,1,0:T(8,128)(2,1)S(1)} %get-tuple-element.59), channel_id=1, source_target_pairs={{0,1},{1,0},{2,3},{3,2},{4,5},{5,4},{6,7},{7,6},{8,9},{9,8},{10,11... | collective-permute-start | bytes 589832 | tf_op jit(solution)/shard_map/ppermute | solution.py:521
  53.3 19.4 %collective-permute-start.4 = (bf16[3,8,16,256]{3,2,1,0:T(8,128)(2,1)S(1)}, bf16[3,8,16,256]{3,2,1,0:T(8,128)(2,1)S(1)}, u32[]{:S(2)}, u32[]{:S(2)}) collective-permute-start(bf16[3,8,16,256]{3,2,1,0:T(8,128)(2,1)S(1)} %get-tuple-element.57), channel_id=1, source_target_pairs={{0,3},{3,0},{1,2},{2,1},{4,7},{7,4},{5,6},{6,5},{8,11},{11,8},{9,1... | collective-permute-start | bytes 589832 | tf_op jit(solution)/shard_map/ppermute | solution.py:521
  67.4 23.0 %collective-permute-start.8 = (bf16[4,8,16,256]{3,2,1,0:T(8,128)(2,1)S(1)}, bf16[4,8,16,256]{3,2,1,0:T(8,128)(2,1)S(1)}, u32[]{:S(2)}, u32[]{:S(2)}) collective-permute-start(bf16[4,8,16,256]{3,2,1,0:T(8,128)(2,1)S(1)} %get-tuple-element.65), channel_id=1, source_target_pairs={{0,2},{2,0},{1,3},{3,1},{4,6},{6,4},{5,7},{7,5},{8,10},{10,8},{9,1... | collective-permute-start | bytes 786440 | tf_op jit(solution)/shard_map/ppermute | solution.py:521
  67.4 21.6 %collective-permute-start.9 = (bf16[4,8,16,256]{3,2,1,0:T(8,128)(2,1)S(1)}, bf16[4,8,16,256]{3,2,1,0:T(8,128)(2,1)S(1)}, u32[]{:S(2)}, u32[]{:S(2)}) collective-permute-start(bf16[4,8,16,256]{3,2,1,0:T(8,128)(2,1)S(1)} %get-tuple-element.66), channel_id=1, source_target_pairs={{0,1},{1,0},{2,3},{3,2},{4,5},{5,4},{6,7},{7,6},{8,9},{9,8},{10,11... | collective-permute-start | bytes 786440 | tf_op jit(solution)/shard_map/ppermute | solution.py:521
  77.1 17.6 %collective-permute-start.7 = (bf16[4,8,16,256]{3,2,1,0:T(8,128)(2,1)S(1)}, bf16[4,8,16,256]{3,2,1,0:T(8,128)(2,1)S(1)}, u32[]{:S(2)}, u32[]{:S(2)}) collective-permute-start(bf16[4,8,16,256]{3,2,1,0:T(8,128)(2,1)S(1)} %get-tuple-element.64), channel_id=1, source_target_pairs={{0,3},{3,0},{1,2},{2,1},{4,7},{7,4},{5,6},{6,5},{8,11},{11,8},{9,1... | collective-permute-start | bytes 786440 | tf_op jit(solution)/shard_map/ppermute | solution.py:521

commit v7 on v6

--- a/solution.py
+++ b/solution.py
@@ -206,7 +206,7 @@
         compiler_params=pltpu.CompilerParams(vmem_limit_bytes=24 * MIB),
         cost_estimate=cost(4 * rows * waves * fields * levels * turns * LANES, 4 * rows * waves * LANES),
         name="synthesis",
-    )(info, recv, table, twiddle)
+    )(info, recv, *[pltpu.with_memory_space_constraint(v, pltpu.VMEM) for v in (table, twiddle)])
 
 
 def edge_kernel(
@@ -556,27 +556,26 @@
     )
     grids = synthesis(recv, table, twiddle, info, tiles, tile)
 
-    middle = list(range(tiles // 2, tiles))
+    middle, inner = list(range(tiles // 2, tiles)), list(range(1, tiles // 2))
     soon, late = middle[: tiles // 4], middle[tiles // 4 :]
-    inner = list(range(1, tiles // 2))
 
     def send(value, k):
         return exchange(value, "lon", partners("lon", k))
 
-    moved = {0: grids[0]} | {k: send(grids[k], k) for k in inner + soon}
+    moved = {0: grids[0]} | {k: send(grids[k], k) for k in soon}
     new, active = None, {}
-    order = [0] + inner + soon + late
-    for k in order:
+    for k in [0] + soon + late + inner:
         new, active[k] = chemistry(
             tracers, halos, moved[k], react, info, k, active_ids.shape[0], waves, new
         )
         if k:
             active[k] = send(active[k], k)
         else:
-            held, active[0] = lax.optimization_barrier(([grids[i] for i in late], active[0]))
-            moved |= {i: send(value, i) for i, value in zip(late, held)}
+            rest = late + inner
+            held, active[0] = lax.optimization_barrier(([grids[i] for i in rest], active[0]))
+            moved |= {i: send(value, i) for i, value in zip(rest, held)}
     spreaded = None
-    for k in order:
+    for k in [0] + soon + inner + late:
         spreaded = spread(active[k], info, k, tiles, spreaded)
     return new, spreaded
 

time: 96.3 us -> 98.2 us (1.020)
  the two profiles are of different devices: /device:TPU:19 before, /device:TPU:2 now
where the time goes in v7:
time: 98.2 us; the launch traced here: 98 us
  Pallas kernels  52 us (53%)
  starting transfers between devices  25.1 us (26%)
  waiting for transfers between devices  15.1 us (15%)
  local copies, waits for them, and re-layouts  5 us (5%)
    ppermute x10, starting transfers between devices, exchange(): lax.ppermute(value, axis, [p for a, b in pairs for p in ((a, b), (b, a))])  20.9 us
    pallas_call x4, Pallas kernels, chemistry(): pl.pallas_call(functools.partial(chem_kernel, scale, k), grid_spec=pltpu....  17.4 us
    ppermute x10, waiting for transfers between devices, exchange(): lax.ppermute(value, axis, [p for a, b in pairs for p in ((a, b), (b, a))])  15.1 us
    pallas_call x1, Pallas kernels, legendre_sums(): pl.pallas_call(legendre_kernel, grid=(share // block,), in_specs=[pl.Bloc...  14.6 us
    pallas_call x4, Pallas kernels, spread(): pl.pallas_call(spread_kernel, grid_spec=pltpu.PrefetchScalarGridSpec(num_...  5.49 us
    pallas_call x1, Pallas kernels, synthesis(): pl.pallas_call(synth_kernel, grid_spec=pltpu.PrefetchScalarGridSpec(num_s...  5.12 us
    unnamed x16, local copies, waits for them, and re-layouts  5 us
    pallas_call x1, Pallas kernels, edges(): pl.pallas_call(edge_kernel, grid_spec=pltpu.PrefetchScalarGridSpec(num_sc...  4.76 us
  transfers between devices with their start and end apart: 11, of which 5 were waited for; matrix products, arithmetic and copies ran while one was open for 0% of the time, Pallas kernels for 32%

profile of v7, /device:TPU:2, one launch (start us, length us, event | category | flops | bytes accessed | tf_op | source)
XLA Modules:
  0.0 98.0 jit_solution(4269365860146123282)
XLA Ops:
  0.6 0.0 copy-start.6
  0.6 0.0 copy-start.7
  0.7 0.0 copy-start.3
  0.7 0.0 copy-start.4
  0.7 14.6 %legendre.1 = bf16[8,8,16,512]{3,2,1,0:T(8,128)(2,1)} custom-call(bf16[6,8,80,1280]{3,2,1,0:T(8,128)(2,1)} %spectral_ref.1, bf16[80,1280,128]{2,1,0:T(8,128)(2,1)} %legendre_ref.1), custom_call_target="tpu_custom_call" | custom-call | flops 1258291200 | bytes 36044800 | tf_op jit(solution)/shard_map/legendre/pallas_call | solution.py:501
  15.2 0.0 copy-start.5
  15.2 0.0 copy-done.6
  15.2 0.0 copy-done.7
  15.3 0.1 pad_add_fusion.info
  15.3 4.3 %all-to-all-start = ((bf16[8,8,16,512]{3,2,1,0:T(8,128)(2,1)}), bf16[8,8,16,512]{3,2,1,0:T(8,128)(2,1)S(1)}, u32[]{:S(2)}, u32[]{:S(2)}) async-start(bf16[8,8,16,512]{3,2,1,0:T(8,128)(2,1)} %legendre.1), calls=%async_computation | async-start | bytes 2097152 | tf_op jit(solution)/shard_map/all_to_all | solution.py:544
  19.6 0.0 copy-done.3
  19.6 0.0 copy-done.4
  19.6 4.8 %edges.1 = (bf16[32,16,256]{2,1,0:T(8,128)(2,1)S(1)}, bf16[32,16,256]{2,1,0:T(8,128)(2,1)S(1)}, bf16[256,128]{1,0:T(8,128)(2,1)S(1)}, bf16[256,128]{1,0:T(8,128)(2,1)S(1)}, bf16[512,512]{1,0:T(8,128)(2,1)S(1)}) custom-call(s32[22]{0:T(128)S(1)} %pad_add_fusion.info, bf16[16,32,16,256]{3,2,1,0:T(8,128)(2,1)} %refs_0_.7, f32[16,16]{1,0:T(8,128)S(1)} %copy-done.3, ...), custom_call_target="tpu_custom_call" | custom-call | flops 268435456 | bytes 4194304 | tf_op jit(solution)/shard_map/edges/pallas_call | solution.py:279
  24.4 0.2 collective-permute-start
  24.6 1.9 %collective-permute-start.1 = (bf16[32,16,256]{2,1,0:T(8,128)(2,1)S(1)}, bf16[32,16,256]{2,1,0:T(8,128)(2,1)S(1)}, u32[]{:S(2)}, u32[]{:S(2)}) collective-permute-start(bf16[32,16,256]{2,1,0:T(8,128)(2,1)S(1)} %get-tuple-element.43), channel_id=1, source_target_pairs={{4,8},{8,4},{12,16},{16,12},{20,24},{24,20},{5,9},{9,5},{13,17},{1... | collective-permute-start | bytes 786440 | tf_op jit(solution)/shard_map/ppermute | solution.py:521
  26.5 1.6 %collective-permute-start.2 = (bf16[256,128]{1,0:T(8,128)(2,1)S(1)}, bf16[256,128]{1,0:T(8,128)(2,1)S(1)}, u32[]{:S(2)}, u32[]{:S(2)}) collective-permute-start(bf16[256,128]{1,0:T(8,128)(2,1)S(1)} %get-tuple-element.44), channel_id=1, source_target_pairs={{0,1},{1,0},{2,3},{3,2},{4,5},{5,4},{6,7},{7,6},{8,9},{9,8},{10,11... | collective-permute-start | bytes 196616 | tf_op jit(solution)/shard_map/ppermute | solution.py:521
  28.1 0.7 collective-permute-start.3
  28.8 0.0 copy-done.5
  28.8 4.6 %tables.1 = (bf16[16,1280,128]{2,1,0:T(8,128)(2,1)S(1)}, f32[16,2,8,640]{3,2,1,0:T(8,128)S(1)}) custom-call(s32[22]{0:T(128)S(1)} %pad_add_fusion.info, s32[1,640]{1,0:T(1,128)S(1)} %broadcast_in_dim.3.waves_ref), custom_call_target="tpu_custom_call" | custom-call | flops 10485760 | bytes 5242880 | tf_op jit(solution)/shard_map/tables/pallas_call | solution.py:88
  33.4 0.0 copy-start.1
  33.4 2.3 %copy-done.1 = bf16[16,1280,128]{2,1,0:T(8,128)(2,1)} copy-done((bf16[16,1280,128]{2,1,0:T(8,128)(2,1)}, bf16[16,1280,128]{2,1,0:T(8,128)(2,1)S(1)}, u32[]{:S(2)}) %copy-start.1) | copy-done | bytes 5242904
  35.8 0.0 collective-permute-done.2.refs_3_
  35.8 0.0 collective-permute-done.3.refs_4_
  35.8 0.0 collective-permute-done.refs_1_
  35.8 1.4 %collective-permute-done.1.refs_2_ = bf16[32,16,256]{2,1,0:T(8,128)(2,1)S(1)} collective-permute-done((bf16[32,16,256]{2,1,0:T(8,128)(2,1)S(1)}, bf16[32,16,256]{2,1,0:T(8,128)(2,1)S(1)}, u32[]{:S(2)}, u32[]{:S(2)}) %collective-permute-start.1) | collective-permute-done | bytes 262176 | tf_op jit(solution)/shard_map/ppermute | solution.py:521
  37.2 0.0 all-to-all-done.recv_ref
  37.2 0.0 copy-start
  37.2 0.0 copy-start.2
  37.2 2.6 %copy-done.2 = bf16[16,1280,128]{2,1,0:T(8,128)(2,1)S(1)} copy-done((bf16[16,1280,128]{2,1,0:T(8,128)(2,1)S(1)}, bf16[16,1280,128]{2,1,0:T(8,128)(2,1)}, u32[]{:S(2)}) %copy-start.2) | copy-done | bytes 5242904
  39.9 5.1 %synthesis.1 = (bf16[3,8,16,256]{3,2,1,0:T(8,128)(2,1)S(1)}, bf16[3,8,16,256]{3,2,1,0:T(8,128)(2,1)S(1)}, bf16[3,8,16,256]{3,2,1,0:T(8,128)(2,1)S(1)}, bf16[3,8,16,256]{3,2,1,0:T(8,128)(2,1)S(1)}) custom-call(s32[22]{0:T(128)S(1)} %pad_add_fusion.info, bf16[8,8,16,512]{3,2,1,0:T(8,128)(2,1)S(1)} %all-to-all-done.recv_ref, ...), custom_call_target="tpu_custom_call" | custom-call | flops 1006632960 | bytes 5242880 | tf_op jit(solution)/shard_map/synthesis/pallas_call | solution.py:189
  45.0 2.7 %collective-permute-start.6 = (bf16[3,8,16,256]{3,2,1,0:T(8,128)(2,1)S(1)}, bf16[3,8,16,256]{3,2,1,0:T(8,128)(2,1)S(1)}, u32[]{:S(2)}, u32[]{:S(2)}) collective-permute-start(bf16[3,8,16,256]{3,2,1,0:T(8,128)(2,1)S(1)} %get-tuple-element.61), channel_id=1, source_target_pairs={{0,2},{2,0},{1,3},{3,1},{4,6},{6,4},{5,7},{7,5},{8,10},{10,8},{9,1... | collective-permute-start | bytes 589832 | tf_op jit(solution)/shard_map/ppermute | solution.py:521
  47.7 0.0 copy-done
  47.7 4.4 %chemistry.4 = (bf16[16,32,16,256]{3,2,1,0:T(8,128)(2,1)}, bf16[4,8,16,256]{3,2,1,0:T(8,128)(2,1)S(1)}) custom-call(s32[22]{0:T(128)S(1)} %pad_add_fusion.info, bf16[16,32,16,256]{3,2,1,0:T(8,128)(2,1)S(1)} %copy-done, bf16[32,16,256]{2,1,0:T(8,128)(2,1)S(1)} %collective-permute-done.refs_1_, bf16[32,16,256]{2,1,0:T(8,128)(2,1)S(1)} %collective-permute-done.1.refs_2_, ...), custom_call_target="tpu_custom_call" | custom-call | flops 524288 | bytes 2048 | tf_op jit(solution)/shard_map/chemistry/pallas_call | solution.py:398
  52.0 2.7 %collective-permute-start.5 = (bf16[3,8,16,256]{3,2,1,0:T(8,128)(2,1)S(1)}, bf16[3,8,16,256]{3,2,1,0:T(8,128)(2,1)S(1)}, u32[]{:S(2)}, u32[]{:S(2)}) collective-permute-start(bf16[3,8,16,256]{3,2,1,0:T(8,128)(2,1)S(1)} %get-tuple-element.60), channel_id=1, source_target_pairs={{0,3},{3,0},{1,2},{2,1},{4,7},{7,4},{5,6},{6,5},{8,11},{11,8},{9,1... | collective-permute-start | bytes 589832 | tf_op jit(solution)/shard_map/ppermute | solution.py:521
  54.8 0.0 collective-permute-start.4
  54.8 2.4 %collective-permute-done.6.refs_5_ = bf16[3,8,16,256]{3,2,1,0:T(8,128)(2,1)S(1)} collective-permute-done((bf16[3,8,16,256]{3,2,1,0:T(8,128)(2,1)S(1)}, bf16[3,8,16,256]{3,2,1,0:T(8,128)(2,1)S(1)}, u32[]{:S(2)}, u32[]{:S(2)}) %collective-permute-start.6) | collective-permute-done | bytes 196640 | tf_op jit(solution)/shard_map/ppermute | solution.py:521
  57.2 4.4 %chemistry.5 = (bf16[16,32,16,256]{3,2,1,0:T(8,128)(2,1)}, bf16[4,8,16,256]{3,2,1,0:T(8,128)(2,1)S(1)}) custom-call(s32[22]{0:T(128)S(1)} %pad_add_fusion.info, bf16[16,32,16,256]{3,2,1,0:T(8,128)(2,1)S(1)} %copy-done, bf16[32,16,256]{2,1,0:T(8,128)(2,1)S(1)} %collective-permute-done.refs_1_, ...), custom_call_target="tpu_custom_call", output_to_operand_aliasing={{0}: (8, {})} | custom-call | flops 524288 | bytes 2048 | tf_op jit(solution)/shard_map/chemistry/pallas_call | solution.py:398
  61.5 0.0 collective-permute-start.9
  61.5 0.0 collective-permute-done.5.refs_5_
  61.5 4.4 %chemistry.6 = (bf16[16,32,16,256]{3,2,1,0:T(8,128)(2,1)}, bf16[4,8,16,256]{3,2,1,0:T(8,128)(2,1)S(1)}) custom-call(s32[22]{0:T(128)S(1)} %pad_add_fusion.info, bf16[16,32,16,256]{3,2,1,0:T(8,128)(2,1)S(1)} %copy-done, bf16[32,16,256]{2,1,0:T(8,128)(2,1)S(1)} %collective-permute-done.refs_1_, ...), custom_call_target="tpu_custom_call", output_to_operand_aliasing={{0}: (8, {})} | custom-call | flops 524288 | bytes 2048 | tf_op jit(solution)/shard_map/chemistry/pallas_call | solution.py:398
  65.9 3.5 %collective-permute-done.4.refs_5_ = bf16[3,8,16,256]{3,2,1,0:T(8,128)(2,1)S(1)} collective-permute-done((bf16[3,8,16,256]{3,2,1,0:T(8,128)(2,1)S(1)}, bf16[3,8,16,256]{3,2,1,0:T(8,128)(2,1)S(1)}, u32[]{:S(2)}, u32[]{:S(2)}) %collective-permute-start.4) | collective-permute-done | bytes 196640 | tf_op jit(solution)/shard_map/ppermute | solution.py:521
  69.3 4.4 %chemistry.7 = (bf16[16,32,16,256]{3,2,1,0:T(8,128)(2,1)}, bf16[4,8,16,256]{3,2,1,0:T(8,128)(2,1)S(1)}) custom-call(s32[22]{0:T(128)S(1)} %pad_add_fusion.info, bf16[16,32,16,256]{3,2,1,0:T(8,128)(2,1)S(1)} %copy-done, bf16[32,16,256]{2,1,0:T(8,128)(2,1)S(1)} %collective-permute-done.refs_1_, ...), custom_call_target="tpu_custom_call", output_to_operand_aliasing={{0}: (8, {})} | custom-call | flops 524288 | bytes 2048 | tf_op jit(solution)/shard_map/chemistry/pallas_call | solution.py:398
  73.7 7.5 %collective-permute-start.8 = (bf16[4,8,16,256]{3,2,1,0:T(8,128)(2,1)S(1)}, bf16[4,8,16,256]{3,2,1,0:T(8,128)(2,1)S(1)}, u32[]{:S(2)}, u32[]{:S(2)}) collective-permute-start(bf16[4,8,16,256]{3,2,1,0:T(8,128)(2,1)S(1)} %get-tuple-element.67), channel_id=1, source_target_pairs={{0,1},{1,0},{2,3},{3,2},{4,5},{5,4},{6,7},{7,6},{8,9},{9,8},{10,11... | collective-permute-start | bytes 786440 | tf_op jit(solution)/shard_map/ppermute | solution.py:521
  81.2 3.5 %collective-permute-start.7 = (bf16[4,8,16,256]{3,2,1,0:T(8,128)(2,1)S(1)}, bf16[4,8,16,256]{3,2,1,0:T(8,128)(2,1)S(1)}, u32[]{:S(2)}, u32[]{:S(2)}) collective-permute-start(bf16[4,8,16,256]{3,2,1,0:T(8,128)(2,1)S(1)} %get-tuple-element.66), channel_id=1, source_target_pairs={{0,3},{3,0},{1,2},{2,1},{4,7},{7,4},{5,6},{6,5},{8,11},{11,8},{9,1... | collective-permute-start | bytes 786440 | tf_op jit(solution)/shard_map/ppermute | solution.py:521
  84.7 1.4 %spread.4.refs_0_ = f32[4,8,16,1024]{3,2,1,0:T(8,128)} custom-call(s32[22]{0:T(128)S(1)} %pad_add_fusion.info, bf16[4,8,16,256]{3,2,1,0:T(8,128)(2,1)S(1)} %get-tuple-element.69.recv_ref), custom_call_target="tpu_custom_call" | custom-call | flops 131072 | bytes 4 | tf_op jit(solution)/shard_map/spread/pallas_call | solution.py:440
  86.1 0.0 collective-permute-done.9.recv_ref
  86.1 1.4 %spread.5.refs_0_ = f32[4,8,16,1024]{3,2,1,0:T(8,128)} custom-call(s32[22]{0:T(128)S(1)} %pad_add_fusion.info, bf16[4,8,16,256]{3,2,1,0:T(8,128)(2,1)S(1)} %collective-permute-done.9.recv_ref, f32[4,8,16,1024]{3,2,1,0:T(8,128)} %spread.4.refs_0_), custom_call_target="tpu_custom_call", output_to_operand_aliasing={{}: (2, {})} | custom-call | flops 131072 | bytes 4 | tf_op jit(solution)/shard_map/spread/pallas_call | solution.py:440
  87.5 0.6 collective-permute-done.8.recv_ref
  88.1 1.4 %spread.6.refs_0_ = f32[4,8,16,1024]{3,2,1,0:T(8,128)} custom-call(s32[22]{0:T(128)S(1)} %pad_add_fusion.info, bf16[4,8,16,256]{3,2,1,0:T(8,128)(2,1)S(1)} %collective-permute-done.8.recv_ref, f32[4,8,16,1024]{3,2,1,0:T(8,128)} %spread.5.refs_0_), custom_call_target="tpu_custom_call", output_to_operand_aliasing={{}: (2, {})} | custom-call | flops 131072 | bytes 4 | tf_op jit(solution)/shard_map/spread/pallas_call | solution.py:440
  89.5 7.2 %collective-permute-done.7.recv_ref = bf16[4,8,16,256]{3,2,1,0:T(8,128)(2,1)S(1)} collective-permute-done((bf16[4,8,16,256]{3,2,1,0:T(8,128)(2,1)S(1)}, bf16[4,8,16,256]{3,2,1,0:T(8,128)(2,1)S(1)}, u32[]{:S(2)}, u32[]{:S(2)}) %collective-permute-start.7) | collective-permute-done | bytes 262176 | tf_op jit(solution)/shard_map/ppermute | solution.py:521
  96.7 1.4 %spread.7 = f32[4,8,16,1024]{3,2,1,0:T(8,128)} custom-call(s32[22]{0:T(128)S(1)} %pad_add_fusion.info, bf16[4,8,16,256]{3,2,1,0:T(8,128)(2,1)S(1)} %collective-permute-done.7.recv_ref, f32[4,8,16,1024]{3,2,1,0:T(8,128)} %spread.6.refs_0_), custom_call_target="tpu_custom_call", output_to_operand_aliasing={{}: (2, {})} | custom-call | flops 131072 | bytes 4 | tf_op jit(solution)/shard_map/spread/pallas_call | solution.py:440
  (1 shorter events, 0.0 us)
Async XLA Ops:
  0.6 14.6 %copy-start.6 = (s32[16]{0:T(128)S(1)}, s32[16]{0:T(128)}, u32[]{:S(2)}) copy-start(s32[16]{0:T(128)} %param.11) | copy-start | bytes 196
  0.6 14.6 %copy-start.7 = (s32[4]{0:T(128)S(1)}, s32[4]{0:T(128)}, u32[]{:S(2)}) copy-start(s32[4]{0:T(128)} %param.15) | copy-start | bytes 52
  0.7 18.9 %copy-start.3 = (f32[16,16]{1,0:T(8,128)S(1)}, f32[16,16]{1,0:T(8,128)}, u32[]{:S(2)}) copy-start(f32[16,16]{1,0:T(8,128)} %base_ref.1) | copy-start | bytes 3076
  0.7 18.9 %copy-start.4 = (f32[16,16]{1,0:T(8,128)S(1)}, f32[16,16]{1,0:T(8,128)}, u32[]{:S(2)}) copy-start(f32[16,16]{1,0:T(8,128)} %temp_ref.1) | copy-start | bytes 3076
  15.2 13.6 %copy-start.5 = (s32[640]{0:T(1024)S(1)}, s32[640]{0:T(1024)}, u32[]{:S(2)}) copy-start(s32[640]{0:T(1024)} %param.10) | copy-start | bytes 7684
  15.3 21.9 %all-to-all-start = ((bf16[8,8,16,512]{3,2,1,0:T(8,128)(2,1)}), bf16[8,8,16,512]{3,2,1,0:T(8,128)(2,1)S(1)}, u32[]{:S(2)}, u32[]{:S(2)}) async-start(bf16[8,8,16,512]{3,2,1,0:T(8,128)(2,1)} %legendre.1), calls=%async_computation | async-start | bytes 2097152 | tf_op jit(solution)/shard_map/all_to_all | solution.py:544
  24.4 11.4 %collective-permute-start = (bf16[32,16,256]{2,1,0:T(8,128)(2,1)S(1)}, bf16[32,16,256]{2,1,0:T(8,128)(2,1)S(1)}, u32[]{:S(2)}, u32[]{:S(2)}) collective-permute-start(bf16[32,16,256]{2,1,0:T(8,128)(2,1)S(1)} %get-tuple-element.42), channel_id=1, source_target_pairs={{0,4},{4,0},{8,12},{12,8},{16,20},{20,16},{24,28},{28,24},{1,5},{5... | collective-permute-start | bytes 786440 | tf_op jit(solution)/shard_map/ppermute | solution.py:521
  24.6 12.7 %collective-permute-start.1 = (bf16[32,16,256]{2,1,0:T(8,128)(2,1)S(1)}, bf16[32,16,256]{2,1,0:T(8,128)(2,1)S(1)}, u32[]{:S(2)}, u32[]{:S(2)}) collective-permute-start(bf16[32,16,256]{2,1,0:T(8,128)(2,1)S(1)} %get-tuple-element.43), channel_id=1, source_target_pairs={{4,8},{8,4},{12,16},{16,12},{20,24},{24,20},{5,9},{9,5},{13,17},{1... | collective-permute-start | bytes 786440 | tf_op jit(solution)/shard_map/ppermute | solution.py:521
  26.5 9.3 %collective-permute-start.2 = (bf16[256,128]{1,0:T(8,128)(2,1)S(1)}, bf16[256,128]{1,0:T(8,128)(2,1)S(1)}, u32[]{:S(2)}, u32[]{:S(2)}) collective-permute-start(bf16[256,128]{1,0:T(8,128)(2,1)S(1)} %get-tuple-element.44), channel_id=1, source_target_pairs={{0,1},{1,0},{2,3},{3,2},{4,5},{5,4},{6,7},{7,6},{8,9},{9,8},{10,11... | collective-permute-start | bytes 196616 | tf_op jit(solution)/shard_map/ppermute | solution.py:521
  28.1 7.6 %collective-permute-start.3 = (bf16[256,128]{1,0:T(8,128)(2,1)S(1)}, bf16[256,128]{1,0:T(8,128)(2,1)S(1)}, u32[]{:S(2)}, u32[]{:S(2)}) collective-permute-start(bf16[256,128]{1,0:T(8,128)(2,1)S(1)} %get-tuple-element.45), channel_id=1, source_target_pairs={{1,2},{2,1},{5,6},{6,5},{9,10},{10,9},{13,14},{14,13},{17,18},{18,... | collective-permute-start | bytes 196616 | tf_op jit(solution)/shard_map/ppermute | solution.py:521
  33.4 2.3 %copy-start.1 = (bf16[16,1280,128]{2,1,0:T(8,128)(2,1)}, bf16[16,1280,128]{2,1,0:T(8,128)(2,1)S(1)}, u32[]{:S(2)}) copy-start(bf16[16,1280,128]{2,1,0:T(8,128)(2,1)S(1)} %get-tuple-element.52.table_ref) | copy-start | bytes 15728644
  37.2 10.4 %copy-start = (bf16[16,32,16,256]{3,2,1,0:T(8,128)(2,1)S(1)}, bf16[16,32,16,256]{3,2,1,0:T(8,128)(2,1)}, u32[]{:S(2)}) copy-start(bf16[16,32,16,256]{3,2,1,0:T(8,128)(2,1)} %refs_0_.7) | copy-start | bytes 12582916
  37.2 2.6 %copy-start.2 = (bf16[16,1280,128]{2,1,0:T(8,128)(2,1)S(1)}, bf16[16,1280,128]{2,1,0:T(8,128)(2,1)}, u32[]{:S(2)}) copy-start(bf16[16,1280,128]{2,1,0:T(8,128)(2,1)} %copy-done.1) | copy-start | bytes 15728644
  45.0 12.2 %collective-permute-start.6 = (bf16[3,8,16,256]{3,2,1,0:T(8,128)(2,1)S(1)}, bf16[3,8,16,256]{3,2,1,0:T(8,128)(2,1)S(1)}, u32[]{:S(2)}, u32[]{:S(2)}) collective-permute-start(bf16[3,8,16,256]{3,2,1,0:T(8,128)(2,1)S(1)} %get-tuple-element.61), channel_id=1, source_target_pairs={{0,2},{2,0},{1,3},{3,1},{4,6},{6,4},{5,7},{7,5},{8,10},{10,8},{9,1... | collective-permute-start | bytes 589832 | tf_op jit(solution)/shard_map/ppermute | solution.py:521
  52.0 9.5 %collective-permute-start.5 = (bf16[3,8,16,256]{3,2,1,0:T(8,128)(2,1)S(1)}, bf16[3,8,16,256]{3,2,1,0:T(8,128)(2,1)S(1)}, u32[]{:S(2)}, u32[]{:S(2)}) collective-permute-start(bf16[3,8,16,256]{3,2,1,0:T(8,128)(2,1)S(1)} %get-tuple-element.60), channel_id=1, source_target_pairs={{0,3},{3,0},{1,2},{2,1},{4,7},{7,4},{5,6},{6,5},{8,11},{11,8},{9,1... | collective-permute-start | bytes 589832 | tf_op jit(solution)/shard_map/ppermute | solution.py:521
  54.8 14.6 %collective-permute-start.4 = (bf16[3,8,16,256]{3,2,1,0:T(8,128)(2,1)S(1)}, bf16[3,8,16,256]{3,2,1,0:T(8,128)(2,1)S(1)}, u32[]{:S(2)}, u32[]{:S(2)}) collective-permute-start(bf16[3,8,16,256]{3,2,1,0:T(8,128)(2,1)S(1)} %get-tuple-element.59), channel_id=1, source_target_pairs={{0,1},{1,0},{2,3},{3,2},{4,5},{5,4},{6,7},{7,6},{8,9},{9,8},{10,11... | collective-permute-start | bytes 589832 | tf_op jit(solution)/shard_map/ppermute | solution.py:521
  61.5 24.6 %collective-permute-start.9 = (bf16[4,8,16,256]{3,2,1,0:T(8,128)(2,1)S(1)}, bf16[4,8,16,256]{3,2,1,0:T(8,128)(2,1)S(1)}, u32[]{:S(2)}, u32[]{:S(2)}) collective-permute-start(bf16[4,8,16,256]{3,2,1,0:T(8,128)(2,1)S(1)} %get-tuple-element.68), channel_id=1, source_target_pairs={{0,2},{2,0},{1,3},{3,1},{4,6},{6,4},{5,7},{7,5},{8,10},{10,8},{9,1... | collective-permute-start | bytes 786440 | tf_op jit(solution)/shard_map/ppermute | solution.py:521
  73.7 14.4 %collective-permute-start.8 = (bf16[4,8,16,256]{3,2,1,0:T(8,128)(2,1)S(1)}, bf16[4,8,16,256]{3,2,1,0:T(8,128)(2,1)S(1)}, u32[]{:S(2)}, u32[]{:S(2)}) collective-permute-start(bf16[4,8,16,256]{3,2,1,0:T(8,128)(2,1)S(1)} %get-tuple-element.67), channel_id=1, source_target_pairs={{0,1},{1,0},{2,3},{3,2},{4,5},{5,4},{6,7},{7,6},{8,9},{9,8},{10,11... | collective-permute-start | bytes 786440 | tf_op jit(solution)/shard_map/ppermute | solution.py:521
  81.2 15.4 %collective-permute-start.7 = (bf16[4,8,16,256]{3,2,1,0:T(8,128)(2,1)S(1)}, bf16[4,8,16,256]{3,2,1,0:T(8,128)(2,1)S(1)}, u32[]{:S(2)}, u32[]{:S(2)}) collective-permute-start(bf16[4,8,16,256]{3,2,1,0:T(8,128)(2,1)S(1)} %get-tuple-element.66), channel_id=1, source_target_pairs={{0,3},{3,0},{1,2},{2,1},{4,7},{7,4},{5,6},{6,5},{8,11},{11,8},{9,1... | collective-permute-start | bytes 786440 | tf_op jit(solution)/shard_map/ppermute | solution.py:521

commit v8 on v7

--- a/solution.py
+++ b/solution.py
@@ -11,7 +11,7 @@
 F32 = jnp.float32
 BF16 = jnp.bfloat16
 LANES = 128
-SUBLANES = 8
+HALF = LANES // 2
 LOW = 16
 STEP = 4
 MIB = 1024 * 1024
@@ -210,7 +210,7 @@
 
 
 def edge_kernel(
-    info, state_ref, base_ref, temp_ref, row_a_ref, row_b_ref, col_a_ref, col_b_ref, react_ref
+    info, state_ref, base_ref, temp_ref, row_a_ref, row_b_ref, column_ref, react_ref
 ):
     tracers, levels, rows, tile = state_ref.shape
     cells = tracers * rows
@@ -237,17 +237,16 @@
     def iota(shape, axis):
         return lax.broadcasted_iota(jnp.int32, shape, axis)
 
-    odd = info[BAND] % 2, info[ME] % 2
-    far, near = (1 - odd[0]) * (rows - 1), odd[0] * (rows - 1)
+    odd = info[BAND] % 2
+    far, near = (1 - odd) * (rows - 1), odd * (rows - 1)
     shape = (2 * tracers, cells)
     end = jnp.where(iota(shape, 0) < tracers, far, near)
     pick = iota(shape, 1) == (iota(shape, 0) % tracers) * rows + end
     pick = jnp.where(pick, 1.0, 0.0).astype(BF16)
-    shape = (tile, 2 * LANES)
-    far, near = (1 - odd[1]) * (tile - 1), odd[1] * (tile - 1)
-    is_end = iota(shape, 0) == jnp.where(iota(shape, 1) < LANES, far, near)
-    level = iota(shape, 1) % LANES - pl.program_id(0) * levels
-    columns = jnp.zeros((cells, 2 * LANES), F32)
+    shape = (tile, LANES)
+    is_end = iota(shape, 0) == jnp.where(iota(shape, 1) < HALF, 0, tile - 1)
+    level = iota(shape, 1) % HALF - pl.program_id(0) * levels
+    columns = jnp.zeros((cells, LANES), F32)
     for l in range(levels):
         x = state_ref[:, l].reshape(cells, tile)
         picked = dot(pick, x, ((1,), (0,)))
@@ -258,13 +257,11 @@
 
     @pl.when(pl.program_id(0) == 0)
     def _():
-        col_a_ref[...] = columns[:, :LANES].astype(BF16)
-        col_b_ref[...] = columns[:, LANES:].astype(BF16)
+        column_ref[...] = columns.astype(BF16)
 
     @pl.when(pl.program_id(0) > 0)
     def _():
-        col_a_ref[...] = (col_a_ref[...].astype(F32) + columns[:, :LANES]).astype(BF16)
-        col_b_ref[...] = (col_b_ref[...].astype(F32) + columns[:, LANES:]).astype(BF16)
+        column_ref[...] = (column_ref[...].astype(F32) + columns).astype(BF16)
 
 
 def edges(state, react_base, react_temp, info):
@@ -287,71 +284,71 @@
                 pl.BlockSpec(react_temp.shape, lambda i, info: (0, 0)),
             ],
             out_specs=[
-                row_spec, row_spec, col_spec, col_spec, pl.BlockSpec(wide, lambda i, info: (0, 0)),
+                row_spec, row_spec, col_spec, pl.BlockSpec(wide, lambda i, info: (0, 0)),
             ],
         ),
-        out_shape=[rowed, rowed, columned, columned, jax.ShapeDtypeStruct(wide, BF16)],
+        out_shape=[rowed, rowed, columned, jax.ShapeDtypeStruct(wide, BF16)],
         compiler_params=pltpu.CompilerParams(vmem_limit_bytes=52 * MIB),
         cost_estimate=cost(4 * state.size * 32, 2 * state.size),
         name="edges",
     )(info, state, react_base, react_temp)
 
 
-def shifted(value, outer, axis, step):
-    size = value[0].shape[axis]
-    turned = [pltpu.roll(v, -step % size, axis) for v in value]
-    place = lax.broadcasted_iota(jnp.int32, value[0].shape, axis)
-    at_end = place == (size - 1 if step == 1 else 0)
+def beside(parts, outer, step):
+    turned = [pltpu.roll(v, -step % LANES, 1) for v in parts]
+    lane = lax.broadcasted_iota(jnp.int32, parts[0].shape, 1)
+    at_end = lane == (LANES - 1 if step == 1 else 0)
     following = turned[1:] + [outer] if step == 1 else [outer] + turned[:-1]
     return [jnp.where(at_end, f, t) for f, t in zip(following, turned)]
 
 
 def chem_kernel(scale, k, info, *refs):
-    state_ref, row_a_ref, row_b_ref, col_a_ref, col_b_ref, grid_ref, react_ref = refs[:7]
-    new_ref, active_ref, south, north, advected, rounded = refs[-6:]
+    state_ref, row_a_ref, row_b_ref, column_ref, grid_ref, react_ref = refs[:6]
+    new_ref, active_ref, column, padded, advected, rounded = refs[-6:]
     tracers, levels, rows, tile = state_ref.shape
+    tiles = column_ref.shape[0]
     cells = tracers * rows
-    odd_band, odd_tile = info[BAND] % 2 == 1, info[ME] % 2 == 1
-    first = ((info[ME] ^ k) * pl.num_programs(0) + pl.program_id(0)) * levels
-
-    def column(value):
-        return pltpu.roll(value, lax.rem(LANES - first, LANES), 1)
-
-    a, b = col_a_ref[...].astype(F32), col_b_ref[...].astype(F32)
-    west, east = column(jnp.where(odd_tile, a, b)), column(jnp.where(odd_tile, b, a))
+    me, odd = info[ME], info[BAND] % 2 == 1
+    first = ((me ^ k) * pl.num_programs(0) + pl.program_id(0)) * levels
+    west = column_ref[jnp.maximum(me - 1, 0)].astype(F32) * jnp.where(me > 0, 1.0, 0.0)
+    east = column_ref[jnp.minimum(me + 1, tiles - 1)].astype(F32) * jnp.where(me < tiles - 1, 1.0, 0.0)
+    column[0] = pltpu.roll(west, lax.rem(LANES + HALF - first, LANES), 1)
+    column[1] = pltpu.roll(east, lax.rem(LANES - first, LANES), 1)
     row = lax.broadcasted_iota(jnp.int32, (rows, tile), 0)
     lane = lax.broadcasted_iota(jnp.int32, (rows, tile), 1)
     ids, points = IDS, IDS + active_ref.shape[0]
     count = jnp.full((rows, tile), info[points], jnp.int32)
     for j in range(1, rows):
         count = jnp.where(row == j, info[points + j], count)
-    mask = jnp.where(info[ME] * tile + lane < count, 1.0, 0.0)
+    mask = jnp.where(me * tile + lane < count, 1.0, 0.0)
     across = [slice(v * LANES, (v + 1) * LANES) for v in range(tile // LANES)]
-    along = [slice(v * SUBLANES, (v + 1) * SUBLANES) for v in range(rows // SUBLANES)]
-
+    pitch = rows + 3
+
+    for l in range(levels):
+        a, b = row_a_ref[l].astype(F32), row_b_ref[l].astype(F32)
+        south, north = jnp.where(odd, a, b), jnp.where(odd, b, a)
+        for v, lanes in enumerate(across):
+            padded[l, v, pl.ds(0, tracers, stride=pitch), :] = south[:, lanes]
+            padded[l, v, pl.ds(rows + 1, tracers, stride=pitch), :] = north[:, lanes]
+            for t in range(tracers):
+                padded[l, v, pl.ds(t * pitch + 1, rows), :] = state_ref[t, l, :, lanes].astype(F32)
     for l in range(levels):
         wind_u = grid_ref[0, l].astype(F32) * (scale * 0.1)
         wind_v = grid_ref[1, l].astype(F32) * (scale * 0.1)
         from_east, from_west = 0.05 - wind_u, 0.05 + wind_u
         from_north, from_south = 0.05 - wind_v, 0.05 + wind_v
-        a, b = row_a_ref[l].astype(F32), row_b_ref[l].astype(F32)
-        south[l] = jnp.where(odd_band, a, b)
-        north[l] = jnp.where(odd_band, b, a)
         for t in range(tracers):
             cell = slice(t * rows, (t + 1) * rows)
-            x = state_ref[t, l].astype(F32)
-            outer = [jnp.broadcast_to(col[cell, l : l + 1], (rows, LANES)) for col in (east, west)]
-            parts = [x[:, v] for v in across]
-            qe = jnp.concatenate(shifted(parts, outer[0], 1, 1), axis=1)
-            qw = jnp.concatenate(shifted(parts, outer[1], 1, -1), axis=1)
-            shape = (SUBLANES, tile)
-            outer = [jnp.broadcast_to(ref[l, t : t + 1], shape) for ref in (north, south)]
-            parts = [x[v] for v in along]
-            qn = jnp.concatenate(shifted(parts, outer[0], 0, 1), axis=0)
-            qs = jnp.concatenate(shifted(parts, outer[1], 0, -1), axis=0)
-            moved = 0.8 * x + from_east * qe + from_west * qw + from_north * qn + from_south * qs
-            advected[l, cell] = moved
-            rounded[l, cell] = moved.astype(BF16)
+            outer = [jnp.broadcast_to(column[i, cell, l : l + 1], (rows, LANES)) for i in (0, 1)]
+            x = [state_ref[t, l, :, lanes].astype(F32) for lanes in across]
+            qw, qe = beside(x, outer[0], -1), beside(x, outer[1], 1)
+            for v, lanes in enumerate(across):
+                qs = padded[l, v, pl.ds(t * pitch, rows), :]
+                qn = padded[l, v, pl.ds(t * pitch + 2, rows), :]
+                moved = 0.8 * x[v] + from_east[:, lanes] * qe[v] + from_west[:, lanes] * qw[v]
+                moved = moved + from_north[:, lanes] * qn + from_south[:, lanes] * qs
+                advected[l, cell, lanes] = moved
+                rounded[l, cell, lanes] = moved.astype(BF16)
     for l in range(levels):
         temper = grid_ref[2, l].astype(F32) * scale
         high = rounded[l]
@@ -386,7 +383,6 @@
         row_spec,
         row_spec,
         whole(halos[2].shape),
-        whole(halos[3].shape),
         pl.BlockSpec((fields, some, rows, tile), lambda i, info: (0, i, 0, 0)),
         whole(react.shape),
     ]
@@ -406,8 +402,8 @@
                 pl.BlockSpec((actives, some, rows, tile), lambda i, info: (0, i, 0, 0)),
             ],
             scratch_shapes=[
-                pltpu.VMEM((some, tracers, tile), F32),
-                pltpu.VMEM((some, tracers, tile), F32),
+                pltpu.VMEM((2, cells, LANES), F32),
+                pltpu.VMEM((some, tile // LANES, tracers * (rows + 3), LANES), F32),
                 pltpu.VMEM((some, cells, tile), F32),
                 pltpu.VMEM((some, cells, tile), BF16),
             ],
@@ -542,17 +538,16 @@
     info = jnp.concatenate([jnp.stack([band, me]), active_ids, points]).astype(jnp.int32)
     sent, info = lax.optimization_barrier((sent, info))
     recv = lax.all_to_all(sent, "lat", split_axis=0, concat_axis=0, tiled=True)
-    *ends, react = edges(tracers, react_base, react_temp, info)
+    row_a, row_b, column, react = edges(tracers, react_base, react_temp, info)
     halos = (
-        exchange(ends[0], "lat", neighbours("lat", 0)),
-        exchange(ends[1], "lat", neighbours("lat", 1)),
-        exchange(ends[2], "lon", neighbours("lon", 0)),
-        exchange(ends[3], "lon", neighbours("lon", 1)),
+        exchange(row_a, "lat", neighbours("lat", 0)),
+        exchange(row_b, "lat", neighbours("lat", 1)),
+        lax.all_gather(column, "lon", axis=0),
     )
     react, wave_ids = lax.optimization_barrier((react, wave_ids))
     table, twiddle = tables(info, wave_ids, rows, tiles * tile // LANES)
-    recv, table, twiddle, halos, react = lax.optimization_barrier(
-        (recv, table, twiddle, halos, react)
+    recv, table, twiddle, react, halos = lax.optimization_barrier(
+        (recv, table, twiddle, react, halos)
     )
     grids = synthesis(recv, table, twiddle, info, tiles, tile)
 

time: 98.2 us -> 104 us (1.059)
  the two profiles are of different devices: /device:TPU:2 before, /device:TPU:0 now
where the time goes in v8:
time: 104 us
  Pallas kernels  53.5 us (51%)
  waiting for transfers between devices  15.2 us (15%)
  blocking collectives  14.8 us (14%)
  starting transfers between devices  14.4 us (14%)
  local copies, waits for them, and re-layouts  5.01 us (5%)
    pallas_call x4, Pallas kernels, chemistry(): pl.pallas_call(functools.partial(chem_kernel, scale, k), grid_spec=pltpu....  19 us
    ppermute x8, waiting for transfers between devices, exchange(): lax.ppermute(value, axis, [p for a, b in pairs for p in ((a, b), (b, a))])  15.2 us
    all_gather x1, blocking collectives, body(): lax.all_gather(column, 'lon', axis=0)  14.8 us
    pallas_call x1, Pallas kernels, legendre_sums(): pl.pallas_call(legendre_kernel, grid=(share // block,), in_specs=[pl.Bloc...  14.6 us
    ppermute x8, starting transfers between devices, exchange(): lax.ppermute(value, axis, [p for a, b in pairs for p in ((a, b), (b, a))])  9.19 us
    pallas_call x4, Pallas kernels, spread(): pl.pallas_call(spread_kernel, grid_spec=pltpu.PrefetchScalarGridSpec(num_...  5.49 us
    all_to_all x1, starting transfers between devices, body(): recv = lax.all_to_all(sent, 'lat', split_axis=0, concat_axis=0, tiled=True)  5.17 us
    pallas_call x1, Pallas kernels, synthesis(): pl.pallas_call(synth_kernel, grid_spec=pltpu.PrefetchScalarGridSpec(num_s...  5.12 us
  transfers between devices with their start and end apart: 9, of which 3 were waited for; matrix products, arithmetic and copies ran while one was open for 0% of the time, Pallas kernels for 31%

profile of v8, /device:TPU:0, one launch (start us, length us, event | category | flops | bytes accessed | tf_op | source)
XLA Modules:
  0.0 103.7 jit_solution(16716009402491344766)
XLA Ops:
  0.6 0.0 copy-start.6
  0.6 0.0 copy-start.7
  0.7 0.0 copy-start.3
  0.7 0.0 copy-start.4
  0.7 14.6 %legendre.1 = bf16[8,8,16,512]{3,2,1,0:T(8,128)(2,1)} custom-call(bf16[6,8,80,1280]{3,2,1,0:T(8,128)(2,1)} %spectral_ref.1, bf16[80,1280,128]{2,1,0:T(8,128)(2,1)} %legendre_ref.1), custom_call_target="tpu_custom_call" | custom-call | flops 1258291200 | bytes 36044800 | tf_op jit(solution)/shard_map/legendre/pallas_call | solution.py:497
  15.2 0.0 copy-start.5
  15.2 0.0 copy-done.6
  15.2 0.0 copy-done.7
  15.3 0.1 pad_add_fusion.info
  15.3 5.2 %all-to-all-start = ((bf16[8,8,16,512]{3,2,1,0:T(8,128)(2,1)}), bf16[8,8,16,512]{3,2,1,0:T(8,128)(2,1)S(1)}, u32[]{:S(2)}, u32[]{:S(2)}) async-start(bf16[8,8,16,512]{3,2,1,0:T(8,128)(2,1)} %legendre.1), calls=%async_computation | async-start | bytes 2097152 | tf_op jit(solution)/shard_map/all_to_all | solution.py:540
  20.5 0.0 copy-done.3
  20.5 0.0 copy-done.4
  20.5 4.7 %edges.1 = (bf16[32,16,256]{2,1,0:T(8,128)(2,1)S(1)}, bf16[32,16,256]{2,1,0:T(8,128)(2,1)S(1)}, bf16[256,128]{1,0:T(8,128)(2,1)S(1)}, bf16[512,512]{1,0:T(8,128)(2,1)S(1)}) custom-call(s32[22]{0:T(128)S(1)} %pad_add_fusion.info, bf16[16,32,16,256]{3,2,1,0:T(8,128)(2,1)} %refs_0_.7, f32[16,16]{1,0:T(8,128)S(1)} %copy-done.3, f32[16,16]{1,0:T(8,128)S(1)} %copy-done.4), custom_call_target="tpu_custom_call" | custom-call | flops 268435456 | bytes 4194304 | tf_op jit(solution)/shard_map/edges/pallas_call | solution.py:276
  25.3 0.6 collective-permute-start
  25.8 0.7 collective-permute-start.1
  26.5 0.0 copy-done.5
  26.5 4.6 %tables.1 = (bf16[16,1280,128]{2,1,0:T(8,128)(2,1)S(1)}, f32[16,2,8,640]{3,2,1,0:T(8,128)S(1)}) custom-call(s32[22]{0:T(128)S(1)} %pad_add_fusion.info, s32[1,640]{1,0:T(1,128)S(1)} %broadcast_in_dim.3.waves_ref), custom_call_target="tpu_custom_call" | custom-call | flops 10485760 | bytes 5242880 | tf_op jit(solution)/shard_map/tables/pallas_call | solution.py:88
  31.1 0.0 copy-start.1
  31.1 2.3 %copy-done.1 = bf16[16,1280,128]{2,1,0:T(8,128)(2,1)} copy-done((bf16[16,1280,128]{2,1,0:T(8,128)(2,1)}, bf16[16,1280,128]{2,1,0:T(8,128)(2,1)S(1)}, u32[]{:S(2)}) %copy-start.1) | copy-done | bytes 5242904
  33.5 14.8 %all-gather = bf16[1024,128]{1,0:T(8,128)(2,1)S(1)} all-gather(bf16[256,128]{1,0:T(8,128)(2,1)S(1)} %get-tuple-element.43), channel_id=2, replica_groups=mesh['lat'=8,'lon'=4] {'lon'}, dimensions={0}, use_global_device_ids=true | all-gather | bytes 327680 | tf_op jit(solution)/shard_map/all_gather | solution.py:545
  48.3 0.0 collective-permute-done.refs_1_
  48.3 0.0 collective-permute-done.1.refs_2_
  48.3 0.0 all-to-all-done.recv_ref
  48.3 0.0 copy-start
  48.3 0.0 copy-start.2
  48.3 2.6 %copy-done.2 = bf16[16,1280,128]{2,1,0:T(8,128)(2,1)S(1)} copy-done((bf16[16,1280,128]{2,1,0:T(8,128)(2,1)S(1)}, bf16[16,1280,128]{2,1,0:T(8,128)(2,1)}, u32[]{:S(2)}) %copy-start.2) | copy-done | bytes 5242904
  50.9 5.1 %synthesis.1 = (bf16[3,8,16,256]{3,2,1,0:T(8,128)(2,1)S(1)}, bf16[3,8,16,256]{3,2,1,0:T(8,128)(2,1)S(1)}, bf16[3,8,16,256]{3,2,1,0:T(8,128)(2,1)S(1)}, bf16[3,8,16,256]{3,2,1,0:T(8,128)(2,1)S(1)}) custom-call(s32[22]{0:T(128)S(1)} %pad_add_fusion.info, bf16[8,8,16,512]{3,2,1,0:T(8,128)(2,1)S(1)} %all-to-all-done.recv_ref, ...), custom_call_target="tpu_custom_call" | custom-call | flops 1006632960 | bytes 5242880 | tf_op jit(solution)/shard_map/synthesis/pallas_call | solution.py:189
  56.1 0.8 collective-permute-start.4
  56.9 0.0 copy-done
  56.9 4.7 %chemistry.4 = (bf16[16,32,16,256]{3,2,1,0:T(8,128)(2,1)}, bf16[4,8,16,256]{3,2,1,0:T(8,128)(2,1)S(1)}) custom-call(s32[22]{0:T(128)S(1)} %pad_add_fusion.info, bf16[16,32,16,256]{3,2,1,0:T(8,128)(2,1)S(1)} %copy-done, bf16[32,16,256]{2,1,0:T(8,128)(2,1)S(1)} %collective-permute-done.refs_1_, bf16[32,16,256]{2,1,0:T(8,128)(2,1)S(1)} %collective-permute-done.1.refs_2_, ...), custom_call_target="tpu_custom_call" | custom-call | flops 524288 | bytes 2048 | tf_op jit(solution)/shard_map/chemistry/pallas_call | solution.py:394
  61.6 2.5 %collective-permute-start.3 = (bf16[3,8,16,256]{3,2,1,0:T(8,128)(2,1)S(1)}, bf16[3,8,16,256]{3,2,1,0:T(8,128)(2,1)S(1)}, u32[]{:S(2)}, u32[]{:S(2)}) collective-permute-start(bf16[3,8,16,256]{3,2,1,0:T(8,128)(2,1)S(1)} %get-tuple-element.56), channel_id=1, source_target_pairs={{0,3},{3,0},{1,2},{2,1},{4,7},{7,4},{5,6},{6,5},{8,11},{11,8},{9,1... | collective-permute-start | bytes 589832 | tf_op jit(solution)/shard_map/ppermute | solution.py:517
  64.2 0.2 collective-permute-start.2
  64.4 8.8 %collective-permute-done.4.refs_4_ = bf16[3,8,16,256]{3,2,1,0:T(8,128)(2,1)S(1)} collective-permute-done((bf16[3,8,16,256]{3,2,1,0:T(8,128)(2,1)S(1)}, bf16[3,8,16,256]{3,2,1,0:T(8,128)(2,1)S(1)}, u32[]{:S(2)}, u32[]{:S(2)}) %collective-permute-start.4) | collective-permute-done | bytes 196640 | tf_op jit(solution)/shard_map/ppermute | solution.py:517
  73.2 4.8 %chemistry.5 = (bf16[16,32,16,256]{3,2,1,0:T(8,128)(2,1)}, bf16[4,8,16,256]{3,2,1,0:T(8,128)(2,1)S(1)}) custom-call(s32[22]{0:T(128)S(1)} %pad_add_fusion.info, bf16[16,32,16,256]{3,2,1,0:T(8,128)(2,1)S(1)} %copy-done, bf16[32,16,256]{2,1,0:T(8,128)(2,1)S(1)} %collective-permute-done.refs_1_, ...), custom_call_target="tpu_custom_call", output_to_operand_aliasing={{0}: (7, {})} | custom-call | flops 524288 | bytes 2048 | tf_op jit(solution)/shard_map/chemistry/pallas_call | solution.py:394
  78.0 0.0 collective-permute-start.7
  78.0 0.0 collective-permute-done.3.refs_4_
  78.0 4.8 %chemistry.6 = (bf16[16,32,16,256]{3,2,1,0:T(8,128)(2,1)}, bf16[4,8,16,256]{3,2,1,0:T(8,128)(2,1)S(1)}) custom-call(s32[22]{0:T(128)S(1)} %pad_add_fusion.info, bf16[16,32,16,256]{3,2,1,0:T(8,128)(2,1)S(1)} %copy-done, bf16[32,16,256]{2,1,0:T(8,128)(2,1)S(1)} %collective-permute-done.refs_1_, ...), custom_call_target="tpu_custom_call", output_to_operand_aliasing={{0}: (7, {})} | custom-call | flops 524288 | bytes 2048 | tf_op jit(solution)/shard_map/chemistry/pallas_call | solution.py:394
  82.8 0.0 collective-permute-done.2.refs_4_
  82.8 4.8 %chemistry.7 = (bf16[16,32,16,256]{3,2,1,0:T(8,128)(2,1)}, bf16[4,8,16,256]{3,2,1,0:T(8,128)(2,1)S(1)}) custom-call(s32[22]{0:T(128)S(1)} %pad_add_fusion.info, bf16[16,32,16,256]{3,2,1,0:T(8,128)(2,1)S(1)} %copy-done, bf16[32,16,256]{2,1,0:T(8,128)(2,1)S(1)} %collective-permute-done.refs_1_, ...), custom_call_target="tpu_custom_call", output_to_operand_aliasing={{0}: (7, {})} | custom-call | flops 524288 | bytes 2048 | tf_op jit(solution)/shard_map/chemistry/pallas_call | solution.py:394
  87.5 1.5 %collective-permute-start.6 = (bf16[4,8,16,256]{3,2,1,0:T(8,128)(2,1)S(1)}, bf16[4,8,16,256]{3,2,1,0:T(8,128)(2,1)S(1)}, u32[]{:S(2)}, u32[]{:S(2)}) collective-permute-start(bf16[4,8,16,256]{3,2,1,0:T(8,128)(2,1)S(1)} %get-tuple-element.63), channel_id=1, source_target_pairs={{0,1},{1,0},{2,3},{3,2},{4,5},{5,4},{6,7},{7,6},{8,9},{9,8},{10,11... | collective-permute-start | bytes 786440 | tf_op jit(solution)/shard_map/ppermute | solution.py:517
  89.0 2.9 %collective-permute-start.5 = (bf16[4,8,16,256]{3,2,1,0:T(8,128)(2,1)S(1)}, bf16[4,8,16,256]{3,2,1,0:T(8,128)(2,1)S(1)}, u32[]{:S(2)}, u32[]{:S(2)}) collective-permute-start(bf16[4,8,16,256]{3,2,1,0:T(8,128)(2,1)S(1)} %get-tuple-element.62), channel_id=1, source_target_pairs={{0,3},{3,0},{1,2},{2,1},{4,7},{7,4},{5,6},{6,5},{8,11},{11,8},{9,1... | collective-permute-start | bytes 786440 | tf_op jit(solution)/shard_map/ppermute | solution.py:517
  91.9 1.4 %spread.4.refs_0_ = f32[4,8,16,1024]{3,2,1,0:T(8,128)} custom-call(s32[22]{0:T(128)S(1)} %pad_add_fusion.info, bf16[4,8,16,256]{3,2,1,0:T(8,128)(2,1)S(1)} %get-tuple-element.65.recv_ref), custom_call_target="tpu_custom_call" | custom-call | flops 131072 | bytes 4 | tf_op jit(solution)/shard_map/spread/pallas_call | solution.py:436
  93.3 0.0 collective-permute-done.7.recv_ref
  93.3 1.4 %spread.5.refs_0_ = f32[4,8,16,1024]{3,2,1,0:T(8,128)} custom-call(s32[22]{0:T(128)S(1)} %pad_add_fusion.info, bf16[4,8,16,256]{3,2,1,0:T(8,128)(2,1)S(1)} %collective-permute-done.7.recv_ref, f32[4,8,16,1024]{3,2,1,0:T(8,128)} %spread.4.refs_0_), custom_call_target="tpu_custom_call", output_to_operand_aliasing={{}: (2, {})} | custom-call | flops 131072 | bytes 4 | tf_op jit(solution)/shard_map/spread/pallas_call | solution.py:436
  94.6 4.5 %collective-permute-done.6.recv_ref = bf16[4,8,16,256]{3,2,1,0:T(8,128)(2,1)S(1)} collective-permute-done((bf16[4,8,16,256]{3,2,1,0:T(8,128)(2,1)S(1)}, bf16[4,8,16,256]{3,2,1,0:T(8,128)(2,1)S(1)}, u32[]{:S(2)}, u32[]{:S(2)}) %collective-permute-start.6) | collective-permute-done | bytes 262176 | tf_op jit(solution)/shard_map/ppermute | solution.py:517
  99.2 1.4 %spread.6.refs_0_ = f32[4,8,16,1024]{3,2,1,0:T(8,128)} custom-call(s32[22]{0:T(128)S(1)} %pad_add_fusion.info, bf16[4,8,16,256]{3,2,1,0:T(8,128)(2,1)S(1)} %collective-permute-done.6.recv_ref, f32[4,8,16,1024]{3,2,1,0:T(8,128)} %spread.5.refs_0_), custom_call_target="tpu_custom_call", output_to_operand_aliasing={{}: (2, {})} | custom-call | flops 131072 | bytes 4 | tf_op jit(solution)/shard_map/spread/pallas_call | solution.py:436
  100.5 1.8 %collective-permute-done.5.recv_ref = bf16[4,8,16,256]{3,2,1,0:T(8,128)(2,1)S(1)} collective-permute-done((bf16[4,8,16,256]{3,2,1,0:T(8,128)(2,1)S(1)}, bf16[4,8,16,256]{3,2,1,0:T(8,128)(2,1)S(1)}, u32[]{:S(2)}, u32[]{:S(2)}) %collective-permute-start.5) | collective-permute-done | bytes 262176 | tf_op jit(solution)/shard_map/ppermute | solution.py:517
  102.3 1.4 %spread.7 = f32[4,8,16,1024]{3,2,1,0:T(8,128)} custom-call(s32[22]{0:T(128)S(1)} %pad_add_fusion.info, bf16[4,8,16,256]{3,2,1,0:T(8,128)(2,1)S(1)} %collective-permute-done.5.recv_ref, f32[4,8,16,1024]{3,2,1,0:T(8,128)} %spread.6.refs_0_), custom_call_target="tpu_custom_call", output_to_operand_aliasing={{}: (2, {})} | custom-call | flops 131072 | bytes 4 | tf_op jit(solution)/shard_map/spread/pallas_call | solution.py:436
  (1 shorter events, 0.0 us)
Async XLA Ops:
  0.6 14.6 %copy-start.6 = (s32[16]{0:T(128)S(1)}, s32[16]{0:T(128)}, u32[]{:S(2)}) copy-start(s32[16]{0:T(128)} %param.11) | copy-start | bytes 196
  0.6 14.6 %copy-start.7 = (s32[4]{0:T(128)S(1)}, s32[4]{0:T(128)}, u32[]{:S(2)}) copy-start(s32[4]{0:T(128)} %param.15) | copy-start | bytes 52
  0.7 19.9 %copy-start.3 = (f32[16,16]{1,0:T(8,128)S(1)}, f32[16,16]{1,0:T(8,128)}, u32[]{:S(2)}) copy-start(f32[16,16]{1,0:T(8,128)} %base_ref.1) | copy-start | bytes 3076
  0.7 19.8 %copy-start.4 = (f32[16,16]{1,0:T(8,128)S(1)}, f32[16,16]{1,0:T(8,128)}, u32[]{:S(2)}) copy-start(f32[16,16]{1,0:T(8,128)} %temp_ref.1) | copy-start | bytes 3076
  15.2 11.3 %copy-start.5 = (s32[640]{0:T(1024)S(1)}, s32[640]{0:T(1024)}, u32[]{:S(2)}) copy-start(s32[640]{0:T(1024)} %param.10) | copy-start | bytes 7684
  15.3 32.9 %all-to-all-start = ((bf16[8,8,16,512]{3,2,1,0:T(8,128)(2,1)}), bf16[8,8,16,512]{3,2,1,0:T(8,128)(2,1)S(1)}, u32[]{:S(2)}, u32[]{:S(2)}) async-start(bf16[8,8,16,512]{3,2,1,0:T(8,128)(2,1)} %legendre.1), calls=%async_computation | async-start | bytes 2097152 | tf_op jit(solution)/shard_map/all_to_all | solution.py:540
  25.3 23.0 %collective-permute-start = (bf16[32,16,256]{2,1,0:T(8,128)(2,1)S(1)}, bf16[32,16,256]{2,1,0:T(8,128)(2,1)S(1)}, u32[]{:S(2)}, u32[]{:S(2)}) collective-permute-start(bf16[32,16,256]{2,1,0:T(8,128)(2,1)S(1)} %get-tuple-element.41), channel_id=1, source_target_pairs={{0,4},{4,0},{8,12},{12,8},{16,20},{20,16},{24,28},{28,24},{1,5},{5... | collective-permute-start | bytes 786440 | tf_op jit(solution)/shard_map/ppermute | solution.py:517
  25.8 22.4 %collective-permute-start.1 = (bf16[32,16,256]{2,1,0:T(8,128)(2,1)S(1)}, bf16[32,16,256]{2,1,0:T(8,128)(2,1)S(1)}, u32[]{:S(2)}, u32[]{:S(2)}) collective-permute-start(bf16[32,16,256]{2,1,0:T(8,128)(2,1)S(1)} %get-tuple-element.42), channel_id=1, source_target_pairs={{4,8},{8,4},{12,16},{16,12},{20,24},{24,20},{5,9},{9,5},{13,17},{1... | collective-permute-start | bytes 786440 | tf_op jit(solution)/shard_map/ppermute | solution.py:517
  31.1 2.4 %copy-start.1 = (bf16[16,1280,128]{2,1,0:T(8,128)(2,1)}, bf16[16,1280,128]{2,1,0:T(8,128)(2,1)S(1)}, u32[]{:S(2)}) copy-start(bf16[16,1280,128]{2,1,0:T(8,128)(2,1)S(1)} %get-tuple-element.48.table_ref) | copy-start | bytes 15728644
  48.3 8.6 %copy-start = (bf16[16,32,16,256]{3,2,1,0:T(8,128)(2,1)S(1)}, bf16[16,32,16,256]{3,2,1,0:T(8,128)(2,1)}, u32[]{:S(2)}) copy-start(bf16[16,32,16,256]{3,2,1,0:T(8,128)(2,1)} %refs_0_.7) | copy-start | bytes 12582916
  48.3 2.6 %copy-start.2 = (bf16[16,1280,128]{2,1,0:T(8,128)(2,1)S(1)}, bf16[16,1280,128]{2,1,0:T(8,128)(2,1)}, u32[]{:S(2)}) copy-start(bf16[16,1280,128]{2,1,0:T(8,128)(2,1)} %copy-done.1) | copy-start | bytes 15728644
  56.1 17.2 %collective-permute-start.4 = (bf16[3,8,16,256]{3,2,1,0:T(8,128)(2,1)S(1)}, bf16[3,8,16,256]{3,2,1,0:T(8,128)(2,1)S(1)}, u32[]{:S(2)}, u32[]{:S(2)}) collective-permute-start(bf16[3,8,16,256]{3,2,1,0:T(8,128)(2,1)S(1)} %get-tuple-element.57), channel_id=1, source_target_pairs={{0,2},{2,0},{1,3},{3,1},{4,6},{6,4},{5,7},{7,5},{8,10},{10,8},{9,1... | collective-permute-start | bytes 589832 | tf_op jit(solution)/shard_map/ppermute | solution.py:517
  61.6 16.4 %collective-permute-start.3 = (bf16[3,8,16,256]{3,2,1,0:T(8,128)(2,1)S(1)}, bf16[3,8,16,256]{3,2,1,0:T(8,128)(2,1)S(1)}, u32[]{:S(2)}, u32[]{:S(2)}) collective-permute-start(bf16[3,8,16,256]{3,2,1,0:T(8,128)(2,1)S(1)} %get-tuple-element.56), channel_id=1, source_target_pairs={{0,3},{3,0},{1,2},{2,1},{4,7},{7,4},{5,6},{6,5},{8,11},{11,8},{9,1... | collective-permute-start | bytes 589832 | tf_op jit(solution)/shard_map/ppermute | solution.py:517
  64.2 18.6 %collective-permute-start.2 = (bf16[3,8,16,256]{3,2,1,0:T(8,128)(2,1)S(1)}, bf16[3,8,16,256]{3,2,1,0:T(8,128)(2,1)S(1)}, u32[]{:S(2)}, u32[]{:S(2)}) collective-permute-start(bf16[3,8,16,256]{3,2,1,0:T(8,128)(2,1)S(1)} %get-tuple-element.55), channel_id=1, source_target_pairs={{0,1},{1,0},{2,3},{3,2},{4,5},{5,4},{6,7},{7,6},{8,9},{9,8},{10,11... | collective-permute-start | bytes 589832 | tf_op jit(solution)/shard_map/ppermute | solution.py:517
  78.0 15.3 %collective-permute-start.7 = (bf16[4,8,16,256]{3,2,1,0:T(8,128)(2,1)S(1)}, bf16[4,8,16,256]{3,2,1,0:T(8,128)(2,1)S(1)}, u32[]{:S(2)}, u32[]{:S(2)}) collective-permute-start(bf16[4,8,16,256]{3,2,1,0:T(8,128)(2,1)S(1)} %get-tuple-element.64), channel_id=1, source_target_pairs={{0,2},{2,0},{1,3},{3,1},{4,6},{6,4},{5,7},{7,5},{8,10},{10,8},{9,1... | collective-permute-start | bytes 786440 | tf_op jit(solution)/shard_map/ppermute | solution.py:517
  87.5 11.7 %collective-permute-start.6 = (bf16[4,8,16,256]{3,2,1,0:T(8,128)(2,1)S(1)}, bf16[4,8,16,256]{3,2,1,0:T(8,128)(2,1)S(1)}, u32[]{:S(2)}, u32[]{:S(2)}) collective-permute-start(bf16[4,8,16,256]{3,2,1,0:T(8,128)(2,1)S(1)} %get-tuple-element.63), channel_id=1, source_target_pairs={{0,1},{1,0},{2,3},{3,2},{4,5},{5,4},{6,7},{7,6},{8,9},{9,8},{10,11... | collective-permute-start | bytes 786440 | tf_op jit(solution)/shard_map/ppermute | solution.py:517
  89.0 13.3 %collective-permute-start.5 = (bf16[4,8,16,256]{3,2,1,0:T(8,128)(2,1)S(1)}, bf16[4,8,16,256]{3,2,1,0:T(8,128)(2,1)S(1)}, u32[]{:S(2)}, u32[]{:S(2)}) collective-permute-start(bf16[4,8,16,256]{3,2,1,0:T(8,128)(2,1)S(1)} %get-tuple-element.62), channel_id=1, source_target_pairs={{0,3},{3,0},{1,2},{2,1},{4,7},{7,4},{5,6},{6,5},{8,11},{11,8},{9,1... | collective-permute-start | bytes 786440 | tf_op jit(solution)/shard_map/ppermute | solution.py:517

commit v9 on v7

--- a/solution.py
+++ b/solution.py
@@ -543,16 +543,16 @@
     sent, info = lax.optimization_barrier((sent, info))
     recv = lax.all_to_all(sent, "lat", split_axis=0, concat_axis=0, tiled=True)
     *ends, react = edges(tracers, react_base, react_temp, info)
+    react, wave_ids = lax.optimization_barrier((react, wave_ids))
+    table, twiddle = tables(info, wave_ids, rows, tiles * tile // LANES)
+    recv, table, twiddle, react, ends = lax.optimization_barrier(
+        (recv, table, twiddle, react, ends)
+    )
     halos = (
         exchange(ends[0], "lat", neighbours("lat", 0)),
         exchange(ends[1], "lat", neighbours("lat", 1)),
         exchange(ends[2], "lon", neighbours("lon", 0)),
         exchange(ends[3], "lon", neighbours("lon", 1)),
-    )
-    react, wave_ids = lax.optimization_barrier((react, wave_ids))
-    table, twiddle = tables(info, wave_ids, rows, tiles * tile // LANES)
-    recv, table, twiddle, halos, react = lax.optimization_barrier(
-        (recv, table, twiddle, halos, react)
     )
     grids = synthesis(recv, table, twiddle, info, tiles, tile)
 

time: 98.2 us -> 95.8 us (0.976)
  waiting for transfers between devices: 15.1 us -> 12.1 us
    ppermute x10, waiting for transfers between devices: 15.1 us -> 9.92 us  [exchange(): lax.ppermute(value, axis, [p for a, b in pairs for p in ((a, b), (b, a))])]
    all_to_all x1, waiting for transfers between devices: 0.01 us -> 2.16 us  [body(): recv = lax.all_to_all(sent, 'lat', split_axis=0, concat_axis=0, tiled=True)]
  transfers between devices with their start and end apart: 11 -> 11, of which waited for: 5 -> 3; matrix products, arithmetic and copies ran while one was open for 0% -> 0% of each run, Pallas kernels for 32% -> 38%
where the time goes in v9:
time: 95.8 us; the launch traced here: 95.6 us
  Pallas kernels  52 us (54%)
  starting transfers between devices  25.8 us (27%)
  waiting for transfers between devices  12.1 us (13%)
  local copies, waits for them, and re-layouts  4.85 us (5%)
    ppermute x10, starting transfers between devices, exchange(): lax.ppermute(value, axis, [p for a, b in pairs for p in ((a, b), (b, a))])  21.6 us
    pallas_call x4, Pallas kernels, chemistry(): pl.pallas_call(functools.partial(chem_kernel, scale, k), grid_spec=pltpu....  17.4 us
    pallas_call x1, Pallas kernels, legendre_sums(): pl.pallas_call(legendre_kernel, grid=(share // block,), in_specs=[pl.Bloc...  14.6 us
    ppermute x10, waiting for transfers between devices, exchange(): lax.ppermute(value, axis, [p for a, b in pairs for p in ((a, b), (b, a))])  9.92 us
    pallas_call x4, Pallas kernels, spread(): pl.pallas_call(spread_kernel, grid_spec=pltpu.PrefetchScalarGridSpec(num_...  5.49 us
    pallas_call x1, Pallas kernels, synthesis(): pl.pallas_call(synth_kernel, grid_spec=pltpu.PrefetchScalarGridSpec(num_s...  5.12 us
    unnamed x16, local copies, waits for them, and re-layouts  4.84 us
    pallas_call x1, Pallas kernels, edges(): pl.pallas_call(edge_kernel, grid_spec=pltpu.PrefetchScalarGridSpec(num_sc...  4.76 us
  transfers between devices with their start and end apart: 11, of which 3 were waited for; matrix products, arithmetic and copies ran while one was open for 0% of the time, Pallas kernels for 38%

profile of v9, /device:TPU:2, one launch (start us, length us, event | category | flops | bytes accessed | tf_op | source)
XLA Modules:
  0.0 95.6 jit_solution(4201256185523626274)
XLA Ops:
  0.6 0.0 copy-start.6
  0.6 0.0 copy-start.7
  0.7 0.0 copy-start.3
  0.7 0.0 copy-start.4
  0.7 14.6 %legendre.1 = bf16[8,8,16,512]{3,2,1,0:T(8,128)(2,1)} custom-call(bf16[6,8,80,1280]{3,2,1,0:T(8,128)(2,1)} %spectral_ref.1, bf16[80,1280,128]{2,1,0:T(8,128)(2,1)} %legendre_ref.1), custom_call_target="tpu_custom_call" | custom-call | flops 1258291200 | bytes 36044800 | tf_op jit(solution)/shard_map/legendre/pallas_call | solution.py:501
  15.2 0.0 copy-start.5
  15.2 0.0 copy-done.6
  15.2 0.0 copy-done.7
  15.3 0.1 pad_add_fusion.info
  15.3 4.3 %all-to-all-start = ((bf16[8,8,16,512]{3,2,1,0:T(8,128)(2,1)}), bf16[8,8,16,512]{3,2,1,0:T(8,128)(2,1)S(1)}, u32[]{:S(2)}, u32[]{:S(2)}) async-start(bf16[8,8,16,512]{3,2,1,0:T(8,128)(2,1)} %legendre.1), calls=%async_computation | async-start | bytes 2097152 | tf_op jit(solution)/shard_map/all_to_all | solution.py:544
  19.6 0.0 copy-done.3
  19.6 0.0 copy-done.4
  19.6 4.8 %edges.1 = (bf16[32,16,256]{2,1,0:T(8,128)(2,1)S(1)}, bf16[32,16,256]{2,1,0:T(8,128)(2,1)S(1)}, bf16[256,128]{1,0:T(8,128)(2,1)S(1)}, bf16[256,128]{1,0:T(8,128)(2,1)S(1)}, bf16[512,512]{1,0:T(8,128)(2,1)S(1)}) custom-call(s32[22]{0:T(128)S(1)} %pad_add_fusion.info, bf16[16,32,16,256]{3,2,1,0:T(8,128)(2,1)} %refs_0_.7, f32[16,16]{1,0:T(8,128)S(1)} %copy-done.3, ...), custom_call_target="tpu_custom_call" | custom-call | flops 268435456 | bytes 4194304 | tf_op jit(solution)/shard_map/edges/pallas_call | solution.py:279
  24.4 0.0 copy-done.5
  24.4 4.6 %tables.1 = (bf16[16,1280,128]{2,1,0:T(8,128)(2,1)S(1)}, f32[16,2,8,640]{3,2,1,0:T(8,128)S(1)}) custom-call(s32[22]{0:T(128)S(1)} %pad_add_fusion.info, s32[1,640]{1,0:T(1,128)S(1)} %broadcast_in_dim.3.waves_ref), custom_call_target="tpu_custom_call" | custom-call | flops 10485760 | bytes 5242880 | tf_op jit(solution)/shard_map/tables/pallas_call | solution.py:88
  29.0 0.0 copy-start.1
  29.0 2.3 %copy-done.1 = bf16[16,1280,128]{2,1,0:T(8,128)(2,1)} copy-done((bf16[16,1280,128]{2,1,0:T(8,128)(2,1)}, bf16[16,1280,128]{2,1,0:T(8,128)(2,1)S(1)}, u32[]{:S(2)}) %copy-start.1) | copy-done | bytes 5242904
  31.3 2.2 %all-to-all-done.recv_ref = bf16[8,8,16,512]{3,2,1,0:T(8,128)(2,1)S(1)} async-done(((bf16[8,8,16,512]{3,2,1,0:T(8,128)(2,1)}), bf16[8,8,16,512]{3,2,1,0:T(8,128)(2,1)S(1)}, u32[]{:S(2)}, u32[]{:S(2)}) %all-to-all-start) | async-done | bytes 1048608 | tf_op jit(solution)/shard_map/all_to_all | solution.py:544
  33.5 0.0 copy-start
  33.5 0.1 collective-permute-start
  33.6 3.5 %collective-permute-start.1 = (bf16[32,16,256]{2,1,0:T(8,128)(2,1)S(1)}, bf16[32,16,256]{2,1,0:T(8,128)(2,1)S(1)}, u32[]{:S(2)}, u32[]{:S(2)}) collective-permute-start(bf16[32,16,256]{2,1,0:T(8,128)(2,1)S(1)} %get-tuple-element.48), channel_id=1, source_target_pairs={{4,8},{8,4},{12,16},{16,12},{20,24},{24,20},{5,9},{9,5},{13,17},{1... | collective-permute-start | bytes 786440 | tf_op jit(solution)/shard_map/ppermute | solution.py:521
  37.0 1.6 %collective-permute-start.2 = (bf16[256,128]{1,0:T(8,128)(2,1)S(1)}, bf16[256,128]{1,0:T(8,128)(2,1)S(1)}, u32[]{:S(2)}, u32[]{:S(2)}) collective-permute-start(bf16[256,128]{1,0:T(8,128)(2,1)S(1)} %get-tuple-element.49), channel_id=1, source_target_pairs={{0,1},{1,0},{2,3},{3,2},{4,5},{5,4},{6,7},{7,6},{8,9},{9,8},{10,11... | collective-permute-start | bytes 196616 | tf_op jit(solution)/shard_map/ppermute | solution.py:521
  38.7 0.7 collective-permute-start.3
  39.3 0.0 copy-start.2
  39.3 2.5 %copy-done.2 = bf16[16,1280,128]{2,1,0:T(8,128)(2,1)S(1)} copy-done((bf16[16,1280,128]{2,1,0:T(8,128)(2,1)S(1)}, bf16[16,1280,128]{2,1,0:T(8,128)(2,1)}, u32[]{:S(2)}) %copy-start.2) | copy-done | bytes 5242904
  41.8 5.1 %synthesis.1 = (bf16[3,8,16,256]{3,2,1,0:T(8,128)(2,1)S(1)}, bf16[3,8,16,256]{3,2,1,0:T(8,128)(2,1)S(1)}, bf16[3,8,16,256]{3,2,1,0:T(8,128)(2,1)S(1)}, bf16[3,8,16,256]{3,2,1,0:T(8,128)(2,1)S(1)}) custom-call(s32[22]{0:T(128)S(1)} %pad_add_fusion.info, bf16[8,8,16,512]{3,2,1,0:T(8,128)(2,1)S(1)} %all-to-all-done.recv_ref, ...), custom_call_target="tpu_custom_call" | custom-call | flops 1006632960 | bytes 5242880 | tf_op jit(solution)/shard_map/synthesis/pallas_call | solution.py:189
  46.9 3.9 %collective-permute-start.6 = (bf16[3,8,16,256]{3,2,1,0:T(8,128)(2,1)S(1)}, bf16[3,8,16,256]{3,2,1,0:T(8,128)(2,1)S(1)}, u32[]{:S(2)}, u32[]{:S(2)}) collective-permute-start(bf16[3,8,16,256]{3,2,1,0:T(8,128)(2,1)S(1)} %get-tuple-element.61), channel_id=1, source_target_pairs={{0,2},{2,0},{1,3},{3,1},{4,6},{6,4},{5,7},{7,5},{8,10},{10,8},{9,1... | collective-permute-start | bytes 589832 | tf_op jit(solution)/shard_map/ppermute | solution.py:521
  50.9 0.0 collective-permute-done.2.refs_3_
  50.9 0.0 collective-permute-done.3.refs_4_
  50.9 0.0 collective-permute-done.refs_1_
  50.9 0.0 collective-permute-done.1.refs_2_
  50.9 0.0 copy-done
  50.9 4.4 %chemistry.4 = (bf16[16,32,16,256]{3,2,1,0:T(8,128)(2,1)}, bf16[4,8,16,256]{3,2,1,0:T(8,128)(2,1)S(1)}) custom-call(s32[22]{0:T(128)S(1)} %pad_add_fusion.info, bf16[16,32,16,256]{3,2,1,0:T(8,128)(2,1)S(1)} %copy-done, bf16[32,16,256]{2,1,0:T(8,128)(2,1)S(1)} %collective-permute-done.refs_1_, bf16[32,16,256]{2,1,0:T(8,128)(2,1)S(1)} %collective-permute-done.1.refs_2_, ...), custom_call_target="tpu_custom_call" | custom-call | flops 524288 | bytes 2048 | tf_op jit(solution)/shard_map/chemistry/pallas_call | solution.py:398
  55.2 2.9 %collective-permute-start.5 = (bf16[3,8,16,256]{3,2,1,0:T(8,128)(2,1)S(1)}, bf16[3,8,16,256]{3,2,1,0:T(8,128)(2,1)S(1)}, u32[]{:S(2)}, u32[]{:S(2)}) collective-permute-start(bf16[3,8,16,256]{3,2,1,0:T(8,128)(2,1)S(1)} %get-tuple-element.60), channel_id=1, source_target_pairs={{0,3},{3,0},{1,2},{2,1},{4,7},{7,4},{5,6},{6,5},{8,11},{11,8},{9,1... | collective-permute-start | bytes 589832 | tf_op jit(solution)/shard_map/ppermute | solution.py:521
  58.2 0.0 collective-permute-start.4
  58.2 6.9 %collective-permute-done.6.refs_5_ = bf16[3,8,16,256]{3,2,1,0:T(8,128)(2,1)S(1)} collective-permute-done((bf16[3,8,16,256]{3,2,1,0:T(8,128)(2,1)S(1)}, bf16[3,8,16,256]{3,2,1,0:T(8,128)(2,1)S(1)}, u32[]{:S(2)}, u32[]{:S(2)}) %collective-permute-start.6) | collective-permute-done | bytes 196640 | tf_op jit(solution)/shard_map/ppermute | solution.py:521
  65.0 4.4 %chemistry.5 = (bf16[16,32,16,256]{3,2,1,0:T(8,128)(2,1)}, bf16[4,8,16,256]{3,2,1,0:T(8,128)(2,1)S(1)}) custom-call(s32[22]{0:T(128)S(1)} %pad_add_fusion.info, bf16[16,32,16,256]{3,2,1,0:T(8,128)(2,1)S(1)} %copy-done, bf16[32,16,256]{2,1,0:T(8,128)(2,1)S(1)} %collective-permute-done.refs_1_, ...), custom_call_target="tpu_custom_call", output_to_operand_aliasing={{0}: (8, {})} | custom-call | flops 524288 | bytes 2048 | tf_op jit(solution)/shard_map/chemistry/pallas_call | solution.py:398
  69.4 0.0 collective-permute-start.9
  69.4 0.0 collective-permute-done.5.refs_5_
  69.4 4.4 %chemistry.6 = (bf16[16,32,16,256]{3,2,1,0:T(8,128)(2,1)}, bf16[4,8,16,256]{3,2,1,0:T(8,128)(2,1)S(1)}) custom-call(s32[22]{0:T(128)S(1)} %pad_add_fusion.info, bf16[16,32,16,256]{3,2,1,0:T(8,128)(2,1)S(1)} %copy-done, bf16[32,16,256]{2,1,0:T(8,128)(2,1)S(1)} %collective-permute-done.refs_1_, ...), custom_call_target="tpu_custom_call", output_to_operand_aliasing={{0}: (8, {})} | custom-call | flops 524288 | bytes 2048 | tf_op jit(solution)/shard_map/chemistry/pallas_call | solution.py:398
  73.8 0.0 collective-permute-done.4.refs_5_
  73.8 4.4 %chemistry.7 = (bf16[16,32,16,256]{3,2,1,0:T(8,128)(2,1)}, bf16[4,8,16,256]{3,2,1,0:T(8,128)(2,1)S(1)}) custom-call(s32[22]{0:T(128)S(1)} %pad_add_fusion.info, bf16[16,32,16,256]{3,2,1,0:T(8,128)(2,1)S(1)} %copy-done, bf16[32,16,256]{2,1,0:T(8,128)(2,1)S(1)} %collective-permute-done.refs_1_, ...), custom_call_target="tpu_custom_call", output_to_operand_aliasing={{0}: (8, {})} | custom-call | flops 524288 | bytes 2048 | tf_op jit(solution)/shard_map/chemistry/pallas_call | solution.py:398
  78.1 3.5 %collective-permute-start.8 = (bf16[4,8,16,256]{3,2,1,0:T(8,128)(2,1)S(1)}, bf16[4,8,16,256]{3,2,1,0:T(8,128)(2,1)S(1)}, u32[]{:S(2)}, u32[]{:S(2)}) collective-permute-start(bf16[4,8,16,256]{3,2,1,0:T(8,128)(2,1)S(1)} %get-tuple-element.67), channel_id=1, source_target_pairs={{0,1},{1,0},{2,3},{3,2},{4,5},{5,4},{6,7},{7,6},{8,9},{9,8},{10,11... | collective-permute-start | bytes 786440 | tf_op jit(solution)/shard_map/ppermute | solution.py:521
  81.6 5.5 %collective-permute-start.7 = (bf16[4,8,16,256]{3,2,1,0:T(8,128)(2,1)S(1)}, bf16[4,8,16,256]{3,2,1,0:T(8,128)(2,1)S(1)}, u32[]{:S(2)}, u32[]{:S(2)}) collective-permute-start(bf16[4,8,16,256]{3,2,1,0:T(8,128)(2,1)S(1)} %get-tuple-element.66), channel_id=1, source_target_pairs={{0,3},{3,0},{1,2},{2,1},{4,7},{7,4},{5,6},{6,5},{8,11},{11,8},{9,1... | collective-permute-start | bytes 786440 | tf_op jit(solution)/shard_map/ppermute | solution.py:521
  87.1 1.4 %spread.4.refs_0_ = f32[4,8,16,1024]{3,2,1,0:T(8,128)} custom-call(s32[22]{0:T(128)S(1)} %pad_add_fusion.info, bf16[4,8,16,256]{3,2,1,0:T(8,128)(2,1)S(1)} %get-tuple-element.69.recv_ref), custom_call_target="tpu_custom_call" | custom-call | flops 131072 | bytes 4 | tf_op jit(solution)/shard_map/spread/pallas_call | solution.py:440
  88.4 0.0 collective-permute-done.9.recv_ref
  88.4 1.4 %spread.5.refs_0_ = f32[4,8,16,1024]{3,2,1,0:T(8,128)} custom-call(s32[22]{0:T(128)S(1)} %pad_add_fusion.info, bf16[4,8,16,256]{3,2,1,0:T(8,128)(2,1)S(1)} %collective-permute-done.9.recv_ref, f32[4,8,16,1024]{3,2,1,0:T(8,128)} %spread.4.refs_0_), custom_call_target="tpu_custom_call", output_to_operand_aliasing={{}: (2, {})} | custom-call | flops 131072 | bytes 4 | tf_op jit(solution)/shard_map/spread/pallas_call | solution.py:440
  89.8 0.0 collective-permute-done.8.recv_ref
  89.8 1.4 %spread.6.refs_0_ = f32[4,8,16,1024]{3,2,1,0:T(8,128)} custom-call(s32[22]{0:T(128)S(1)} %pad_add_fusion.info, bf16[4,8,16,256]{3,2,1,0:T(8,128)(2,1)S(1)} %collective-permute-done.8.recv_ref, f32[4,8,16,1024]{3,2,1,0:T(8,128)} %spread.5.refs_0_), custom_call_target="tpu_custom_call", output_to_operand_aliasing={{}: (2, {})} | custom-call | flops 131072 | bytes 4 | tf_op jit(solution)/shard_map/spread/pallas_call | solution.py:440
  91.2 3.0 %collective-permute-done.7.recv_ref = bf16[4,8,16,256]{3,2,1,0:T(8,128)(2,1)S(1)} collective-permute-done((bf16[4,8,16,256]{3,2,1,0:T(8,128)(2,1)S(1)}, bf16[4,8,16,256]{3,2,1,0:T(8,128)(2,1)S(1)}, u32[]{:S(2)}, u32[]{:S(2)}) %collective-permute-start.7) | collective-permute-done | bytes 262176 | tf_op jit(solution)/shard_map/ppermute | solution.py:521
  94.2 1.4 %spread.7 = f32[4,8,16,1024]{3,2,1,0:T(8,128)} custom-call(s32[22]{0:T(128)S(1)} %pad_add_fusion.info, bf16[4,8,16,256]{3,2,1,0:T(8,128)(2,1)S(1)} %collective-permute-done.7.recv_ref, f32[4,8,16,1024]{3,2,1,0:T(8,128)} %spread.6.refs_0_), custom_call_target="tpu_custom_call", output_to_operand_aliasing={{}: (2, {})} | custom-call | flops 131072 | bytes 4 | tf_op jit(solution)/shard_map/spread/pallas_call | solution.py:440
  (1 shorter events, 0.0 us)
Async XLA Ops:
  0.6 14.6 %copy-start.6 = (s32[16]{0:T(128)S(1)}, s32[16]{0:T(128)}, u32[]{:S(2)}) copy-start(s32[16]{0:T(128)} %param.11) | copy-start | bytes 196
  0.6 14.6 %copy-start.7 = (s32[4]{0:T(128)S(1)}, s32[4]{0:T(128)}, u32[]{:S(2)}) copy-start(s32[4]{0:T(128)} %param.15) | copy-start | bytes 52
  0.7 18.9 %copy-start.3 = (f32[16,16]{1,0:T(8,128)S(1)}, f32[16,16]{1,0:T(8,128)}, u32[]{:S(2)}) copy-start(f32[16,16]{1,0:T(8,128)} %base_ref.1) | copy-start | bytes 3076
  0.7 18.9 %copy-start.4 = (f32[16,16]{1,0:T(8,128)S(1)}, f32[16,16]{1,0:T(8,128)}, u32[]{:S(2)}) copy-start(f32[16,16]{1,0:T(8,128)} %temp_ref.1) | copy-start | bytes 3076
  15.2 9.1 %copy-start.5 = (s32[640]{0:T(1024)S(1)}, s32[640]{0:T(1024)}, u32[]{:S(2)}) copy-start(s32[640]{0:T(1024)} %param.10) | copy-start | bytes 7684
  15.3 18.2 %all-to-all-start = ((bf16[8,8,16,512]{3,2,1,0:T(8,128)(2,1)}), bf16[8,8,16,512]{3,2,1,0:T(8,128)(2,1)S(1)}, u32[]{:S(2)}, u32[]{:S(2)}) async-start(bf16[8,8,16,512]{3,2,1,0:T(8,128)(2,1)} %legendre.1), calls=%async_computation | async-start | bytes 2097152 | tf_op jit(solution)/shard_map/all_to_all | solution.py:544
  29.0 2.3 %copy-start.1 = (bf16[16,1280,128]{2,1,0:T(8,128)(2,1)}, bf16[16,1280,128]{2,1,0:T(8,128)(2,1)S(1)}, u32[]{:S(2)}) copy-start(bf16[16,1280,128]{2,1,0:T(8,128)(2,1)S(1)} %get-tuple-element.52.table_ref) | copy-start | bytes 15728644
  33.5 17.4 %copy-start = (bf16[16,32,16,256]{3,2,1,0:T(8,128)(2,1)S(1)}, bf16[16,32,16,256]{3,2,1,0:T(8,128)(2,1)}, u32[]{:S(2)}) copy-start(bf16[16,32,16,256]{3,2,1,0:T(8,128)(2,1)} %refs_0_.7) | copy-start | bytes 12582916
  33.5 17.4 %collective-permute-start = (bf16[32,16,256]{2,1,0:T(8,128)(2,1)S(1)}, bf16[32,16,256]{2,1,0:T(8,128)(2,1)S(1)}, u32[]{:S(2)}, u32[]{:S(2)}) collective-permute-start(bf16[32,16,256]{2,1,0:T(8,128)(2,1)S(1)} %get-tuple-element.47), channel_id=1, source_target_pairs={{0,4},{4,0},{8,12},{12,8},{16,20},{20,16},{24,28},{28,24},{1,5},{5... | collective-permute-start | bytes 786440 | tf_op jit(solution)/shard_map/ppermute | solution.py:521
  33.6 17.3 %collective-permute-start.1 = (bf16[32,16,256]{2,1,0:T(8,128)(2,1)S(1)}, bf16[32,16,256]{2,1,0:T(8,128)(2,1)S(1)}, u32[]{:S(2)}, u32[]{:S(2)}) collective-permute-start(bf16[32,16,256]{2,1,0:T(8,128)(2,1)S(1)} %get-tuple-element.48), channel_id=1, source_target_pairs={{4,8},{8,4},{12,16},{16,12},{20,24},{24,20},{5,9},{9,5},{13,17},{1... | collective-permute-start | bytes 786440 | tf_op jit(solution)/shard_map/ppermute | solution.py:521
  37.0 13.8 %collective-permute-start.2 = (bf16[256,128]{1,0:T(8,128)(2,1)S(1)}, bf16[256,128]{1,0:T(8,128)(2,1)S(1)}, u32[]{:S(2)}, u32[]{:S(2)}) collective-permute-start(bf16[256,128]{1,0:T(8,128)(2,1)S(1)} %get-tuple-element.49), channel_id=1, source_target_pairs={{0,1},{1,0},{2,3},{3,2},{4,5},{5,4},{6,7},{7,6},{8,9},{9,8},{10,11... | collective-permute-start | bytes 196616 | tf_op jit(solution)/shard_map/ppermute | solution.py:521
  38.7 12.2 %collective-permute-start.3 = (bf16[256,128]{1,0:T(8,128)(2,1)S(1)}, bf16[256,128]{1,0:T(8,128)(2,1)S(1)}, u32[]{:S(2)}, u32[]{:S(2)}) collective-permute-start(bf16[256,128]{1,0:T(8,128)(2,1)S(1)} %get-tuple-element.50), channel_id=1, source_target_pairs={{1,2},{2,1},{5,6},{6,5},{9,10},{10,9},{13,14},{14,13},{17,18},{18,... | collective-permute-start | bytes 196616 | tf_op jit(solution)/shard_map/ppermute | solution.py:521
  39.3 2.5 %copy-start.2 = (bf16[16,1280,128]{2,1,0:T(8,128)(2,1)S(1)}, bf16[16,1280,128]{2,1,0:T(8,128)(2,1)}, u32[]{:S(2)}) copy-start(bf16[16,1280,128]{2,1,0:T(8,128)(2,1)} %copy-done.1) | copy-start | bytes 15728644
  46.9 18.1 %collective-permute-start.6 = (bf16[3,8,16,256]{3,2,1,0:T(8,128)(2,1)S(1)}, bf16[3,8,16,256]{3,2,1,0:T(8,128)(2,1)S(1)}, u32[]{:S(2)}, u32[]{:S(2)}) collective-permute-start(bf16[3,8,16,256]{3,2,1,0:T(8,128)(2,1)S(1)} %get-tuple-element.61), channel_id=1, source_target_pairs={{0,2},{2,0},{1,3},{3,1},{4,6},{6,4},{5,7},{7,5},{8,10},{10,8},{9,1... | collective-permute-start | bytes 589832 | tf_op jit(solution)/shard_map/ppermute | solution.py:521
  55.2 14.2 %collective-permute-start.5 = (bf16[3,8,16,256]{3,2,1,0:T(8,128)(2,1)S(1)}, bf16[3,8,16,256]{3,2,1,0:T(8,128)(2,1)S(1)}, u32[]{:S(2)}, u32[]{:S(2)}) collective-permute-start(bf16[3,8,16,256]{3,2,1,0:T(8,128)(2,1)S(1)} %get-tuple-element.60), channel_id=1, source_target_pairs={{0,3},{3,0},{1,2},{2,1},{4,7},{7,4},{5,6},{6,5},{8,11},{11,8},{9,1... | collective-permute-start | bytes 589832 | tf_op jit(solution)/shard_map/ppermute | solution.py:521
  58.2 15.6 %collective-permute-start.4 = (bf16[3,8,16,256]{3,2,1,0:T(8,128)(2,1)S(1)}, bf16[3,8,16,256]{3,2,1,0:T(8,128)(2,1)S(1)}, u32[]{:S(2)}, u32[]{:S(2)}) collective-permute-start(bf16[3,8,16,256]{3,2,1,0:T(8,128)(2,1)S(1)} %get-tuple-element.59), channel_id=1, source_target_pairs={{0,1},{1,0},{2,3},{3,2},{4,5},{5,4},{6,7},{7,6},{8,9},{9,8},{10,11... | collective-permute-start | bytes 589832 | tf_op jit(solution)/shard_map/ppermute | solution.py:521
  69.4 19.0 %collective-permute-start.9 = (bf16[4,8,16,256]{3,2,1,0:T(8,128)(2,1)S(1)}, bf16[4,8,16,256]{3,2,1,0:T(8,128)(2,1)S(1)}, u32[]{:S(2)}, u32[]{:S(2)}) collective-permute-start(bf16[4,8,16,256]{3,2,1,0:T(8,128)(2,1)S(1)} %get-tuple-element.68), channel_id=1, source_target_pairs={{0,2},{2,0},{1,3},{3,1},{4,6},{6,4},{5,7},{7,5},{8,10},{10,8},{9,1... | collective-permute-start | bytes 786440 | tf_op jit(solution)/shard_map/ppermute | solution.py:521
  78.1 11.7 %collective-permute-start.8 = (bf16[4,8,16,256]{3,2,1,0:T(8,128)(2,1)S(1)}, bf16[4,8,16,256]{3,2,1,0:T(8,128)(2,1)S(1)}, u32[]{:S(2)}, u32[]{:S(2)}) collective-permute-start(bf16[4,8,16,256]{3,2,1,0:T(8,128)(2,1)S(1)} %get-tuple-element.67), channel_id=1, source_target_pairs={{0,1},{1,0},{2,3},{3,2},{4,5},{5,4},{6,7},{7,6},{8,9},{9,8},{10,11... | collective-permute-start | bytes 786440 | tf_op jit(solution)/shard_map/ppermute | solution.py:521
  81.6 12.6 %collective-permute-start.7 = (bf16[4,8,16,256]{3,2,1,0:T(8,128)(2,1)S(1)}, bf16[4,8,16,256]{3,2,1,0:T(8,128)(2,1)S(1)}, u32[]{:S(2)}, u32[]{:S(2)}) collective-permute-start(bf16[4,8,16,256]{3,2,1,0:T(8,128)(2,1)S(1)} %get-tuple-element.66), channel_id=1, source_target_pairs={{0,3},{3,0},{1,2},{2,1},{4,7},{7,4},{5,6},{6,5},{8,11},{11,8},{9,1... | collective-permute-start | bytes 786440 | tf_op jit(solution)/shard_map/ppermute | solution.py:521

commit v10 on v9

--- a/solution.py
+++ b/solution.py
@@ -62,12 +62,10 @@
     return cosine, sine * y
 
 
-def table_kernel(first, info, waves_ref, table_ref, twiddle_ref):
-    size, turns = waves_ref.shape[1], twiddle_ref.shape[2]
-    waves = waves_ref[...].astype(F32)
+def make_tables(points, first, waves, table_ref, twiddle_ref):
+    size, turns = waves.shape[1], twiddle_ref.shape[2]
     for k in range(table_ref.shape[0]):
-        row = pl.program_id(0) * table_ref.shape[0] + k
-        count = jnp.full(waves.shape, info[first + row], jnp.int32).astype(F32)
+        count = jnp.full(waves.shape, points[first + k], jnp.int32).astype(F32)
         cos_low, sin_low = unit_circle(1, LOW, waves, count)
         cos_high, sin_high = unit_circle(LOW, LANES // LOW, waves, count)
         cosine, sine = [], []
@@ -80,30 +78,6 @@
         cos_turn, sin_turn = unit_circle(LANES, turns, waves, count)
         twiddle_ref[k, 0] = cos_turn
         twiddle_ref[k, 1] = sin_turn
-
-
-def tables(info, wave_ids, rows, turns):
-    waves = wave_ids.shape[0]
-    each = STEP if rows % STEP == 0 else 1
-    return pl.pallas_call(
-        functools.partial(table_kernel, info.shape[0] - rows),
-        grid_spec=pltpu.PrefetchScalarGridSpec(
-            num_scalar_prefetch=1,
-            grid=(rows // each,),
-            in_specs=[pl.BlockSpec((1, waves), lambda j, p: (0, 0))],
-            out_specs=[
-                pl.BlockSpec((each, 2 * waves, LANES), lambda j, p: (j, 0, 0)),
-                pl.BlockSpec((each, 2, turns, waves), lambda j, p: (j, 0, 0, 0)),
-            ],
-        ),
-        out_shape=[
-            pltpu.VMEM((rows, 2 * waves, LANES), BF16),
-            pltpu.VMEM((rows, 2, turns, waves), F32),
-        ],
-        compiler_params=pltpu.CompilerParams(vmem_limit_bytes=20 * MIB),
-        cost_estimate=cost(rows * waves * LANES * 8, rows * waves * LANES * 4),
-        name="tables",
-    )(info, wave_ids[None, :])
 
 
 def place(pieces, width):
@@ -206,7 +180,7 @@
         compiler_params=pltpu.CompilerParams(vmem_limit_bytes=24 * MIB),
         cost_estimate=cost(4 * rows * waves * fields * levels * turns * LANES, 4 * rows * waves * LANES),
         name="synthesis",
-    )(info, recv, *[pltpu.with_memory_space_constraint(v, pltpu.VMEM) for v in (table, twiddle)])
+    )(info, recv, table, twiddle)
 
 
 def edge_kernel(
@@ -453,7 +427,8 @@
     )(info, *operands)
 
 
-def legendre_kernel(spectral_ref, legendre_ref, out_ref, rows_of, sums):
+def legendre_kernel(points, waves_ref, spectral_ref, legendre_ref, *refs):
+    out_ref, table_ref, twiddle_ref, rows_of, sums = refs
     parts, own, block, size = spectral_ref.shape
     bands, _, rows, pitch = out_ref.shape
     share = block * pl.num_programs(0)
@@ -467,6 +442,10 @@
             for l in range(own):
                 tail = pl.ds(l * stretch + parts * share, pitch - parts * share)
                 sums[h, tail, :] = jnp.zeros((pitch - parts * share, LANES), F32)
+
+    each = table_ref.shape[0]
+    first = jnp.minimum(step, points.shape[0] // each - 1) * each
+    make_tables(points, first, waves_ref[...].astype(F32), table_ref, twiddle_ref)
 
     for v in range(size // LANES):
         part = spectral_ref[:, :, :, v * LANES : (v + 1) * LANES].astype(F32)
@@ -492,29 +471,48 @@
                 out_ref[h * some : (h + 1) * some, l] = turned.reshape(some, rows, pitch)
 
 
-def legendre_sums(spectral, legendre, bands):
+def legendre_sums(spectral, legendre, points, wave_ids, bands, turns):
     parts, own, share, size = spectral.shape
+    waves, count = wave_ids.shape[0], points.shape[0]
     rows = legendre.shape[2] // bands
     pitch = -(-parts * share // LANES) * LANES
     block = 16 if share % 16 == 0 else 8
+    steps = share // block
+    each = min(e for e in range(1, count + 1) if count % e == 0 and e * steps >= count)
     shape = (bands, own, rows, pitch)
+
+    def of_rows(i, points):
+        return jnp.minimum(i, count // each - 1)
+
     return pl.pallas_call(
         legendre_kernel,
-        grid=(share // block,),
-        in_specs=[
-            pl.BlockSpec((parts, own, block, size), lambda i: (0, 0, i, 0)),
-            pl.BlockSpec((block,) + legendre.shape[1:], lambda i: (i, 0, 0)),
-        ],
-        out_specs=pl.BlockSpec(shape, lambda i: (0, 0, 0, 0)),
-        out_shape=jax.ShapeDtypeStruct(shape, BF16),
-        scratch_shapes=[
-            pltpu.VMEM((size // LANES, parts * own * (block + 1), LANES), F32),
-            pltpu.VMEM((legendre.shape[2] // LANES, own * (pitch + 1), LANES), F32),
+        grid_spec=pltpu.PrefetchScalarGridSpec(
+            num_scalar_prefetch=1,
+            grid=(steps,),
+            in_specs=[
+                pl.BlockSpec((1, waves), lambda i, points: (0, 0)),
+                pl.BlockSpec((parts, own, block, size), lambda i, points: (0, 0, i, 0)),
+                pl.BlockSpec((block,) + legendre.shape[1:], lambda i, points: (i, 0, 0)),
+            ],
+            out_specs=[
+                pl.BlockSpec(shape, lambda i, points: (0, 0, 0, 0)),
+                pl.BlockSpec((each, 2 * waves, LANES), lambda i, p: (of_rows(i, p), 0, 0)),
+                pl.BlockSpec((each, 2, turns, waves), lambda i, p: (of_rows(i, p), 0, 0, 0)),
+            ],
+            scratch_shapes=[
+                pltpu.VMEM((size // LANES, parts * own * (block + 1), LANES), F32),
+                pltpu.VMEM((legendre.shape[2] // LANES, own * (pitch + 1), LANES), F32),
+            ],
+        ),
+        out_shape=[
+            jax.ShapeDtypeStruct(shape, BF16),
+            jax.ShapeDtypeStruct((count, 2 * waves, LANES), BF16),
+            jax.ShapeDtypeStruct((count, 2, turns, waves), F32),
         ],
         compiler_params=pltpu.CompilerParams(vmem_limit_bytes=56 * MIB),
         cost_estimate=cost(2 * parts * own * legendre.size, 2 * (spectral.size + legendre.size)),
         name="legendre",
-    )(spectral, legendre)
+    )(points, wave_ids[None, :], spectral, legendre)
 
 
 def exchange(value, axis, pairs):
@@ -533,27 +531,23 @@
 def body(spectral, legendre, wave_ids, points, tracers, react_base, react_temp, active_ids):
     bands, tiles = lax.axis_size("lat"), lax.axis_size("lon")
     tile = tracers.shape[3]
-    waves = wave_ids.shape[0]
+    waves, rows = wave_ids.shape[0], points.shape[0]
     band, me = lax.axis_index("lat"), lax.axis_index("lon")
 
-    sent = legendre_sums(spectral, legendre, bands)
-
-    rows = points.shape[0]
+    sent, table, twiddle = legendre_sums(
+        spectral, legendre, points, wave_ids, bands, tiles * tile // LANES
+    )
     info = jnp.concatenate([jnp.stack([band, me]), active_ids, points]).astype(jnp.int32)
     sent, info = lax.optimization_barrier((sent, info))
     recv = lax.all_to_all(sent, "lat", split_axis=0, concat_axis=0, tiled=True)
     *ends, react = edges(tracers, react_base, react_temp, info)
-    react, wave_ids = lax.optimization_barrier((react, wave_ids))
-    table, twiddle = tables(info, wave_ids, rows, tiles * tile // LANES)
-    recv, table, twiddle, react, ends = lax.optimization_barrier(
-        (recv, table, twiddle, react, ends)
-    )
-    halos = (
+    halos = [
         exchange(ends[0], "lat", neighbours("lat", 0)),
         exchange(ends[1], "lat", neighbours("lat", 1)),
         exchange(ends[2], "lon", neighbours("lon", 0)),
         exchange(ends[3], "lon", neighbours("lon", 1)),
-    )
+    ]
+    recv, react, halos = lax.optimization_barrier((recv, react, halos))
     grids = synthesis(recv, table, twiddle, info, tiles, tile)
 
     middle, inner = list(range(tiles // 2, tiles)), list(range(1, tiles // 2))

time: 95.8 us -> 104 us (1.086)
  waiting for transfers between devices: 12.1 us -> 20.6 us
    ppermute x10, waiting for transfers between devices: 9.92 us -> 20.6 us  [exchange(): lax.ppermute(value, axis, [p for a, b in pairs for p in ((a, b), (b, a))])]
    unnamed x16 -> x14, local copies, waits for them, and re-layouts: 4.84 us -> 2.66 us
    all_to_all x1, waiting for transfers between devices: 2.16 us -> 0.01 us  [body(): recv = lax.all_to_all(sent, 'lat', split_axis=0, concat_axis=0, tiled=True)]
    broadcast_in_dim x1, local copies, waits for them, and re-layouts: 0.01 us -> 1.28 us  [legendre_sums(): wave_ids[None, :]]
    pallas_call x2 -> x1, Pallas kernels: 19.2 us -> 19 us  [legendre_sums(): pl.pallas_call(legendre_kernel, grid_spec=pltpu.PrefetchScalarGridSpec(nu...]
  transfers between devices with their start and end apart: 11 -> 11, of which waited for: 3 -> 6; matrix products, arithmetic and copies ran while one was open for 0% -> 0% of each run, Pallas kernels for 38% -> 25%
where the time goes in v10:
time: 104 us
  Pallas kernels  51.8 us (50%)
  starting transfers between devices  26.8 us (26%)
  waiting for transfers between devices  20.6 us (20%)
  local copies, waits for them, and re-layouts  3.93 us (4%)
    ppermute x10, starting transfers between devices, exchange(): lax.ppermute(value, axis, [p for a, b in pairs for p in ((a, b), (b, a))])  22.4 us
    ppermute x10, waiting for transfers between devices, exchange(): lax.ppermute(value, axis, [p for a, b in pairs for p in ((a, b), (b, a))])  20.6 us
    pallas_call x1, Pallas kernels, legendre_sums(): pl.pallas_call(legendre_kernel, grid_spec=pltpu.PrefetchScalarGridSpec(nu...  19 us
    pallas_call x4, Pallas kernels, chemistry(): pl.pallas_call(functools.partial(chem_kernel, scale, k), grid_spec=pltpu....  17.4 us
    pallas_call x4, Pallas kernels, spread(): pl.pallas_call(spread_kernel, grid_spec=pltpu.PrefetchScalarGridSpec(num_...  5.49 us
    pallas_call x1, Pallas kernels, synthesis(): pl.pallas_call(synth_kernel, grid_spec=pltpu.PrefetchScalarGridSpec(num_s...  5.12 us
    pallas_call x1, Pallas kernels, edges(): pl.pallas_call(edge_kernel, grid_spec=pltpu.PrefetchScalarGridSpec(num_sc...  4.76 us
    all_to_all x1, starting transfers between devices, body(): recv = lax.all_to_all(sent, 'lat', split_axis=0, concat_axis=0, tiled=True)  4.39 us
  transfers between devices with their start and end apart: 11, of which 6 were waited for; matrix products, arithmetic and copies ran while one was open for 0% of the time, Pallas kernels for 25%

profile of v10, /device:TPU:2, one launch (start us, length us, event | category | flops | bytes accessed | tf_op | source)
XLA Modules:
  0.0 103.9 jit_solution(11987761737728640720)
XLA Ops:
  0.6 1.3 %broadcast_in_dim.3.waves_ref = s32[1,640]{1,0:T(1,128)} reshape(s32[640]{0:T(1024)} %param.10) | data formatting | bytes 5120 | tf_op jit(solution)/shard_map/broadcast_in_dim | solution.py:515
  1.9 0.0 copy-start.5
  1.9 0.0 copy-start.6
  1.9 0.0 copy-start.3
  1.9 0.0 copy-start.4
  1.9 19.0 %legendre.1 = (bf16[8,8,16,512]{3,2,1,0:T(8,128)(2,1)}, bf16[16,1280,128]{2,1,0:T(8,128)(2,1)}, f32[16,2,8,640]{3,2,1,0:T(8,128)}) custom-call(s32[16]{0:T(128)} %points.1, s32[1,640]{1,0:T(1,128)} %broadcast_in_dim.3.waves_ref, bf16[6,8,80,1280]{3,2,1,0:T(8,128)(2,1)} %spectral_ref.1, bf16[80,1280,128]{2,1,0:T(8,128)(2,1)} %legendre_ref.1), custom_call_target="tpu_custom_call" | custom-call | flops 1258291200 | bytes 36044800 | tf_op jit(solution)/shard_map/legendre/pallas_call | solution.py:487
  20.9 0.0 copy-start.2
  20.9 0.0 copy-done.5
  20.9 0.0 copy-done.6
  20.9 0.1 pad_add_fusion.info
  21.0 4.4 %all-to-all-start = ((bf16[8,8,16,512]{3,2,1,0:T(8,128)(2,1)}), bf16[8,8,16,512]{3,2,1,0:T(8,128)(2,1)S(1)}, u32[]{:S(2)}, u32[]{:S(2)}) async-start(bf16[8,8,16,512]{3,2,1,0:T(8,128)(2,1)} %get-tuple-element.35), calls=%async_computation | async-start | bytes 2097152 | tf_op jit(solution)/shard_map/all_to_all | solution.py:542
  25.4 0.0 copy-done.3
  25.4 0.0 copy-done.4
  25.4 4.8 %edges.1 = (bf16[32,16,256]{2,1,0:T(8,128)(2,1)S(1)}, bf16[32,16,256]{2,1,0:T(8,128)(2,1)S(1)}, bf16[256,128]{1,0:T(8,128)(2,1)S(1)}, bf16[256,128]{1,0:T(8,128)(2,1)S(1)}, bf16[512,512]{1,0:T(8,128)(2,1)S(1)}) custom-call(s32[22]{0:T(128)S(1)} %pad_add_fusion.info, bf16[16,32,16,256]{3,2,1,0:T(8,128)(2,1)} %refs_0_.7, f32[16,16]{1,0:T(8,128)S(1)} %copy-done.3, ...), custom_call_target="tpu_custom_call" | custom-call | flops 268435456 | bytes 4194304 | tf_op jit(solution)/shard_map/edges/pallas_call | solution.py:253
  30.2 0.2 collective-permute-start
  30.4 1.9 %collective-permute-start.1 = (bf16[32,16,256]{2,1,0:T(8,128)(2,1)S(1)}, bf16[32,16,256]{2,1,0:T(8,128)(2,1)S(1)}, u32[]{:S(2)}, u32[]{:S(2)}) collective-permute-start(bf16[32,16,256]{2,1,0:T(8,128)(2,1)S(1)} %get-tuple-element.38), channel_id=1, source_target_pairs={{4,8},{8,4},{12,16},{16,12},{20,24},{24,20},{5,9},{9,5},{13,17},{1... | collective-permute-start | bytes 786440 | tf_op jit(solution)/shard_map/ppermute | solution.py:519
  32.3 1.6 %collective-permute-start.2 = (bf16[256,128]{1,0:T(8,128)(2,1)S(1)}, bf16[256,128]{1,0:T(8,128)(2,1)S(1)}, u32[]{:S(2)}, u32[]{:S(2)}) collective-permute-start(bf16[256,128]{1,0:T(8,128)(2,1)S(1)} %get-tuple-element.39), channel_id=1, source_target_pairs={{0,1},{1,0},{2,3},{3,2},{4,5},{5,4},{6,7},{7,6},{8,9},{9,8},{10,11... | collective-permute-start | bytes 196616 | tf_op jit(solution)/shard_map/ppermute | solution.py:519
  34.0 0.7 collective-permute-start.3
  34.6 2.2 %collective-permute-done.2.refs_3_ = bf16[256,128]{1,0:T(8,128)(2,1)S(1)} collective-permute-done((bf16[256,128]{1,0:T(8,128)(2,1)S(1)}, bf16[256,128]{1,0:T(8,128)(2,1)S(1)}, u32[]{:S(2)}, u32[]{:S(2)}) %collective-permute-start.2) | collective-permute-done | bytes 65568 | tf_op jit(solution)/shard_map/ppermute | solution.py:519
  36.8 0.0 collective-permute-done.3.refs_4_
  36.8 0.0 collective-permute-done.refs_1_
  36.8 6.2 %collective-permute-done.1.refs_2_ = bf16[32,16,256]{2,1,0:T(8,128)(2,1)S(1)} collective-permute-done((bf16[32,16,256]{2,1,0:T(8,128)(2,1)S(1)}, bf16[32,16,256]{2,1,0:T(8,128)(2,1)S(1)}, u32[]{:S(2)}, u32[]{:S(2)}) %collective-permute-start.1) | collective-permute-done | bytes 262176 | tf_op jit(solution)/shard_map/ppermute | solution.py:519
  43.1 0.0 all-to-all-done.recv_ref
  43.1 0.0 copy-start
  43.1 0.0 copy-done.2
  43.1 0.0 copy-start.1
  43.1 2.6 %copy-done.1 = bf16[16,1280,128]{2,1,0:T(8,128)(2,1)S(1)} copy-done((bf16[16,1280,128]{2,1,0:T(8,128)(2,1)S(1)}, bf16[16,1280,128]{2,1,0:T(8,128)(2,1)}, u32[]{:S(2)}) %copy-start.1) | copy-done | bytes 5242904
  45.7 5.1 %synthesis.1 = (bf16[3,8,16,256]{3,2,1,0:T(8,128)(2,1)S(1)}, bf16[3,8,16,256]{3,2,1,0:T(8,128)(2,1)S(1)}, bf16[3,8,16,256]{3,2,1,0:T(8,128)(2,1)S(1)}, bf16[3,8,16,256]{3,2,1,0:T(8,128)(2,1)S(1)}) custom-call(s32[22]{0:T(128)S(1)} %pad_add_fusion.info, bf16[8,8,16,512]{3,2,1,0:T(8,128)(2,1)S(1)} %all-to-all-done.recv_ref, ...), custom_call_target="tpu_custom_call" | custom-call | flops 1006632960 | bytes 5242880 | tf_op jit(solution)/shard_map/synthesis/pallas_call | solution.py:163
  50.8 2.7 %collective-permute-start.6 = (bf16[3,8,16,256]{3,2,1,0:T(8,128)(2,1)S(1)}, bf16[3,8,16,256]{3,2,1,0:T(8,128)(2,1)S(1)}, u32[]{:S(2)}, u32[]{:S(2)}) collective-permute-start(bf16[3,8,16,256]{3,2,1,0:T(8,128)(2,1)S(1)} %get-tuple-element.55), channel_id=1, source_target_pairs={{0,2},{2,0},{1,3},{3,1},{4,6},{6,4},{5,7},{7,5},{8,10},{10,8},{9,1... | collective-permute-start | bytes 589832 | tf_op jit(solution)/shard_map/ppermute | solution.py:519
  53.5 0.0 copy-done
  53.5 4.4 %chemistry.4 = (bf16[16,32,16,256]{3,2,1,0:T(8,128)(2,1)}, bf16[4,8,16,256]{3,2,1,0:T(8,128)(2,1)S(1)}) custom-call(s32[22]{0:T(128)S(1)} %pad_add_fusion.info, bf16[16,32,16,256]{3,2,1,0:T(8,128)(2,1)S(1)} %copy-done, bf16[32,16,256]{2,1,0:T(8,128)(2,1)S(1)} %collective-permute-done.refs_1_, bf16[32,16,256]{2,1,0:T(8,128)(2,1)S(1)} %collective-permute-done.1.refs_2_, ...), custom_call_target="tpu_custom_call" | custom-call | flops 524288 | bytes 2048 | tf_op jit(solution)/shard_map/chemistry/pallas_call | solution.py:372
  57.8 1.3 %collective-permute-start.5 = (bf16[3,8,16,256]{3,2,1,0:T(8,128)(2,1)S(1)}, bf16[3,8,16,256]{3,2,1,0:T(8,128)(2,1)S(1)}, u32[]{:S(2)}, u32[]{:S(2)}) collective-permute-start(bf16[3,8,16,256]{3,2,1,0:T(8,128)(2,1)S(1)} %get-tuple-element.54), channel_id=1, source_target_pairs={{0,3},{3,0},{1,2},{2,1},{4,7},{7,4},{5,6},{6,5},{8,11},{11,8},{9,1... | collective-permute-start | bytes 589832 | tf_op jit(solution)/shard_map/ppermute | solution.py:519
  59.2 0.2 collective-permute-start.4
  59.4 3.6 %collective-permute-done.6.refs_5_ = bf16[3,8,16,256]{3,2,1,0:T(8,128)(2,1)S(1)} collective-permute-done((bf16[3,8,16,256]{3,2,1,0:T(8,128)(2,1)S(1)}, bf16[3,8,16,256]{3,2,1,0:T(8,128)(2,1)S(1)}, u32[]{:S(2)}, u32[]{:S(2)}) %collective-permute-start.6) | collective-permute-done | bytes 196640 | tf_op jit(solution)/shard_map/ppermute | solution.py:519
  63.0 4.4 %chemistry.5 = (bf16[16,32,16,256]{3,2,1,0:T(8,128)(2,1)}, bf16[4,8,16,256]{3,2,1,0:T(8,128)(2,1)S(1)}) custom-call(s32[22]{0:T(128)S(1)} %pad_add_fusion.info, bf16[16,32,16,256]{3,2,1,0:T(8,128)(2,1)S(1)} %copy-done, bf16[32,16,256]{2,1,0:T(8,128)(2,1)S(1)} %collective-permute-done.refs_1_, ...), custom_call_target="tpu_custom_call", output_to_operand_aliasing={{0}: (8, {})} | custom-call | flops 524288 | bytes 2048 | tf_op jit(solution)/shard_map/chemistry/pallas_call | solution.py:372
  67.4 0.0 collective-permute-start.9
  67.4 0.0 collective-permute-done.5.refs_5_
  67.4 4.4 %chemistry.6 = (bf16[16,32,16,256]{3,2,1,0:T(8,128)(2,1)}, bf16[4,8,16,256]{3,2,1,0:T(8,128)(2,1)S(1)}) custom-call(s32[22]{0:T(128)S(1)} %pad_add_fusion.info, bf16[16,32,16,256]{3,2,1,0:T(8,128)(2,1)S(1)} %copy-done, bf16[32,16,256]{2,1,0:T(8,128)(2,1)S(1)} %collective-permute-done.refs_1_, ...), custom_call_target="tpu_custom_call", output_to_operand_aliasing={{0}: (8, {})} | custom-call | flops 524288 | bytes 2048 | tf_op jit(solution)/shard_map/chemistry/pallas_call | solution.py:372
  71.7 0.7 collective-permute-done.4.refs_5_
  72.5 4.4 %chemistry.7 = (bf16[16,32,16,256]{3,2,1,0:T(8,128)(2,1)}, bf16[4,8,16,256]{3,2,1,0:T(8,128)(2,1)S(1)}) custom-call(s32[22]{0:T(128)S(1)} %pad_add_fusion.info, bf16[16,32,16,256]{3,2,1,0:T(8,128)(2,1)S(1)} %copy-done, bf16[32,16,256]{2,1,0:T(8,128)(2,1)S(1)} %collective-permute-done.refs_1_, ...), custom_call_target="tpu_custom_call", output_to_operand_aliasing={{0}: (8, {})} | custom-call | flops 524288 | bytes 2048 | tf_op jit(solution)/shard_map/chemistry/pallas_call | solution.py:372
  76.8 10.2 %collective-permute-start.8 = (bf16[4,8,16,256]{3,2,1,0:T(8,128)(2,1)S(1)}, bf16[4,8,16,256]{3,2,1,0:T(8,128)(2,1)S(1)}, u32[]{:S(2)}, u32[]{:S(2)}) collective-permute-start(bf16[4,8,16,256]{3,2,1,0:T(8,128)(2,1)S(1)} %get-tuple-element.61), channel_id=1, source_target_pairs={{0,1},{1,0},{2,3},{3,2},{4,5},{5,4},{6,7},{7,6},{8,9},{9,8},{10,11... | collective-permute-start | bytes 786440 | tf_op jit(solution)/shard_map/ppermute | solution.py:519
  87.0 3.5 %collective-permute-start.7 = (bf16[4,8,16,256]{3,2,1,0:T(8,128)(2,1)S(1)}, bf16[4,8,16,256]{3,2,1,0:T(8,128)(2,1)S(1)}, u32[]{:S(2)}, u32[]{:S(2)}) collective-permute-start(bf16[4,8,16,256]{3,2,1,0:T(8,128)(2,1)S(1)} %get-tuple-element.60), channel_id=1, source_target_pairs={{0,3},{3,0},{1,2},{2,1},{4,7},{7,4},{5,6},{6,5},{8,11},{11,8},{9,1... | collective-permute-start | bytes 786440 | tf_op jit(solution)/shard_map/ppermute | solution.py:519
  90.6 1.4 %spread.4.refs_0_ = f32[4,8,16,1024]{3,2,1,0:T(8,128)} custom-call(s32[22]{0:T(128)S(1)} %pad_add_fusion.info, bf16[4,8,16,256]{3,2,1,0:T(8,128)(2,1)S(1)} %get-tuple-element.63.recv_ref), custom_call_target="tpu_custom_call" | custom-call | flops 131072 | bytes 4 | tf_op jit(solution)/shard_map/spread/pallas_call | solution.py:414
  91.9 0.0 collective-permute-done.9.recv_ref
  91.9 1.4 %spread.5.refs_0_ = f32[4,8,16,1024]{3,2,1,0:T(8,128)} custom-call(s32[22]{0:T(128)S(1)} %pad_add_fusion.info, bf16[4,8,16,256]{3,2,1,0:T(8,128)(2,1)S(1)} %collective-permute-done.9.recv_ref, f32[4,8,16,1024]{3,2,1,0:T(8,128)} %spread.4.refs_0_), custom_call_target="tpu_custom_call", output_to_operand_aliasing={{}: (2, {})} | custom-call | flops 131072 | bytes 4 | tf_op jit(solution)/shard_map/spread/pallas_call | solution.py:414
  93.3 0.6 collective-permute-done.8.recv_ref
  93.9 1.4 %spread.6.refs_0_ = f32[4,8,16,1024]{3,2,1,0:T(8,128)} custom-call(s32[22]{0:T(128)S(1)} %pad_add_fusion.info, bf16[4,8,16,256]{3,2,1,0:T(8,128)(2,1)S(1)} %collective-permute-done.8.recv_ref, f32[4,8,16,1024]{3,2,1,0:T(8,128)} %spread.5.refs_0_), custom_call_target="tpu_custom_call", output_to_operand_aliasing={{}: (2, {})} | custom-call | flops 131072 | bytes 4 | tf_op jit(solution)/shard_map/spread/pallas_call | solution.py:414
  95.3 7.2 %collective-permute-done.7.recv_ref = bf16[4,8,16,256]{3,2,1,0:T(8,128)(2,1)S(1)} collective-permute-done((bf16[4,8,16,256]{3,2,1,0:T(8,128)(2,1)S(1)}, bf16[4,8,16,256]{3,2,1,0:T(8,128)(2,1)S(1)}, u32[]{:S(2)}, u32[]{:S(2)}) %collective-permute-start.7) | collective-permute-done | bytes 262176 | tf_op jit(solution)/shard_map/ppermute | solution.py:519
  102.5 1.4 %spread.7 = f32[4,8,16,1024]{3,2,1,0:T(8,128)} custom-call(s32[22]{0:T(128)S(1)} %pad_add_fusion.info, bf16[4,8,16,256]{3,2,1,0:T(8,128)(2,1)S(1)} %collective-permute-done.7.recv_ref, f32[4,8,16,1024]{3,2,1,0:T(8,128)} %spread.6.refs_0_), custom_call_target="tpu_custom_call", output_to_operand_aliasing={{}: (2, {})} | custom-call | flops 131072 | bytes 4 | tf_op jit(solution)/shard_map/spread/pallas_call | solution.py:414
Async XLA Ops:
  1.9 19.0 %copy-start.5 = (s32[16]{0:T(128)S(1)}, s32[16]{0:T(128)}, u32[]{:S(2)}) copy-start(s32[16]{0:T(128)} %points.1) | copy-start | bytes 196
  1.9 19.0 %copy-start.6 = (s32[4]{0:T(128)S(1)}, s32[4]{0:T(128)}, u32[]{:S(2)}) copy-start(s32[4]{0:T(128)} %param.15) | copy-start | bytes 52
  1.9 23.5 %copy-start.3 = (f32[16,16]{1,0:T(8,128)S(1)}, f32[16,16]{1,0:T(8,128)}, u32[]{:S(2)}) copy-start(f32[16,16]{1,0:T(8,128)} %base_ref.1) | copy-start | bytes 3076
  1.9 23.5 %copy-start.4 = (f32[16,16]{1,0:T(8,128)S(1)}, f32[16,16]{1,0:T(8,128)}, u32[]{:S(2)}) copy-start(f32[16,16]{1,0:T(8,128)} %temp_ref.1) | copy-start | bytes 3076
  20.9 22.1 %copy-start.2 = (f32[16,2,8,640]{3,2,1,0:T(8,128)S(1)}, f32[16,2,8,640]{3,2,1,0:T(8,128)}, u32[]{:S(2)}) copy-start(f32[16,2,8,640]{3,2,1,0:T(8,128)} %get-tuple-element.47.twiddle_ref) | copy-start | bytes 1966084
  21.0 22.0 %all-to-all-start = ((bf16[8,8,16,512]{3,2,1,0:T(8,128)(2,1)}), bf16[8,8,16,512]{3,2,1,0:T(8,128)(2,1)S(1)}, u32[]{:S(2)}, u32[]{:S(2)}) async-start(bf16[8,8,16,512]{3,2,1,0:T(8,128)(2,1)} %get-tuple-element.35), calls=%async_computation | async-start | bytes 2097152 | tf_op jit(solution)/shard_map/all_to_all | solution.py:542
  30.2 6.6 %collective-permute-start = (bf16[32,16,256]{2,1,0:T(8,128)(2,1)S(1)}, bf16[32,16,256]{2,1,0:T(8,128)(2,1)S(1)}, u32[]{:S(2)}, u32[]{:S(2)}) collective-permute-start(bf16[32,16,256]{2,1,0:T(8,128)(2,1)S(1)} %get-tuple-element.37), channel_id=1, source_target_pairs={{0,4},{4,0},{8,12},{12,8},{16,20},{20,16},{24,28},{28,24},{1,5},{5... | collective-permute-start | bytes 786440 | tf_op jit(solution)/shard_map/ppermute | solution.py:519
  30.4 12.7 %collective-permute-start.1 = (bf16[32,16,256]{2,1,0:T(8,128)(2,1)S(1)}, bf16[32,16,256]{2,1,0:T(8,128)(2,1)S(1)}, u32[]{:S(2)}, u32[]{:S(2)}) collective-permute-start(bf16[32,16,256]{2,1,0:T(8,128)(2,1)S(1)} %get-tuple-element.38), channel_id=1, source_target_pairs={{4,8},{8,4},{12,16},{16,12},{20,24},{24,20},{5,9},{9,5},{13,17},{1... | collective-permute-start | bytes 786440 | tf_op jit(solution)/shard_map/ppermute | solution.py:519
  32.3 4.5 %collective-permute-start.2 = (bf16[256,128]{1,0:T(8,128)(2,1)S(1)}, bf16[256,128]{1,0:T(8,128)(2,1)S(1)}, u32[]{:S(2)}, u32[]{:S(2)}) collective-permute-start(bf16[256,128]{1,0:T(8,128)(2,1)S(1)} %get-tuple-element.39), channel_id=1, source_target_pairs={{0,1},{1,0},{2,3},{3,2},{4,5},{5,4},{6,7},{7,6},{8,9},{9,8},{10,11... | collective-permute-start | bytes 196616 | tf_op jit(solution)/shard_map/ppermute | solution.py:519
  34.0 2.9 %collective-permute-start.3 = (bf16[256,128]{1,0:T(8,128)(2,1)S(1)}, bf16[256,128]{1,0:T(8,128)(2,1)S(1)}, u32[]{:S(2)}, u32[]{:S(2)}) collective-permute-start(bf16[256,128]{1,0:T(8,128)(2,1)S(1)} %get-tuple-element.40), channel_id=1, source_target_pairs={{1,2},{2,1},{5,6},{6,5},{9,10},{10,9},{13,14},{14,13},{17,18},{18,... | collective-permute-start | bytes 196616 | tf_op jit(solution)/shard_map/ppermute | solution.py:519
  43.1 10.4 %copy-start = (bf16[16,32,16,256]{3,2,1,0:T(8,128)(2,1)S(1)}, bf16[16,32,16,256]{3,2,1,0:T(8,128)(2,1)}, u32[]{:S(2)}) copy-start(bf16[16,32,16,256]{3,2,1,0:T(8,128)(2,1)} %refs_0_.7) | copy-start | bytes 12582916
  43.1 2.6 %copy-start.1 = (bf16[16,1280,128]{2,1,0:T(8,128)(2,1)S(1)}, bf16[16,1280,128]{2,1,0:T(8,128)(2,1)}, u32[]{:S(2)}) copy-start(bf16[16,1280,128]{2,1,0:T(8,128)(2,1)} %get-tuple-element.46.table_ref) | copy-start | bytes 15728644
  50.8 12.2 %collective-permute-start.6 = (bf16[3,8,16,256]{3,2,1,0:T(8,128)(2,1)S(1)}, bf16[3,8,16,256]{3,2,1,0:T(8,128)(2,1)S(1)}, u32[]{:S(2)}, u32[]{:S(2)}) collective-permute-start(bf16[3,8,16,256]{3,2,1,0:T(8,128)(2,1)S(1)} %get-tuple-element.55), channel_id=1, source_target_pairs={{0,2},{2,0},{1,3},{3,1},{4,6},{6,4},{5,7},{7,5},{8,10},{10,8},{9,1... | collective-permute-start | bytes 589832 | tf_op jit(solution)/shard_map/ppermute | solution.py:519
  57.8 9.5 %collective-permute-start.5 = (bf16[3,8,16,256]{3,2,1,0:T(8,128)(2,1)S(1)}, bf16[3,8,16,256]{3,2,1,0:T(8,128)(2,1)S(1)}, u32[]{:S(2)}, u32[]{:S(2)}) collective-permute-start(bf16[3,8,16,256]{3,2,1,0:T(8,128)(2,1)S(1)} %get-tuple-element.54), channel_id=1, source_target_pairs={{0,3},{3,0},{1,2},{2,1},{4,7},{7,4},{5,6},{6,5},{8,11},{11,8},{9,1... | collective-permute-start | bytes 589832 | tf_op jit(solution)/shard_map/ppermute | solution.py:519
  59.2 13.3 %collective-permute-start.4 = (bf16[3,8,16,256]{3,2,1,0:T(8,128)(2,1)S(1)}, bf16[3,8,16,256]{3,2,1,0:T(8,128)(2,1)S(1)}, u32[]{:S(2)}, u32[]{:S(2)}) collective-permute-start(bf16[3,8,16,256]{3,2,1,0:T(8,128)(2,1)S(1)} %get-tuple-element.53), channel_id=1, source_target_pairs={{0,1},{1,0},{2,3},{3,2},{4,5},{5,4},{6,7},{7,6},{8,9},{9,8},{10,11... | collective-permute-start | bytes 589832 | tf_op jit(solution)/shard_map/ppermute | solution.py:519
  67.4 24.6 %collective-permute-start.9 = (bf16[4,8,16,256]{3,2,1,0:T(8,128)(2,1)S(1)}, bf16[4,8,16,256]{3,2,1,0:T(8,128)(2,1)S(1)}, u32[]{:S(2)}, u32[]{:S(2)}) collective-permute-start(bf16[4,8,16,256]{3,2,1,0:T(8,128)(2,1)S(1)} %get-tuple-element.62), channel_id=1, source_target_pairs={{0,2},{2,0},{1,3},{3,1},{4,6},{6,4},{5,7},{7,5},{8,10},{10,8},{9,1... | collective-permute-start | bytes 786440 | tf_op jit(solution)/shard_map/ppermute | solution.py:519
  76.8 17.1 %collective-permute-start.8 = (bf16[4,8,16,256]{3,2,1,0:T(8,128)(2,1)S(1)}, bf16[4,8,16,256]{3,2,1,0:T(8,128)(2,1)S(1)}, u32[]{:S(2)}, u32[]{:S(2)}) collective-permute-start(bf16[4,8,16,256]{3,2,1,0:T(8,128)(2,1)S(1)} %get-tuple-element.61), channel_id=1, source_target_pairs={{0,1},{1,0},{2,3},{3,2},{4,5},{5,4},{6,7},{7,6},{8,9},{9,8},{10,11... | collective-permute-start | bytes 786440 | tf_op jit(solution)/shard_map/ppermute | solution.py:519
  87.0 15.4 %collective-permute-start.7 = (bf16[4,8,16,256]{3,2,1,0:T(8,128)(2,1)S(1)}, bf16[4,8,16,256]{3,2,1,0:T(8,128)(2,1)S(1)}, u32[]{:S(2)}, u32[]{:S(2)}) collective-permute-start(bf16[4,8,16,256]{3,2,1,0:T(8,128)(2,1)S(1)} %get-tuple-element.60), channel_id=1, source_target_pairs={{0,3},{3,0},{1,2},{2,1},{4,7},{7,4},{5,6},{6,5},{8,11},{11,8},{9,1... | collective-permute-start | bytes 786440 | tf_op jit(solution)/shard_map/ppermute | solution.py:519

commit v11 on v7

--- a/solution.py
+++ b/solution.py
@@ -473,15 +473,24 @@
         part = part.reshape(lines, block, LANES)
         for i in range(lines):
             rows_of[v, pl.ds(i * apart, block), :] = part[i]
-    for m in range(block):
+    def line(m):
         x = [rows_of[v, pl.ds(m, lines, stride=apart), :] for v in range(size // LANES)]
-        x = jnp.concatenate(x, axis=1).astype(BF16)
-        result = dot(x, legendre_ref[m], ((1,), (0,)))
-        for r in range(parts):
-            at = r * share + step * block + m
-            for h in range(sums.shape[0]):
-                piece = result[r * own : (r + 1) * own, h * LANES : (h + 1) * LANES]
-                sums[h, pl.ds(at, own, stride=stretch), :] = piece
+        return jnp.concatenate(x, axis=1).astype(BF16)
+
+    wide = legendre_ref.shape[2]
+    group = max(1, 2 * LANES // wide)
+    for m in range(0, block, group):
+        both = range(m, m + group)
+        x = jnp.concatenate([line(i) for i in both], axis=0)
+        y = jnp.concatenate([legendre_ref[i] for i in both], axis=1)
+        product = dot(x, y, ((1,), (0,)))
+        for i in both:
+            result = product[(i - m) * lines : (i - m + 1) * lines, (i - m) * wide : (i - m + 1) * wide]
+            for r in range(parts):
+                at = r * share + step * block + i
+                for h in range(sums.shape[0]):
+                    piece = result[r * own : (r + 1) * own, h * LANES : (h + 1) * LANES]
+                    sums[h, pl.ds(at, own, stride=stretch), :] = piece
 
     @pl.when(step == pl.num_programs(0) - 1)
     def _():
@@ -543,17 +552,17 @@
     sent, info = lax.optimization_barrier((sent, info))
     recv = lax.all_to_all(sent, "lat", split_axis=0, concat_axis=0, tiled=True)
     *ends, react = edges(tracers, react_base, react_temp, info)
-    halos = (
+    halos = [
         exchange(ends[0], "lat", neighbours("lat", 0)),
-        exchange(ends[1], "lat", neighbours("lat", 1)),
         exchange(ends[2], "lon", neighbours("lon", 0)),
         exchange(ends[3], "lon", neighbours("lon", 1)),
-    )
+    ]
     react, wave_ids = lax.optimization_barrier((react, wave_ids))
     table, twiddle = tables(info, wave_ids, rows, tiles * tile // LANES)
-    recv, table, twiddle, halos, react = lax.optimization_barrier(
-        (recv, table, twiddle, halos, react)
+    recv, table, twiddle, react, halos, last = lax.optimization_barrier(
+        (recv, table, twiddle, react, halos, ends[1])
     )
+    halos.insert(1, exchange(last, "lat", neighbours("lat", 1)))
     grids = synthesis(recv, table, twiddle, info, tiles, tile)
 
     middle, inner = list(range(tiles // 2, tiles)), list(range(1, tiles // 2))

time: 98.2 us -> 97.9 us (level)
  the two profiles are of different devices: /device:TPU:2 before, /device:TPU:0 now
where the time goes in v11:
time: 97.9 us; the launch traced here: 97.7 us
  Pallas kernels  51.3 us (52%)
  starting transfers between devices  26.6 us (27%)
  waiting for transfers between devices  13.7 us (14%)
  local copies, waits for them, and re-layouts  5.24 us (5%)
    ppermute x10, starting transfers between devices, exchange(): lax.ppermute(value, axis, [p for a, b in pairs for p in ((a, b), (b, a))])  21.4 us
    pallas_call x4, Pallas kernels, chemistry(): pl.pallas_call(functools.partial(chem_kernel, scale, k), grid_spec=pltpu....  17.1 us
    pallas_call x1, Pallas kernels, legendre_sums(): pl.pallas_call(legendre_kernel, grid=(share // block,), in_specs=[pl.Bloc...  14.3 us
    ppermute x10, waiting for transfers between devices, exchange(): lax.ppermute(value, axis, [p for a, b in pairs for p in ((a, b), (b, a))])  12.9 us
    pallas_call x4, Pallas kernels, spread(): pl.pallas_call(spread_kernel, grid_spec=pltpu.PrefetchScalarGridSpec(num_...  5.49 us
    unnamed x16, local copies, waits for them, and re-layouts  5.24 us
    all_to_all x1, starting transfers between devices, body(): recv = lax.all_to_all(sent, 'lat', split_axis=0, concat_axis=0, tiled=True)  5.17 us
    pallas_call x1, Pallas kernels, synthesis(): pl.pallas_call(synth_kernel, grid_spec=pltpu.PrefetchScalarGridSpec(num_s...  5.09 us
  transfers between devices with their start and end apart: 11, of which 3 were waited for; matrix products, arithmetic and copies ran while one was open for 0% of the time, Pallas kernels for 36%

profile of v11, /device:TPU:0, one launch (start us, length us, event | category | flops | bytes accessed | tf_op | source)
XLA Modules:
  0.0 97.7 jit_solution(11233574873889930708)
XLA Ops:
  0.6 0.0 copy-start.6
  0.6 0.0 copy-start.7
  0.7 0.0 copy-start.3
  0.7 0.0 copy-start.4
  0.7 14.3 %legendre.1 = bf16[8,8,16,512]{3,2,1,0:T(8,128)(2,1)} custom-call(bf16[6,8,80,1280]{3,2,1,0:T(8,128)(2,1)} %spectral_ref.1, bf16[80,1280,128]{2,1,0:T(8,128)(2,1)} %legendre_ref.1), custom_call_target="tpu_custom_call" | custom-call | flops 1258291200 | bytes 36044800 | tf_op jit(solution)/shard_map/legendre/pallas_call | solution.py:510
  15.0 0.0 copy-start.5
  15.0 0.0 copy-done.6
  15.0 0.0 copy-done.7
  15.0 0.1 pad_add_fusion.info
  15.1 5.2 %all-to-all-start = ((bf16[8,8,16,512]{3,2,1,0:T(8,128)(2,1)}), bf16[8,8,16,512]{3,2,1,0:T(8,128)(2,1)S(1)}, u32[]{:S(2)}, u32[]{:S(2)}) async-start(bf16[8,8,16,512]{3,2,1,0:T(8,128)(2,1)} %legendre.1), calls=%async_computation | async-start | bytes 2097152 | tf_op jit(solution)/shard_map/all_to_all | solution.py:553
  20.2 0.0 copy-done.3
  20.2 0.0 copy-done.4
  20.3 4.8 %edges.1 = (bf16[32,16,256]{2,1,0:T(8,128)(2,1)S(1)}, bf16[32,16,256]{2,1,0:T(8,128)(2,1)S(1)}, bf16[256,128]{1,0:T(8,128)(2,1)S(1)}, bf16[256,128]{1,0:T(8,128)(2,1)S(1)}, bf16[512,512]{1,0:T(8,128)(2,1)S(1)}) custom-call(s32[22]{0:T(128)S(1)} %pad_add_fusion.info, bf16[16,32,16,256]{3,2,1,0:T(8,128)(2,1)} %refs_0_.7, f32[16,16]{1,0:T(8,128)S(1)} %copy-done.3, ...), custom_call_target="tpu_custom_call" | custom-call | flops 268435456 | bytes 4194304 | tf_op jit(solution)/shard_map/edges/pallas_call | solution.py:279
  25.0 0.6 collective-permute-start
  25.6 1.6 %collective-permute-start.1 = (bf16[256,128]{1,0:T(8,128)(2,1)S(1)}, bf16[256,128]{1,0:T(8,128)(2,1)S(1)}, u32[]{:S(2)}, u32[]{:S(2)}) collective-permute-start(bf16[256,128]{1,0:T(8,128)(2,1)S(1)} %get-tuple-element.44), channel_id=1, source_target_pairs={{0,1},{1,0},{2,3},{3,2},{4,5},{5,4},{6,7},{7,6},{8,9},{9,8},{10,11... | collective-permute-start | bytes 196616 | tf_op jit(solution)/shard_map/ppermute | solution.py:530
  27.2 0.7 collective-permute-start.2
  27.8 0.0 copy-done.5
  27.8 4.6 %tables.1 = (bf16[16,1280,128]{2,1,0:T(8,128)(2,1)S(1)}, f32[16,2,8,640]{3,2,1,0:T(8,128)S(1)}) custom-call(s32[22]{0:T(128)S(1)} %pad_add_fusion.info, s32[1,640]{1,0:T(1,128)S(1)} %broadcast_in_dim.3.waves_ref), custom_call_target="tpu_custom_call" | custom-call | flops 10485760 | bytes 5242880 | tf_op jit(solution)/shard_map/tables/pallas_call | solution.py:88
  32.4 0.0 copy-start.1
  32.5 2.3 %copy-done.1 = bf16[16,1280,128]{2,1,0:T(8,128)(2,1)} copy-done((bf16[16,1280,128]{2,1,0:T(8,128)(2,1)}, bf16[16,1280,128]{2,1,0:T(8,128)(2,1)S(1)}, u32[]{:S(2)}) %copy-start.1) | copy-done | bytes 5242904
  34.8 0.0 collective-permute-done.1.refs_3_
  34.8 0.0 collective-permute-done.2.refs_4_
  34.8 0.0 collective-permute-done.refs_1_
  34.8 0.8 all-to-all-done.recv_ref
  35.6 0.0 copy-start
  35.7 0.8 collective-permute-start.3
  36.5 0.0 copy-start.2
  36.5 2.9 %copy-done.2 = bf16[16,1280,128]{2,1,0:T(8,128)(2,1)S(1)} copy-done((bf16[16,1280,128]{2,1,0:T(8,128)(2,1)S(1)}, bf16[16,1280,128]{2,1,0:T(8,128)(2,1)}, u32[]{:S(2)}) %copy-start.2) | copy-done | bytes 5242904
  39.3 5.1 %synthesis.1 = (bf16[3,8,16,256]{3,2,1,0:T(8,128)(2,1)S(1)}, bf16[3,8,16,256]{3,2,1,0:T(8,128)(2,1)S(1)}, bf16[3,8,16,256]{3,2,1,0:T(8,128)(2,1)S(1)}, bf16[3,8,16,256]{3,2,1,0:T(8,128)(2,1)S(1)}) custom-call(s32[22]{0:T(128)S(1)} %pad_add_fusion.info, bf16[8,8,16,512]{3,2,1,0:T(8,128)(2,1)S(1)} %all-to-all-done.recv_ref, ...), custom_call_target="tpu_custom_call" | custom-call | flops 1006632960 | bytes 5242880 | tf_op jit(solution)/shard_map/synthesis/pallas_call | solution.py:189
  44.4 3.1 %collective-permute-start.6 = (bf16[3,8,16,256]{3,2,1,0:T(8,128)(2,1)S(1)}, bf16[3,8,16,256]{3,2,1,0:T(8,128)(2,1)S(1)}, u32[]{:S(2)}, u32[]{:S(2)}) collective-permute-start(bf16[3,8,16,256]{3,2,1,0:T(8,128)(2,1)S(1)} %get-tuple-element.61), channel_id=1, source_target_pairs={{0,2},{2,0},{1,3},{3,1},{4,6},{6,4},{5,7},{7,5},{8,10},{10,8},{9,1... | collective-permute-start | bytes 589832 | tf_op jit(solution)/shard_map/ppermute | solution.py:530
  47.5 0.0 collective-permute-done.3.refs_2_
  47.5 0.0 copy-done
  47.6 4.3 %chemistry.4 = (bf16[16,32,16,256]{3,2,1,0:T(8,128)(2,1)}, bf16[4,8,16,256]{3,2,1,0:T(8,128)(2,1)S(1)}) custom-call(s32[22]{0:T(128)S(1)} %pad_add_fusion.info, bf16[16,32,16,256]{3,2,1,0:T(8,128)(2,1)S(1)} %copy-done, bf16[32,16,256]{2,1,0:T(8,128)(2,1)S(1)} %collective-permute-done.refs_1_, bf16[32,16,256]{2,1,0:T(8,128)(2,1)S(1)} %collective-permute-done.3.refs_2_, ...), custom_call_target="tpu_custom_call" | custom-call | flops 524288 | bytes 2048 | tf_op jit(solution)/shard_map/chemistry/pallas_call | solution.py:398
  51.8 2.9 %collective-permute-start.5 = (bf16[3,8,16,256]{3,2,1,0:T(8,128)(2,1)S(1)}, bf16[3,8,16,256]{3,2,1,0:T(8,128)(2,1)S(1)}, u32[]{:S(2)}, u32[]{:S(2)}) collective-permute-start(bf16[3,8,16,256]{3,2,1,0:T(8,128)(2,1)S(1)} %get-tuple-element.60), channel_id=1, source_target_pairs={{0,3},{3,0},{1,2},{2,1},{4,7},{7,4},{5,6},{6,5},{8,11},{11,8},{9,1... | collective-permute-start | bytes 589832 | tf_op jit(solution)/shard_map/ppermute | solution.py:530
  54.7 0.0 collective-permute-start.4
  54.7 0.0 collective-permute-done.6.refs_5_
  54.7 4.3 %chemistry.5 = (bf16[16,32,16,256]{3,2,1,0:T(8,128)(2,1)}, bf16[4,8,16,256]{3,2,1,0:T(8,128)(2,1)S(1)}) custom-call(s32[22]{0:T(128)S(1)} %pad_add_fusion.info, bf16[16,32,16,256]{3,2,1,0:T(8,128)(2,1)S(1)} %copy-done, bf16[32,16,256]{2,1,0:T(8,128)(2,1)S(1)} %collective-permute-done.refs_1_, ...), custom_call_target="tpu_custom_call", output_to_operand_aliasing={{0}: (8, {})} | custom-call | flops 524288 | bytes 2048 | tf_op jit(solution)/shard_map/chemistry/pallas_call | solution.py:398
  59.0 1.5 %collective-permute-start.9 = (bf16[4,8,16,256]{3,2,1,0:T(8,128)(2,1)S(1)}, bf16[4,8,16,256]{3,2,1,0:T(8,128)(2,1)S(1)}, u32[]{:S(2)}, u32[]{:S(2)}) collective-permute-start(bf16[4,8,16,256]{3,2,1,0:T(8,128)(2,1)S(1)} %get-tuple-element.68), channel_id=1, source_target_pairs={{0,2},{2,0},{1,3},{3,1},{4,6},{6,4},{5,7},{7,5},{8,10},{10,8},{9,1... | collective-permute-start | bytes 786440 | tf_op jit(solution)/shard_map/ppermute | solution.py:530
  60.5 0.0 collective-permute-done.5.refs_5_
  60.5 4.3 %chemistry.6 = (bf16[16,32,16,256]{3,2,1,0:T(8,128)(2,1)}, bf16[4,8,16,256]{3,2,1,0:T(8,128)(2,1)S(1)}) custom-call(s32[22]{0:T(128)S(1)} %pad_add_fusion.info, bf16[16,32,16,256]{3,2,1,0:T(8,128)(2,1)S(1)} %copy-done, bf16[32,16,256]{2,1,0:T(8,128)(2,1)S(1)} %collective-permute-done.refs_1_, ...), custom_call_target="tpu_custom_call", output_to_operand_aliasing={{0}: (8, {})} | custom-call | flops 524288 | bytes 2048 | tf_op jit(solution)/shard_map/chemistry/pallas_call | solution.py:398
  64.7 4.4 %collective-permute-done.4.refs_5_ = bf16[3,8,16,256]{3,2,1,0:T(8,128)(2,1)S(1)} collective-permute-done((bf16[3,8,16,256]{3,2,1,0:T(8,128)(2,1)S(1)}, bf16[3,8,16,256]{3,2,1,0:T(8,128)(2,1)S(1)}, u32[]{:S(2)}, u32[]{:S(2)}) %collective-permute-start.4) | collective-permute-done | bytes 196640 | tf_op jit(solution)/shard_map/ppermute | solution.py:530
  69.1 4.3 %chemistry.7 = (bf16[16,32,16,256]{3,2,1,0:T(8,128)(2,1)}, bf16[4,8,16,256]{3,2,1,0:T(8,128)(2,1)S(1)}) custom-call(s32[22]{0:T(128)S(1)} %pad_add_fusion.info, bf16[16,32,16,256]{3,2,1,0:T(8,128)(2,1)S(1)} %copy-done, bf16[32,16,256]{2,1,0:T(8,128)(2,1)S(1)} %collective-permute-done.refs_1_, ...), custom_call_target="tpu_custom_call", output_to_operand_aliasing={{0}: (8, {})} | custom-call | flops 524288 | bytes 2048 | tf_op jit(solution)/shard_map/chemistry/pallas_call | solution.py:398
  73.4 3.6 %collective-permute-start.8 = (bf16[4,8,16,256]{3,2,1,0:T(8,128)(2,1)S(1)}, bf16[4,8,16,256]{3,2,1,0:T(8,128)(2,1)S(1)}, u32[]{:S(2)}, u32[]{:S(2)}) collective-permute-start(bf16[4,8,16,256]{3,2,1,0:T(8,128)(2,1)S(1)} %get-tuple-element.67), channel_id=1, source_target_pairs={{0,1},{1,0},{2,3},{3,2},{4,5},{5,4},{6,7},{7,6},{8,9},{9,8},{10,11... | collective-permute-start | bytes 786440 | tf_op jit(solution)/shard_map/ppermute | solution.py:530
  77.0 6.7 %collective-permute-start.7 = (bf16[4,8,16,256]{3,2,1,0:T(8,128)(2,1)S(1)}, bf16[4,8,16,256]{3,2,1,0:T(8,128)(2,1)S(1)}, u32[]{:S(2)}, u32[]{:S(2)}) collective-permute-start(bf16[4,8,16,256]{3,2,1,0:T(8,128)(2,1)S(1)} %get-tuple-element.66), channel_id=1, source_target_pairs={{0,3},{3,0},{1,2},{2,1},{4,7},{7,4},{5,6},{6,5},{8,11},{11,8},{9,1... | collective-permute-start | bytes 786440 | tf_op jit(solution)/shard_map/ppermute | solution.py:530
  83.7 1.4 %spread.4.refs_0_ = f32[4,8,16,1024]{3,2,1,0:T(8,128)} custom-call(s32[22]{0:T(128)S(1)} %pad_add_fusion.info, bf16[4,8,16,256]{3,2,1,0:T(8,128)(2,1)S(1)} %get-tuple-element.69.recv_ref), custom_call_target="tpu_custom_call" | custom-call | flops 131072 | bytes 4 | tf_op jit(solution)/shard_map/spread/pallas_call | solution.py:440
  85.0 0.0 collective-permute-done.9.recv_ref
  85.1 1.4 %spread.5.refs_0_ = f32[4,8,16,1024]{3,2,1,0:T(8,128)} custom-call(s32[22]{0:T(128)S(1)} %pad_add_fusion.info, bf16[4,8,16,256]{3,2,1,0:T(8,128)(2,1)S(1)} %collective-permute-done.9.recv_ref, f32[4,8,16,1024]{3,2,1,0:T(8,128)} %spread.4.refs_0_), custom_call_target="tpu_custom_call", output_to_operand_aliasing={{}: (2, {})} | custom-call | flops 131072 | bytes 4 | tf_op jit(solution)/shard_map/spread/pallas_call | solution.py:440
  86.4 0.0 collective-permute-done.8.recv_ref
  86.4 1.4 %spread.6.refs_0_ = f32[4,8,16,1024]{3,2,1,0:T(8,128)} custom-call(s32[22]{0:T(128)S(1)} %pad_add_fusion.info, bf16[4,8,16,256]{3,2,1,0:T(8,128)(2,1)S(1)} %collective-permute-done.8.recv_ref, f32[4,8,16,1024]{3,2,1,0:T(8,128)} %spread.5.refs_0_), custom_call_target="tpu_custom_call", output_to_operand_aliasing={{}: (2, {})} | custom-call | flops 131072 | bytes 4 | tf_op jit(solution)/shard_map/spread/pallas_call | solution.py:440
  87.8 8.5 %collective-permute-done.7.recv_ref = bf16[4,8,16,256]{3,2,1,0:T(8,128)(2,1)S(1)} collective-permute-done((bf16[4,8,16,256]{3,2,1,0:T(8,128)(2,1)S(1)}, bf16[4,8,16,256]{3,2,1,0:T(8,128)(2,1)S(1)}, u32[]{:S(2)}, u32[]{:S(2)}) %collective-permute-start.7) | collective-permute-done | bytes 262176 | tf_op jit(solution)/shard_map/ppermute | solution.py:530
  96.3 1.4 %spread.7 = f32[4,8,16,1024]{3,2,1,0:T(8,128)} custom-call(s32[22]{0:T(128)S(1)} %pad_add_fusion.info, bf16[4,8,16,256]{3,2,1,0:T(8,128)(2,1)S(1)} %collective-permute-done.7.recv_ref, f32[4,8,16,1024]{3,2,1,0:T(8,128)} %spread.6.refs_0_), custom_call_target="tpu_custom_call", output_to_operand_aliasing={{}: (2, {})} | custom-call | flops 131072 | bytes 4 | tf_op jit(solution)/shard_map/spread/pallas_call | solution.py:440
  (1 shorter events, 0.0 us)
Async XLA Ops:
  0.6 14.3 %copy-start.6 = (s32[16]{0:T(128)S(1)}, s32[16]{0:T(128)}, u32[]{:S(2)}) copy-start(s32[16]{0:T(128)} %param.11) | copy-start | bytes 196
  0.6 14.3 %copy-start.7 = (s32[4]{0:T(128)S(1)}, s32[4]{0:T(128)}, u32[]{:S(2)}) copy-start(s32[4]{0:T(128)} %param.15) | copy-start | bytes 52
  0.7 19.6 %copy-start.3 = (f32[16,16]{1,0:T(8,128)S(1)}, f32[16,16]{1,0:T(8,128)}, u32[]{:S(2)}) copy-start(f32[16,16]{1,0:T(8,128)} %base_ref.1) | copy-start | bytes 3076
  0.7 19.6 %copy-start.4 = (f32[16,16]{1,0:T(8,128)S(1)}, f32[16,16]{1,0:T(8,128)}, u32[]{:S(2)}) copy-start(f32[16,16]{1,0:T(8,128)} %temp_ref.1) | copy-start | bytes 3076
  15.0 12.8 %copy-start.5 = (s32[640]{0:T(1024)S(1)}, s32[640]{0:T(1024)}, u32[]{:S(2)}) copy-start(s32[640]{0:T(1024)} %param.10) | copy-start | bytes 7684
  15.1 20.6 %all-to-all-start = ((bf16[8,8,16,512]{3,2,1,0:T(8,128)(2,1)}), bf16[8,8,16,512]{3,2,1,0:T(8,128)(2,1)S(1)}, u32[]{:S(2)}, u32[]{:S(2)}) async-start(bf16[8,8,16,512]{3,2,1,0:T(8,128)(2,1)} %legendre.1), calls=%async_computation | async-start | bytes 2097152 | tf_op jit(solution)/shard_map/all_to_all | solution.py:553
  25.0 9.8 %collective-permute-start = (bf16[32,16,256]{2,1,0:T(8,128)(2,1)S(1)}, bf16[32,16,256]{2,1,0:T(8,128)(2,1)S(1)}, u32[]{:S(2)}, u32[]{:S(2)}) collective-permute-start(bf16[32,16,256]{2,1,0:T(8,128)(2,1)S(1)} %get-tuple-element.43), channel_id=1, source_target_pairs={{0,4},{4,0},{8,12},{12,8},{16,20},{20,16},{24,28},{28,24},{1,5},{5... | collective-permute-start | bytes 786440 | tf_op jit(solution)/shard_map/ppermute | solution.py:530
  25.6 9.2 %collective-permute-start.1 = (bf16[256,128]{1,0:T(8,128)(2,1)S(1)}, bf16[256,128]{1,0:T(8,128)(2,1)S(1)}, u32[]{:S(2)}, u32[]{:S(2)}) collective-permute-start(bf16[256,128]{1,0:T(8,128)(2,1)S(1)} %get-tuple-element.44), channel_id=1, source_target_pairs={{0,1},{1,0},{2,3},{3,2},{4,5},{5,4},{6,7},{7,6},{8,9},{9,8},{10,11... | collective-permute-start | bytes 196616 | tf_op jit(solution)/shard_map/ppermute | solution.py:530
  27.2 7.6 %collective-permute-start.2 = (bf16[256,128]{1,0:T(8,128)(2,1)S(1)}, bf16[256,128]{1,0:T(8,128)(2,1)S(1)}, u32[]{:S(2)}, u32[]{:S(2)}) collective-permute-start(bf16[256,128]{1,0:T(8,128)(2,1)S(1)} %get-tuple-element.45), channel_id=1, source_target_pairs={{1,2},{2,1},{5,6},{6,5},{9,10},{10,9},{13,14},{14,13},{17,18},{18,... | collective-permute-start | bytes 196616 | tf_op jit(solution)/shard_map/ppermute | solution.py:530
  32.4 2.3 %copy-start.1 = (bf16[16,1280,128]{2,1,0:T(8,128)(2,1)}, bf16[16,1280,128]{2,1,0:T(8,128)(2,1)S(1)}, u32[]{:S(2)}) copy-start(bf16[16,1280,128]{2,1,0:T(8,128)(2,1)S(1)} %get-tuple-element.52.table_ref) | copy-start | bytes 15728644
  35.6 11.9 %copy-start = (bf16[16,32,16,256]{3,2,1,0:T(8,128)(2,1)S(1)}, bf16[16,32,16,256]{3,2,1,0:T(8,128)(2,1)}, u32[]{:S(2)}) copy-start(bf16[16,32,16,256]{3,2,1,0:T(8,128)(2,1)} %refs_0_.7) | copy-start | bytes 12582916
  35.7 11.9 %collective-permute-start.3 = (bf16[32,16,256]{2,1,0:T(8,128)(2,1)S(1)}, bf16[32,16,256]{2,1,0:T(8,128)(2,1)S(1)}, u32[]{:S(2)}, u32[]{:S(2)}) collective-permute-start(bf16[32,16,256]{2,1,0:T(8,128)(2,1)S(1)} %get-tuple-element.48), channel_id=1, source_target_pairs={{4,8},{8,4},{12,16},{16,12},{20,24},{24,20},{5,9},{9,5},{13,17},{1... | collective-permute-start | bytes 786440 | tf_op jit(solution)/shard_map/ppermute | solution.py:530
  36.5 2.9 %copy-start.2 = (bf16[16,1280,128]{2,1,0:T(8,128)(2,1)S(1)}, bf16[16,1280,128]{2,1,0:T(8,128)(2,1)}, u32[]{:S(2)}) copy-start(bf16[16,1280,128]{2,1,0:T(8,128)(2,1)} %copy-done.1) | copy-start | bytes 15728644
  44.4 10.3 %collective-permute-start.6 = (bf16[3,8,16,256]{3,2,1,0:T(8,128)(2,1)S(1)}, bf16[3,8,16,256]{3,2,1,0:T(8,128)(2,1)S(1)}, u32[]{:S(2)}, u32[]{:S(2)}) collective-permute-start(bf16[3,8,16,256]{3,2,1,0:T(8,128)(2,1)S(1)} %get-tuple-element.61), channel_id=1, source_target_pairs={{0,2},{2,0},{1,3},{3,1},{4,6},{6,4},{5,7},{7,5},{8,10},{10,8},{9,1... | collective-permute-start | bytes 589832 | tf_op jit(solution)/shard_map/ppermute | solution.py:530
  51.8 8.7 %collective-permute-start.5 = (bf16[3,8,16,256]{3,2,1,0:T(8,128)(2,1)S(1)}, bf16[3,8,16,256]{3,2,1,0:T(8,128)(2,1)S(1)}, u32[]{:S(2)}, u32[]{:S(2)}) collective-permute-start(bf16[3,8,16,256]{3,2,1,0:T(8,128)(2,1)S(1)} %get-tuple-element.60), channel_id=1, source_target_pairs={{0,3},{3,0},{1,2},{2,1},{4,7},{7,4},{5,6},{6,5},{8,11},{11,8},{9,1... | collective-permute-start | bytes 589832 | tf_op jit(solution)/shard_map/ppermute | solution.py:530
  54.7 14.4 %collective-permute-start.4 = (bf16[3,8,16,256]{3,2,1,0:T(8,128)(2,1)S(1)}, bf16[3,8,16,256]{3,2,1,0:T(8,128)(2,1)S(1)}, u32[]{:S(2)}, u32[]{:S(2)}) collective-permute-start(bf16[3,8,16,256]{3,2,1,0:T(8,128)(2,1)S(1)} %get-tuple-element.59), channel_id=1, source_target_pairs={{0,1},{1,0},{2,3},{3,2},{4,5},{5,4},{6,7},{7,6},{8,9},{9,8},{10,11... | collective-permute-start | bytes 589832 | tf_op jit(solution)/shard_map/ppermute | solution.py:530
  59.0 26.1 %collective-permute-start.9 = (bf16[4,8,16,256]{3,2,1,0:T(8,128)(2,1)S(1)}, bf16[4,8,16,256]{3,2,1,0:T(8,128)(2,1)S(1)}, u32[]{:S(2)}, u32[]{:S(2)}) collective-permute-start(bf16[4,8,16,256]{3,2,1,0:T(8,128)(2,1)S(1)} %get-tuple-element.68), channel_id=1, source_target_pairs={{0,2},{2,0},{1,3},{3,1},{4,6},{6,4},{5,7},{7,5},{8,10},{10,8},{9,1... | collective-permute-start | bytes 786440 | tf_op jit(solution)/shard_map/ppermute | solution.py:530
  73.4 13.1 %collective-permute-start.8 = (bf16[4,8,16,256]{3,2,1,0:T(8,128)(2,1)S(1)}, bf16[4,8,16,256]{3,2,1,0:T(8,128)(2,1)S(1)}, u32[]{:S(2)}, u32[]{:S(2)}) collective-permute-start(bf16[4,8,16,256]{3,2,1,0:T(8,128)(2,1)S(1)} %get-tuple-element.67), channel_id=1, source_target_pairs={{0,1},{1,0},{2,3},{3,2},{4,5},{5,4},{6,7},{7,6},{8,9},{9,8},{10,11... | collective-permute-start | bytes 786440 | tf_op jit(solution)/shard_map/ppermute | solution.py:530
  77.0 19.3 %collective-permute-start.7 = (bf16[4,8,16,256]{3,2,1,0:T(8,128)(2,1)S(1)}, bf16[4,8,16,256]{3,2,1,0:T(8,128)(2,1)S(1)}, u32[]{:S(2)}, u32[]{:S(2)}) collective-permute-start(bf16[4,8,16,256]{3,2,1,0:T(8,128)(2,1)S(1)} %get-tuple-element.66), channel_id=1, source_target_pairs={{0,3},{3,0},{1,2},{2,1},{4,7},{7,4},{5,6},{6,5},{8,11},{11,8},{9,1... | collective-permute-start | bytes 786440 | tf_op jit(solution)/shard_map/ppermute | solution.py:530

commit v12 on v11

--- a/solution.py
+++ b/solution.py
@@ -423,34 +423,30 @@
     )(info, *operands)
 
 
-def spread_kernel(info, recv_ref, *refs):
-    refs[-1][...] = recv_ref[...].astype(F32)
-
-
-def spread(recv, info, k, sources, before):
-    actives, own, rows, tile = recv.shape
-    each = 2 if actives % 2 == 0 else 1
-    operands = [recv]
-    in_specs = [pl.BlockSpec((each, own, rows, tile), lambda a, info: (a, 0, 0, 0))]
-    aliases = {}
-    if before is not None:
-        operands.append(before)
-        in_specs.append(pl.BlockSpec(memory_space=pl.ANY))
-        aliases = {2: 0}
+def spread_kernel(order, info, *refs):
+    *recv_refs, out_ref = refs
+    tile = recv_refs[0].shape[3]
+    for k, recv_ref in zip(order, recv_refs):
+        start = pl.multiple_of((info[ME] ^ k) * tile, LANES)
+        out_ref[:, :, :, pl.ds(start, tile)] = recv_ref[...].astype(F32)
+
+
+def spread(parts, order, info):
+    actives, own, rows, tile = parts[0].shape
+    wide = len(parts) * tile
     return pl.pallas_call(
-        spread_kernel,
+        functools.partial(spread_kernel, order),
         grid_spec=pltpu.PrefetchScalarGridSpec(
             num_scalar_prefetch=1,
-            grid=(actives // each,),
-            in_specs=in_specs,
-            out_specs=pl.BlockSpec((each, own, rows, tile), lambda a, info: (a, 0, 0, info[ME] ^ k)),
+            grid=(actives,),
+            in_specs=[pl.BlockSpec((1, own, rows, tile), lambda a, info: (a, 0, 0, 0))] * len(parts),
+            out_specs=pl.BlockSpec((1, own, rows, wide), lambda a, info: (a, 0, 0, 0)),
         ),
-        out_shape=jax.ShapeDtypeStruct((actives, own, rows, sources * tile), F32),
-        input_output_aliases=aliases,
+        out_shape=jax.ShapeDtypeStruct((actives, own, rows, wide), F32),
         compiler_params=pltpu.CompilerParams(vmem_limit_bytes=8 * MIB),
-        cost_estimate=cost(recv.size, recv.shape[0]),
+        cost_estimate=cost(actives, actives),
         name="spread",
-    )(info, *operands)
+    )(info, *parts)
 
 
 def legendre_kernel(spectral_ref, legendre_ref, out_ref, rows_of, sums):
@@ -583,10 +579,11 @@
             rest = late + inner
             held, active[0] = lax.optimization_barrier(([grids[i] for i in rest], active[0]))
             moved |= {i: send(value, i) for i, value in zip(rest, held)}
-    spreaded = None
-    for k in [0] + soon + inner + late:
-        spreaded = spread(active[k], info, k, tiles, spreaded)
-    return new, spreaded
+    order = [0] + soon + late + inner
+    through = lax.optimization_barrier([active[k] for k in soon + late])
+    active |= zip(soon + late, through)
+    active = dict(zip(order, lax.optimization_barrier([active[k] for k in order])))
+    return new, spread([active[k] for k in order], order, info)
 
 
 def solution(mesh):

time: 97.9 us -> 95.1 us (0.971); the launches traced: 97.7 us -> 93.3 us
  waiting for transfers between devices: 13.7 us -> 8.78 us
  starting transfers between devices: 26.6 us -> 29.8 us
  Pallas kernels: 51.3 us -> 48.6 us
    ppermute x10, waiting for transfers between devices: 12.9 us -> 7.94 us  [exchange(): lax.ppermute(value, axis, [p for a, b in pairs for p in ((a, b), (b, a))])]
    ppermute x10, starting transfers between devices: 21.4 us -> 24.7 us  [exchange(): lax.ppermute(value, axis, [p for a, b in pairs for p in ((a, b), (b, a))])]
    pallas_call x4 -> x1, Pallas kernels: 5.49 us -> 2.41 us  [spread(): pl.pallas_call(functools.partial(spread_kernel, order), grid_spec=pltpu.P...]
  transfers between devices with their start and end apart: 11 -> 11, of which waited for: 3 -> 2; matrix products, arithmetic and copies ran while one was open for 0% -> 0% of each run, Pallas kernels for 36% -> 34%
where the time goes in v12:
time: 95.1 us; the launch traced here: 93.3 us
  Pallas kernels  48.6 us (51%)
  starting transfers between devices  29.8 us (31%)
  waiting for transfers between devices  8.78 us (9%)
  local copies, waits for them, and re-layouts  5.24 us (6%)
    ppermute x10, starting transfers between devices, exchange(): lax.ppermute(value, axis, [p for a, b in pairs for p in ((a, b), (b, a))])  24.7 us
    pallas_call x4, Pallas kernels, chemistry(): pl.pallas_call(functools.partial(chem_kernel, scale, k), grid_spec=pltpu....  17.4 us
    pallas_call x1, Pallas kernels, legendre_sums(): pl.pallas_call(legendre_kernel, grid=(share // block,), in_specs=[pl.Bloc...  14.3 us
    ppermute x10, waiting for transfers between devices, exchange(): lax.ppermute(value, axis, [p for a, b in pairs for p in ((a, b), (b, a))])  7.94 us
    unnamed x16, local copies, waits for them, and re-layouts  5.24 us
    all_to_all x1, starting transfers between devices, body(): recv = lax.all_to_all(sent, 'lat', split_axis=0, concat_axis=0, tiled=True)  5.17 us
    pallas_call x1, Pallas kernels, synthesis(): pl.pallas_call(synth_kernel, grid_spec=pltpu.PrefetchScalarGridSpec(num_s...  5.12 us
    pallas_call x1, Pallas kernels, edges(): pl.pallas_call(edge_kernel, grid_spec=pltpu.PrefetchScalarGridSpec(num_sc...  4.76 us
  transfers between devices with their start and end apart: 11, of which 2 were waited for; matrix products, arithmetic and copies ran while one was open for 0% of the time, Pallas kernels for 34%

profile of v12, /device:TPU:0, one launch (start us, length us, event | category | flops | bytes accessed | tf_op | source)
XLA Modules:
  0.0 93.3 jit_solution(8350839410572463441)
XLA Ops:
  0.6 0.0 copy-start.6
  0.6 0.0 copy-start.7
  0.7 0.0 copy-start.3
  0.7 0.0 copy-start.4
  0.7 14.3 %legendre.1 = bf16[8,8,16,512]{3,2,1,0:T(8,128)(2,1)} custom-call(bf16[6,8,80,1280]{3,2,1,0:T(8,128)(2,1)} %spectral_ref.1, bf16[80,1280,128]{2,1,0:T(8,128)(2,1)} %legendre_ref.1), custom_call_target="tpu_custom_call" | custom-call | flops 1258291200 | bytes 36044800 | tf_op jit(solution)/shard_map/legendre/pallas_call | solution.py:506
  15.0 0.0 copy-start.5
  15.0 0.0 copy-done.6
  15.0 0.0 copy-done.7
  15.0 0.1 pad_add_fusion.info
  15.1 5.2 %all-to-all-start = ((bf16[8,8,16,512]{3,2,1,0:T(8,128)(2,1)}), bf16[8,8,16,512]{3,2,1,0:T(8,128)(2,1)S(1)}, u32[]{:S(2)}, u32[]{:S(2)}) async-start(bf16[8,8,16,512]{3,2,1,0:T(8,128)(2,1)} %legendre.1), calls=%async_computation | async-start | bytes 2097152 | tf_op jit(solution)/shard_map/all_to_all | solution.py:549
  20.2 0.0 copy-done.3
  20.2 0.0 copy-done.4
  20.3 4.8 %edges.1 = (bf16[32,16,256]{2,1,0:T(8,128)(2,1)S(1)}, bf16[32,16,256]{2,1,0:T(8,128)(2,1)S(1)}, bf16[256,128]{1,0:T(8,128)(2,1)S(1)}, bf16[256,128]{1,0:T(8,128)(2,1)S(1)}, bf16[512,512]{1,0:T(8,128)(2,1)S(1)}) custom-call(s32[22]{0:T(128)S(1)} %pad_add_fusion.info, bf16[16,32,16,256]{3,2,1,0:T(8,128)(2,1)} %refs_0_.7, f32[16,16]{1,0:T(8,128)S(1)} %copy-done.3, ...), custom_call_target="tpu_custom_call" | custom-call | flops 268435456 | bytes 4194304 | tf_op jit(solution)/shard_map/edges/pallas_call | solution.py:279
  25.0 0.6 collective-permute-start
  25.6 1.6 %collective-permute-start.1 = (bf16[256,128]{1,0:T(8,128)(2,1)S(1)}, bf16[256,128]{1,0:T(8,128)(2,1)S(1)}, u32[]{:S(2)}, u32[]{:S(2)}) collective-permute-start(bf16[256,128]{1,0:T(8,128)(2,1)S(1)} %get-tuple-element.50), channel_id=1, source_target_pairs={{0,1},{1,0},{2,3},{3,2},{4,5},{5,4},{6,7},{7,6},{8,9},{9,8},{10,11... | collective-permute-start | bytes 196616 | tf_op jit(solution)/shard_map/ppermute | solution.py:526
  27.2 0.7 collective-permute-start.2
  27.8 0.0 copy-done.5
  27.8 4.6 %tables.1 = (bf16[16,1280,128]{2,1,0:T(8,128)(2,1)S(1)}, f32[16,2,8,640]{3,2,1,0:T(8,128)S(1)}) custom-call(s32[22]{0:T(128)S(1)} %pad_add_fusion.info, s32[1,640]{1,0:T(1,128)S(1)} %broadcast_in_dim.3.waves_ref), custom_call_target="tpu_custom_call" | custom-call | flops 10485760 | bytes 5242880 | tf_op jit(solution)/shard_map/tables/pallas_call | solution.py:88
  32.4 0.0 copy-start.1
  32.5 2.3 %copy-done.1 = bf16[16,1280,128]{2,1,0:T(8,128)(2,1)} copy-done((bf16[16,1280,128]{2,1,0:T(8,128)(2,1)}, bf16[16,1280,128]{2,1,0:T(8,128)(2,1)S(1)}, u32[]{:S(2)}) %copy-start.1) | copy-done | bytes 5242904
  34.8 0.0 collective-permute-done.1.refs_3_
  34.8 0.0 collective-permute-done.2.refs_4_
  34.8 0.0 collective-permute-done.refs_1_
  34.8 0.8 all-to-all-done.recv_ref
  35.6 0.0 copy-start
  35.7 0.8 collective-permute-start.3
  36.5 0.0 copy-start.2
  36.5 2.9 %copy-done.2 = bf16[16,1280,128]{2,1,0:T(8,128)(2,1)S(1)} copy-done((bf16[16,1280,128]{2,1,0:T(8,128)(2,1)S(1)}, bf16[16,1280,128]{2,1,0:T(8,128)(2,1)}, u32[]{:S(2)}) %copy-start.2) | copy-done | bytes 5242904
  39.3 5.1 %synthesis.1 = (bf16[3,8,16,256]{3,2,1,0:T(8,128)(2,1)S(1)}, bf16[3,8,16,256]{3,2,1,0:T(8,128)(2,1)S(1)}, bf16[3,8,16,256]{3,2,1,0:T(8,128)(2,1)S(1)}, bf16[3,8,16,256]{3,2,1,0:T(8,128)(2,1)S(1)}) custom-call(s32[22]{0:T(128)S(1)} %pad_add_fusion.info, bf16[8,8,16,512]{3,2,1,0:T(8,128)(2,1)S(1)} %all-to-all-done.recv_ref, ...), custom_call_target="tpu_custom_call" | custom-call | flops 1006632960 | bytes 5242880 | tf_op jit(solution)/shard_map/synthesis/pallas_call | solution.py:189
  44.5 3.1 %collective-permute-start.6 = (bf16[3,8,16,256]{3,2,1,0:T(8,128)(2,1)S(1)}, bf16[3,8,16,256]{3,2,1,0:T(8,128)(2,1)S(1)}, u32[]{:S(2)}, u32[]{:S(2)}) collective-permute-start(bf16[3,8,16,256]{3,2,1,0:T(8,128)(2,1)S(1)} %get-tuple-element.67), channel_id=1, source_target_pairs={{0,2},{2,0},{1,3},{3,1},{4,6},{6,4},{5,7},{7,5},{8,10},{10,8},{9,1... | collective-permute-start | bytes 589832 | tf_op jit(solution)/shard_map/ppermute | solution.py:526
  47.6 0.0 collective-permute-done.3.refs_2_
  47.6 0.0 copy-done
  47.6 4.4 %chemistry.4 = (bf16[16,32,16,256]{3,2,1,0:T(8,128)(2,1)}, bf16[4,8,16,256]{3,2,1,0:T(8,128)(2,1)S(1)}) custom-call(s32[22]{0:T(128)S(1)} %pad_add_fusion.info, bf16[16,32,16,256]{3,2,1,0:T(8,128)(2,1)S(1)} %copy-done, bf16[32,16,256]{2,1,0:T(8,128)(2,1)S(1)} %collective-permute-done.refs_1_, bf16[32,16,256]{2,1,0:T(8,128)(2,1)S(1)} %collective-permute-done.3.refs_2_, ...), custom_call_target="tpu_custom_call" | custom-call | flops 524288 | bytes 2048 | tf_op jit(solution)/shard_map/chemistry/pallas_call | solution.py:398
  51.9 2.9 %collective-permute-start.5 = (bf16[3,8,16,256]{3,2,1,0:T(8,128)(2,1)S(1)}, bf16[3,8,16,256]{3,2,1,0:T(8,128)(2,1)S(1)}, u32[]{:S(2)}, u32[]{:S(2)}) collective-permute-start(bf16[3,8,16,256]{3,2,1,0:T(8,128)(2,1)S(1)} %get-tuple-element.66), channel_id=1, source_target_pairs={{0,3},{3,0},{1,2},{2,1},{4,7},{7,4},{5,6},{6,5},{8,11},{11,8},{9,1... | collective-permute-start | bytes 589832 | tf_op jit(solution)/shard_map/ppermute | solution.py:526
  54.9 0.0 collective-permute-start.4
  54.9 0.0 collective-permute-done.6.refs_5_
  54.9 4.4 %chemistry.5 = (bf16[16,32,16,256]{3,2,1,0:T(8,128)(2,1)}, bf16[4,8,16,256]{3,2,1,0:T(8,128)(2,1)S(1)}) custom-call(s32[22]{0:T(128)S(1)} %pad_add_fusion.info, bf16[16,32,16,256]{3,2,1,0:T(8,128)(2,1)S(1)} %copy-done, bf16[32,16,256]{2,1,0:T(8,128)(2,1)S(1)} %collective-permute-done.refs_1_, ...), custom_call_target="tpu_custom_call", output_to_operand_aliasing={{0}: (8, {})} | custom-call | flops 524288 | bytes 2048 | tf_op jit(solution)/shard_map/chemistry/pallas_call | solution.py:398
  59.2 1.5 %collective-permute-start.7 = (bf16[4,8,16,256]{3,2,1,0:T(8,128)(2,1)S(1)}, bf16[4,8,16,256]{3,2,1,0:T(8,128)(2,1)S(1)}, u32[]{:S(2)}, u32[]{:S(2)}) collective-permute-start(bf16[4,8,16,256]{3,2,1,0:T(8,128)(2,1)S(1)} %get-tuple-element.73), channel_id=1, source_target_pairs={{0,2},{2,0},{1,3},{3,1},{4,6},{6,4},{5,7},{7,5},{8,10},{10,8},{9,1... | collective-permute-start | bytes 786440 | tf_op jit(solution)/shard_map/ppermute | solution.py:526
  60.7 0.0 collective-permute-done.5.refs_5_
  60.7 4.4 %chemistry.6 = (bf16[16,32,16,256]{3,2,1,0:T(8,128)(2,1)}, bf16[4,8,16,256]{3,2,1,0:T(8,128)(2,1)S(1)}) custom-call(s32[22]{0:T(128)S(1)} %pad_add_fusion.info, bf16[16,32,16,256]{3,2,1,0:T(8,128)(2,1)S(1)} %copy-done, bf16[32,16,256]{2,1,0:T(8,128)(2,1)S(1)} %collective-permute-done.refs_1_, ...), custom_call_target="tpu_custom_call", output_to_operand_aliasing={{0}: (8, {})} | custom-call | flops 524288 | bytes 2048 | tf_op jit(solution)/shard_map/chemistry/pallas_call | solution.py:398
  65.1 7.2 %collective-permute-start.8 = (bf16[4,8,16,256]{3,2,1,0:T(8,128)(2,1)S(1)}, bf16[4,8,16,256]{3,2,1,0:T(8,128)(2,1)S(1)}, u32[]{:S(2)}, u32[]{:S(2)}) collective-permute-start(bf16[4,8,16,256]{3,2,1,0:T(8,128)(2,1)S(1)} %get-tuple-element.74), channel_id=1, source_target_pairs={{0,3},{3,0},{1,2},{2,1},{4,7},{7,4},{5,6},{6,5},{8,11},{11,8},{9,1... | collective-permute-start | bytes 786440 | tf_op jit(solution)/shard_map/ppermute | solution.py:526
  72.3 0.0 collective-permute-done.4.refs_5_
  72.3 4.4 %chemistry.7 = (bf16[16,32,16,256]{3,2,1,0:T(8,128)(2,1)}, bf16[4,8,16,256]{3,2,1,0:T(8,128)(2,1)S(1)}) custom-call(s32[22]{0:T(128)S(1)} %pad_add_fusion.info, bf16[16,32,16,256]{3,2,1,0:T(8,128)(2,1)S(1)} %copy-done, bf16[32,16,256]{2,1,0:T(8,128)(2,1)S(1)} %collective-permute-done.refs_1_, ...), custom_call_target="tpu_custom_call", output_to_operand_aliasing={{0}: (8, {})} | custom-call | flops 524288 | bytes 2048 | tf_op jit(solution)/shard_map/chemistry/pallas_call | solution.py:398
  76.7 6.3 %collective-permute-start.9 = (bf16[4,8,16,256]{3,2,1,0:T(8,128)(2,1)S(1)}, bf16[4,8,16,256]{3,2,1,0:T(8,128)(2,1)S(1)}, u32[]{:S(2)}, u32[]{:S(2)}) collective-permute-start(bf16[4,8,16,256]{3,2,1,0:T(8,128)(2,1)S(1)} %get-tuple-element.77), channel_id=1, source_target_pairs={{0,1},{1,0},{2,3},{3,2},{4,5},{5,4},{6,7},{7,6},{8,9},{9,8},{10,11... | collective-permute-start | bytes 786440 | tf_op jit(solution)/shard_map/ppermute | solution.py:526
  83.0 0.0 collective-permute-done.7.refs_1_
  83.0 0.0 collective-permute-done.8.refs_2_
  83.0 7.9 %collective-permute-done.9.refs_3_ = bf16[4,8,16,256]{3,2,1,0:T(8,128)(2,1)S(1)} collective-permute-done((bf16[4,8,16,256]{3,2,1,0:T(8,128)(2,1)S(1)}, bf16[4,8,16,256]{3,2,1,0:T(8,128)(2,1)S(1)}, u32[]{:S(2)}, u32[]{:S(2)}) %collective-permute-start.9) | collective-permute-done | bytes 262176 | tf_op jit(solution)/shard_map/ppermute | solution.py:526
  90.9 2.4 %spread.1 = f32[4,8,16,1024]{3,2,1,0:T(8,128)} custom-call(s32[22]{0:T(128)S(1)} %pad_add_fusion.info, bf16[4,8,16,256]{3,2,1,0:T(8,128)(2,1)S(1)} %get-tuple-element.78.refs_0_, bf16[4,8,16,256]{3,2,1,0:T(8,128)(2,1)S(1)} %collective-permute-done.7.refs_1_, bf16[4,8,16,256]{3,2,1,0:T(8,128)(2,1)S(1)} %collective-permute-done.8.refs_2_, ...), custom_call_target="tpu_custom_call" | custom-call | flops 4 | bytes 4 | tf_op jit(solution)/shard_map/spread/pallas_call | solution.py:437
  (1 shorter events, 0.0 us)
Async XLA Ops:
  0.6 14.3 %copy-start.6 = (s32[16]{0:T(128)S(1)}, s32[16]{0:T(128)}, u32[]{:S(2)}) copy-start(s32[16]{0:T(128)} %param.11) | copy-start | bytes 196
  0.6 14.3 %copy-start.7 = (s32[4]{0:T(128)S(1)}, s32[4]{0:T(128)}, u32[]{:S(2)}) copy-start(s32[4]{0:T(128)} %param.15) | copy-start | bytes 52
  0.7 19.6 %copy-start.3 = (f32[16,16]{1,0:T(8,128)S(1)}, f32[16,16]{1,0:T(8,128)}, u32[]{:S(2)}) copy-start(f32[16,16]{1,0:T(8,128)} %base_ref.1) | copy-start | bytes 3076
  0.7 19.6 %copy-start.4 = (f32[16,16]{1,0:T(8,128)S(1)}, f32[16,16]{1,0:T(8,128)}, u32[]{:S(2)}) copy-start(f32[16,16]{1,0:T(8,128)} %temp_ref.1) | copy-start | bytes 3076
  15.0 12.8 %copy-start.5 = (s32[640]{0:T(1024)S(1)}, s32[640]{0:T(1024)}, u32[]{:S(2)}) copy-start(s32[640]{0:T(1024)} %param.10) | copy-start | bytes 7684
  15.1 20.6 %all-to-all-start = ((bf16[8,8,16,512]{3,2,1,0:T(8,128)(2,1)}), bf16[8,8,16,512]{3,2,1,0:T(8,128)(2,1)S(1)}, u32[]{:S(2)}, u32[]{:S(2)}) async-start(bf16[8,8,16,512]{3,2,1,0:T(8,128)(2,1)} %legendre.1), calls=%async_computation | async-start | bytes 2097152 | tf_op jit(solution)/shard_map/all_to_all | solution.py:549
  25.0 9.8 %collective-permute-start = (bf16[32,16,256]{2,1,0:T(8,128)(2,1)S(1)}, bf16[32,16,256]{2,1,0:T(8,128)(2,1)S(1)}, u32[]{:S(2)}, u32[]{:S(2)}) collective-permute-start(bf16[32,16,256]{2,1,0:T(8,128)(2,1)S(1)} %get-tuple-element.49), channel_id=1, source_target_pairs={{0,4},{4,0},{8,12},{12,8},{16,20},{20,16},{24,28},{28,24},{1,5},{5... | collective-permute-start | bytes 786440 | tf_op jit(solution)/shard_map/ppermute | solution.py:526
  25.6 9.2 %collective-permute-start.1 = (bf16[256,128]{1,0:T(8,128)(2,1)S(1)}, bf16[256,128]{1,0:T(8,128)(2,1)S(1)}, u32[]{:S(2)}, u32[]{:S(2)}) collective-permute-start(bf16[256,128]{1,0:T(8,128)(2,1)S(1)} %get-tuple-element.50), channel_id=1, source_target_pairs={{0,1},{1,0},{2,3},{3,2},{4,5},{5,4},{6,7},{7,6},{8,9},{9,8},{10,11... | collective-permute-start | bytes 196616 | tf_op jit(solution)/shard_map/ppermute | solution.py:526
  27.2 7.6 %collective-permute-start.2 = (bf16[256,128]{1,0:T(8,128)(2,1)S(1)}, bf16[256,128]{1,0:T(8,128)(2,1)S(1)}, u32[]{:S(2)}, u32[]{:S(2)}) collective-permute-start(bf16[256,128]{1,0:T(8,128)(2,1)S(1)} %get-tuple-element.51), channel_id=1, source_target_pairs={{1,2},{2,1},{5,6},{6,5},{9,10},{10,9},{13,14},{14,13},{17,18},{18,... | collective-permute-start | bytes 196616 | tf_op jit(solution)/shard_map/ppermute | solution.py:526
  32.4 2.3 %copy-start.1 = (bf16[16,1280,128]{2,1,0:T(8,128)(2,1)}, bf16[16,1280,128]{2,1,0:T(8,128)(2,1)S(1)}, u32[]{:S(2)}) copy-start(bf16[16,1280,128]{2,1,0:T(8,128)(2,1)S(1)} %get-tuple-element.58.table_ref) | copy-start | bytes 15728644
  35.6 11.9 %copy-start = (bf16[16,32,16,256]{3,2,1,0:T(8,128)(2,1)S(1)}, bf16[16,32,16,256]{3,2,1,0:T(8,128)(2,1)}, u32[]{:S(2)}) copy-start(bf16[16,32,16,256]{3,2,1,0:T(8,128)(2,1)} %refs_0_.7) | copy-start | bytes 12582916
  35.7 11.9 %collective-permute-start.3 = (bf16[32,16,256]{2,1,0:T(8,128)(2,1)S(1)}, bf16[32,16,256]{2,1,0:T(8,128)(2,1)S(1)}, u32[]{:S(2)}, u32[]{:S(2)}) collective-permute-start(bf16[32,16,256]{2,1,0:T(8,128)(2,1)S(1)} %get-tuple-element.54), channel_id=1, source_target_pairs={{4,8},{8,4},{12,16},{16,12},{20,24},{24,20},{5,9},{9,5},{13,17},{1... | collective-permute-start | bytes 786440 | tf_op jit(solution)/shard_map/ppermute | solution.py:526
  36.5 2.9 %copy-start.2 = (bf16[16,1280,128]{2,1,0:T(8,128)(2,1)S(1)}, bf16[16,1280,128]{2,1,0:T(8,128)(2,1)}, u32[]{:S(2)}) copy-start(bf16[16,1280,128]{2,1,0:T(8,128)(2,1)} %copy-done.1) | copy-start | bytes 15728644
  44.5 10.4 %collective-permute-start.6 = (bf16[3,8,16,256]{3,2,1,0:T(8,128)(2,1)S(1)}, bf16[3,8,16,256]{3,2,1,0:T(8,128)(2,1)S(1)}, u32[]{:S(2)}, u32[]{:S(2)}) collective-permute-start(bf16[3,8,16,256]{3,2,1,0:T(8,128)(2,1)S(1)} %get-tuple-element.67), channel_id=1, source_target_pairs={{0,2},{2,0},{1,3},{3,1},{4,6},{6,4},{5,7},{7,5},{8,10},{10,8},{9,1... | collective-permute-start | bytes 589832 | tf_op jit(solution)/shard_map/ppermute | solution.py:526
  51.9 8.8 %collective-permute-start.5 = (bf16[3,8,16,256]{3,2,1,0:T(8,128)(2,1)S(1)}, bf16[3,8,16,256]{3,2,1,0:T(8,128)(2,1)S(1)}, u32[]{:S(2)}, u32[]{:S(2)}) collective-permute-start(bf16[3,8,16,256]{3,2,1,0:T(8,128)(2,1)S(1)} %get-tuple-element.66), channel_id=1, source_target_pairs={{0,3},{3,0},{1,2},{2,1},{4,7},{7,4},{5,6},{6,5},{8,11},{11,8},{9,1... | collective-permute-start | bytes 589832 | tf_op jit(solution)/shard_map/ppermute | solution.py:526
  54.9 17.4 %collective-permute-start.4 = (bf16[3,8,16,256]{3,2,1,0:T(8,128)(2,1)S(1)}, bf16[3,8,16,256]{3,2,1,0:T(8,128)(2,1)S(1)}, u32[]{:S(2)}, u32[]{:S(2)}) collective-permute-start(bf16[3,8,16,256]{3,2,1,0:T(8,128)(2,1)S(1)} %get-tuple-element.65), channel_id=1, source_target_pairs={{0,1},{1,0},{2,3},{3,2},{4,5},{5,4},{6,7},{7,6},{8,9},{9,8},{10,11... | collective-permute-start | bytes 589832 | tf_op jit(solution)/shard_map/ppermute | solution.py:526
  59.2 23.8 %collective-permute-start.7 = (bf16[4,8,16,256]{3,2,1,0:T(8,128)(2,1)S(1)}, bf16[4,8,16,256]{3,2,1,0:T(8,128)(2,1)S(1)}, u32[]{:S(2)}, u32[]{:S(2)}) collective-permute-start(bf16[4,8,16,256]{3,2,1,0:T(8,128)(2,1)S(1)} %get-tuple-element.73), channel_id=1, source_target_pairs={{0,2},{2,0},{1,3},{3,1},{4,6},{6,4},{5,7},{7,5},{8,10},{10,8},{9,1... | collective-permute-start | bytes 786440 | tf_op jit(solution)/shard_map/ppermute | solution.py:526
  65.1 17.9 %collective-permute-start.8 = (bf16[4,8,16,256]{3,2,1,0:T(8,128)(2,1)S(1)}, bf16[4,8,16,256]{3,2,1,0:T(8,128)(2,1)S(1)}, u32[]{:S(2)}, u32[]{:S(2)}) collective-permute-start(bf16[4,8,16,256]{3,2,1,0:T(8,128)(2,1)S(1)} %get-tuple-element.74), channel_id=1, source_target_pairs={{0,3},{3,0},{1,2},{2,1},{4,7},{7,4},{5,6},{6,5},{8,11},{11,8},{9,1... | collective-permute-start | bytes 786440 | tf_op jit(solution)/shard_map/ppermute | solution.py:526
  76.7 14.3 %collective-permute-start.9 = (bf16[4,8,16,256]{3,2,1,0:T(8,128)(2,1)S(1)}, bf16[4,8,16,256]{3,2,1,0:T(8,128)(2,1)S(1)}, u32[]{:S(2)}, u32[]{:S(2)}) collective-permute-start(bf16[4,8,16,256]{3,2,1,0:T(8,128)(2,1)S(1)} %get-tuple-element.77), channel_id=1, source_target_pairs={{0,1},{1,0},{2,3},{3,2},{4,5},{5,4},{6,7},{7,6},{8,9},{9,8},{10,11... | collective-permute-start | bytes 786440 | tf_op jit(solution)/shard_map/ppermute | solution.py:526

commit v13 on v12

--- a/solution.py
+++ b/solution.py
@@ -62,48 +62,16 @@
     return cosine, sine * y
 
 
-def table_kernel(first, info, waves_ref, table_ref, twiddle_ref):
-    size, turns = waves_ref.shape[1], twiddle_ref.shape[2]
-    waves = waves_ref[...].astype(F32)
-    for k in range(table_ref.shape[0]):
-        row = pl.program_id(0) * table_ref.shape[0] + k
-        count = jnp.full(waves.shape, info[first + row], jnp.int32).astype(F32)
-        cos_low, sin_low = unit_circle(1, LOW, waves, count)
-        cos_high, sin_high = unit_circle(LOW, LANES // LOW, waves, count)
-        cosine, sine = [], []
-        for a in range(LANES // LOW):
-            ch, sh = cos_high[a : a + 1], sin_high[a : a + 1]
-            cosine.append(ch * cos_low - sh * sin_low)
-            sine.append(-sh * cos_low - ch * sin_low)
-        table_ref[k, :size, :] = jnp.concatenate(cosine, axis=0).T.astype(BF16)
-        table_ref[k, size:, :] = jnp.concatenate(sine, axis=0).T.astype(BF16)
-        cos_turn, sin_turn = unit_circle(LANES, turns, waves, count)
-        twiddle_ref[k, 0] = cos_turn
-        twiddle_ref[k, 1] = sin_turn
-
-
-def tables(info, wave_ids, rows, turns):
-    waves = wave_ids.shape[0]
-    each = STEP if rows % STEP == 0 else 1
-    return pl.pallas_call(
-        functools.partial(table_kernel, info.shape[0] - rows),
-        grid_spec=pltpu.PrefetchScalarGridSpec(
-            num_scalar_prefetch=1,
-            grid=(rows // each,),
-            in_specs=[pl.BlockSpec((1, waves), lambda j, p: (0, 0))],
-            out_specs=[
-                pl.BlockSpec((each, 2 * waves, LANES), lambda j, p: (j, 0, 0)),
-                pl.BlockSpec((each, 2, turns, waves), lambda j, p: (j, 0, 0, 0)),
-            ],
-        ),
-        out_shape=[
-            pltpu.VMEM((rows, 2 * waves, LANES), BF16),
-            pltpu.VMEM((rows, 2, turns, waves), F32),
-        ],
-        compiler_params=pltpu.CompilerParams(vmem_limit_bytes=20 * MIB),
-        cost_estimate=cost(rows * waves * LANES * 8, rows * waves * LANES * 4),
-        name="tables",
-    )(info, wave_ids[None, :])
+def row_tables(count, waves, turns):
+    cos_low, sin_low = unit_circle(1, LOW, waves, count)
+    cos_high, sin_high = unit_circle(LOW, LANES // LOW, waves, count)
+    cosine, sine = [], []
+    for a in range(LANES // LOW):
+        ch, sh = cos_high[a : a + 1], sin_high[a : a + 1]
+        cosine.append(ch * cos_low - sh * sin_low)
+        sine.append(-sh * cos_low - ch * sin_low)
+    table = [jnp.concatenate(part, axis=0).T.astype(BF16) for part in (cosine, sine)]
+    return jnp.concatenate(table, axis=0), *unit_circle(LANES, turns, waves, count)
 
 
 def place(pieces, width):
@@ -126,31 +94,34 @@
     return out
 
 
-def synth_kernel(info, recv_ref, table_ref, twiddle_ref, *refs):
+def synth_kernel(info, waves_ref, recv_ref, *refs):
     *out_refs, coef, grid = refs
-    sources, levels, rows, _ = recv_ref.shape
+    pieces, levels, rows, _ = recv_ref.shape
     fields, waves = coef.shape[0] // 2, coef.shape[1] * LANES
-    share = waves // sources
-    each, _, turns = twiddle_ref.shape[:3]
+    share = waves // pieces
+    turns = grid.shape[0] // (fields * levels * (rows + 1))
     pitch = rows + 1
-    step = pl.program_id(0)
+    step, steps = pl.program_id(0), pl.num_programs(0)
+    each = rows // steps
 
     @pl.when(step == 0)
     def _():
         def level(l, carry):
-            values = [recv_ref[s, l].astype(F32) for s in range(sources)]
+            values = [recv_ref[s, l].astype(F32) for s in range(pieces)]
             for r in range(2 * fields):
-                windows = [
-                    (values[s], r * share, share, s * share) for s in range(sources)
-                ]
+                windows = [(values[s], r * share, share, s * share) for s in range(pieces)]
                 for v, part in enumerate(place(windows, waves)):
                     coef[r, v, pl.ds(l * pitch, rows), :] = part
             return carry
 
         lax.fori_loop(0, levels, level, 0)
 
+    wave_line = waves_ref[...].astype(F32)
+    first = info.shape[0] - rows
     for k in range(each):
         j = step * each + k
+        count = jnp.full(wave_line.shape, info[first + j], jnp.int32).astype(F32)
+        table, cos_turn, sin_turn = row_tables(count, wave_line, turns)
 
         def own_row(r):
             parts = [coef[r, v, pl.ds(j, levels, stride=pitch), :] for v in range(waves // LANES)]
@@ -159,16 +130,16 @@
         values = [own_row(r) for r in range(2 * fields)]
         real, imag = [], []
         for t in range(turns):
-            c, s = twiddle_ref[k, 0, t : t + 1], twiddle_ref[k, 1, t : t + 1]
+            c, s = cos_turn[t : t + 1], sin_turn[t : t + 1]
             for f in range(fields):
                 re, im = values[2 * f], values[2 * f + 1]
                 real.append(re * c - im * s)
                 imag.append(re * s + im * c)
         both = [jnp.concatenate(part, axis=0).astype(BF16) for part in (real, imag)]
-        result = dot(jnp.concatenate(both, axis=1), table_ref[k], ((1,), (0,)))
+        result = dot(jnp.concatenate(both, axis=1), table, ((1,), (0,)))
         grid[pl.ds(j, turns * fields * levels, stride=pitch), :] = result
 
-    @pl.when(step == pl.num_programs(0) - 1)
+    @pl.when(step == steps - 1)
     def _():
         tiles = turns // len(out_refs)
         for k, out_ref in enumerate(out_refs):
@@ -180,10 +151,10 @@
                         out_ref[f, l, :, t * LANES : (t + 1) * LANES] = block
 
 
-def synthesis(recv, table, twiddle, info, dests, tile):
-    sources, levels, rows, lanes = recv.shape
-    turns, waves = twiddle.shape[2:]
-    fields = 3
+def synthesis(recv, wave_ids, info, dests, tile):
+    levels, rows = recv.shape[1:3]
+    waves = wave_ids.shape[0]
+    turns, fields = dests * tile // LANES, 3
     each = STEP if rows % STEP == 0 else 1
     shape = (fields, levels, rows, tile)
     return pl.pallas_call(
@@ -192,9 +163,8 @@
             num_scalar_prefetch=1,
             grid=(rows // each,),
             in_specs=[
+                pl.BlockSpec((1, waves), lambda j, info: (0, 0)),
                 pl.BlockSpec(recv.shape, lambda j, info: (0, 0, 0, 0)),
-                pl.BlockSpec((each, 2 * waves, LANES), lambda j, info: (j, 0, 0)),
-                pl.BlockSpec((each, 2, turns, waves), lambda j, info: (j, 0, 0, 0)),
             ],
             out_specs=[pl.BlockSpec(shape, lambda j, info: (0, 0, 0, 0))] * dests,
             scratch_shapes=[
@@ -206,7 +176,7 @@
         compiler_params=pltpu.CompilerParams(vmem_limit_bytes=24 * MIB),
         cost_estimate=cost(4 * rows * waves * fields * levels * turns * LANES, 4 * rows * waves * LANES),
         name="synthesis",
-    )(info, recv, *[pltpu.with_memory_space_constraint(v, pltpu.VMEM) for v in (table, twiddle)])
+    )(info, wave_ids[None, :], recv)
 
 
 def edge_kernel(
@@ -553,13 +523,9 @@
         exchange(ends[2], "lon", neighbours("lon", 0)),
         exchange(ends[3], "lon", neighbours("lon", 1)),
     ]
-    react, wave_ids = lax.optimization_barrier((react, wave_ids))
-    table, twiddle = tables(info, wave_ids, rows, tiles * tile // LANES)
-    recv, table, twiddle, react, halos, last = lax.optimization_barrier(
-        (recv, table, twiddle, react, halos, ends[1])
-    )
+    recv, react, halos, last = lax.optimization_barrier((recv, react, halos, ends[1]))
     halos.insert(1, exchange(last, "lat", neighbours("lat", 1)))
-    grids = synthesis(recv, table, twiddle, info, tiles, tile)
+    grids = synthesis(recv, wave_ids, info, tiles, tile)
 
     middle, inner = list(range(tiles // 2, tiles)), list(range(1, tiles // 2))
     soon, late = middle[: tiles // 4], middle[tiles // 4 :]

time: 95.1 us -> 93.3 us (0.981); the launches traced: 93.3 us -> 93.1 us
  waiting for transfers between devices: 8.78 us -> 15.9 us
  starting transfers between devices: 29.8 us -> 26.1 us
  local copies, waits for them, and re-layouts: 5.24 us -> 2.21 us
    all_to_all x1, waiting for transfers between devices: 0.84 us -> 5.79 us  [body(): recv = lax.all_to_all(sent, 'lat', split_axis=0, concat_axis=0, tiled=True)]
    pallas_call x1 -> x0, Pallas kernels: 4.59 us -> none  [tables(): pl.pallas_call(functools.partial(table_kernel, info.shape[0] - rows), gri...]
    pallas_call x1, Pallas kernels: 5.12 us -> 9.12 us  [synthesis(): pl.pallas_call(synth_kernel, grid_spec=pltpu.PrefetchScalarGridSpec(num_s...]
    ppermute x10, starting transfers between devices: 24.7 us -> 21 us  [exchange(): lax.ppermute(value, axis, [p for a, b in pairs for p in ((a, b), (b, a))])]
    unnamed x16 -> x12, local copies, waits for them, and re-layouts: 5.24 us -> 2.21 us
    ppermute x10, waiting for transfers between devices: 7.94 us -> 10.1 us  [exchange(): lax.ppermute(value, axis, [p for a, b in pairs for p in ((a, b), (b, a))])]
  transfers between devices with their start and end apart: 11 -> 11, of which waited for: 2 -> 5; matrix products, arithmetic and copies ran while one was open for 0% -> 0% of each run, Pallas kernels for 34% -> 34%
where the time goes in v13:
time: 93.3 us; the launch traced here: 93.1 us
  Pallas kernels  48 us (51%)
  starting transfers between devices  26.1 us (28%)
  waiting for transfers between devices  15.9 us (17%)
  local copies, waits for them, and re-layouts  2.21 us (2%)
    ppermute x10, starting transfers between devices, exchange(): lax.ppermute(value, axis, [p for a, b in pairs for p in ((a, b), (b, a))])  21 us
    pallas_call x4, Pallas kernels, chemistry(): pl.pallas_call(functools.partial(chem_kernel, scale, k), grid_spec=pltpu....  17.5 us
    pallas_call x1, Pallas kernels, legendre_sums(): pl.pallas_call(legendre_kernel, grid=(share // block,), in_specs=[pl.Bloc...  14.3 us
    ppermute x10, waiting for transfers between devices, exchange(): lax.ppermute(value, axis, [p for a, b in pairs for p in ((a, b), (b, a))])  10.1 us
    pallas_call x1, Pallas kernels, synthesis(): pl.pallas_call(synth_kernel, grid_spec=pltpu.PrefetchScalarGridSpec(num_s...  9.12 us
    all_to_all x1, waiting for transfers between devices, body(): recv = lax.all_to_all(sent, 'lat', split_axis=0, concat_axis=0, tiled=True)  5.79 us
    all_to_all x1, starting transfers between devices, body(): recv = lax.all_to_all(sent, 'lat', split_axis=0, concat_axis=0, tiled=True)  5.17 us
    pallas_call x1, Pallas kernels, edges(): pl.pallas_call(edge_kernel, grid_spec=pltpu.PrefetchScalarGridSpec(num_sc...  4.75 us
  transfers between devices with their start and end apart: 11, of which 5 were waited for; matrix products, arithmetic and copies ran while one was open for 0% of the time, Pallas kernels for 34%

profile of v13, /device:TPU:0, one launch (start us, length us, event | category | flops | bytes accessed | tf_op | source)
XLA Modules:
  0.0 93.1 jit_solution(16898670936513563795)
XLA Ops:
  0.6 0.0 copy-start.4
  0.6 0.0 copy-start.5
  0.7 0.0 copy-start.1
  0.7 0.0 copy-start.2
  0.7 14.3 %legendre.1 = bf16[8,8,16,512]{3,2,1,0:T(8,128)(2,1)} custom-call(bf16[6,8,80,1280]{3,2,1,0:T(8,128)(2,1)} %spectral_ref.1, bf16[80,1280,128]{2,1,0:T(8,128)(2,1)} %legendre_ref.1), custom_call_target="tpu_custom_call" | custom-call | flops 1258291200 | bytes 36044800 | tf_op jit(solution)/shard_map/legendre/pallas_call | solution.py:476
  15.0 0.0 copy-start.3
  15.0 0.0 copy-done.4
  15.0 0.0 copy-done.5
  15.0 0.1 pad_add_fusion.info
  15.1 5.2 %all-to-all-start = ((bf16[8,8,16,512]{3,2,1,0:T(8,128)(2,1)}), bf16[8,8,16,512]{3,2,1,0:T(8,128)(2,1)S(1)}, u32[]{:S(2)}, u32[]{:S(2)}) async-start(bf16[8,8,16,512]{3,2,1,0:T(8,128)(2,1)} %legendre.1), calls=%async_computation | async-start | bytes 2097152 | tf_op jit(solution)/shard_map/all_to_all | solution.py:519
  20.2 0.0 copy-done.1
  20.2 0.0 copy-done.2
  20.3 4.8 %edges.1 = (bf16[32,16,256]{2,1,0:T(8,128)(2,1)S(1)}, bf16[32,16,256]{2,1,0:T(8,128)(2,1)S(1)}, bf16[256,128]{1,0:T(8,128)(2,1)S(1)}, bf16[256,128]{1,0:T(8,128)(2,1)S(1)}, bf16[512,512]{1,0:T(8,128)(2,1)S(1)}) custom-call(s32[22]{0:T(128)S(1)} %pad_add_fusion.info, bf16[16,32,16,256]{3,2,1,0:T(8,128)(2,1)} %refs_0_.7, f32[16,16]{1,0:T(8,128)S(1)} %copy-done.1, ...), custom_call_target="tpu_custom_call" | custom-call | flops 268435456 | bytes 4194304 | tf_op jit(solution)/shard_map/edges/pallas_call | solution.py:249
  25.0 0.6 collective-permute-start
  25.6 1.6 %collective-permute-start.1 = (bf16[256,128]{1,0:T(8,128)(2,1)S(1)}, bf16[256,128]{1,0:T(8,128)(2,1)S(1)}, u32[]{:S(2)}, u32[]{:S(2)}) collective-permute-start(bf16[256,128]{1,0:T(8,128)(2,1)S(1)} %get-tuple-element.40), channel_id=1, source_target_pairs={{0,1},{1,0},{2,3},{3,2},{4,5},{5,4},{6,7},{7,6},{8,9},{9,8},{10,11... | collective-permute-start | bytes 196616 | tf_op jit(solution)/shard_map/ppermute | solution.py:496
  27.2 0.7 collective-permute-start.2
  27.8 2.0 %collective-permute-done.1.refs_3_ = bf16[256,128]{1,0:T(8,128)(2,1)S(1)} collective-permute-done((bf16[256,128]{1,0:T(8,128)(2,1)S(1)}, bf16[256,128]{1,0:T(8,128)(2,1)S(1)}, u32[]{:S(2)}, u32[]{:S(2)}) %collective-permute-start.1) | collective-permute-done | bytes 65568 | tf_op jit(solution)/shard_map/ppermute | solution.py:496
  29.8 0.0 collective-permute-done.2.refs_4_
  29.9 0.0 collective-permute-done.refs_1_
  29.9 5.8 %all-to-all-done.recv_ref = bf16[8,8,16,512]{3,2,1,0:T(8,128)(2,1)S(1)} async-done(((bf16[8,8,16,512]{3,2,1,0:T(8,128)(2,1)}), bf16[8,8,16,512]{3,2,1,0:T(8,128)(2,1)S(1)}, u32[]{:S(2)}, u32[]{:S(2)}) %all-to-all-start) | async-done | bytes 1048608 | tf_op jit(solution)/shard_map/all_to_all | solution.py:519
  35.6 0.7 collective-permute-start.3
  36.3 0.0 copy-done.3
  36.3 9.1 %synthesis.1 = (bf16[3,8,16,256]{3,2,1,0:T(8,128)(2,1)S(1)}, bf16[3,8,16,256]{3,2,1,0:T(8,128)(2,1)S(1)}, bf16[3,8,16,256]{3,2,1,0:T(8,128)(2,1)S(1)}, bf16[3,8,16,256]{3,2,1,0:T(8,128)(2,1)S(1)}) custom-call(s32[22]{0:T(128)S(1)} %pad_add_fusion.info, s32[1,640]{1,0:T(1,128)S(1)} %broadcast_in_dim.3.waves_ref, bf16[8,8,16,512]{3,2,1,0:T(8,128)(2,1)S(1)} %all-to-all-done.recv_ref), custom_call_target="tpu_custom_call" | custom-call | flops 1006632960 | bytes 5242880 | tf_op jit(solution)/shard_map/synthesis/pallas_call | solution.py:160
  45.5 2.7 %collective-permute-start.6 = (bf16[3,8,16,256]{3,2,1,0:T(8,128)(2,1)S(1)}, bf16[3,8,16,256]{3,2,1,0:T(8,128)(2,1)S(1)}, u32[]{:S(2)}, u32[]{:S(2)}) collective-permute-start(bf16[3,8,16,256]{3,2,1,0:T(8,128)(2,1)S(1)} %get-tuple-element.55), channel_id=1, source_target_pairs={{0,2},{2,0},{1,3},{3,1},{4,6},{6,4},{5,7},{7,5},{8,10},{10,8},{9,1... | collective-permute-start | bytes 589832 | tf_op jit(solution)/shard_map/ppermute | solution.py:496
  48.1 0.0 collective-permute-done.3.refs_2_
  48.1 0.0 copy-start
  48.1 2.2 %copy-done = bf16[16,32,16,256]{3,2,1,0:T(8,128)(2,1)S(1)} copy-done((bf16[16,32,16,256]{3,2,1,0:T(8,128)(2,1)S(1)}, bf16[16,32,16,256]{3,2,1,0:T(8,128)(2,1)}, u32[]{:S(2)}) %copy-start) | copy-done | bytes 4194328
  50.3 4.4 %chemistry.4 = (bf16[16,32,16,256]{3,2,1,0:T(8,128)(2,1)}, bf16[4,8,16,256]{3,2,1,0:T(8,128)(2,1)S(1)}) custom-call(s32[22]{0:T(128)S(1)} %pad_add_fusion.info, bf16[16,32,16,256]{3,2,1,0:T(8,128)(2,1)S(1)} %copy-done, bf16[32,16,256]{2,1,0:T(8,128)(2,1)S(1)} %collective-permute-done.refs_1_, bf16[32,16,256]{2,1,0:T(8,128)(2,1)S(1)} %collective-permute-done.3.refs_2_, ...), custom_call_target="tpu_custom_call" | custom-call | flops 524288 | bytes 2048 | tf_op jit(solution)/shard_map/chemistry/pallas_call | solution.py:368
  54.7 1.3 %collective-permute-start.5 = (bf16[3,8,16,256]{3,2,1,0:T(8,128)(2,1)S(1)}, bf16[3,8,16,256]{3,2,1,0:T(8,128)(2,1)S(1)}, u32[]{:S(2)}, u32[]{:S(2)}) collective-permute-start(bf16[3,8,16,256]{3,2,1,0:T(8,128)(2,1)S(1)} %get-tuple-element.54), channel_id=1, source_target_pairs={{0,3},{3,0},{1,2},{2,1},{4,7},{7,4},{5,6},{6,5},{8,11},{11,8},{9,1... | collective-permute-start | bytes 589832 | tf_op jit(solution)/shard_map/ppermute | solution.py:496
  56.0 0.2 collective-permute-start.4
  56.3 1.3 %collective-permute-done.6.refs_5_ = bf16[3,8,16,256]{3,2,1,0:T(8,128)(2,1)S(1)} collective-permute-done((bf16[3,8,16,256]{3,2,1,0:T(8,128)(2,1)S(1)}, bf16[3,8,16,256]{3,2,1,0:T(8,128)(2,1)S(1)}, u32[]{:S(2)}, u32[]{:S(2)}) %collective-permute-start.6) | collective-permute-done | bytes 196640 | tf_op jit(solution)/shard_map/ppermute | solution.py:496
  57.5 4.4 %chemistry.5 = (bf16[16,32,16,256]{3,2,1,0:T(8,128)(2,1)}, bf16[4,8,16,256]{3,2,1,0:T(8,128)(2,1)S(1)}) custom-call(s32[22]{0:T(128)S(1)} %pad_add_fusion.info, bf16[16,32,16,256]{3,2,1,0:T(8,128)(2,1)S(1)} %copy-done, bf16[32,16,256]{2,1,0:T(8,128)(2,1)S(1)} %collective-permute-done.refs_1_, ...), custom_call_target="tpu_custom_call", output_to_operand_aliasing={{0}: (8, {})} | custom-call | flops 524288 | bytes 2048 | tf_op jit(solution)/shard_map/chemistry/pallas_call | solution.py:368
  61.9 1.5 %collective-permute-start.7 = (bf16[4,8,16,256]{3,2,1,0:T(8,128)(2,1)S(1)}, bf16[4,8,16,256]{3,2,1,0:T(8,128)(2,1)S(1)}, u32[]{:S(2)}, u32[]{:S(2)}) collective-permute-start(bf16[4,8,16,256]{3,2,1,0:T(8,128)(2,1)S(1)} %get-tuple-element.61), channel_id=1, source_target_pairs={{0,2},{2,0},{1,3},{3,1},{4,6},{6,4},{5,7},{7,5},{8,10},{10,8},{9,1... | collective-permute-start | bytes 786440 | tf_op jit(solution)/shard_map/ppermute | solution.py:496
  63.4 0.4 collective-permute-done.5.refs_5_
  63.9 4.4 %chemistry.6 = (bf16[16,32,16,256]{3,2,1,0:T(8,128)(2,1)}, bf16[4,8,16,256]{3,2,1,0:T(8,128)(2,1)S(1)}) custom-call(s32[22]{0:T(128)S(1)} %pad_add_fusion.info, bf16[16,32,16,256]{3,2,1,0:T(8,128)(2,1)S(1)} %copy-done, bf16[32,16,256]{2,1,0:T(8,128)(2,1)S(1)} %collective-permute-done.refs_1_, ...), custom_call_target="tpu_custom_call", output_to_operand_aliasing={{0}: (8, {})} | custom-call | flops 524288 | bytes 2048 | tf_op jit(solution)/shard_map/chemistry/pallas_call | solution.py:368
  68.2 6.5 %collective-permute-start.8 = (bf16[4,8,16,256]{3,2,1,0:T(8,128)(2,1)S(1)}, bf16[4,8,16,256]{3,2,1,0:T(8,128)(2,1)S(1)}, u32[]{:S(2)}, u32[]{:S(2)}) collective-permute-start(bf16[4,8,16,256]{3,2,1,0:T(8,128)(2,1)S(1)} %get-tuple-element.62), channel_id=1, source_target_pairs={{0,3},{3,0},{1,2},{2,1},{4,7},{7,4},{5,6},{6,5},{8,11},{11,8},{9,1... | collective-permute-start | bytes 786440 | tf_op jit(solution)/shard_map/ppermute | solution.py:496
  74.7 0.0 collective-permute-done.4.refs_5_
  74.7 4.4 %chemistry.7 = (bf16[16,32,16,256]{3,2,1,0:T(8,128)(2,1)}, bf16[4,8,16,256]{3,2,1,0:T(8,128)(2,1)S(1)}) custom-call(s32[22]{0:T(128)S(1)} %pad_add_fusion.info, bf16[16,32,16,256]{3,2,1,0:T(8,128)(2,1)S(1)} %copy-done, bf16[32,16,256]{2,1,0:T(8,128)(2,1)S(1)} %collective-permute-done.refs_1_, ...), custom_call_target="tpu_custom_call", output_to_operand_aliasing={{0}: (8, {})} | custom-call | flops 524288 | bytes 2048 | tf_op jit(solution)/shard_map/chemistry/pallas_call | solution.py:368
  79.1 5.2 %collective-permute-start.9 = (bf16[4,8,16,256]{3,2,1,0:T(8,128)(2,1)S(1)}, bf16[4,8,16,256]{3,2,1,0:T(8,128)(2,1)S(1)}, u32[]{:S(2)}, u32[]{:S(2)}) collective-permute-start(bf16[4,8,16,256]{3,2,1,0:T(8,128)(2,1)S(1)} %get-tuple-element.65), channel_id=1, source_target_pairs={{0,1},{1,0},{2,3},{3,2},{4,5},{5,4},{6,7},{7,6},{8,9},{9,8},{10,11... | collective-permute-start | bytes 786440 | tf_op jit(solution)/shard_map/ppermute | solution.py:496
  84.3 0.0 collective-permute-done.7.refs_1_
  84.3 0.0 collective-permute-done.8.refs_2_
  84.3 6.4 %collective-permute-done.9.refs_3_ = bf16[4,8,16,256]{3,2,1,0:T(8,128)(2,1)S(1)} collective-permute-done((bf16[4,8,16,256]{3,2,1,0:T(8,128)(2,1)S(1)}, bf16[4,8,16,256]{3,2,1,0:T(8,128)(2,1)S(1)}, u32[]{:S(2)}, u32[]{:S(2)}) %collective-permute-start.9) | collective-permute-done | bytes 262176 | tf_op jit(solution)/shard_map/ppermute | solution.py:496
  90.7 2.4 %spread.1 = f32[4,8,16,1024]{3,2,1,0:T(8,128)} custom-call(s32[22]{0:T(128)S(1)} %pad_add_fusion.info, bf16[4,8,16,256]{3,2,1,0:T(8,128)(2,1)S(1)} %get-tuple-element.66.refs_0_, bf16[4,8,16,256]{3,2,1,0:T(8,128)(2,1)S(1)} %collective-permute-done.7.refs_1_, bf16[4,8,16,256]{3,2,1,0:T(8,128)(2,1)S(1)} %collective-permute-done.8.refs_2_, ...), custom_call_target="tpu_custom_call" | custom-call | flops 4 | bytes 4 | tf_op jit(solution)/shard_map/spread/pallas_call | solution.py:407
  (1 shorter events, 0.0 us)
Async XLA Ops:
  0.6 14.3 %copy-start.4 = (s32[16]{0:T(128)S(1)}, s32[16]{0:T(128)}, u32[]{:S(2)}) copy-start(s32[16]{0:T(128)} %param.11) | copy-start | bytes 196
  0.6 14.3 %copy-start.5 = (s32[4]{0:T(128)S(1)}, s32[4]{0:T(128)}, u32[]{:S(2)}) copy-start(s32[4]{0:T(128)} %param.15) | copy-start | bytes 52
  0.7 19.6 %copy-start.1 = (f32[16,16]{1,0:T(8,128)S(1)}, f32[16,16]{1,0:T(8,128)}, u32[]{:S(2)}) copy-start(f32[16,16]{1,0:T(8,128)} %base_ref.1) | copy-start | bytes 3076
  0.7 19.6 %copy-start.2 = (f32[16,16]{1,0:T(8,128)S(1)}, f32[16,16]{1,0:T(8,128)}, u32[]{:S(2)}) copy-start(f32[16,16]{1,0:T(8,128)} %temp_ref.1) | copy-start | bytes 3076
  15.0 21.3 %copy-start.3 = (s32[640]{0:T(1024)S(1)}, s32[640]{0:T(1024)}, u32[]{:S(2)}) copy-start(s32[640]{0:T(1024)} %param.10) | copy-start | bytes 7684
  15.1 20.6 %all-to-all-start = ((bf16[8,8,16,512]{3,2,1,0:T(8,128)(2,1)}), bf16[8,8,16,512]{3,2,1,0:T(8,128)(2,1)S(1)}, u32[]{:S(2)}, u32[]{:S(2)}) async-start(bf16[8,8,16,512]{3,2,1,0:T(8,128)(2,1)} %legendre.1), calls=%async_computation | async-start | bytes 2097152 | tf_op jit(solution)/shard_map/all_to_all | solution.py:519
  25.0 4.8 %collective-permute-start = (bf16[32,16,256]{2,1,0:T(8,128)(2,1)S(1)}, bf16[32,16,256]{2,1,0:T(8,128)(2,1)S(1)}, u32[]{:S(2)}, u32[]{:S(2)}) collective-permute-start(bf16[32,16,256]{2,1,0:T(8,128)(2,1)S(1)} %get-tuple-element.39), channel_id=1, source_target_pairs={{0,4},{4,0},{8,12},{12,8},{16,20},{20,16},{24,28},{28,24},{1,5},{5... | collective-permute-start | bytes 786440 | tf_op jit(solution)/shard_map/ppermute | solution.py:496
  25.6 4.3 %collective-permute-start.1 = (bf16[256,128]{1,0:T(8,128)(2,1)S(1)}, bf16[256,128]{1,0:T(8,128)(2,1)S(1)}, u32[]{:S(2)}, u32[]{:S(2)}) collective-permute-start(bf16[256,128]{1,0:T(8,128)(2,1)S(1)} %get-tuple-element.40), channel_id=1, source_target_pairs={{0,1},{1,0},{2,3},{3,2},{4,5},{5,4},{6,7},{7,6},{8,9},{9,8},{10,11... | collective-permute-start | bytes 196616 | tf_op jit(solution)/shard_map/ppermute | solution.py:496
  27.2 2.7 %collective-permute-start.2 = (bf16[256,128]{1,0:T(8,128)(2,1)S(1)}, bf16[256,128]{1,0:T(8,128)(2,1)S(1)}, u32[]{:S(2)}, u32[]{:S(2)}) collective-permute-start(bf16[256,128]{1,0:T(8,128)(2,1)S(1)} %get-tuple-element.41), channel_id=1, source_target_pairs={{1,2},{2,1},{5,6},{6,5},{9,10},{10,9},{13,14},{14,13},{17,18},{18,... | collective-permute-start | bytes 196616 | tf_op jit(solution)/shard_map/ppermute | solution.py:496
  35.6 12.5 %collective-permute-start.3 = (bf16[32,16,256]{2,1,0:T(8,128)(2,1)S(1)}, bf16[32,16,256]{2,1,0:T(8,128)(2,1)S(1)}, u32[]{:S(2)}, u32[]{:S(2)}) collective-permute-start(bf16[32,16,256]{2,1,0:T(8,128)(2,1)S(1)} %get-tuple-element.44), channel_id=1, source_target_pairs={{4,8},{8,4},{12,16},{16,12},{20,24},{24,20},{5,9},{9,5},{13,17},{1... | collective-permute-start | bytes 786440 | tf_op jit(solution)/shard_map/ppermute | solution.py:496
  45.5 12.1 %collective-permute-start.6 = (bf16[3,8,16,256]{3,2,1,0:T(8,128)(2,1)S(1)}, bf16[3,8,16,256]{3,2,1,0:T(8,128)(2,1)S(1)}, u32[]{:S(2)}, u32[]{:S(2)}) collective-permute-start(bf16[3,8,16,256]{3,2,1,0:T(8,128)(2,1)S(1)} %get-tuple-element.55), channel_id=1, source_target_pairs={{0,2},{2,0},{1,3},{3,1},{4,6},{6,4},{5,7},{7,5},{8,10},{10,8},{9,1... | collective-permute-start | bytes 589832 | tf_op jit(solution)/shard_map/ppermute | solution.py:496
  48.1 2.2 %copy-start = (bf16[16,32,16,256]{3,2,1,0:T(8,128)(2,1)S(1)}, bf16[16,32,16,256]{3,2,1,0:T(8,128)(2,1)}, u32[]{:S(2)}) copy-start(bf16[16,32,16,256]{3,2,1,0:T(8,128)(2,1)} %refs_0_.7) | copy-start | bytes 12582916
  54.7 9.2 %collective-permute-start.5 = (bf16[3,8,16,256]{3,2,1,0:T(8,128)(2,1)S(1)}, bf16[3,8,16,256]{3,2,1,0:T(8,128)(2,1)S(1)}, u32[]{:S(2)}, u32[]{:S(2)}) collective-permute-start(bf16[3,8,16,256]{3,2,1,0:T(8,128)(2,1)S(1)} %get-tuple-element.54), channel_id=1, source_target_pairs={{0,3},{3,0},{1,2},{2,1},{4,7},{7,4},{5,6},{6,5},{8,11},{11,8},{9,1... | collective-permute-start | bytes 589832 | tf_op jit(solution)/shard_map/ppermute | solution.py:496
  56.0 18.7 %collective-permute-start.4 = (bf16[3,8,16,256]{3,2,1,0:T(8,128)(2,1)S(1)}, bf16[3,8,16,256]{3,2,1,0:T(8,128)(2,1)S(1)}, u32[]{:S(2)}, u32[]{:S(2)}) collective-permute-start(bf16[3,8,16,256]{3,2,1,0:T(8,128)(2,1)S(1)} %get-tuple-element.53), channel_id=1, source_target_pairs={{0,1},{1,0},{2,3},{3,2},{4,5},{5,4},{6,7},{7,6},{8,9},{9,8},{10,11... | collective-permute-start | bytes 589832 | tf_op jit(solution)/shard_map/ppermute | solution.py:496
  61.9 22.4 %collective-permute-start.7 = (bf16[4,8,16,256]{3,2,1,0:T(8,128)(2,1)S(1)}, bf16[4,8,16,256]{3,2,1,0:T(8,128)(2,1)S(1)}, u32[]{:S(2)}, u32[]{:S(2)}) collective-permute-start(bf16[4,8,16,256]{3,2,1,0:T(8,128)(2,1)S(1)} %get-tuple-element.61), channel_id=1, source_target_pairs={{0,2},{2,0},{1,3},{3,1},{4,6},{6,4},{5,7},{7,5},{8,10},{10,8},{9,1... | collective-permute-start | bytes 786440 | tf_op jit(solution)/shard_map/ppermute | solution.py:496
  68.2 16.1 %collective-permute-start.8 = (bf16[4,8,16,256]{3,2,1,0:T(8,128)(2,1)S(1)}, bf16[4,8,16,256]{3,2,1,0:T(8,128)(2,1)S(1)}, u32[]{:S(2)}, u32[]{:S(2)}) collective-permute-start(bf16[4,8,16,256]{3,2,1,0:T(8,128)(2,1)S(1)} %get-tuple-element.62), channel_id=1, source_target_pairs={{0,3},{3,0},{1,2},{2,1},{4,7},{7,4},{5,6},{6,5},{8,11},{11,8},{9,1... | collective-permute-start | bytes 786440 | tf_op jit(solution)/shard_map/ppermute | solution.py:496
  79.1 11.6 %collective-permute-start.9 = (bf16[4,8,16,256]{3,2,1,0:T(8,128)(2,1)S(1)}, bf16[4,8,16,256]{3,2,1,0:T(8,128)(2,1)S(1)}, u32[]{:S(2)}, u32[]{:S(2)}) collective-permute-start(bf16[4,8,16,256]{3,2,1,0:T(8,128)(2,1)S(1)} %get-tuple-element.65), channel_id=1, source_target_pairs={{0,1},{1,0},{2,3},{3,2},{4,5},{5,4},{6,7},{7,6},{8,9},{9,8},{10,11... | collective-permute-start | bytes 786440 | tf_op jit(solution)/shard_map/ppermute | solution.py:496

commit v14 on v12

--- a/solution.py
+++ b/solution.py
@@ -97,8 +97,8 @@
             ],
         ),
         out_shape=[
-            pltpu.VMEM((rows, 2 * waves, LANES), BF16),
-            pltpu.VMEM((rows, 2, turns, waves), F32),
+            pltpu.HBM((rows, 2 * waves, LANES), BF16),
+            pltpu.HBM((rows, 2, turns, waves), F32),
         ],
         compiler_params=pltpu.CompilerParams(vmem_limit_bytes=20 * MIB),
         cost_estimate=cost(rows * waves * LANES * 8, rows * waves * LANES * 4),
@@ -206,7 +206,7 @@
         compiler_params=pltpu.CompilerParams(vmem_limit_bytes=24 * MIB),
         cost_estimate=cost(4 * rows * waves * fields * levels * turns * LANES, 4 * rows * waves * LANES),
         name="synthesis",
-    )(info, recv, *[pltpu.with_memory_space_constraint(v, pltpu.VMEM) for v in (table, twiddle)])
+    )(info, recv, *[pltpu.with_memory_space_constraint(v, pltpu.HBM) for v in (table, twiddle)])
 
 
 def edge_kernel(
@@ -380,6 +380,7 @@
     state_spec = pl.BlockSpec(
         (tracers, some, rows, tile), lambda i, info: (0, (info[ME] ^ k) * steps + i, 0, 0)
     )
+    state = pltpu.with_memory_space_constraint(state, pltpu.HBM)
     operands = [state, *halos, grid, react]
     in_specs = [
         state_spec,

time: 95.1 us -> 93.1 us (0.979); the launches traced: 93.3 us -> 92.7 us
  Pallas kernels: 48.6 us -> 55.3 us
  local copies, waits for them, and re-layouts: 5.24 us -> 0.02 us
  starting transfers between devices: 29.8 us -> 26.5 us
  waiting for transfers between devices: 8.78 us -> 9.98 us
    unnamed x16 -> x10, local copies, waits for them, and re-layouts: 5.24 us -> 0.02 us
    pallas_call x4, Pallas kernels: 17.4 us -> 21.2 us  [chemistry(): pl.pallas_call(functools.partial(chem_kernel, scale, k), grid_spec=pltpu....]
    ppermute x10, starting transfers between devices: 24.7 us -> 21.4 us  [exchange(): lax.ppermute(value, axis, [p for a, b in pairs for p in ((a, b), (b, a))])]
    pallas_call x1, Pallas kernels: 5.12 us -> 6.95 us  [synthesis(): pl.pallas_call(synth_kernel, grid_spec=pltpu.PrefetchScalarGridSpec(num_s...]
    all_to_all x1, waiting for transfers between devices: 0.84 us -> 2.06 us  [body(): recv = lax.all_to_all(sent, 'lat', split_axis=0, concat_axis=0, tiled=True)]
    pallas_call x1, Pallas kernels: 4.59 us -> 5.73 us  [tables(): pl.pallas_call(functools.partial(table_kernel, info.shape[0] - rows), gri...]
  transfers between devices with their start and end apart: 11 -> 11, of which waited for: 2 -> 3; matrix products, arithmetic and copies ran while one was open for 0% -> 0% of each run, Pallas kernels for 34% -> 42%
where the time goes in v14:
time: 93.1 us; the launch traced here: 92.7 us
  Pallas kernels  55.3 us (59%)
  starting transfers between devices  26.5 us (28%)
  waiting for transfers between devices  9.98 us (11%)
    ppermute x10, starting transfers between devices, exchange(): lax.ppermute(value, axis, [p for a, b in pairs for p in ((a, b), (b, a))])  21.4 us
    pallas_call x4, Pallas kernels, chemistry(): pl.pallas_call(functools.partial(chem_kernel, scale, k), grid_spec=pltpu....  21.2 us
    pallas_call x1, Pallas kernels, legendre_sums(): pl.pallas_call(legendre_kernel, grid=(share // block,), in_specs=[pl.Bloc...  14.3 us
    ppermute x10, waiting for transfers between devices, exchange(): lax.ppermute(value, axis, [p for a, b in pairs for p in ((a, b), (b, a))])  7.92 us
    pallas_call x1, Pallas kernels, synthesis(): pl.pallas_call(synth_kernel, grid_spec=pltpu.PrefetchScalarGridSpec(num_s...  6.95 us
    pallas_call x1, Pallas kernels, tables(): pl.pallas_call(functools.partial(table_kernel, info.shape[0] - rows), gri...  5.73 us
    all_to_all x1, starting transfers between devices, body(): recv = lax.all_to_all(sent, 'lat', split_axis=0, concat_axis=0, tiled=True)  5.17 us
    pallas_call x1, Pallas kernels, edges(): pl.pallas_call(edge_kernel, grid_spec=pltpu.PrefetchScalarGridSpec(num_sc...  4.76 us
  transfers between devices with their start and end apart: 11, of which 3 were waited for; matrix products, arithmetic and copies ran while one was open for 0% of the time, Pallas kernels for 42%

profile of v14, /device:TPU:0, one launch (start us, length us, event | category | flops | bytes accessed | tf_op | source)
XLA Modules:
  0.0 92.7 jit_solution(14742829827386724017)
XLA Ops:
  0.6 0.0 copy-start.3
  0.6 0.0 copy-start.4
  0.7 0.0 copy-start
  0.7 0.0 copy-start.1
  0.7 14.3 %legendre.1 = bf16[8,8,16,512]{3,2,1,0:T(8,128)(2,1)} custom-call(bf16[6,8,80,1280]{3,2,1,0:T(8,128)(2,1)} %spectral_ref.1, bf16[80,1280,128]{2,1,0:T(8,128)(2,1)} %legendre_ref.1), custom_call_target="tpu_custom_call" | custom-call | flops 1258291200 | bytes 36044800 | tf_op jit(solution)/shard_map/legendre/pallas_call | solution.py:507
  15.0 0.0 copy-start.2
  15.0 0.0 copy-done.3
  15.0 0.0 copy-done.4
  15.0 0.1 pad_add_fusion.info
  15.1 5.2 %all-to-all-start = ((bf16[8,8,16,512]{3,2,1,0:T(8,128)(2,1)}), bf16[8,8,16,512]{3,2,1,0:T(8,128)(2,1)S(1)}, u32[]{:S(2)}, u32[]{:S(2)}) async-start(bf16[8,8,16,512]{3,2,1,0:T(8,128)(2,1)} %legendre.1), calls=%async_computation | async-start | bytes 2097152 | tf_op jit(solution)/shard_map/all_to_all | solution.py:550
  20.2 0.0 copy-done
  20.2 0.0 copy-done.1
  20.3 4.8 %edges.1 = (bf16[32,16,256]{2,1,0:T(8,128)(2,1)S(1)}, bf16[32,16,256]{2,1,0:T(8,128)(2,1)S(1)}, bf16[256,128]{1,0:T(8,128)(2,1)S(1)}, bf16[256,128]{1,0:T(8,128)(2,1)S(1)}, bf16[512,512]{1,0:T(8,128)(2,1)S(1)}) custom-call(s32[22]{0:T(128)S(1)} %pad_add_fusion.info, bf16[16,32,16,256]{3,2,1,0:T(8,128)(2,1)} %refs_0_.7, f32[16,16]{1,0:T(8,128)S(1)} %copy-done, ...), custom_call_target="tpu_custom_call" | custom-call | flops 268435456 | bytes 4194304 | tf_op jit(solution)/shard_map/edges/pallas_call | solution.py:279
  25.0 0.6 collective-permute-start
  25.6 1.6 %collective-permute-start.1 = (bf16[256,128]{1,0:T(8,128)(2,1)S(1)}, bf16[256,128]{1,0:T(8,128)(2,1)S(1)}, u32[]{:S(2)}, u32[]{:S(2)}) collective-permute-start(bf16[256,128]{1,0:T(8,128)(2,1)S(1)} %get-tuple-element.50), channel_id=1, source_target_pairs={{0,1},{1,0},{2,3},{3,2},{4,5},{5,4},{6,7},{7,6},{8,9},{9,8},{10,11... | collective-permute-start | bytes 196616 | tf_op jit(solution)/shard_map/ppermute | solution.py:527
  27.2 0.7 collective-permute-start.2
  27.8 0.0 copy-done.2
  27.8 5.7 %tables.1 = (bf16[16,1280,128]{2,1,0:T(8,128)(2,1)}, f32[16,2,8,640]{3,2,1,0:T(8,128)}) custom-call(s32[22]{0:T(128)S(1)} %pad_add_fusion.info, s32[1,640]{1,0:T(1,128)S(1)} %broadcast_in_dim.3.waves_ref), custom_call_target="tpu_custom_call" | custom-call | flops 10485760 | bytes 5242880 | tf_op jit(solution)/shard_map/tables/pallas_call | solution.py:88
  33.6 0.0 collective-permute-done.1.refs_3_
  33.6 0.0 collective-permute-done.2.refs_4_
  33.6 0.0 collective-permute-done.refs_1_
  33.6 2.1 %all-to-all-done.recv_ref = bf16[8,8,16,512]{3,2,1,0:T(8,128)(2,1)S(1)} async-done(((bf16[8,8,16,512]{3,2,1,0:T(8,128)(2,1)}), bf16[8,8,16,512]{3,2,1,0:T(8,128)(2,1)S(1)}, u32[]{:S(2)}, u32[]{:S(2)}) %all-to-all-start) | async-done | bytes 1048608 | tf_op jit(solution)/shard_map/all_to_all | solution.py:550
  35.6 0.7 collective-permute-start.3
  36.3 7.0 %synthesis.1 = (bf16[3,8,16,256]{3,2,1,0:T(8,128)(2,1)S(1)}, bf16[3,8,16,256]{3,2,1,0:T(8,128)(2,1)S(1)}, bf16[3,8,16,256]{3,2,1,0:T(8,128)(2,1)S(1)}, bf16[3,8,16,256]{3,2,1,0:T(8,128)(2,1)S(1)}) custom-call(s32[22]{0:T(128)S(1)} %pad_add_fusion.info, bf16[8,8,16,512]{3,2,1,0:T(8,128)(2,1)S(1)} %all-to-all-done.recv_ref, ...), custom_call_target="tpu_custom_call" | custom-call | flops 1006632960 | bytes 5242880 | tf_op jit(solution)/shard_map/synthesis/pallas_call | solution.py:189
  43.3 2.7 %collective-permute-start.6 = (bf16[3,8,16,256]{3,2,1,0:T(8,128)(2,1)S(1)}, bf16[3,8,16,256]{3,2,1,0:T(8,128)(2,1)S(1)}, u32[]{:S(2)}, u32[]{:S(2)}) collective-permute-start(bf16[3,8,16,256]{3,2,1,0:T(8,128)(2,1)S(1)} %get-tuple-element.67), channel_id=1, source_target_pairs={{0,2},{2,0},{1,3},{3,1},{4,6},{6,4},{5,7},{7,5},{8,10},{10,8},{9,1... | collective-permute-start | bytes 589832 | tf_op jit(solution)/shard_map/ppermute | solution.py:527
  45.9 0.0 collective-permute-done.3.refs_2_
  45.9 5.3 %chemistry.4 = (bf16[16,32,16,256]{3,2,1,0:T(8,128)(2,1)}, bf16[4,8,16,256]{3,2,1,0:T(8,128)(2,1)S(1)}) custom-call(s32[22]{0:T(128)S(1)} %pad_add_fusion.info, bf16[16,32,16,256]{3,2,1,0:T(8,128)(2,1)} %refs_0_.7, bf16[32,16,256]{2,1,0:T(8,128)(2,1)S(1)} %collective-permute-done.refs_1_, bf16[32,16,256]{2,1,0:T(8,128)(2,1)S(1)} %collective-permute-done.3.refs_2_, ...), custom_call_target="tpu_custom_call" | custom-call | flops 524288 | bytes 2048 | tf_op jit(solution)/shard_map/chemistry/pallas_call | solution.py:399
  51.2 2.1 %collective-permute-start.5 = (bf16[3,8,16,256]{3,2,1,0:T(8,128)(2,1)S(1)}, bf16[3,8,16,256]{3,2,1,0:T(8,128)(2,1)S(1)}, u32[]{:S(2)}, u32[]{:S(2)}) collective-permute-start(bf16[3,8,16,256]{3,2,1,0:T(8,128)(2,1)S(1)} %get-tuple-element.66), channel_id=1, source_target_pairs={{0,3},{3,0},{1,2},{2,1},{4,7},{7,4},{5,6},{6,5},{8,11},{11,8},{9,1... | collective-permute-start | bytes 589832 | tf_op jit(solution)/shard_map/ppermute | solution.py:527
  53.4 0.0 collective-permute-start.4
  53.4 1.6 %collective-permute-done.6.refs_5_ = bf16[3,8,16,256]{3,2,1,0:T(8,128)(2,1)S(1)} collective-permute-done((bf16[3,8,16,256]{3,2,1,0:T(8,128)(2,1)S(1)}, bf16[3,8,16,256]{3,2,1,0:T(8,128)(2,1)S(1)}, u32[]{:S(2)}, u32[]{:S(2)}) %collective-permute-start.6) | collective-permute-done | bytes 196640 | tf_op jit(solution)/shard_map/ppermute | solution.py:527
  55.0 5.3 %chemistry.5 = (bf16[16,32,16,256]{3,2,1,0:T(8,128)(2,1)}, bf16[4,8,16,256]{3,2,1,0:T(8,128)(2,1)S(1)}) custom-call(s32[22]{0:T(128)S(1)} %pad_add_fusion.info, bf16[16,32,16,256]{3,2,1,0:T(8,128)(2,1)} %refs_0_.7, bf16[32,16,256]{2,1,0:T(8,128)(2,1)S(1)} %collective-permute-done.refs_1_, ...), custom_call_target="tpu_custom_call", output_to_operand_aliasing={{0}: (8, {})} | custom-call | flops 524288 | bytes 2048 | tf_op jit(solution)/shard_map/chemistry/pallas_call | solution.py:399
  60.3 0.6 collective-permute-start.7
  60.9 0.0 collective-permute-done.5.refs_5_
  60.9 5.3 %chemistry.6 = (bf16[16,32,16,256]{3,2,1,0:T(8,128)(2,1)}, bf16[4,8,16,256]{3,2,1,0:T(8,128)(2,1)S(1)}) custom-call(s32[22]{0:T(128)S(1)} %pad_add_fusion.info, bf16[16,32,16,256]{3,2,1,0:T(8,128)(2,1)} %refs_0_.7, bf16[32,16,256]{2,1,0:T(8,128)(2,1)S(1)} %collective-permute-done.refs_1_, ...), custom_call_target="tpu_custom_call", output_to_operand_aliasing={{0}: (8, {})} | custom-call | flops 524288 | bytes 2048 | tf_op jit(solution)/shard_map/chemistry/pallas_call | solution.py:399
  66.2 7.4 %collective-permute-start.8 = (bf16[4,8,16,256]{3,2,1,0:T(8,128)(2,1)S(1)}, bf16[4,8,16,256]{3,2,1,0:T(8,128)(2,1)S(1)}, u32[]{:S(2)}, u32[]{:S(2)}) collective-permute-start(bf16[4,8,16,256]{3,2,1,0:T(8,128)(2,1)S(1)} %get-tuple-element.74), channel_id=1, source_target_pairs={{0,3},{3,0},{1,2},{2,1},{4,7},{7,4},{5,6},{6,5},{8,11},{11,8},{9,1... | collective-permute-start | bytes 786440 | tf_op jit(solution)/shard_map/ppermute | solution.py:527
  73.6 0.0 collective-permute-done.4.refs_5_
  73.6 5.3 %chemistry.7 = (bf16[16,32,16,256]{3,2,1,0:T(8,128)(2,1)}, bf16[4,8,16,256]{3,2,1,0:T(8,128)(2,1)S(1)}) custom-call(s32[22]{0:T(128)S(1)} %pad_add_fusion.info, bf16[16,32,16,256]{3,2,1,0:T(8,128)(2,1)} %refs_0_.7, bf16[32,16,256]{2,1,0:T(8,128)(2,1)S(1)} %collective-permute-done.refs_1_, ...), custom_call_target="tpu_custom_call", output_to_operand_aliasing={{0}: (8, {})} | custom-call | flops 524288 | bytes 2048 | tf_op jit(solution)/shard_map/chemistry/pallas_call | solution.py:399
  78.9 5.1 %collective-permute-start.9 = (bf16[4,8,16,256]{3,2,1,0:T(8,128)(2,1)S(1)}, bf16[4,8,16,256]{3,2,1,0:T(8,128)(2,1)S(1)}, u32[]{:S(2)}, u32[]{:S(2)}) collective-permute-start(bf16[4,8,16,256]{3,2,1,0:T(8,128)(2,1)S(1)} %get-tuple-element.77), channel_id=1, source_target_pairs={{0,1},{1,0},{2,3},{3,2},{4,5},{5,4},{6,7},{7,6},{8,9},{9,8},{10,11... | collective-permute-start | bytes 786440 | tf_op jit(solution)/shard_map/ppermute | solution.py:527
  84.0 0.0 collective-permute-done.7.refs_1_
  84.0 0.0 collective-permute-done.8.refs_2_
  84.0 6.3 %collective-permute-done.9.refs_3_ = bf16[4,8,16,256]{3,2,1,0:T(8,128)(2,1)S(1)} collective-permute-done((bf16[4,8,16,256]{3,2,1,0:T(8,128)(2,1)S(1)}, bf16[4,8,16,256]{3,2,1,0:T(8,128)(2,1)S(1)}, u32[]{:S(2)}, u32[]{:S(2)}) %collective-permute-start.9) | collective-permute-done | bytes 262176 | tf_op jit(solution)/shard_map/ppermute | solution.py:527
  90.3 2.4 %spread.1 = f32[4,8,16,1024]{3,2,1,0:T(8,128)} custom-call(s32[22]{0:T(128)S(1)} %pad_add_fusion.info, bf16[4,8,16,256]{3,2,1,0:T(8,128)(2,1)S(1)} %get-tuple-element.78.refs_0_, bf16[4,8,16,256]{3,2,1,0:T(8,128)(2,1)S(1)} %collective-permute-done.7.refs_1_, bf16[4,8,16,256]{3,2,1,0:T(8,128)(2,1)S(1)} %collective-permute-done.8.refs_2_, ...), custom_call_target="tpu_custom_call" | custom-call | flops 4 | bytes 4 | tf_op jit(solution)/shard_map/spread/pallas_call | solution.py:438
  (1 shorter events, 0.0 us)
Async XLA Ops:
  0.6 14.3 %copy-start.3 = (s32[16]{0:T(128)S(1)}, s32[16]{0:T(128)}, u32[]{:S(2)}) copy-start(s32[16]{0:T(128)} %param.11) | copy-start | bytes 196
  0.6 14.3 %copy-start.4 = (s32[4]{0:T(128)S(1)}, s32[4]{0:T(128)}, u32[]{:S(2)}) copy-start(s32[4]{0:T(128)} %param.15) | copy-start | bytes 52
  0.7 19.6 %copy-start = (f32[16,16]{1,0:T(8,128)S(1)}, f32[16,16]{1,0:T(8,128)}, u32[]{:S(2)}) copy-start(f32[16,16]{1,0:T(8,128)} %base_ref.1) | copy-start | bytes 3076
  0.7 19.6 %copy-start.1 = (f32[16,16]{1,0:T(8,128)S(1)}, f32[16,16]{1,0:T(8,128)}, u32[]{:S(2)}) copy-start(f32[16,16]{1,0:T(8,128)} %temp_ref.1) | copy-start | bytes 3076
  15.0 12.8 %copy-start.2 = (s32[640]{0:T(1024)S(1)}, s32[640]{0:T(1024)}, u32[]{:S(2)}) copy-start(s32[640]{0:T(1024)} %param.10) | copy-start | bytes 7684
  15.1 20.6 %all-to-all-start = ((bf16[8,8,16,512]{3,2,1,0:T(8,128)(2,1)}), bf16[8,8,16,512]{3,2,1,0:T(8,128)(2,1)S(1)}, u32[]{:S(2)}, u32[]{:S(2)}) async-start(bf16[8,8,16,512]{3,2,1,0:T(8,128)(2,1)} %legendre.1), calls=%async_computation | async-start | bytes 2097152 | tf_op jit(solution)/shard_map/all_to_all | solution.py:550
  25.0 8.6 %collective-permute-start = (bf16[32,16,256]{2,1,0:T(8,128)(2,1)S(1)}, bf16[32,16,256]{2,1,0:T(8,128)(2,1)S(1)}, u32[]{:S(2)}, u32[]{:S(2)}) collective-permute-start(bf16[32,16,256]{2,1,0:T(8,128)(2,1)S(1)} %get-tuple-element.49), channel_id=1, source_target_pairs={{0,4},{4,0},{8,12},{12,8},{16,20},{20,16},{24,28},{28,24},{1,5},{5... | collective-permute-start | bytes 786440 | tf_op jit(solution)/shard_map/ppermute | solution.py:527
  25.6 8.0 %collective-permute-start.1 = (bf16[256,128]{1,0:T(8,128)(2,1)S(1)}, bf16[256,128]{1,0:T(8,128)(2,1)S(1)}, u32[]{:S(2)}, u32[]{:S(2)}) collective-permute-start(bf16[256,128]{1,0:T(8,128)(2,1)S(1)} %get-tuple-element.50), channel_id=1, source_target_pairs={{0,1},{1,0},{2,3},{3,2},{4,5},{5,4},{6,7},{7,6},{8,9},{9,8},{10,11... | collective-permute-start | bytes 196616 | tf_op jit(solution)/shard_map/ppermute | solution.py:527
  27.2 6.4 %collective-permute-start.2 = (bf16[256,128]{1,0:T(8,128)(2,1)S(1)}, bf16[256,128]{1,0:T(8,128)(2,1)S(1)}, u32[]{:S(2)}, u32[]{:S(2)}) collective-permute-start(bf16[256,128]{1,0:T(8,128)(2,1)S(1)} %get-tuple-element.51), channel_id=1, source_target_pairs={{1,2},{2,1},{5,6},{6,5},{9,10},{10,9},{13,14},{14,13},{17,18},{18,... | collective-permute-start | bytes 196616 | tf_op jit(solution)/shard_map/ppermute | solution.py:527
  35.6 10.3 %collective-permute-start.3 = (bf16[32,16,256]{2,1,0:T(8,128)(2,1)S(1)}, bf16[32,16,256]{2,1,0:T(8,128)(2,1)S(1)}, u32[]{:S(2)}, u32[]{:S(2)}) collective-permute-start(bf16[32,16,256]{2,1,0:T(8,128)(2,1)S(1)} %get-tuple-element.54), channel_id=1, source_target_pairs={{4,8},{8,4},{12,16},{16,12},{20,24},{24,20},{5,9},{9,5},{13,17},{1... | collective-permute-start | bytes 786440 | tf_op jit(solution)/shard_map/ppermute | solution.py:527
  43.3 11.7 %collective-permute-start.6 = (bf16[3,8,16,256]{3,2,1,0:T(8,128)(2,1)S(1)}, bf16[3,8,16,256]{3,2,1,0:T(8,128)(2,1)S(1)}, u32[]{:S(2)}, u32[]{:S(2)}) collective-permute-start(bf16[3,8,16,256]{3,2,1,0:T(8,128)(2,1)S(1)} %get-tuple-element.67), channel_id=1, source_target_pairs={{0,2},{2,0},{1,3},{3,1},{4,6},{6,4},{5,7},{7,5},{8,10},{10,8},{9,1... | collective-permute-start | bytes 589832 | tf_op jit(solution)/shard_map/ppermute | solution.py:527
  51.2 9.7 %collective-permute-start.5 = (bf16[3,8,16,256]{3,2,1,0:T(8,128)(2,1)S(1)}, bf16[3,8,16,256]{3,2,1,0:T(8,128)(2,1)S(1)}, u32[]{:S(2)}, u32[]{:S(2)}) collective-permute-start(bf16[3,8,16,256]{3,2,1,0:T(8,128)(2,1)S(1)} %get-tuple-element.66), channel_id=1, source_target_pairs={{0,3},{3,0},{1,2},{2,1},{4,7},{7,4},{5,6},{6,5},{8,11},{11,8},{9,1... | collective-permute-start | bytes 589832 | tf_op jit(solution)/shard_map/ppermute | solution.py:527
  53.4 20.3 %collective-permute-start.4 = (bf16[3,8,16,256]{3,2,1,0:T(8,128)(2,1)S(1)}, bf16[3,8,16,256]{3,2,1,0:T(8,128)(2,1)S(1)}, u32[]{:S(2)}, u32[]{:S(2)}) collective-permute-start(bf16[3,8,16,256]{3,2,1,0:T(8,128)(2,1)S(1)} %get-tuple-element.65), channel_id=1, source_target_pairs={{0,1},{1,0},{2,3},{3,2},{4,5},{5,4},{6,7},{7,6},{8,9},{9,8},{10,11... | collective-permute-start | bytes 589832 | tf_op jit(solution)/shard_map/ppermute | solution.py:527
  60.3 23.7 %collective-permute-start.7 = (bf16[4,8,16,256]{3,2,1,0:T(8,128)(2,1)S(1)}, bf16[4,8,16,256]{3,2,1,0:T(8,128)(2,1)S(1)}, u32[]{:S(2)}, u32[]{:S(2)}) collective-permute-start(bf16[4,8,16,256]{3,2,1,0:T(8,128)(2,1)S(1)} %get-tuple-element.73), channel_id=1, source_target_pairs={{0,2},{2,0},{1,3},{3,1},{4,6},{6,4},{5,7},{7,5},{8,10},{10,8},{9,1... | collective-permute-start | bytes 786440 | tf_op jit(solution)/shard_map/ppermute | solution.py:527
  66.2 17.8 %collective-permute-start.8 = (bf16[4,8,16,256]{3,2,1,0:T(8,128)(2,1)S(1)}, bf16[4,8,16,256]{3,2,1,0:T(8,128)(2,1)S(1)}, u32[]{:S(2)}, u32[]{:S(2)}) collective-permute-start(bf16[4,8,16,256]{3,2,1,0:T(8,128)(2,1)S(1)} %get-tuple-element.74), channel_id=1, source_target_pairs={{0,3},{3,0},{1,2},{2,1},{4,7},{7,4},{5,6},{6,5},{8,11},{11,8},{9,1... | collective-permute-start | bytes 786440 | tf_op jit(solution)/shard_map/ppermute | solution.py:527
  78.9 11.4 %collective-permute-start.9 = (bf16[4,8,16,256]{3,2,1,0:T(8,128)(2,1)S(1)}, bf16[4,8,16,256]{3,2,1,0:T(8,128)(2,1)S(1)}, u32[]{:S(2)}, u32[]{:S(2)}) collective-permute-start(bf16[4,8,16,256]{3,2,1,0:T(8,128)(2,1)S(1)} %get-tuple-element.77), channel_id=1, source_target_pairs={{0,1},{1,0},{2,3},{3,2},{4,5},{5,4},{6,7},{7,6},{8,9},{9,8},{10,11... | collective-permute-start | bytes 786440 | tf_op jit(solution)/shard_map/ppermute | solution.py:527

commit v15 on v14

--- a/solution.py
+++ b/solution.py
@@ -126,32 +126,46 @@
     return out
 
 
-def synth_kernel(info, recv_ref, table_ref, twiddle_ref, *refs):
-    *out_refs, coef, grid = refs
+def synth_kernel(info, recv_ref, table_hbm, twiddle_hbm, *refs):
+    *out_refs, coef, grid, table_ref, twiddle_ref, sems = refs
     sources, levels, rows, _ = recv_ref.shape
     fields, waves = coef.shape[0] // 2, coef.shape[1] * LANES
     share = waves // sources
-    each, _, turns = twiddle_ref.shape[:3]
+    turns = twiddle_ref.shape[2]
+    steps = sems.shape[1]
+    each = rows // steps
     pitch = rows + 1
-    step = pl.program_id(0)
-
-    @pl.when(step == 0)
-    def _():
-        def level(l, carry):
-            values = [recv_ref[s, l].astype(F32) for s in range(sources)]
-            for r in range(2 * fields):
-                windows = [
-                    (values[s], r * share, share, s * share) for s in range(sources)
-                ]
-                for v, part in enumerate(place(windows, waves)):
-                    coef[r, v, pl.ds(l * pitch, rows), :] = part
-            return carry
-
-        lax.fori_loop(0, levels, level, 0)
-
-    for k in range(each):
-        j = step * each + k
-
+
+    def copies(step):
+        some = pl.ds(step * each, each)
+        pairs = ((table_hbm, table_ref), (twiddle_hbm, twiddle_ref))
+        return [
+            pltpu.make_async_copy(src.at[some], dst.at[some], sems.at[i, step])
+            for i, (src, dst) in enumerate(pairs)
+        ]
+
+    for step in range(steps):
+        for copy in copies(step):
+            copy.start()
+
+    def level(l, carry):
+        values = [recv_ref[s, l].astype(F32) for s in range(sources)]
+        for r in range(2 * fields):
+            windows = [(values[s], r * share, share, s * share) for s in range(sources)]
+            for v, part in enumerate(place(windows, waves)):
+                coef[r, v, pl.ds(l * pitch, rows), :] = part
+        return carry
+
+    lax.fori_loop(0, levels, level, 0)
+
+    def some_rows(step, carry):
+        for copy in copies(step):
+            copy.wait()
+        for k in range(each):
+            one_row(step * each + k)
+        return carry
+
+    def one_row(j):
         def own_row(r):
             parts = [coef[r, v, pl.ds(j, levels, stride=pitch), :] for v in range(waves // LANES)]
             return jnp.concatenate(parts, axis=1)
@@ -159,25 +173,24 @@
         values = [own_row(r) for r in range(2 * fields)]
         real, imag = [], []
         for t in range(turns):
-            c, s = twiddle_ref[k, 0, t : t + 1], twiddle_ref[k, 1, t : t + 1]
+            c, s = twiddle_ref[j, 0, t : t + 1], twiddle_ref[j, 1, t : t + 1]
             for f in range(fields):
                 re, im = values[2 * f], values[2 * f + 1]
                 real.append(re * c - im * s)
                 imag.append(re * s + im * c)
         both = [jnp.concatenate(part, axis=0).astype(BF16) for part in (real, imag)]
-        result = dot(jnp.concatenate(both, axis=1), table_ref[k], ((1,), (0,)))
+        result = dot(jnp.concatenate(both, axis=1), table_ref[j], ((1,), (0,)))
         grid[pl.ds(j, turns * fields * levels, stride=pitch), :] = result
 
-    @pl.when(step == pl.num_programs(0) - 1)
-    def _():
-        tiles = turns // len(out_refs)
-        for k, out_ref in enumerate(out_refs):
-            for t in range(tiles):
-                for f in range(fields):
-                    start = (((info[ME] ^ k) * tiles + t) * fields + f) * levels
-                    for l in range(levels):
-                        block = grid[pl.ds((start + l) * pitch, rows), :].astype(BF16)
-                        out_ref[f, l, :, t * LANES : (t + 1) * LANES] = block
+    lax.fori_loop(0, steps, some_rows, 0)
+    tiles = turns // len(out_refs)
+    for k, out_ref in enumerate(out_refs):
+        for t in range(tiles):
+            for f in range(fields):
+                start = (((info[ME] ^ k) * tiles + t) * fields + f) * levels
+                for l in range(levels):
+                    block = grid[pl.ds((start + l) * pitch, rows), :].astype(BF16)
+                    out_ref[f, l, :, t * LANES : (t + 1) * LANES] = block
 
 
 def synthesis(recv, table, twiddle, info, dests, tile):
@@ -190,16 +203,19 @@
         synth_kernel,
         grid_spec=pltpu.PrefetchScalarGridSpec(
             num_scalar_prefetch=1,
-            grid=(rows // each,),
+            grid=(1,),
             in_specs=[
                 pl.BlockSpec(recv.shape, lambda j, info: (0, 0, 0, 0)),
-                pl.BlockSpec((each, 2 * waves, LANES), lambda j, info: (j, 0, 0)),
-                pl.BlockSpec((each, 2, turns, waves), lambda j, info: (j, 0, 0, 0)),
+                pl.BlockSpec(memory_space=pl.ANY),
+                pl.BlockSpec(memory_space=pl.ANY),
             ],
             out_specs=[pl.BlockSpec(shape, lambda j, info: (0, 0, 0, 0))] * dests,
             scratch_shapes=[
                 pltpu.VMEM((2 * fields, waves // LANES, levels * (rows + 1), LANES), F32),
                 pltpu.VMEM((turns * fields * levels * (rows + 1), LANES), F32),
+                pltpu.VMEM(table.shape, BF16),
+                pltpu.VMEM(twiddle.shape, F32),
+                pltpu.SemaphoreType.DMA((2, rows // each)),
             ],
         ),
         out_shape=[jax.ShapeDtypeStruct(shape, BF16)] * dests,
@@ -424,30 +440,45 @@
     )(info, *operands)
 
 
-def spread_kernel(order, info, *refs):
-    *recv_refs, out_ref = refs
-    tile = recv_refs[0].shape[3]
-    for k, recv_ref in zip(order, recv_refs):
-        start = pl.multiple_of((info[ME] ^ k) * tile, LANES)
-        out_ref[:, :, :, pl.ds(start, tile)] = recv_ref[...].astype(F32)
-
-
-def spread(parts, order, info):
+def spread(parts, order, info, tiles, before):
     actives, own, rows, tile = parts[0].shape
-    wide = len(parts) * tile
+    count = len(order)
+    operands, aliases = list(parts), {}
+    in_specs = [pl.BlockSpec(parts[0].shape, lambda i, info: (0, 0, 0, 0))] * count
+    if before is not None:
+        operands.append(before)
+        in_specs.append(pl.BlockSpec(memory_space=pl.ANY))
+        aliases = {1 + count: 0}
+
+    def partner(i):
+        k = order[0]
+        for at in range(1, count):
+            k = jnp.where(i == at, order[at], k)
+        return k
+
+    def kernel(info, *refs):
+        for at in range(count):
+
+            @pl.when(pl.program_id(0) == at)
+            def _():
+                refs[-1][...] = refs[at][...].astype(F32)
+
     return pl.pallas_call(
-        functools.partial(spread_kernel, order),
+        kernel,
         grid_spec=pltpu.PrefetchScalarGridSpec(
             num_scalar_prefetch=1,
-            grid=(actives,),
-            in_specs=[pl.BlockSpec((1, own, rows, tile), lambda a, info: (a, 0, 0, 0))] * len(parts),
-            out_specs=pl.BlockSpec((1, own, rows, wide), lambda a, info: (a, 0, 0, 0)),
+            grid=(count,),
+            in_specs=in_specs,
+            out_specs=pl.BlockSpec(
+                (actives, own, rows, tile), lambda i, info: (0, 0, 0, info[ME] ^ partner(i))
+            ),
         ),
-        out_shape=jax.ShapeDtypeStruct((actives, own, rows, wide), F32),
-        compiler_params=pltpu.CompilerParams(vmem_limit_bytes=8 * MIB),
+        out_shape=jax.ShapeDtypeStruct((actives, own, rows, tiles * tile), F32),
+        input_output_aliases=aliases,
+        compiler_params=pltpu.CompilerParams(vmem_limit_bytes=12 * MIB),
         cost_estimate=cost(actives, actives),
         name="spread",
-    )(info, *parts)
+    )(info, *operands)
 
 
 def legendre_kernel(spectral_ref, legendre_ref, out_ref, rows_of, sums):
@@ -580,11 +611,11 @@
             rest = late + inner
             held, active[0] = lax.optimization_barrier(([grids[i] for i in rest], active[0]))
             moved |= {i: send(value, i) for i, value in zip(rest, held)}
-    order = [0] + soon + late + inner
-    through = lax.optimization_barrier([active[k] for k in soon + late])
-    active |= zip(soon + late, through)
-    active = dict(zip(order, lax.optimization_barrier([active[k] for k in order])))
-    return new, spread([active[k] for k in order], order, info)
+    early, last = [0] + soon, late + inner
+    spreaded = spread([active[k] for k in early], early, info, tiles, None)
+    through = lax.optimization_barrier([active[k] for k in late])
+    parts = lax.optimization_barrier(through + [active[k] for k in inner])
+    return new, spread(parts, last, info, tiles, spreaded)
 
 
 def solution(mesh):

time: 93.1 us -> 90.6 us (0.973)
  waiting for transfers between devices: 9.98 us -> 8.41 us
    pallas_call x1, Pallas kernels: 6.95 us -> 5.36 us  [synthesis(): pl.pallas_call(synth_kernel, grid_spec=pltpu.PrefetchScalarGridSpec(num_s...]
    ppermute x10, waiting for transfers between devices: 7.92 us -> 6.35 us  [exchange(): lax.ppermute(value, axis, [p for a, b in pairs for p in ((a, b), (b, a))])]
    pallas_call x1 -> x2, Pallas kernels: 2.41 us -> 3.16 us  [spread(): pl.pallas_call(kernel, grid_spec=pltpu.PrefetchScalarGridSpec(num_scalar_...]
  transfers between devices with their start and end apart: 11 -> 11, of which waited for: 3 -> 3; matrix products, arithmetic and copies ran while one was open for 0% -> 0% of each run, Pallas kernels for 42% -> 43%
where the time goes in v15:
time: 90.6 us; the launch traced here: 90.3 us
  Pallas kernels  54.5 us (60%)
  starting transfers between devices  26.5 us (29%)
  waiting for transfers between devices  8.41 us (9%)
    ppermute x10, starting transfers between devices, exchange(): lax.ppermute(value, axis, [p for a, b in pairs for p in ((a, b), (b, a))])  21.4 us
    pallas_call x4, Pallas kernels, chemistry(): pl.pallas_call(functools.partial(chem_kernel, scale, k), grid_spec=pltpu....  21.2 us
    pallas_call x1, Pallas kernels, legendre_sums(): pl.pallas_call(legendre_kernel, grid=(share // block,), in_specs=[pl.Bloc...  14.3 us
    ppermute x10, waiting for transfers between devices, exchange(): lax.ppermute(value, axis, [p for a, b in pairs for p in ((a, b), (b, a))])  6.35 us
    pallas_call x1, Pallas kernels, tables(): pl.pallas_call(functools.partial(table_kernel, info.shape[0] - rows), gri...  5.73 us
    pallas_call x1, Pallas kernels, synthesis(): pl.pallas_call(synth_kernel, grid_spec=pltpu.PrefetchScalarGridSpec(num_s...  5.36 us
    all_to_all x1, starting transfers between devices, body(): recv = lax.all_to_all(sent, 'lat', split_axis=0, concat_axis=0, tiled=True)  5.17 us
    pallas_call x1, Pallas kernels, edges(): pl.pallas_call(edge_kernel, grid_spec=pltpu.PrefetchScalarGridSpec(num_sc...  4.76 us
  transfers between devices with their start and end apart: 11, of which 3 were waited for; matrix products, arithmetic and copies ran while one was open for 0% of the time, Pallas kernels for 43%

profile of v15, /device:TPU:0, one launch (start us, length us, event | category | flops | bytes accessed | tf_op | source)
XLA Modules:
  0.0 90.3 jit_solution(13305633335687098761)
XLA Ops:
  0.6 0.0 copy-start.3
  0.6 0.0 copy-start.4
  0.7 0.0 copy-start
  0.7 0.0 copy-start.1
  0.7 14.3 %legendre.1 = bf16[8,8,16,512]{3,2,1,0:T(8,128)(2,1)} custom-call(bf16[6,8,80,1280]{3,2,1,0:T(8,128)(2,1)} %spectral_ref.1, bf16[80,1280,128]{2,1,0:T(8,128)(2,1)} %legendre_ref.1), custom_call_target="tpu_custom_call" | custom-call | flops 1258291200 | bytes 36044800 | tf_op jit(solution)/shard_map/legendre/pallas_call | solution.py:538
  15.0 0.0 copy-start.2
  15.0 0.0 copy-done.3
  15.0 0.0 copy-done.4
  15.0 0.1 pad_add_fusion.info
  15.1 5.2 %all-to-all-start = ((bf16[8,8,16,512]{3,2,1,0:T(8,128)(2,1)}), bf16[8,8,16,512]{3,2,1,0:T(8,128)(2,1)S(1)}, u32[]{:S(2)}, u32[]{:S(2)}) async-start(bf16[8,8,16,512]{3,2,1,0:T(8,128)(2,1)} %legendre.1), calls=%async_computation | async-start | bytes 2097152 | tf_op jit(solution)/shard_map/all_to_all | solution.py:581
  20.2 0.0 copy-done
  20.2 0.0 copy-done.1
  20.3 4.8 %edges.1 = (bf16[32,16,256]{2,1,0:T(8,128)(2,1)S(1)}, bf16[32,16,256]{2,1,0:T(8,128)(2,1)S(1)}, bf16[256,128]{1,0:T(8,128)(2,1)S(1)}, bf16[256,128]{1,0:T(8,128)(2,1)S(1)}, bf16[512,512]{1,0:T(8,128)(2,1)S(1)}) custom-call(s32[22]{0:T(128)S(1)} %pad_add_fusion.info, bf16[16,32,16,256]{3,2,1,0:T(8,128)(2,1)} %refs_0_.7, f32[16,16]{1,0:T(8,128)S(1)} %copy-done, ...), custom_call_target="tpu_custom_call" | custom-call | flops 268435456 | bytes 4194304 | tf_op jit(solution)/shard_map/edges/pallas_call | solution.py:295
  25.0 0.6 collective-permute-start
  25.6 1.6 %collective-permute-start.1 = (bf16[256,128]{1,0:T(8,128)(2,1)S(1)}, bf16[256,128]{1,0:T(8,128)(2,1)S(1)}, u32[]{:S(2)}, u32[]{:S(2)}) collective-permute-start(bf16[256,128]{1,0:T(8,128)(2,1)S(1)} %get-tuple-element.46), channel_id=1, source_target_pairs={{0,1},{1,0},{2,3},{3,2},{4,5},{5,4},{6,7},{7,6},{8,9},{9,8},{10,11... | collective-permute-start | bytes 196616 | tf_op jit(solution)/shard_map/ppermute | solution.py:558
  27.2 0.7 collective-permute-start.2
  27.8 0.0 copy-done.2
  27.8 5.7 %tables.1 = (bf16[16,1280,128]{2,1,0:T(8,128)(2,1)}, f32[16,2,8,640]{3,2,1,0:T(8,128)}) custom-call(s32[22]{0:T(128)S(1)} %pad_add_fusion.info, s32[1,640]{1,0:T(1,128)S(1)} %broadcast_in_dim.3.waves_ref), custom_call_target="tpu_custom_call" | custom-call | flops 10485760 | bytes 5242880 | tf_op jit(solution)/shard_map/tables/pallas_call | solution.py:88
  33.6 0.0 collective-permute-done.1.refs_3_
  33.6 0.0 collective-permute-done.2.refs_4_
  33.6 0.0 collective-permute-done.refs_1_
  33.6 2.1 %all-to-all-done.recv_ref = bf16[8,8,16,512]{3,2,1,0:T(8,128)(2,1)S(1)} async-done(((bf16[8,8,16,512]{3,2,1,0:T(8,128)(2,1)}), bf16[8,8,16,512]{3,2,1,0:T(8,128)(2,1)S(1)}, u32[]{:S(2)}, u32[]{:S(2)}) %all-to-all-start) | async-done | bytes 1048608 | tf_op jit(solution)/shard_map/all_to_all | solution.py:581
  35.6 0.7 collective-permute-start.3
  36.3 5.4 %synthesis.1 = (bf16[3,8,16,256]{3,2,1,0:T(8,128)(2,1)S(1)}, bf16[3,8,16,256]{3,2,1,0:T(8,128)(2,1)S(1)}, bf16[3,8,16,256]{3,2,1,0:T(8,128)(2,1)S(1)}, bf16[3,8,16,256]{3,2,1,0:T(8,128)(2,1)S(1)}) custom-call(s32[22]{0:T(128)S(1)} %pad_add_fusion.info, bf16[8,8,16,512]{3,2,1,0:T(8,128)(2,1)S(1)} %all-to-all-done.recv_ref, ...), custom_call_target="tpu_custom_call" | custom-call | flops 1006632960 | bytes 5242880 | tf_op jit(solution)/shard_map/synthesis/pallas_call | solution.py:202
  41.7 2.7 %collective-permute-start.6 = (bf16[3,8,16,256]{3,2,1,0:T(8,128)(2,1)S(1)}, bf16[3,8,16,256]{3,2,1,0:T(8,128)(2,1)S(1)}, u32[]{:S(2)}, u32[]{:S(2)}) collective-permute-start(bf16[3,8,16,256]{3,2,1,0:T(8,128)(2,1)S(1)} %get-tuple-element.63), channel_id=1, source_target_pairs={{0,2},{2,0},{1,3},{3,1},{4,6},{6,4},{5,7},{7,5},{8,10},{10,8},{9,1... | collective-permute-start | bytes 589832 | tf_op jit(solution)/shard_map/ppermute | solution.py:558
  44.3 0.0 collective-permute-done.3.refs_2_
  44.3 5.3 %chemistry.4 = (bf16[16,32,16,256]{3,2,1,0:T(8,128)(2,1)}, bf16[4,8,16,256]{3,2,1,0:T(8,128)(2,1)S(1)}) custom-call(s32[22]{0:T(128)S(1)} %pad_add_fusion.info, bf16[16,32,16,256]{3,2,1,0:T(8,128)(2,1)} %refs_0_.7, bf16[32,16,256]{2,1,0:T(8,128)(2,1)S(1)} %collective-permute-done.refs_1_, bf16[32,16,256]{2,1,0:T(8,128)(2,1)S(1)} %collective-permute-done.3.refs_2_, ...), custom_call_target="tpu_custom_call" | custom-call | flops 524288 | bytes 2048 | tf_op jit(solution)/shard_map/chemistry/pallas_call | solution.py:415
  49.6 2.1 %collective-permute-start.5 = (bf16[3,8,16,256]{3,2,1,0:T(8,128)(2,1)S(1)}, bf16[3,8,16,256]{3,2,1,0:T(8,128)(2,1)S(1)}, u32[]{:S(2)}, u32[]{:S(2)}) collective-permute-start(bf16[3,8,16,256]{3,2,1,0:T(8,128)(2,1)S(1)} %get-tuple-element.62), channel_id=1, source_target_pairs={{0,3},{3,0},{1,2},{2,1},{4,7},{7,4},{5,6},{6,5},{8,11},{11,8},{9,1... | collective-permute-start | bytes 589832 | tf_op jit(solution)/shard_map/ppermute | solution.py:558
  51.8 0.0 collective-permute-start.4
  51.8 1.6 %collective-permute-done.6.refs_5_ = bf16[3,8,16,256]{3,2,1,0:T(8,128)(2,1)S(1)} collective-permute-done((bf16[3,8,16,256]{3,2,1,0:T(8,128)(2,1)S(1)}, bf16[3,8,16,256]{3,2,1,0:T(8,128)(2,1)S(1)}, u32[]{:S(2)}, u32[]{:S(2)}) %collective-permute-start.6) | collective-permute-done | bytes 196640 | tf_op jit(solution)/shard_map/ppermute | solution.py:558
  53.4 5.3 %chemistry.5 = (bf16[16,32,16,256]{3,2,1,0:T(8,128)(2,1)}, bf16[4,8,16,256]{3,2,1,0:T(8,128)(2,1)S(1)}) custom-call(s32[22]{0:T(128)S(1)} %pad_add_fusion.info, bf16[16,32,16,256]{3,2,1,0:T(8,128)(2,1)} %refs_0_.7, bf16[32,16,256]{2,1,0:T(8,128)(2,1)S(1)} %collective-permute-done.refs_1_, ...), custom_call_target="tpu_custom_call", output_to_operand_aliasing={{0}: (8, {})} | custom-call | flops 524288 | bytes 2048 | tf_op jit(solution)/shard_map/chemistry/pallas_call | solution.py:415
  58.7 0.6 collective-permute-start.9
  59.3 0.0 collective-permute-done.5.refs_5_
  59.3 5.3 %chemistry.6 = (bf16[16,32,16,256]{3,2,1,0:T(8,128)(2,1)}, bf16[4,8,16,256]{3,2,1,0:T(8,128)(2,1)S(1)}) custom-call(s32[22]{0:T(128)S(1)} %pad_add_fusion.info, bf16[16,32,16,256]{3,2,1,0:T(8,128)(2,1)} %refs_0_.7, bf16[32,16,256]{2,1,0:T(8,128)(2,1)S(1)} %collective-permute-done.refs_1_, ...), custom_call_target="tpu_custom_call", output_to_operand_aliasing={{0}: (8, {})} | custom-call | flops 524288 | bytes 2048 | tf_op jit(solution)/shard_map/chemistry/pallas_call | solution.py:415
  64.6 7.4 %collective-permute-start.7 = (bf16[4,8,16,256]{3,2,1,0:T(8,128)(2,1)S(1)}, bf16[4,8,16,256]{3,2,1,0:T(8,128)(2,1)S(1)}, u32[]{:S(2)}, u32[]{:S(2)}) collective-permute-start(bf16[4,8,16,256]{3,2,1,0:T(8,128)(2,1)S(1)} %get-tuple-element.68), channel_id=1, source_target_pairs={{0,3},{3,0},{1,2},{2,1},{4,7},{7,4},{5,6},{6,5},{8,11},{11,8},{9,1... | collective-permute-start | bytes 786440 | tf_op jit(solution)/shard_map/ppermute | solution.py:558
  72.0 0.0 collective-permute-done.4.refs_5_
  72.0 5.3 %chemistry.7 = (bf16[16,32,16,256]{3,2,1,0:T(8,128)(2,1)}, bf16[4,8,16,256]{3,2,1,0:T(8,128)(2,1)S(1)}) custom-call(s32[22]{0:T(128)S(1)} %pad_add_fusion.info, bf16[16,32,16,256]{3,2,1,0:T(8,128)(2,1)} %refs_0_.7, bf16[32,16,256]{2,1,0:T(8,128)(2,1)S(1)} %collective-permute-done.refs_1_, ...), custom_call_target="tpu_custom_call", output_to_operand_aliasing={{0}: (8, {})} | custom-call | flops 524288 | bytes 2048 | tf_op jit(solution)/shard_map/chemistry/pallas_call | solution.py:415
  77.3 5.1 %collective-permute-start.8 = (bf16[4,8,16,256]{3,2,1,0:T(8,128)(2,1)S(1)}, bf16[4,8,16,256]{3,2,1,0:T(8,128)(2,1)S(1)}, u32[]{:S(2)}, u32[]{:S(2)}) collective-permute-start(bf16[4,8,16,256]{3,2,1,0:T(8,128)(2,1)S(1)} %get-tuple-element.69), channel_id=1, source_target_pairs={{0,1},{1,0},{2,3},{3,2},{4,5},{5,4},{6,7},{7,6},{8,9},{9,8},{10,11... | collective-permute-start | bytes 786440 | tf_op jit(solution)/shard_map/ppermute | solution.py:558
  82.4 0.0 collective-permute-done.9.refs_1_
  82.4 1.6 %spread.2.refs_2_ = f32[4,8,16,1024]{3,2,1,0:T(8,128)} custom-call(s32[22]{0:T(128)S(1)} %pad_add_fusion.info, bf16[4,8,16,256]{3,2,1,0:T(8,128)(2,1)S(1)} %get-tuple-element.72.refs_0_, bf16[4,8,16,256]{3,2,1,0:T(8,128)(2,1)S(1)} %collective-permute-done.9.refs_1_), custom_call_target="tpu_custom_call" | custom-call | flops 4 | bytes 4 | tf_op jit(solution)/shard_map/spread/pallas_call | solution.py:466
  84.0 0.0 collective-permute-done.7.refs_0_
  84.0 4.7 %collective-permute-done.8.refs_1_ = bf16[4,8,16,256]{3,2,1,0:T(8,128)(2,1)S(1)} collective-permute-done((bf16[4,8,16,256]{3,2,1,0:T(8,128)(2,1)S(1)}, bf16[4,8,16,256]{3,2,1,0:T(8,128)(2,1)S(1)}, u32[]{:S(2)}, u32[]{:S(2)}) %collective-permute-start.8) | collective-permute-done | bytes 262176 | tf_op jit(solution)/shard_map/ppermute | solution.py:558
  88.7 1.6 %spread.3 = f32[4,8,16,1024]{3,2,1,0:T(8,128)} custom-call(s32[22]{0:T(128)S(1)} %pad_add_fusion.info, bf16[4,8,16,256]{3,2,1,0:T(8,128)(2,1)S(1)} %collective-permute-done.7.refs_0_, bf16[4,8,16,256]{3,2,1,0:T(8,128)(2,1)S(1)} %collective-permute-done.8.refs_1_, f32[4,8,16,1024]{3,2,1,0:T(8,128)} %spread.2.refs_2_), custom_call_target="tpu_custom_call", output_to_operand_aliasing={{}: (3, {})} | custom-call | flops 4 | bytes 4 | tf_op jit(solution)/shard_map/spread/pallas_call | solution.py:466
  (1 shorter events, 0.0 us)
Async XLA Ops:
  0.6 14.3 %copy-start.3 = (s32[16]{0:T(128)S(1)}, s32[16]{0:T(128)}, u32[]{:S(2)}) copy-start(s32[16]{0:T(128)} %param.11) | copy-start | bytes 196
  0.6 14.3 %copy-start.4 = (s32[4]{0:T(128)S(1)}, s32[4]{0:T(128)}, u32[]{:S(2)}) copy-start(s32[4]{0:T(128)} %param.15) | copy-start | bytes 52
  0.7 19.6 %copy-start = (f32[16,16]{1,0:T(8,128)S(1)}, f32[16,16]{1,0:T(8,128)}, u32[]{:S(2)}) copy-start(f32[16,16]{1,0:T(8,128)} %base_ref.1) | copy-start | bytes 3076
  0.7 19.6 %copy-start.1 = (f32[16,16]{1,0:T(8,128)S(1)}, f32[16,16]{1,0:T(8,128)}, u32[]{:S(2)}) copy-start(f32[16,16]{1,0:T(8,128)} %temp_ref.1) | copy-start | bytes 3076
  15.0 12.8 %copy-start.2 = (s32[640]{0:T(1024)S(1)}, s32[640]{0:T(1024)}, u32[]{:S(2)}) copy-start(s32[640]{0:T(1024)} %param.10) | copy-start | bytes 7684
  15.1 20.6 %all-to-all-start = ((bf16[8,8,16,512]{3,2,1,0:T(8,128)(2,1)}), bf16[8,8,16,512]{3,2,1,0:T(8,128)(2,1)S(1)}, u32[]{:S(2)}, u32[]{:S(2)}) async-start(bf16[8,8,16,512]{3,2,1,0:T(8,128)(2,1)} %legendre.1), calls=%async_computation | async-start | bytes 2097152 | tf_op jit(solution)/shard_map/all_to_all | solution.py:581
  25.0 8.6 %collective-permute-start = (bf16[32,16,256]{2,1,0:T(8,128)(2,1)S(1)}, bf16[32,16,256]{2,1,0:T(8,128)(2,1)S(1)}, u32[]{:S(2)}, u32[]{:S(2)}) collective-permute-start(bf16[32,16,256]{2,1,0:T(8,128)(2,1)S(1)} %get-tuple-element.45), channel_id=1, source_target_pairs={{0,4},{4,0},{8,12},{12,8},{16,20},{20,16},{24,28},{28,24},{1,5},{5... | collective-permute-start | bytes 786440 | tf_op jit(solution)/shard_map/ppermute | solution.py:558
  25.6 8.0 %collective-permute-start.1 = (bf16[256,128]{1,0:T(8,128)(2,1)S(1)}, bf16[256,128]{1,0:T(8,128)(2,1)S(1)}, u32[]{:S(2)}, u32[]{:S(2)}) collective-permute-start(bf16[256,128]{1,0:T(8,128)(2,1)S(1)} %get-tuple-element.46), channel_id=1, source_target_pairs={{0,1},{1,0},{2,3},{3,2},{4,5},{5,4},{6,7},{7,6},{8,9},{9,8},{10,11... | collective-permute-start | bytes 196616 | tf_op jit(solution)/shard_map/ppermute | solution.py:558
  27.2 6.4 %collective-permute-start.2 = (bf16[256,128]{1,0:T(8,128)(2,1)S(1)}, bf16[256,128]{1,0:T(8,128)(2,1)S(1)}, u32[]{:S(2)}, u32[]{:S(2)}) collective-permute-start(bf16[256,128]{1,0:T(8,128)(2,1)S(1)} %get-tuple-element.47), channel_id=1, source_target_pairs={{1,2},{2,1},{5,6},{6,5},{9,10},{10,9},{13,14},{14,13},{17,18},{18,... | collective-permute-start | bytes 196616 | tf_op jit(solution)/shard_map/ppermute | solution.py:558
  35.6 8.7 %collective-permute-start.3 = (bf16[32,16,256]{2,1,0:T(8,128)(2,1)S(1)}, bf16[32,16,256]{2,1,0:T(8,128)(2,1)S(1)}, u32[]{:S(2)}, u32[]{:S(2)}) collective-permute-start(bf16[32,16,256]{2,1,0:T(8,128)(2,1)S(1)} %get-tuple-element.50), channel_id=1, source_target_pairs={{4,8},{8,4},{12,16},{16,12},{20,24},{24,20},{5,9},{9,5},{13,17},{1... | collective-permute-start | bytes 786440 | tf_op jit(solution)/shard_map/ppermute | solution.py:558
  41.7 11.7 %collective-permute-start.6 = (bf16[3,8,16,256]{3,2,1,0:T(8,128)(2,1)S(1)}, bf16[3,8,16,256]{3,2,1,0:T(8,128)(2,1)S(1)}, u32[]{:S(2)}, u32[]{:S(2)}) collective-permute-start(bf16[3,8,16,256]{3,2,1,0:T(8,128)(2,1)S(1)} %get-tuple-element.63), channel_id=1, source_target_pairs={{0,2},{2,0},{1,3},{3,1},{4,6},{6,4},{5,7},{7,5},{8,10},{10,8},{9,1... | collective-permute-start | bytes 589832 | tf_op jit(solution)/shard_map/ppermute | solution.py:558
  49.6 9.7 %collective-permute-start.5 = (bf16[3,8,16,256]{3,2,1,0:T(8,128)(2,1)S(1)}, bf16[3,8,16,256]{3,2,1,0:T(8,128)(2,1)S(1)}, u32[]{:S(2)}, u32[]{:S(2)}) collective-permute-start(bf16[3,8,16,256]{3,2,1,0:T(8,128)(2,1)S(1)} %get-tuple-element.62), channel_id=1, source_target_pairs={{0,3},{3,0},{1,2},{2,1},{4,7},{7,4},{5,6},{6,5},{8,11},{11,8},{9,1... | collective-permute-start | bytes 589832 | tf_op jit(solution)/shard_map/ppermute | solution.py:558
  51.8 20.3 %collective-permute-start.4 = (bf16[3,8,16,256]{3,2,1,0:T(8,128)(2,1)S(1)}, bf16[3,8,16,256]{3,2,1,0:T(8,128)(2,1)S(1)}, u32[]{:S(2)}, u32[]{:S(2)}) collective-permute-start(bf16[3,8,16,256]{3,2,1,0:T(8,128)(2,1)S(1)} %get-tuple-element.61), channel_id=1, source_target_pairs={{0,1},{1,0},{2,3},{3,2},{4,5},{5,4},{6,7},{7,6},{8,9},{9,8},{10,11... | collective-permute-start | bytes 589832 | tf_op jit(solution)/shard_map/ppermute | solution.py:558
  58.7 23.7 %collective-permute-start.9 = (bf16[4,8,16,256]{3,2,1,0:T(8,128)(2,1)S(1)}, bf16[4,8,16,256]{3,2,1,0:T(8,128)(2,1)S(1)}, u32[]{:S(2)}, u32[]{:S(2)}) collective-permute-start(bf16[4,8,16,256]{3,2,1,0:T(8,128)(2,1)S(1)} %get-tuple-element.73), channel_id=1, source_target_pairs={{0,2},{2,0},{1,3},{3,1},{4,6},{6,4},{5,7},{7,5},{8,10},{10,8},{9,1... | collective-permute-start | bytes 786440 | tf_op jit(solution)/shard_map/ppermute | solution.py:558
  64.6 19.4 %collective-permute-start.7 = (bf16[4,8,16,256]{3,2,1,0:T(8,128)(2,1)S(1)}, bf16[4,8,16,256]{3,2,1,0:T(8,128)(2,1)S(1)}, u32[]{:S(2)}, u32[]{:S(2)}) collective-permute-start(bf16[4,8,16,256]{3,2,1,0:T(8,128)(2,1)S(1)} %get-tuple-element.68), channel_id=1, source_target_pairs={{0,3},{3,0},{1,2},{2,1},{4,7},{7,4},{5,6},{6,5},{8,11},{11,8},{9,1... | collective-permute-start | bytes 786440 | tf_op jit(solution)/shard_map/ppermute | solution.py:558
  77.3 11.4 %collective-permute-start.8 = (bf16[4,8,16,256]{3,2,1,0:T(8,128)(2,1)S(1)}, bf16[4,8,16,256]{3,2,1,0:T(8,128)(2,1)S(1)}, u32[]{:S(2)}, u32[]{:S(2)}) collective-permute-start(bf16[4,8,16,256]{3,2,1,0:T(8,128)(2,1)S(1)} %get-tuple-element.69), channel_id=1, source_target_pairs={{0,1},{1,0},{2,3},{3,2},{4,5},{5,4},{6,7},{7,6},{8,9},{9,8},{10,11... | collective-permute-start | bytes 786440 | tf_op jit(solution)/shard_map/ppermute | solution.py:558

commit v16 on v15

--- a/solution.py
+++ b/solution.py
@@ -35,17 +35,13 @@
     3.238137510515757,
 )
 
-
 def dot(a, b, dims):
     return lax.dot_general(a, b, (dims, ((), ())), preferred_element_type=F32)
 
-
 BAND, ME, IDS = 0, 1, 2
-
 
 def cost(flops, moved):
     return pl.CostEstimate(flops=int(flops), bytes_accessed=int(moved), transcendentals=0)
-
 
 def unit_circle(step, rows, waves, count):
     index = lax.broadcasted_iota(jnp.int32, (rows, waves.shape[1]), 0) * step
@@ -60,7 +56,6 @@
         cosine = cosine * z + c
         sine = sine * z + s
     return cosine, sine * y
-
 
 def table_kernel(first, info, waves_ref, table_ref, twiddle_ref):
     size, turns = waves_ref.shape[1], twiddle_ref.shape[2]
@@ -80,7 +75,6 @@
         cos_turn, sin_turn = unit_circle(LANES, turns, waves, count)
         twiddle_ref[k, 0] = cos_turn
         twiddle_ref[k, 1] = sin_turn
-
 
 def tables(info, wave_ids, rows, turns):
     waves = wave_ids.shape[0]
@@ -105,7 +99,6 @@
         name="tables",
     )(info, wave_ids[None, :])
 
-
 def place(pieces, width):
     out = [None] * (width // LANES)
     lane = lax.broadcasted_iota(jnp.int32, (pieces[0][0].shape[0], LANES), 1)
@@ -125,7 +118,6 @@
                     out[v] = jnp.where((lane >= low) & (lane < high), part, out[v])
     return out
 
-
 def synth_kernel(info, recv_ref, table_hbm, twiddle_hbm, *refs):
     *out_refs, coef, grid, table_ref, twiddle_ref, sems = refs
     sources, levels, rows, _ = recv_ref.shape
@@ -191,7 +183,6 @@
                 for l in range(levels):
                     block = grid[pl.ds((start + l) * pitch, rows), :].astype(BF16)
                     out_ref[f, l, :, t * LANES : (t + 1) * LANES] = block
-
 
 def synthesis(recv, table, twiddle, info, dests, tile):
     sources, levels, rows, lanes = recv.shape
@@ -224,7 +215,6 @@
         name="synthesis",
     )(info, recv, *[pltpu.with_memory_space_constraint(v, pltpu.HBM) for v in (table, twiddle)])
 
-
 def edge_kernel(
     info, state_ref, base_ref, temp_ref, row_a_ref, row_b_ref, col_a_ref, col_b_ref, react_ref
 ):
@@ -281,7 +271,6 @@
     def _():
         col_a_ref[...] = (col_a_ref[...].astype(F32) + columns[:, :LANES]).astype(BF16)
         col_b_ref[...] = (col_b_ref[...].astype(F32) + columns[:, LANES:]).astype(BF16)
-
 
 def edges(state, react_base, react_temp, info):
     tracers, levels, rows, tile = state.shape
@@ -312,7 +301,6 @@
         name="edges",
     )(info, state, react_base, react_temp)
 
-
 def shifted(value, outer, axis, step):
     size = value[0].shape[axis]
     turned = [pltpu.roll(v, -step % size, axis) for v in value]
@@ -320,7 +308,6 @@
     at_end = place == (size - 1 if step == 1 else 0)
     following = turned[1:] + [outer] if step == 1 else [outer] + turned[:-1]
     return [jnp.where(at_end, f, t) for f, t in zip(following, turned)]
-
 
 def chem_kernel(scale, k, info, *refs):
     state_ref, row_a_ref, row_b_ref, col_a_ref, col_b_ref, grid_ref, react_ref = refs[:7]
@@ -380,7 +367,6 @@
     for a in range(active_ref.shape[0]):
         active_ref[a] = new_ref[info[ids + a]]
 
-
 def chemistry(state, halos, grid, react, info, k, actives, waves, before):
     tracers, levels, rows, tile = state.shape
     fields, own = grid.shape[:2]
@@ -396,7 +382,7 @@
     state_spec = pl.BlockSpec(
         (tracers, some, rows, tile), lambda i, info: (0, (info[ME] ^ k) * steps + i, 0, 0)
     )
-    state = pltpu.with_memory_space_constraint(state, pltpu.HBM)
+
     operands = [state, *halos, grid, react]
     in_specs = [
         state_spec,
@@ -439,7 +425,6 @@
         name="chemistry",
     )(info, *operands)
 
-
 def spread(parts, order, info, tiles, before):
     actives, own, rows, tile = parts[0].shape
     count = len(order)
@@ -480,7 +465,6 @@
         name="spread",
     )(info, *operands)
 
-
 def legendre_kernel(spectral_ref, legendre_ref, out_ref, rows_of, sums):
     parts, own, block, size = spectral_ref.shape
     bands, _, rows, pitch = out_ref.shape
@@ -528,7 +512,6 @@
                 turned = sums[h, pl.ds(l * stretch, pitch), :].T.astype(BF16)
                 out_ref[h * some : (h + 1) * some, l] = turned.reshape(some, rows, pitch)
 
-
 def legendre_sums(spectral, legendre, bands):
     parts, own, share, size = spectral.shape
     rows = legendre.shape[2] // bands
@@ -543,29 +526,25 @@
             pl.BlockSpec((block,) + legendre.shape[1:], lambda i: (i, 0, 0)),
         ],
         out_specs=pl.BlockSpec(shape, lambda i: (0, 0, 0, 0)),
-        out_shape=jax.ShapeDtypeStruct(shape, BF16),
+        out_shape=pltpu.VMEM(shape, BF16),
         scratch_shapes=[
             pltpu.VMEM((size // LANES, parts * own * (block + 1), LANES), F32),
             pltpu.VMEM((legendre.shape[2] // LANES, own * (pitch + 1), LANES), F32),
         ],
-        compiler_params=pltpu.CompilerParams(vmem_limit_bytes=56 * MIB),
+        compiler_params=pltpu.CompilerParams(vmem_limit_bytes=54 * MIB),
         cost_estimate=cost(2 * parts * own * legendre.size, 2 * (spectral.size + legendre.size)),
         name="legendre",
     )(spectral, legendre)
 
-
 def exchange(value, axis, pairs):
     return lax.ppermute(value, axis, [p for a, b in pairs for p in ((a, b), (b, a))])
-
 
 def neighbours(axis, first):
     size = lax.axis_size(axis)
     return [(i, i + 1) for i in range(first, size - 1, 2)]
 
-
 def partners(axis, k):
     return [(i, i ^ k) for i in range(lax.axis_size(axis)) if i < i ^ k]
-
 
 def body(spectral, legendre, wave_ids, points, tracers, react_base, react_temp, active_ids):
     bands, tiles = lax.axis_size("lat"), lax.axis_size("lon")
@@ -617,7 +596,6 @@
     parts = lax.optimization_barrier(through + [active[k] for k in inner])
     return new, spread(parts, last, info, tiles, spreaded)
 
-
 def solution(mesh):
     return jax.shard_map(
         body,

time: 90.6 us -> 90.4 us (level)
  Pallas kernels: 54.5 us -> 50.4 us
  waiting for transfers between devices: 8.41 us -> 10.8 us
  starting transfers between devices: 26.5 us -> 27.9 us
    pallas_call x4, Pallas kernels: 21.2 us -> 17.1 us  [chemistry(): pl.pallas_call(functools.partial(chem_kernel, scale, k), grid_spec=pltpu....]
    ppermute x10, waiting for transfers between devices: 6.35 us -> 8.77 us  [exchange(): lax.ppermute(value, axis, [p for a, b in pairs for p in ((a, b), (b, a))])]
    ppermute x10, starting transfers between devices: 21.4 us -> 22.7 us  [exchange(): lax.ppermute(value, axis, [p for a, b in pairs for p in ((a, b), (b, a))])]
  transfers between devices with their start and end apart: 11 -> 11, of which waited for: 3 -> 3; matrix products, arithmetic and copies ran while one was open for 0% -> 0% of each run, Pallas kernels for 43% -> 38%
where the time goes in v16:
time: 90.4 us; the launch traced here: 89.9 us
  Pallas kernels  50.4 us (56%)
  starting transfers between devices  27.9 us (31%)
  waiting for transfers between devices  10.8 us (12%)
    ppermute x10, starting transfers between devices, exchange(): lax.ppermute(value, axis, [p for a, b in pairs for p in ((a, b), (b, a))])  22.7 us
    pallas_call x4, Pallas kernels, chemistry(): pl.pallas_call(functools.partial(chem_kernel, scale, k), grid_spec=pltpu....  17.1 us
    pallas_call x1, Pallas kernels, legendre_sums(): pl.pallas_call(legendre_kernel, grid=(share // block,), in_specs=[pl.Bloc...  14.3 us
    ppermute x10, waiting for transfers between devices, exchange(): lax.ppermute(value, axis, [p for a, b in pairs for p in ((a, b), (b, a))])  8.77 us
    pallas_call x1, Pallas kernels, tables(): pl.pallas_call(functools.partial(table_kernel, info.shape[0] - rows), gri...  5.75 us
    pallas_call x1, Pallas kernels, synthesis(): pl.pallas_call(synth_kernel, grid_spec=pltpu.PrefetchScalarGridSpec(num_s...  5.34 us
    all_to_all x1, starting transfers between devices, body(): recv = lax.all_to_all(sent, 'lat', split_axis=0, concat_axis=0, tiled=True)  5.17 us
    pallas_call x1, Pallas kernels, edges(): pl.pallas_call(edge_kernel, grid_spec=pltpu.PrefetchScalarGridSpec(num_sc...  4.75 us
  transfers between devices with their start and end apart: 11, of which 3 were waited for; matrix products, arithmetic and copies ran while one was open for 0% of the time, Pallas kernels for 38%

profile of v16, /device:TPU:0, one launch (start us, length us, event | category | flops | bytes accessed | tf_op | source)
XLA Modules:
  0.0 89.9 jit_solution(14349367812705688228)
XLA Ops:
  0.6 0.0 copy-start.4
  0.6 0.0 copy-start.5
  0.7 0.0 copy-start.1
  0.7 0.0 copy-start.2
  0.7 14.3 %legendre.1 = bf16[8,8,16,512]{3,2,1,0:T(8,128)(2,1)} custom-call(bf16[6,8,80,1280]{3,2,1,0:T(8,128)(2,1)} %spectral_ref.1, bf16[80,1280,128]{2,1,0:T(8,128)(2,1)} %legendre_ref.1), custom_call_target="tpu_custom_call" | custom-call | flops 1258291200 | bytes 36044800 | tf_op jit(solution)/shard_map/legendre/pallas_call | solution.py:521
  15.0 0.0 copy-start.3
  15.0 0.0 copy-done.4
  15.0 0.0 copy-done.5
  15.0 0.1 pad_add_fusion.info
  15.1 5.2 %all-to-all-start = ((bf16[8,8,16,512]{3,2,1,0:T(8,128)(2,1)}), bf16[8,8,16,512]{3,2,1,0:T(8,128)(2,1)S(1)}, u32[]{:S(2)}, u32[]{:S(2)}) async-start(bf16[8,8,16,512]{3,2,1,0:T(8,128)(2,1)} %legendre.1), calls=%async_computation | async-start | bytes 2097152 | tf_op jit(solution)/shard_map/all_to_all | solution.py:560
  20.2 0.0 copy-done.1
  20.2 0.0 copy-done.2
  20.3 4.8 %edges.1 = (bf16[32,16,256]{2,1,0:T(8,128)(2,1)S(1)}, bf16[32,16,256]{2,1,0:T(8,128)(2,1)S(1)}, bf16[256,128]{1,0:T(8,128)(2,1)S(1)}, bf16[256,128]{1,0:T(8,128)(2,1)S(1)}, bf16[512,512]{1,0:T(8,128)(2,1)S(1)}) custom-call(s32[22]{0:T(128)S(1)} %pad_add_fusion.info, bf16[16,32,16,256]{3,2,1,0:T(8,128)(2,1)} %refs_0_.7, f32[16,16]{1,0:T(8,128)S(1)} %copy-done.1, ...), custom_call_target="tpu_custom_call" | custom-call | flops 268435456 | bytes 4194304 | tf_op jit(solution)/shard_map/edges/pallas_call | solution.py:284
  25.0 0.6 collective-permute-start
  25.6 1.6 %collective-permute-start.1 = (bf16[256,128]{1,0:T(8,128)(2,1)S(1)}, bf16[256,128]{1,0:T(8,128)(2,1)S(1)}, u32[]{:S(2)}, u32[]{:S(2)}) collective-permute-start(bf16[256,128]{1,0:T(8,128)(2,1)S(1)} %get-tuple-element.46), channel_id=1, source_target_pairs={{0,1},{1,0},{2,3},{3,2},{4,5},{5,4},{6,7},{7,6},{8,9},{9,8},{10,11... | collective-permute-start | bytes 196616 | tf_op jit(solution)/shard_map/ppermute | solution.py:540
  27.2 0.7 collective-permute-start.2
  27.8 0.0 copy-done.3
  27.8 5.8 %tables.1 = (bf16[16,1280,128]{2,1,0:T(8,128)(2,1)}, f32[16,2,8,640]{3,2,1,0:T(8,128)}) custom-call(s32[22]{0:T(128)S(1)} %pad_add_fusion.info, s32[1,640]{1,0:T(1,128)S(1)} %broadcast_in_dim.3.waves_ref), custom_call_target="tpu_custom_call" | custom-call | flops 10485760 | bytes 5242880 | tf_op jit(solution)/shard_map/tables/pallas_call | solution.py:82
  33.6 0.0 collective-permute-done.1.refs_3_
  33.6 0.0 collective-permute-done.2.refs_4_
  33.6 0.0 collective-permute-done.refs_1_
  33.6 2.0 %all-to-all-done.recv_ref = bf16[8,8,16,512]{3,2,1,0:T(8,128)(2,1)S(1)} async-done(((bf16[8,8,16,512]{3,2,1,0:T(8,128)(2,1)}), bf16[8,8,16,512]{3,2,1,0:T(8,128)(2,1)S(1)}, u32[]{:S(2)}, u32[]{:S(2)}) %all-to-all-start) | async-done | bytes 1048608 | tf_op jit(solution)/shard_map/all_to_all | solution.py:560
  35.6 0.0 copy-start
  35.7 0.8 collective-permute-start.3
  36.5 5.3 %synthesis.1 = (bf16[3,8,16,256]{3,2,1,0:T(8,128)(2,1)S(1)}, bf16[3,8,16,256]{3,2,1,0:T(8,128)(2,1)S(1)}, bf16[3,8,16,256]{3,2,1,0:T(8,128)(2,1)S(1)}, bf16[3,8,16,256]{3,2,1,0:T(8,128)(2,1)S(1)}) custom-call(s32[22]{0:T(128)S(1)} %pad_add_fusion.info, bf16[8,8,16,512]{3,2,1,0:T(8,128)(2,1)S(1)} %all-to-all-done.recv_ref, ...), custom_call_target="tpu_custom_call" | custom-call | flops 1006632960 | bytes 5242880 | tf_op jit(solution)/shard_map/synthesis/pallas_call | solution.py:193
  41.8 2.7 %collective-permute-start.6 = (bf16[3,8,16,256]{3,2,1,0:T(8,128)(2,1)S(1)}, bf16[3,8,16,256]{3,2,1,0:T(8,128)(2,1)S(1)}, u32[]{:S(2)}, u32[]{:S(2)}) collective-permute-start(bf16[3,8,16,256]{3,2,1,0:T(8,128)(2,1)S(1)} %get-tuple-element.63), channel_id=1, source_target_pairs={{0,2},{2,0},{1,3},{3,1},{4,6},{6,4},{5,7},{7,5},{8,10},{10,8},{9,1... | collective-permute-start | bytes 589832 | tf_op jit(solution)/shard_map/ppermute | solution.py:540
  44.5 0.0 collective-permute-done.3.refs_2_
  44.5 0.0 copy-done
  44.5 4.3 %chemistry.4 = (bf16[16,32,16,256]{3,2,1,0:T(8,128)(2,1)}, bf16[4,8,16,256]{3,2,1,0:T(8,128)(2,1)S(1)}) custom-call(s32[22]{0:T(128)S(1)} %pad_add_fusion.info, bf16[16,32,16,256]{3,2,1,0:T(8,128)(2,1)S(1)} %copy-done, bf16[32,16,256]{2,1,0:T(8,128)(2,1)S(1)} %collective-permute-done.refs_1_, bf16[32,16,256]{2,1,0:T(8,128)(2,1)S(1)} %collective-permute-done.3.refs_2_, ...), custom_call_target="tpu_custom_call" | custom-call | flops 524288 | bytes 2048 | tf_op jit(solution)/shard_map/chemistry/pallas_call | solution.py:401
  48.7 2.2 %collective-permute-start.5 = (bf16[3,8,16,256]{3,2,1,0:T(8,128)(2,1)S(1)}, bf16[3,8,16,256]{3,2,1,0:T(8,128)(2,1)S(1)}, u32[]{:S(2)}, u32[]{:S(2)}) collective-permute-start(bf16[3,8,16,256]{3,2,1,0:T(8,128)(2,1)S(1)} %get-tuple-element.62), channel_id=1, source_target_pairs={{0,3},{3,0},{1,2},{2,1},{4,7},{7,4},{5,6},{6,5},{8,11},{11,8},{9,1... | collective-permute-start | bytes 589832 | tf_op jit(solution)/shard_map/ppermute | solution.py:540
  50.9 0.0 collective-permute-start.4
  50.9 2.4 %collective-permute-done.6.refs_5_ = bf16[3,8,16,256]{3,2,1,0:T(8,128)(2,1)S(1)} collective-permute-done((bf16[3,8,16,256]{3,2,1,0:T(8,128)(2,1)S(1)}, bf16[3,8,16,256]{3,2,1,0:T(8,128)(2,1)S(1)}, u32[]{:S(2)}, u32[]{:S(2)}) %collective-permute-start.6) | collective-permute-done | bytes 196640 | tf_op jit(solution)/shard_map/ppermute | solution.py:540
  53.3 4.3 %chemistry.5 = (bf16[16,32,16,256]{3,2,1,0:T(8,128)(2,1)}, bf16[4,8,16,256]{3,2,1,0:T(8,128)(2,1)S(1)}) custom-call(s32[22]{0:T(128)S(1)} %pad_add_fusion.info, bf16[16,32,16,256]{3,2,1,0:T(8,128)(2,1)S(1)} %copy-done, bf16[32,16,256]{2,1,0:T(8,128)(2,1)S(1)} %collective-permute-done.refs_1_, ...), custom_call_target="tpu_custom_call", output_to_operand_aliasing={{0}: (8, {})} | custom-call | flops 524288 | bytes 2048 | tf_op jit(solution)/shard_map/chemistry/pallas_call | solution.py:401
  57.6 0.0 collective-permute-start.9
  57.6 0.0 collective-permute-done.5.refs_5_
  57.6 4.3 %chemistry.6 = (bf16[16,32,16,256]{3,2,1,0:T(8,128)(2,1)}, bf16[4,8,16,256]{3,2,1,0:T(8,128)(2,1)S(1)}) custom-call(s32[22]{0:T(128)S(1)} %pad_add_fusion.info, bf16[16,32,16,256]{3,2,1,0:T(8,128)(2,1)S(1)} %copy-done, bf16[32,16,256]{2,1,0:T(8,128)(2,1)S(1)} %collective-permute-done.refs_1_, ...), custom_call_target="tpu_custom_call", output_to_operand_aliasing={{0}: (8, {})} | custom-call | flops 524288 | bytes 2048 | tf_op jit(solution)/shard_map/chemistry/pallas_call | solution.py:401
  61.8 9.1 %collective-permute-start.7 = (bf16[4,8,16,256]{3,2,1,0:T(8,128)(2,1)S(1)}, bf16[4,8,16,256]{3,2,1,0:T(8,128)(2,1)S(1)}, u32[]{:S(2)}, u32[]{:S(2)}) collective-permute-start(bf16[4,8,16,256]{3,2,1,0:T(8,128)(2,1)S(1)} %get-tuple-element.68), channel_id=1, source_target_pairs={{0,3},{3,0},{1,2},{2,1},{4,7},{7,4},{5,6},{6,5},{8,11},{11,8},{9,1... | collective-permute-start | bytes 786440 | tf_op jit(solution)/shard_map/ppermute | solution.py:540
  70.9 0.0 collective-permute-done.4.refs_5_
  71.0 4.3 %chemistry.7 = (bf16[16,32,16,256]{3,2,1,0:T(8,128)(2,1)}, bf16[4,8,16,256]{3,2,1,0:T(8,128)(2,1)S(1)}) custom-call(s32[22]{0:T(128)S(1)} %pad_add_fusion.info, bf16[16,32,16,256]{3,2,1,0:T(8,128)(2,1)S(1)} %copy-done, bf16[32,16,256]{2,1,0:T(8,128)(2,1)S(1)} %collective-permute-done.refs_1_, ...), custom_call_target="tpu_custom_call", output_to_operand_aliasing={{0}: (8, {})} | custom-call | flops 524288 | bytes 2048 | tf_op jit(solution)/shard_map/chemistry/pallas_call | solution.py:401
  75.2 5.2 %collective-permute-start.8 = (bf16[4,8,16,256]{3,2,1,0:T(8,128)(2,1)S(1)}, bf16[4,8,16,256]{3,2,1,0:T(8,128)(2,1)S(1)}, u32[]{:S(2)}, u32[]{:S(2)}) collective-permute-start(bf16[4,8,16,256]{3,2,1,0:T(8,128)(2,1)S(1)} %get-tuple-element.69), channel_id=1, source_target_pairs={{0,1},{1,0},{2,3},{3,2},{4,5},{5,4},{6,7},{7,6},{8,9},{9,8},{10,11... | collective-permute-start | bytes 786440 | tf_op jit(solution)/shard_map/ppermute | solution.py:540
  80.4 0.0 collective-permute-done.9.refs_1_
  80.4 1.6 %spread.2.refs_2_ = f32[4,8,16,1024]{3,2,1,0:T(8,128)} custom-call(s32[22]{0:T(128)S(1)} %pad_add_fusion.info, bf16[4,8,16,256]{3,2,1,0:T(8,128)(2,1)S(1)} %get-tuple-element.72.refs_0_, bf16[4,8,16,256]{3,2,1,0:T(8,128)(2,1)S(1)} %collective-permute-done.9.refs_1_), custom_call_target="tpu_custom_call" | custom-call | flops 4 | bytes 4 | tf_op jit(solution)/shard_map/spread/pallas_call | solution.py:451
  82.0 0.0 collective-permute-done.7.refs_0_
  82.0 6.3 %collective-permute-done.8.refs_1_ = bf16[4,8,16,256]{3,2,1,0:T(8,128)(2,1)S(1)} collective-permute-done((bf16[4,8,16,256]{3,2,1,0:T(8,128)(2,1)S(1)}, bf16[4,8,16,256]{3,2,1,0:T(8,128)(2,1)S(1)}, u32[]{:S(2)}, u32[]{:S(2)}) %collective-permute-start.8) | collective-permute-done | bytes 262176 | tf_op jit(solution)/shard_map/ppermute | solution.py:540
  88.3 1.6 %spread.3 = f32[4,8,16,1024]{3,2,1,0:T(8,128)} custom-call(s32[22]{0:T(128)S(1)} %pad_add_fusion.info, bf16[4,8,16,256]{3,2,1,0:T(8,128)(2,1)S(1)} %collective-permute-done.7.refs_0_, bf16[4,8,16,256]{3,2,1,0:T(8,128)(2,1)S(1)} %collective-permute-done.8.refs_1_, f32[4,8,16,1024]{3,2,1,0:T(8,128)} %spread.2.refs_2_), custom_call_target="tpu_custom_call", output_to_operand_aliasing={{}: (3, {})} | custom-call | flops 4 | bytes 4 | tf_op jit(solution)/shard_map/spread/pallas_call | solution.py:451
  (1 shorter events, 0.0 us)
Async XLA Ops:
  0.6 14.3 %copy-start.4 = (s32[16]{0:T(128)S(1)}, s32[16]{0:T(128)}, u32[]{:S(2)}) copy-start(s32[16]{0:T(128)} %param.11) | copy-start | bytes 196
  0.6 14.3 %copy-start.5 = (s32[4]{0:T(128)S(1)}, s32[4]{0:T(128)}, u32[]{:S(2)}) copy-start(s32[4]{0:T(128)} %param.15) | copy-start | bytes 52
  0.7 19.6 %copy-start.1 = (f32[16,16]{1,0:T(8,128)S(1)}, f32[16,16]{1,0:T(8,128)}, u32[]{:S(2)}) copy-start(f32[16,16]{1,0:T(8,128)} %base_ref.1) | copy-start | bytes 3076
  0.7 19.6 %copy-start.2 = (f32[16,16]{1,0:T(8,128)S(1)}, f32[16,16]{1,0:T(8,128)}, u32[]{:S(2)}) copy-start(f32[16,16]{1,0:T(8,128)} %temp_ref.1) | copy-start | bytes 3076
  15.0 12.8 %copy-start.3 = (s32[640]{0:T(1024)S(1)}, s32[640]{0:T(1024)}, u32[]{:S(2)}) copy-start(s32[640]{0:T(1024)} %param.10) | copy-start | bytes 7684
  15.1 20.6 %all-to-all-start = ((bf16[8,8,16,512]{3,2,1,0:T(8,128)(2,1)}), bf16[8,8,16,512]{3,2,1,0:T(8,128)(2,1)S(1)}, u32[]{:S(2)}, u32[]{:S(2)}) async-start(bf16[8,8,16,512]{3,2,1,0:T(8,128)(2,1)} %legendre.1), calls=%async_computation | async-start | bytes 2097152 | tf_op jit(solution)/shard_map/all_to_all | solution.py:560
  25.0 8.6 %collective-permute-start = (bf16[32,16,256]{2,1,0:T(8,128)(2,1)S(1)}, bf16[32,16,256]{2,1,0:T(8,128)(2,1)S(1)}, u32[]{:S(2)}, u32[]{:S(2)}) collective-permute-start(bf16[32,16,256]{2,1,0:T(8,128)(2,1)S(1)} %get-tuple-element.45), channel_id=1, source_target_pairs={{0,4},{4,0},{8,12},{12,8},{16,20},{20,16},{24,28},{28,24},{1,5},{5... | collective-permute-start | bytes 786440 | tf_op jit(solution)/shard_map/ppermute | solution.py:540
  25.6 8.0 %collective-permute-start.1 = (bf16[256,128]{1,0:T(8,128)(2,1)S(1)}, bf16[256,128]{1,0:T(8,128)(2,1)S(1)}, u32[]{:S(2)}, u32[]{:S(2)}) collective-permute-start(bf16[256,128]{1,0:T(8,128)(2,1)S(1)} %get-tuple-element.46), channel_id=1, source_target_pairs={{0,1},{1,0},{2,3},{3,2},{4,5},{5,4},{6,7},{7,6},{8,9},{9,8},{10,11... | collective-permute-start | bytes 196616 | tf_op jit(solution)/shard_map/ppermute | solution.py:540
  27.2 6.4 %collective-permute-start.2 = (bf16[256,128]{1,0:T(8,128)(2,1)S(1)}, bf16[256,128]{1,0:T(8,128)(2,1)S(1)}, u32[]{:S(2)}, u32[]{:S(2)}) collective-permute-start(bf16[256,128]{1,0:T(8,128)(2,1)S(1)} %get-tuple-element.47), channel_id=1, source_target_pairs={{1,2},{2,1},{5,6},{6,5},{9,10},{10,9},{13,14},{14,13},{17,18},{18,... | collective-permute-start | bytes 196616 | tf_op jit(solution)/shard_map/ppermute | solution.py:540
  35.6 8.8 %copy-start = (bf16[16,32,16,256]{3,2,1,0:T(8,128)(2,1)S(1)}, bf16[16,32,16,256]{3,2,1,0:T(8,128)(2,1)}, u32[]{:S(2)}) copy-start(bf16[16,32,16,256]{3,2,1,0:T(8,128)(2,1)} %refs_0_.7) | copy-start | bytes 12582916
  35.7 8.8 %collective-permute-start.3 = (bf16[32,16,256]{2,1,0:T(8,128)(2,1)S(1)}, bf16[32,16,256]{2,1,0:T(8,128)(2,1)S(1)}, u32[]{:S(2)}, u32[]{:S(2)}) collective-permute-start(bf16[32,16,256]{2,1,0:T(8,128)(2,1)S(1)} %get-tuple-element.50), channel_id=1, source_target_pairs={{4,8},{8,4},{12,16},{16,12},{20,24},{24,20},{5,9},{9,5},{13,17},{1... | collective-permute-start | bytes 786440 | tf_op jit(solution)/shard_map/ppermute | solution.py:540
  41.8 11.5 %collective-permute-start.6 = (bf16[3,8,16,256]{3,2,1,0:T(8,128)(2,1)S(1)}, bf16[3,8,16,256]{3,2,1,0:T(8,128)(2,1)S(1)}, u32[]{:S(2)}, u32[]{:S(2)}) collective-permute-start(bf16[3,8,16,256]{3,2,1,0:T(8,128)(2,1)S(1)} %get-tuple-element.63), channel_id=1, source_target_pairs={{0,2},{2,0},{1,3},{3,1},{4,6},{6,4},{5,7},{7,5},{8,10},{10,8},{9,1... | collective-permute-start | bytes 589832 | tf_op jit(solution)/shard_map/ppermute | solution.py:540
  48.7 8.9 %collective-permute-start.5 = (bf16[3,8,16,256]{3,2,1,0:T(8,128)(2,1)S(1)}, bf16[3,8,16,256]{3,2,1,0:T(8,128)(2,1)S(1)}, u32[]{:S(2)}, u32[]{:S(2)}) collective-permute-start(bf16[3,8,16,256]{3,2,1,0:T(8,128)(2,1)S(1)} %get-tuple-element.62), channel_id=1, source_target_pairs={{0,3},{3,0},{1,2},{2,1},{4,7},{7,4},{5,6},{6,5},{8,11},{11,8},{9,1... | collective-permute-start | bytes 589832 | tf_op jit(solution)/shard_map/ppermute | solution.py:540
  50.9 20.1 %collective-permute-start.4 = (bf16[3,8,16,256]{3,2,1,0:T(8,128)(2,1)S(1)}, bf16[3,8,16,256]{3,2,1,0:T(8,128)(2,1)S(1)}, u32[]{:S(2)}, u32[]{:S(2)}) collective-permute-start(bf16[3,8,16,256]{3,2,1,0:T(8,128)(2,1)S(1)} %get-tuple-element.61), channel_id=1, source_target_pairs={{0,1},{1,0},{2,3},{3,2},{4,5},{5,4},{6,7},{7,6},{8,9},{9,8},{10,11... | collective-permute-start | bytes 589832 | tf_op jit(solution)/shard_map/ppermute | solution.py:540
  57.6 22.9 %collective-permute-start.9 = (bf16[4,8,16,256]{3,2,1,0:T(8,128)(2,1)S(1)}, bf16[4,8,16,256]{3,2,1,0:T(8,128)(2,1)S(1)}, u32[]{:S(2)}, u32[]{:S(2)}) collective-permute-start(bf16[4,8,16,256]{3,2,1,0:T(8,128)(2,1)S(1)} %get-tuple-element.73), channel_id=1, source_target_pairs={{0,2},{2,0},{1,3},{3,1},{4,6},{6,4},{5,7},{7,5},{8,10},{10,8},{9,1... | collective-permute-start | bytes 786440 | tf_op jit(solution)/shard_map/ppermute | solution.py:540
  61.8 20.2 %collective-permute-start.7 = (bf16[4,8,16,256]{3,2,1,0:T(8,128)(2,1)S(1)}, bf16[4,8,16,256]{3,2,1,0:T(8,128)(2,1)S(1)}, u32[]{:S(2)}, u32[]{:S(2)}) collective-permute-start(bf16[4,8,16,256]{3,2,1,0:T(8,128)(2,1)S(1)} %get-tuple-element.68), channel_id=1, source_target_pairs={{0,3},{3,0},{1,2},{2,1},{4,7},{7,4},{5,6},{6,5},{8,11},{11,8},{9,1... | collective-permute-start | bytes 786440 | tf_op jit(solution)/shard_map/ppermute | solution.py:540
  75.2 13.1 %collective-permute-start.8 = (bf16[4,8,16,256]{3,2,1,0:T(8,128)(2,1)S(1)}, bf16[4,8,16,256]{3,2,1,0:T(8,128)(2,1)S(1)}, u32[]{:S(2)}, u32[]{:S(2)}) collective-permute-start(bf16[4,8,16,256]{3,2,1,0:T(8,128)(2,1)S(1)} %get-tuple-element.69), channel_id=1, source_target_pairs={{0,1},{1,0},{2,3},{3,2},{4,5},{5,4},{6,7},{7,6},{8,9},{9,8},{10,11... | collective-permute-start | bytes 786440 | tf_op jit(solution)/shard_map/ppermute | solution.py:540

commit v17 on v16

--- a/solution.py
+++ b/solution.py
@@ -469,11 +469,11 @@
     parts, own, block, size = spectral_ref.shape
     bands, _, rows, pitch = out_ref.shape
     share = block * pl.num_programs(0)
-    step = pl.program_id(0)
+    step, half = pl.program_id(0), pl.program_id(1)
     lines = parts * own
     apart, stretch = block + 1, pitch + 1
 
-    @pl.when(step == 0)
+    @pl.when((step == 0) & (half == 0))
     def _():
         for h in range(sums.shape[0]):
             for l in range(own):
@@ -502,9 +502,11 @@
                 at = r * share + step * block + i
                 for h in range(sums.shape[0]):
                     piece = result[r * own : (r + 1) * own, h * LANES : (h + 1) * LANES]
-                    sums[h, pl.ds(at, own, stride=stretch), :] = piece
-
-    @pl.when(step == pl.num_programs(0) - 1)
+                    place_of = pl.ds(at, own, stride=stretch)
+                    before = jnp.where(half > 0, sums[h, place_of, :], 0.0)
+                    sums[h, place_of, :] = before + piece
+
+    @pl.when((step == pl.num_programs(0) - 1) & (half == pl.num_programs(1) - 1))
     def _():
         some = LANES // rows
         for l in range(own):
@@ -517,18 +519,20 @@
     rows = legendre.shape[2] // bands
     pitch = -(-parts * share // LANES) * LANES
     block = 16 if share % 16 == 0 else 8
+    halves = 2 if size % (2 * LANES) == 0 else 1
+    depth = size // halves
     shape = (bands, own, rows, pitch)
     return pl.pallas_call(
         legendre_kernel,
-        grid=(share // block,),
+        grid=(share // block, halves),
         in_specs=[
-            pl.BlockSpec((parts, own, block, size), lambda i: (0, 0, i, 0)),
-            pl.BlockSpec((block,) + legendre.shape[1:], lambda i: (i, 0, 0)),
+            pl.BlockSpec((parts, own, block, depth), lambda i, n: (0, 0, i, n)),
+            pl.BlockSpec((block, depth, legendre.shape[2]), lambda i, n: (i, n, 0)),
         ],
-        out_specs=pl.BlockSpec(shape, lambda i: (0, 0, 0, 0)),
+        out_specs=pl.BlockSpec(shape, lambda i, n: (0, 0, 0, 0)),
         out_shape=pltpu.VMEM(shape, BF16),
         scratch_shapes=[
-            pltpu.VMEM((size // LANES, parts * own * (block + 1), LANES), F32),
+            pltpu.VMEM((depth // LANES, parts * own * (block + 1), LANES), F32),
             pltpu.VMEM((legendre.shape[2] // LANES, own * (pitch + 1), LANES), F32),
         ],
         compiler_params=pltpu.CompilerParams(vmem_limit_bytes=54 * MIB),

time: 90.4 us -> 93.2 us (1.031)
  Pallas kernels: 50.4 us -> 53.1 us
    pallas_call x1, Pallas kernels: 14.3 us -> 17.1 us  [legendre_sums(): pl.pallas_call(legendre_kernel, grid=(share // block, halves), in_specs=[...]
  transfers between devices with their start and end apart: 11 -> 11, of which waited for: 3 -> 3; matrix products, arithmetic and copies ran while one was open for 0% -> 0% of each run, Pallas kernels for 38% -> 37%
where the time goes in v17:
time: 93.2 us; the launch traced here: 92.7 us
  Pallas kernels  53.1 us (57%)
  starting transfers between devices  27.9 us (30%)
  waiting for transfers between devices  10.8 us (12%)
    ppermute x10, starting transfers between devices, exchange(): lax.ppermute(value, axis, [p for a, b in pairs for p in ((a, b), (b, a))])  22.7 us
    pallas_call x1, Pallas kernels, legendre_sums(): pl.pallas_call(legendre_kernel, grid=(share // block, halves), in_specs=[...  17.1 us
    pallas_call x4, Pallas kernels, chemistry(): pl.pallas_call(functools.partial(chem_kernel, scale, k), grid_spec=pltpu....  17.1 us
    ppermute x10, waiting for transfers between devices, exchange(): lax.ppermute(value, axis, [p for a, b in pairs for p in ((a, b), (b, a))])  8.76 us
    pallas_call x1, Pallas kernels, tables(): pl.pallas_call(functools.partial(table_kernel, info.shape[0] - rows), gri...  5.75 us
    pallas_call x1, Pallas kernels, synthesis(): pl.pallas_call(synth_kernel, grid_spec=pltpu.PrefetchScalarGridSpec(num_s...  5.34 us
    all_to_all x1, starting transfers between devices, body(): recv = lax.all_to_all(sent, 'lat', split_axis=0, concat_axis=0, tiled=True)  5.17 us
    pallas_call x1, Pallas kernels, edges(): pl.pallas_call(edge_kernel, grid_spec=pltpu.PrefetchScalarGridSpec(num_sc...  4.76 us
  transfers between devices with their start and end apart: 11, of which 3 were waited for; matrix products, arithmetic and copies ran while one was open for 0% of the time, Pallas kernels for 37%

profile of v17, /device:TPU:0, one launch (start us, length us, event | category | flops | bytes accessed | tf_op | source)
XLA Modules:
  0.0 92.7 jit_solution(10456751998591037438)
XLA Ops:
  0.6 0.0 copy-start.4
  0.6 0.0 copy-start.5
  0.7 0.0 copy-start.1
  0.7 0.0 copy-start.2
  0.7 17.1 %legendre.1 = bf16[8,8,16,512]{3,2,1,0:T(8,128)(2,1)} custom-call(bf16[6,8,80,1280]{3,2,1,0:T(8,128)(2,1)} %spectral_ref.1, bf16[80,1280,128]{2,1,0:T(8,128)(2,1)} %legendre_ref.1), custom_call_target="tpu_custom_call" | custom-call | flops 1258291200 | bytes 36044800 | tf_op jit(solution)/shard_map/legendre/pallas_call | solution.py:525
  17.8 0.0 copy-start.3
  17.8 0.0 copy-done.4
  17.8 0.0 copy-done.5
  17.8 0.1 pad_add_fusion.info
  17.9 5.2 %all-to-all-start = ((bf16[8,8,16,512]{3,2,1,0:T(8,128)(2,1)}), bf16[8,8,16,512]{3,2,1,0:T(8,128)(2,1)S(1)}, u32[]{:S(2)}, u32[]{:S(2)}) async-start(bf16[8,8,16,512]{3,2,1,0:T(8,128)(2,1)} %legendre.1), calls=%async_computation | async-start | bytes 2097152 | tf_op jit(solution)/shard_map/all_to_all | solution.py:564
  23.0 0.0 copy-done.1
  23.0 0.0 copy-done.2
  23.0 4.8 %edges.1 = (bf16[32,16,256]{2,1,0:T(8,128)(2,1)S(1)}, bf16[32,16,256]{2,1,0:T(8,128)(2,1)S(1)}, bf16[256,128]{1,0:T(8,128)(2,1)S(1)}, bf16[256,128]{1,0:T(8,128)(2,1)S(1)}, bf16[512,512]{1,0:T(8,128)(2,1)S(1)}) custom-call(s32[22]{0:T(128)S(1)} %pad_add_fusion.info, bf16[16,32,16,256]{3,2,1,0:T(8,128)(2,1)} %refs_0_.7, f32[16,16]{1,0:T(8,128)S(1)} %copy-done.1, ...), custom_call_target="tpu_custom_call" | custom-call | flops 268435456 | bytes 4194304 | tf_op jit(solution)/shard_map/edges/pallas_call | solution.py:284
  27.8 0.6 collective-permute-start
  28.4 1.6 %collective-permute-start.1 = (bf16[256,128]{1,0:T(8,128)(2,1)S(1)}, bf16[256,128]{1,0:T(8,128)(2,1)S(1)}, u32[]{:S(2)}, u32[]{:S(2)}) collective-permute-start(bf16[256,128]{1,0:T(8,128)(2,1)S(1)} %get-tuple-element.46), channel_id=1, source_target_pairs={{0,1},{1,0},{2,3},{3,2},{4,5},{5,4},{6,7},{7,6},{8,9},{9,8},{10,11... | collective-permute-start | bytes 196616 | tf_op jit(solution)/shard_map/ppermute | solution.py:544
  29.9 0.7 collective-permute-start.2
  30.6 0.0 copy-done.3
  30.6 5.8 %tables.1 = (bf16[16,1280,128]{2,1,0:T(8,128)(2,1)}, f32[16,2,8,640]{3,2,1,0:T(8,128)}) custom-call(s32[22]{0:T(128)S(1)} %pad_add_fusion.info, s32[1,640]{1,0:T(1,128)S(1)} %broadcast_in_dim.3.waves_ref), custom_call_target="tpu_custom_call" | custom-call | flops 10485760 | bytes 5242880 | tf_op jit(solution)/shard_map/tables/pallas_call | solution.py:82
  36.4 0.0 collective-permute-done.1.refs_3_
  36.4 0.0 collective-permute-done.2.refs_4_
  36.4 0.0 collective-permute-done.refs_1_
  36.4 2.0 %all-to-all-done.recv_ref = bf16[8,8,16,512]{3,2,1,0:T(8,128)(2,1)S(1)} async-done(((bf16[8,8,16,512]{3,2,1,0:T(8,128)(2,1)}), bf16[8,8,16,512]{3,2,1,0:T(8,128)(2,1)S(1)}, u32[]{:S(2)}, u32[]{:S(2)}) %all-to-all-start) | async-done | bytes 1048608 | tf_op jit(solution)/shard_map/all_to_all | solution.py:564
  38.4 0.0 copy-start
  38.4 0.8 collective-permute-start.3
  39.2 5.3 %synthesis.1 = (bf16[3,8,16,256]{3,2,1,0:T(8,128)(2,1)S(1)}, bf16[3,8,16,256]{3,2,1,0:T(8,128)(2,1)S(1)}, bf16[3,8,16,256]{3,2,1,0:T(8,128)(2,1)S(1)}, bf16[3,8,16,256]{3,2,1,0:T(8,128)(2,1)S(1)}) custom-call(s32[22]{0:T(128)S(1)} %pad_add_fusion.info, bf16[8,8,16,512]{3,2,1,0:T(8,128)(2,1)S(1)} %all-to-all-done.recv_ref, ...), custom_call_target="tpu_custom_call" | custom-call | flops 1006632960 | bytes 5242880 | tf_op jit(solution)/shard_map/synthesis/pallas_call | solution.py:193
  44.6 2.7 %collective-permute-start.6 = (bf16[3,8,16,256]{3,2,1,0:T(8,128)(2,1)S(1)}, bf16[3,8,16,256]{3,2,1,0:T(8,128)(2,1)S(1)}, u32[]{:S(2)}, u32[]{:S(2)}) collective-permute-start(bf16[3,8,16,256]{3,2,1,0:T(8,128)(2,1)S(1)} %get-tuple-element.63), channel_id=1, source_target_pairs={{0,2},{2,0},{1,3},{3,1},{4,6},{6,4},{5,7},{7,5},{8,10},{10,8},{9,1... | collective-permute-start | bytes 589832 | tf_op jit(solution)/shard_map/ppermute | solution.py:544
  47.2 0.0 collective-permute-done.3.refs_2_
  47.3 0.0 copy-done
  47.3 4.3 %chemistry.4 = (bf16[16,32,16,256]{3,2,1,0:T(8,128)(2,1)}, bf16[4,8,16,256]{3,2,1,0:T(8,128)(2,1)S(1)}) custom-call(s32[22]{0:T(128)S(1)} %pad_add_fusion.info, bf16[16,32,16,256]{3,2,1,0:T(8,128)(2,1)S(1)} %copy-done, bf16[32,16,256]{2,1,0:T(8,128)(2,1)S(1)} %collective-permute-done.refs_1_, bf16[32,16,256]{2,1,0:T(8,128)(2,1)S(1)} %collective-permute-done.3.refs_2_, ...), custom_call_target="tpu_custom_call" | custom-call | flops 524288 | bytes 2048 | tf_op jit(solution)/shard_map/chemistry/pallas_call | solution.py:401
  51.5 2.2 %collective-permute-start.5 = (bf16[3,8,16,256]{3,2,1,0:T(8,128)(2,1)S(1)}, bf16[3,8,16,256]{3,2,1,0:T(8,128)(2,1)S(1)}, u32[]{:S(2)}, u32[]{:S(2)}) collective-permute-start(bf16[3,8,16,256]{3,2,1,0:T(8,128)(2,1)S(1)} %get-tuple-element.62), channel_id=1, source_target_pairs={{0,3},{3,0},{1,2},{2,1},{4,7},{7,4},{5,6},{6,5},{8,11},{11,8},{9,1... | collective-permute-start | bytes 589832 | tf_op jit(solution)/shard_map/ppermute | solution.py:544
  53.7 0.0 collective-permute-start.4
  53.7 2.4 %collective-permute-done.6.refs_5_ = bf16[3,8,16,256]{3,2,1,0:T(8,128)(2,1)S(1)} collective-permute-done((bf16[3,8,16,256]{3,2,1,0:T(8,128)(2,1)S(1)}, bf16[3,8,16,256]{3,2,1,0:T(8,128)(2,1)S(1)}, u32[]{:S(2)}, u32[]{:S(2)}) %collective-permute-start.6) | collective-permute-done | bytes 196640 | tf_op jit(solution)/shard_map/ppermute | solution.py:544
  56.1 4.3 %chemistry.5 = (bf16[16,32,16,256]{3,2,1,0:T(8,128)(2,1)}, bf16[4,8,16,256]{3,2,1,0:T(8,128)(2,1)S(1)}) custom-call(s32[22]{0:T(128)S(1)} %pad_add_fusion.info, bf16[16,32,16,256]{3,2,1,0:T(8,128)(2,1)S(1)} %copy-done, bf16[32,16,256]{2,1,0:T(8,128)(2,1)S(1)} %collective-permute-done.refs_1_, ...), custom_call_target="tpu_custom_call", output_to_operand_aliasing={{0}: (8, {})} | custom-call | flops 524288 | bytes 2048 | tf_op jit(solution)/shard_map/chemistry/pallas_call | solution.py:401
  60.4 0.0 collective-permute-start.9
  60.4 0.0 collective-permute-done.5.refs_5_
  60.4 4.3 %chemistry.6 = (bf16[16,32,16,256]{3,2,1,0:T(8,128)(2,1)}, bf16[4,8,16,256]{3,2,1,0:T(8,128)(2,1)S(1)}) custom-call(s32[22]{0:T(128)S(1)} %pad_add_fusion.info, bf16[16,32,16,256]{3,2,1,0:T(8,128)(2,1)S(1)} %copy-done, bf16[32,16,256]{2,1,0:T(8,128)(2,1)S(1)} %collective-permute-done.refs_1_, ...), custom_call_target="tpu_custom_call", output_to_operand_aliasing={{0}: (8, {})} | custom-call | flops 524288 | bytes 2048 | tf_op jit(solution)/shard_map/chemistry/pallas_call | solution.py:401
  64.6 9.1 %collective-permute-start.7 = (bf16[4,8,16,256]{3,2,1,0:T(8,128)(2,1)S(1)}, bf16[4,8,16,256]{3,2,1,0:T(8,128)(2,1)S(1)}, u32[]{:S(2)}, u32[]{:S(2)}) collective-permute-start(bf16[4,8,16,256]{3,2,1,0:T(8,128)(2,1)S(1)} %get-tuple-element.68), channel_id=1, source_target_pairs={{0,3},{3,0},{1,2},{2,1},{4,7},{7,4},{5,6},{6,5},{8,11},{11,8},{9,1... | collective-permute-start | bytes 786440 | tf_op jit(solution)/shard_map/ppermute | solution.py:544
  73.7 0.0 collective-permute-done.4.refs_5_
  73.7 4.3 %chemistry.7 = (bf16[16,32,16,256]{3,2,1,0:T(8,128)(2,1)}, bf16[4,8,16,256]{3,2,1,0:T(8,128)(2,1)S(1)}) custom-call(s32[22]{0:T(128)S(1)} %pad_add_fusion.info, bf16[16,32,16,256]{3,2,1,0:T(8,128)(2,1)S(1)} %copy-done, bf16[32,16,256]{2,1,0:T(8,128)(2,1)S(1)} %collective-permute-done.refs_1_, ...), custom_call_target="tpu_custom_call", output_to_operand_aliasing={{0}: (8, {})} | custom-call | flops 524288 | bytes 2048 | tf_op jit(solution)/shard_map/chemistry/pallas_call | solution.py:401
  78.0 5.2 %collective-permute-start.8 = (bf16[4,8,16,256]{3,2,1,0:T(8,128)(2,1)S(1)}, bf16[4,8,16,256]{3,2,1,0:T(8,128)(2,1)S(1)}, u32[]{:S(2)}, u32[]{:S(2)}) collective-permute-start(bf16[4,8,16,256]{3,2,1,0:T(8,128)(2,1)S(1)} %get-tuple-element.69), channel_id=1, source_target_pairs={{0,1},{1,0},{2,3},{3,2},{4,5},{5,4},{6,7},{7,6},{8,9},{9,8},{10,11... | collective-permute-start | bytes 786440 | tf_op jit(solution)/shard_map/ppermute | solution.py:544
  83.2 0.0 collective-permute-done.9.refs_1_
  83.2 1.6 %spread.2.refs_2_ = f32[4,8,16,1024]{3,2,1,0:T(8,128)} custom-call(s32[22]{0:T(128)S(1)} %pad_add_fusion.info, bf16[4,8,16,256]{3,2,1,0:T(8,128)(2,1)S(1)} %get-tuple-element.72.refs_0_, bf16[4,8,16,256]{3,2,1,0:T(8,128)(2,1)S(1)} %collective-permute-done.9.refs_1_), custom_call_target="tpu_custom_call" | custom-call | flops 4 | bytes 4 | tf_op jit(solution)/shard_map/spread/pallas_call | solution.py:451
  84.8 0.0 collective-permute-done.7.refs_0_
  84.8 6.3 %collective-permute-done.8.refs_1_ = bf16[4,8,16,256]{3,2,1,0:T(8,128)(2,1)S(1)} collective-permute-done((bf16[4,8,16,256]{3,2,1,0:T(8,128)(2,1)S(1)}, bf16[4,8,16,256]{3,2,1,0:T(8,128)(2,1)S(1)}, u32[]{:S(2)}, u32[]{:S(2)}) %collective-permute-start.8) | collective-permute-done | bytes 262176 | tf_op jit(solution)/shard_map/ppermute | solution.py:544
  91.1 1.6 %spread.3 = f32[4,8,16,1024]{3,2,1,0:T(8,128)} custom-call(s32[22]{0:T(128)S(1)} %pad_add_fusion.info, bf16[4,8,16,256]{3,2,1,0:T(8,128)(2,1)S(1)} %collective-permute-done.7.refs_0_, bf16[4,8,16,256]{3,2,1,0:T(8,128)(2,1)S(1)} %collective-permute-done.8.refs_1_, f32[4,8,16,1024]{3,2,1,0:T(8,128)} %spread.2.refs_2_), custom_call_target="tpu_custom_call", output_to_operand_aliasing={{}: (3, {})} | custom-call | flops 4 | bytes 4 | tf_op jit(solution)/shard_map/spread/pallas_call | solution.py:451
  (1 shorter events, 0.0 us)
Async XLA Ops:
  0.6 17.1 %copy-start.4 = (s32[16]{0:T(128)S(1)}, s32[16]{0:T(128)}, u32[]{:S(2)}) copy-start(s32[16]{0:T(128)} %param.11) | copy-start | bytes 196
  0.6 17.1 %copy-start.5 = (s32[4]{0:T(128)S(1)}, s32[4]{0:T(128)}, u32[]{:S(2)}) copy-start(s32[4]{0:T(128)} %param.15) | copy-start | bytes 52
  0.7 22.4 %copy-start.1 = (f32[16,16]{1,0:T(8,128)S(1)}, f32[16,16]{1,0:T(8,128)}, u32[]{:S(2)}) copy-start(f32[16,16]{1,0:T(8,128)} %base_ref.1) | copy-start | bytes 3076
  0.7 22.4 %copy-start.2 = (f32[16,16]{1,0:T(8,128)S(1)}, f32[16,16]{1,0:T(8,128)}, u32[]{:S(2)}) copy-start(f32[16,16]{1,0:T(8,128)} %temp_ref.1) | copy-start | bytes 3076
  17.8 12.8 %copy-start.3 = (s32[640]{0:T(1024)S(1)}, s32[640]{0:T(1024)}, u32[]{:S(2)}) copy-start(s32[640]{0:T(1024)} %param.10) | copy-start | bytes 7684
  17.9 20.6 %all-to-all-start = ((bf16[8,8,16,512]{3,2,1,0:T(8,128)(2,1)}), bf16[8,8,16,512]{3,2,1,0:T(8,128)(2,1)S(1)}, u32[]{:S(2)}, u32[]{:S(2)}) async-start(bf16[8,8,16,512]{3,2,1,0:T(8,128)(2,1)} %legendre.1), calls=%async_computation | async-start | bytes 2097152 | tf_op jit(solution)/shard_map/all_to_all | solution.py:564
  27.8 8.6 %collective-permute-start = (bf16[32,16,256]{2,1,0:T(8,128)(2,1)S(1)}, bf16[32,16,256]{2,1,0:T(8,128)(2,1)S(1)}, u32[]{:S(2)}, u32[]{:S(2)}) collective-permute-start(bf16[32,16,256]{2,1,0:T(8,128)(2,1)S(1)} %get-tuple-element.45), channel_id=1, source_target_pairs={{0,4},{4,0},{8,12},{12,8},{16,20},{20,16},{24,28},{28,24},{1,5},{5... | collective-permute-start | bytes 786440 | tf_op jit(solution)/shard_map/ppermute | solution.py:544
  28.4 8.0 %collective-permute-start.1 = (bf16[256,128]{1,0:T(8,128)(2,1)S(1)}, bf16[256,128]{1,0:T(8,128)(2,1)S(1)}, u32[]{:S(2)}, u32[]{:S(2)}) collective-permute-start(bf16[256,128]{1,0:T(8,128)(2,1)S(1)} %get-tuple-element.46), channel_id=1, source_target_pairs={{0,1},{1,0},{2,3},{3,2},{4,5},{5,4},{6,7},{7,6},{8,9},{9,8},{10,11... | collective-permute-start | bytes 196616 | tf_op jit(solution)/shard_map/ppermute | solution.py:544
  29.9 6.4 %collective-permute-start.2 = (bf16[256,128]{1,0:T(8,128)(2,1)S(1)}, bf16[256,128]{1,0:T(8,128)(2,1)S(1)}, u32[]{:S(2)}, u32[]{:S(2)}) collective-permute-start(bf16[256,128]{1,0:T(8,128)(2,1)S(1)} %get-tuple-element.47), channel_id=1, source_target_pairs={{1,2},{2,1},{5,6},{6,5},{9,10},{10,9},{13,14},{14,13},{17,18},{18,... | collective-permute-start | bytes 196616 | tf_op jit(solution)/shard_map/ppermute | solution.py:544
  38.4 8.8 %copy-start = (bf16[16,32,16,256]{3,2,1,0:T(8,128)(2,1)S(1)}, bf16[16,32,16,256]{3,2,1,0:T(8,128)(2,1)}, u32[]{:S(2)}) copy-start(bf16[16,32,16,256]{3,2,1,0:T(8,128)(2,1)} %refs_0_.7) | copy-start | bytes 12582916
  38.4 8.8 %collective-permute-start.3 = (bf16[32,16,256]{2,1,0:T(8,128)(2,1)S(1)}, bf16[32,16,256]{2,1,0:T(8,128)(2,1)S(1)}, u32[]{:S(2)}, u32[]{:S(2)}) collective-permute-start(bf16[32,16,256]{2,1,0:T(8,128)(2,1)S(1)} %get-tuple-element.50), channel_id=1, source_target_pairs={{4,8},{8,4},{12,16},{16,12},{20,24},{24,20},{5,9},{9,5},{13,17},{1... | collective-permute-start | bytes 786440 | tf_op jit(solution)/shard_map/ppermute | solution.py:544
  44.6 11.5 %collective-permute-start.6 = (bf16[3,8,16,256]{3,2,1,0:T(8,128)(2,1)S(1)}, bf16[3,8,16,256]{3,2,1,0:T(8,128)(2,1)S(1)}, u32[]{:S(2)}, u32[]{:S(2)}) collective-permute-start(bf16[3,8,16,256]{3,2,1,0:T(8,128)(2,1)S(1)} %get-tuple-element.63), channel_id=1, source_target_pairs={{0,2},{2,0},{1,3},{3,1},{4,6},{6,4},{5,7},{7,5},{8,10},{10,8},{9,1... | collective-permute-start | bytes 589832 | tf_op jit(solution)/shard_map/ppermute | solution.py:544
  51.5 8.9 %collective-permute-start.5 = (bf16[3,8,16,256]{3,2,1,0:T(8,128)(2,1)S(1)}, bf16[3,8,16,256]{3,2,1,0:T(8,128)(2,1)S(1)}, u32[]{:S(2)}, u32[]{:S(2)}) collective-permute-start(bf16[3,8,16,256]{3,2,1,0:T(8,128)(2,1)S(1)} %get-tuple-element.62), channel_id=1, source_target_pairs={{0,3},{3,0},{1,2},{2,1},{4,7},{7,4},{5,6},{6,5},{8,11},{11,8},{9,1... | collective-permute-start | bytes 589832 | tf_op jit(solution)/shard_map/ppermute | solution.py:544
  53.7 20.1 %collective-permute-start.4 = (bf16[3,8,16,256]{3,2,1,0:T(8,128)(2,1)S(1)}, bf16[3,8,16,256]{3,2,1,0:T(8,128)(2,1)S(1)}, u32[]{:S(2)}, u32[]{:S(2)}) collective-permute-start(bf16[3,8,16,256]{3,2,1,0:T(8,128)(2,1)S(1)} %get-tuple-element.61), channel_id=1, source_target_pairs={{0,1},{1,0},{2,3},{3,2},{4,5},{5,4},{6,7},{7,6},{8,9},{9,8},{10,11... | collective-permute-start | bytes 589832 | tf_op jit(solution)/shard_map/ppermute | solution.py:544
  60.4 22.9 %collective-permute-start.9 = (bf16[4,8,16,256]{3,2,1,0:T(8,128)(2,1)S(1)}, bf16[4,8,16,256]{3,2,1,0:T(8,128)(2,1)S(1)}, u32[]{:S(2)}, u32[]{:S(2)}) collective-permute-start(bf16[4,8,16,256]{3,2,1,0:T(8,128)(2,1)S(1)} %get-tuple-element.73), channel_id=1, source_target_pairs={{0,2},{2,0},{1,3},{3,1},{4,6},{6,4},{5,7},{7,5},{8,10},{10,8},{9,1... | collective-permute-start | bytes 786440 | tf_op jit(solution)/shard_map/ppermute | solution.py:544
  64.6 20.2 %collective-permute-start.7 = (bf16[4,8,16,256]{3,2,1,0:T(8,128)(2,1)S(1)}, bf16[4,8,16,256]{3,2,1,0:T(8,128)(2,1)S(1)}, u32[]{:S(2)}, u32[]{:S(2)}) collective-permute-start(bf16[4,8,16,256]{3,2,1,0:T(8,128)(2,1)S(1)} %get-tuple-element.68), channel_id=1, source_target_pairs={{0,3},{3,0},{1,2},{2,1},{4,7},{7,4},{5,6},{6,5},{8,11},{11,8},{9,1... | collective-permute-start | bytes 786440 | tf_op jit(solution)/shard_map/ppermute | solution.py:544
  78.0 13.1 %collective-permute-start.8 = (bf16[4,8,16,256]{3,2,1,0:T(8,128)(2,1)S(1)}, bf16[4,8,16,256]{3,2,1,0:T(8,128)(2,1)S(1)}, u32[]{:S(2)}, u32[]{:S(2)}) collective-permute-start(bf16[4,8,16,256]{3,2,1,0:T(8,128)(2,1)S(1)} %get-tuple-element.69), channel_id=1, source_target_pairs={{0,1},{1,0},{2,3},{3,2},{4,5},{5,4},{6,7},{7,6},{8,9},{9,8},{10,11... | collective-permute-start | bytes 786440 | tf_op jit(solution)/shard_map/ppermute | solution.py:544

commit v18 on v16

--- a/solution.py
+++ b/solution.py
@@ -561,15 +561,15 @@
     *ends, react = edges(tracers, react_base, react_temp, info)
     halos = [
         exchange(ends[0], "lat", neighbours("lat", 0)),
+        exchange(ends[1], "lat", neighbours("lat", 1)),
         exchange(ends[2], "lon", neighbours("lon", 0)),
         exchange(ends[3], "lon", neighbours("lon", 1)),
     ]
     react, wave_ids = lax.optimization_barrier((react, wave_ids))
     table, twiddle = tables(info, wave_ids, rows, tiles * tile // LANES)
-    recv, table, twiddle, react, halos, last = lax.optimization_barrier(
-        (recv, table, twiddle, react, halos, ends[1])
+    recv, table, twiddle, react, halos = lax.optimization_barrier(
+        (recv, table, twiddle, react, halos)
     )
-    halos.insert(1, exchange(last, "lat", neighbours("lat", 1)))
     grids = synthesis(recv, table, twiddle, info, tiles, tile)
 
     middle, inner = list(range(tiles // 2, tiles)), list(range(1, tiles // 2))

time: 90.4 us -> 97.6 us (1.080)
  the two profiles are of different devices: /device:TPU:0 before, /device:TPU:2 now
where the time goes in v18:
time: 97.6 us; the launch traced here: 97.4 us
  Pallas kernels  50.6 us (52%)
  waiting for transfers between devices  24 us (25%)
  starting transfers between devices  22 us (23%)
    ppermute x10, waiting for transfers between devices, exchange(): lax.ppermute(value, axis, [p for a, b in pairs for p in ((a, b), (b, a))])  24 us
    ppermute x10, starting transfers between devices, exchange(): lax.ppermute(value, axis, [p for a, b in pairs for p in ((a, b), (b, a))])  17.7 us
    pallas_call x4, Pallas kernels, chemistry(): pl.pallas_call(functools.partial(chem_kernel, scale, k), grid_spec=pltpu....  17 us
    pallas_call x1, Pallas kernels, legendre_sums(): pl.pallas_call(legendre_kernel, grid=(share // block,), in_specs=[pl.Bloc...  14.3 us
    pallas_call x1, Pallas kernels, tables(): pl.pallas_call(functools.partial(table_kernel, info.shape[0] - rows), gri...  5.75 us
    pallas_call x1, Pallas kernels, synthesis(): pl.pallas_call(synth_kernel, grid_spec=pltpu.PrefetchScalarGridSpec(num_s...  5.6 us
    pallas_call x1, Pallas kernels, edges(): pl.pallas_call(edge_kernel, grid_spec=pltpu.PrefetchScalarGridSpec(num_sc...  4.76 us
    all_to_all x1, starting transfers between devices, body(): recv = lax.all_to_all(sent, 'lat', split_axis=0, concat_axis=0, tiled=True)  4.25 us
  transfers between devices with their start and end apart: 11, of which 5 were waited for; matrix products, arithmetic and copies ran while one was open for 0% of the time, Pallas kernels for 28%

profile of v18, /device:TPU:2, one launch (start us, length us, event | category | flops | bytes accessed | tf_op | source)
XLA Modules:
  0.0 97.4 jit_solution(1002572857628903794)
XLA Ops:
  0.6 0.0 copy-start.4
  0.6 0.0 copy-start.5
  0.7 0.0 copy-start.1
  0.7 0.0 copy-start.2
  0.7 14.3 %legendre.1 = bf16[8,8,16,512]{3,2,1,0:T(8,128)(2,1)} custom-call(bf16[6,8,80,1280]{3,2,1,0:T(8,128)(2,1)} %spectral_ref.1, bf16[80,1280,128]{2,1,0:T(8,128)(2,1)} %legendre_ref.1), custom_call_target="tpu_custom_call" | custom-call | flops 1258291200 | bytes 36044800 | tf_op jit(solution)/shard_map/legendre/pallas_call | solution.py:521
  15.0 0.0 copy-start.3
  15.0 0.0 copy-done.4
  15.0 0.0 copy-done.5
  15.0 0.1 pad_add_fusion.info
  15.1 4.3 %all-to-all-start = ((bf16[8,8,16,512]{3,2,1,0:T(8,128)(2,1)}), bf16[8,8,16,512]{3,2,1,0:T(8,128)(2,1)S(1)}, u32[]{:S(2)}, u32[]{:S(2)}) async-start(bf16[8,8,16,512]{3,2,1,0:T(8,128)(2,1)} %legendre.1), calls=%async_computation | async-start | bytes 2097152 | tf_op jit(solution)/shard_map/all_to_all | solution.py:560
  19.3 0.0 copy-done.1
  19.3 0.0 copy-done.2
  19.3 4.8 %edges.1 = (bf16[32,16,256]{2,1,0:T(8,128)(2,1)S(1)}, bf16[32,16,256]{2,1,0:T(8,128)(2,1)S(1)}, bf16[256,128]{1,0:T(8,128)(2,1)S(1)}, bf16[256,128]{1,0:T(8,128)(2,1)S(1)}, bf16[512,512]{1,0:T(8,128)(2,1)S(1)}) custom-call(s32[22]{0:T(128)S(1)} %pad_add_fusion.info, bf16[16,32,16,256]{3,2,1,0:T(8,128)(2,1)} %refs_0_.7, f32[16,16]{1,0:T(8,128)S(1)} %copy-done.1, ...), custom_call_target="tpu_custom_call" | custom-call | flops 268435456 | bytes 4194304 | tf_op jit(solution)/shard_map/edges/pallas_call | solution.py:284
  24.1 0.2 collective-permute-start
  24.3 1.9 %collective-permute-start.1 = (bf16[32,16,256]{2,1,0:T(8,128)(2,1)S(1)}, bf16[32,16,256]{2,1,0:T(8,128)(2,1)S(1)}, u32[]{:S(2)}, u32[]{:S(2)}) collective-permute-start(bf16[32,16,256]{2,1,0:T(8,128)(2,1)S(1)} %get-tuple-element.46), channel_id=1, source_target_pairs={{4,8},{8,4},{12,16},{16,12},{20,24},{24,20},{5,9},{9,5},{13,17},{1... | collective-permute-start | bytes 786440 | tf_op jit(solution)/shard_map/ppermute | solution.py:540
  26.2 1.6 %collective-permute-start.2 = (bf16[256,128]{1,0:T(8,128)(2,1)S(1)}, bf16[256,128]{1,0:T(8,128)(2,1)S(1)}, u32[]{:S(2)}, u32[]{:S(2)}) collective-permute-start(bf16[256,128]{1,0:T(8,128)(2,1)S(1)} %get-tuple-element.47), channel_id=1, source_target_pairs={{0,1},{1,0},{2,3},{3,2},{4,5},{5,4},{6,7},{7,6},{8,9},{9,8},{10,11... | collective-permute-start | bytes 196616 | tf_op jit(solution)/shard_map/ppermute | solution.py:540
  27.9 0.7 collective-permute-start.3
  28.5 0.0 copy-done.3
  28.6 5.8 %tables.1 = (bf16[16,1280,128]{2,1,0:T(8,128)(2,1)}, f32[16,2,8,640]{3,2,1,0:T(8,128)}) custom-call(s32[22]{0:T(128)S(1)} %pad_add_fusion.info, s32[1,640]{1,0:T(1,128)S(1)} %broadcast_in_dim.3.waves_ref), custom_call_target="tpu_custom_call" | custom-call | flops 10485760 | bytes 5242880 | tf_op jit(solution)/shard_map/tables/pallas_call | solution.py:82
  34.3 0.0 collective-permute-done.2.refs_3_
  34.3 0.0 collective-permute-done.3.refs_4_
  34.3 0.0 collective-permute-done.refs_1_
  34.3 2.6 %collective-permute-done.1.refs_2_ = bf16[32,16,256]{2,1,0:T(8,128)(2,1)S(1)} collective-permute-done((bf16[32,16,256]{2,1,0:T(8,128)(2,1)S(1)}, bf16[32,16,256]{2,1,0:T(8,128)(2,1)S(1)}, u32[]{:S(2)}, u32[]{:S(2)}) %collective-permute-start.1) | collective-permute-done | bytes 262176 | tf_op jit(solution)/shard_map/ppermute | solution.py:540
  37.0 0.0 all-to-all-done.recv_ref
  37.0 0.0 copy-start
  37.0 5.6 %synthesis.1 = (bf16[3,8,16,256]{3,2,1,0:T(8,128)(2,1)S(1)}, bf16[3,8,16,256]{3,2,1,0:T(8,128)(2,1)S(1)}, bf16[3,8,16,256]{3,2,1,0:T(8,128)(2,1)S(1)}, bf16[3,8,16,256]{3,2,1,0:T(8,128)(2,1)S(1)}) custom-call(s32[22]{0:T(128)S(1)} %pad_add_fusion.info, bf16[8,8,16,512]{3,2,1,0:T(8,128)(2,1)S(1)} %all-to-all-done.recv_ref, ...), custom_call_target="tpu_custom_call" | custom-call | flops 1006632960 | bytes 5242880 | tf_op jit(solution)/shard_map/synthesis/pallas_call | solution.py:193
  42.6 2.7 %collective-permute-start.6 = (bf16[3,8,16,256]{3,2,1,0:T(8,128)(2,1)S(1)}, bf16[3,8,16,256]{3,2,1,0:T(8,128)(2,1)S(1)}, u32[]{:S(2)}, u32[]{:S(2)}) collective-permute-start(bf16[3,8,16,256]{3,2,1,0:T(8,128)(2,1)S(1)} %get-tuple-element.63), channel_id=1, source_target_pairs={{0,2},{2,0},{1,3},{3,1},{4,6},{6,4},{5,7},{7,5},{8,10},{10,8},{9,1... | collective-permute-start | bytes 589832 | tf_op jit(solution)/shard_map/ppermute | solution.py:540
  45.2 0.0 copy-done
  45.2 4.3 %chemistry.4 = (bf16[16,32,16,256]{3,2,1,0:T(8,128)(2,1)}, bf16[4,8,16,256]{3,2,1,0:T(8,128)(2,1)S(1)}) custom-call(s32[22]{0:T(128)S(1)} %pad_add_fusion.info, bf16[16,32,16,256]{3,2,1,0:T(8,128)(2,1)S(1)} %copy-done, bf16[32,16,256]{2,1,0:T(8,128)(2,1)S(1)} %collective-permute-done.refs_1_, bf16[32,16,256]{2,1,0:T(8,128)(2,1)S(1)} %collective-permute-done.1.refs_2_, ...), custom_call_target="tpu_custom_call" | custom-call | flops 524288 | bytes 2048 | tf_op jit(solution)/shard_map/chemistry/pallas_call | solution.py:401
  49.5 1.6 %collective-permute-start.5 = (bf16[3,8,16,256]{3,2,1,0:T(8,128)(2,1)S(1)}, bf16[3,8,16,256]{3,2,1,0:T(8,128)(2,1)S(1)}, u32[]{:S(2)}, u32[]{:S(2)}) collective-permute-start(bf16[3,8,16,256]{3,2,1,0:T(8,128)(2,1)S(1)} %get-tuple-element.62), channel_id=1, source_target_pairs={{0,3},{3,0},{1,2},{2,1},{4,7},{7,4},{5,6},{6,5},{8,11},{11,8},{9,1... | collective-permute-start | bytes 589832 | tf_op jit(solution)/shard_map/ppermute | solution.py:540
  51.1 0.0 collective-permute-start.4
  51.1 3.7 %collective-permute-done.6.refs_5_ = bf16[3,8,16,256]{3,2,1,0:T(8,128)(2,1)S(1)} collective-permute-done((bf16[3,8,16,256]{3,2,1,0:T(8,128)(2,1)S(1)}, bf16[3,8,16,256]{3,2,1,0:T(8,128)(2,1)S(1)}, u32[]{:S(2)}, u32[]{:S(2)}) %collective-permute-start.6) | collective-permute-done | bytes 196640 | tf_op jit(solution)/shard_map/ppermute | solution.py:540
  54.8 4.3 %chemistry.5 = (bf16[16,32,16,256]{3,2,1,0:T(8,128)(2,1)}, bf16[4,8,16,256]{3,2,1,0:T(8,128)(2,1)S(1)}) custom-call(s32[22]{0:T(128)S(1)} %pad_add_fusion.info, bf16[16,32,16,256]{3,2,1,0:T(8,128)(2,1)S(1)} %copy-done, bf16[32,16,256]{2,1,0:T(8,128)(2,1)S(1)} %collective-permute-done.refs_1_, ...), custom_call_target="tpu_custom_call", output_to_operand_aliasing={{0}: (8, {})} | custom-call | flops 524288 | bytes 2048 | tf_op jit(solution)/shard_map/chemistry/pallas_call | solution.py:401
  59.0 0.0 collective-permute-done.5.refs_5_
  59.0 4.3 %chemistry.6 = (bf16[16,32,16,256]{3,2,1,0:T(8,128)(2,1)}, bf16[4,8,16,256]{3,2,1,0:T(8,128)(2,1)S(1)}) custom-call(s32[22]{0:T(128)S(1)} %pad_add_fusion.info, bf16[16,32,16,256]{3,2,1,0:T(8,128)(2,1)S(1)} %copy-done, bf16[32,16,256]{2,1,0:T(8,128)(2,1)S(1)} %collective-permute-done.refs_1_, ...), custom_call_target="tpu_custom_call", output_to_operand_aliasing={{0}: (8, {})} | custom-call | flops 524288 | bytes 2048 | tf_op jit(solution)/shard_map/chemistry/pallas_call | solution.py:401
  63.3 8.5 %collective-permute-start.7 = (bf16[4,8,16,256]{3,2,1,0:T(8,128)(2,1)S(1)}, bf16[4,8,16,256]{3,2,1,0:T(8,128)(2,1)S(1)}, u32[]{:S(2)}, u32[]{:S(2)}) collective-permute-start(bf16[4,8,16,256]{3,2,1,0:T(8,128)(2,1)S(1)} %get-tuple-element.68), channel_id=1, source_target_pairs={{0,3},{3,0},{1,2},{2,1},{4,7},{7,4},{5,6},{6,5},{8,11},{11,8},{9,1... | collective-permute-start | bytes 786440 | tf_op jit(solution)/shard_map/ppermute | solution.py:540
  71.8 0.0 collective-permute-done.4.refs_5_
  71.8 4.3 %chemistry.7 = (bf16[16,32,16,256]{3,2,1,0:T(8,128)(2,1)}, bf16[4,8,16,256]{3,2,1,0:T(8,128)(2,1)S(1)}) custom-call(s32[22]{0:T(128)S(1)} %pad_add_fusion.info, bf16[16,32,16,256]{3,2,1,0:T(8,128)(2,1)S(1)} %copy-done, bf16[32,16,256]{2,1,0:T(8,128)(2,1)S(1)} %collective-permute-done.refs_1_, ...), custom_call_target="tpu_custom_call", output_to_operand_aliasing={{0}: (8, {})} | custom-call | flops 524288 | bytes 2048 | tf_op jit(solution)/shard_map/chemistry/pallas_call | solution.py:401
  76.1 0.0 collective-permute-start.8
  76.1 0.6 collective-permute-start.9
  76.6 2.4 %collective-permute-done.7.refs_0_ = bf16[4,8,16,256]{3,2,1,0:T(8,128)(2,1)S(1)} collective-permute-done((bf16[4,8,16,256]{3,2,1,0:T(8,128)(2,1)S(1)}, bf16[4,8,16,256]{3,2,1,0:T(8,128)(2,1)S(1)}, u32[]{:S(2)}, u32[]{:S(2)}) %collective-permute-start.7) | collective-permute-done | bytes 262176 | tf_op jit(solution)/shard_map/ppermute | solution.py:540
  79.0 7.1 %collective-permute-done.8.refs_1_ = bf16[4,8,16,256]{3,2,1,0:T(8,128)(2,1)S(1)} collective-permute-done((bf16[4,8,16,256]{3,2,1,0:T(8,128)(2,1)S(1)}, bf16[4,8,16,256]{3,2,1,0:T(8,128)(2,1)S(1)}, u32[]{:S(2)}, u32[]{:S(2)}) %collective-permute-start.8) | collective-permute-done | bytes 262176 | tf_op jit(solution)/shard_map/ppermute | solution.py:540
  86.2 8.1 %collective-permute-done.9.refs_1_ = bf16[4,8,16,256]{3,2,1,0:T(8,128)(2,1)S(1)} collective-permute-done((bf16[4,8,16,256]{3,2,1,0:T(8,128)(2,1)S(1)}, bf16[4,8,16,256]{3,2,1,0:T(8,128)(2,1)S(1)}, u32[]{:S(2)}, u32[]{:S(2)}) %collective-permute-start.9) | collective-permute-done | bytes 262176 | tf_op jit(solution)/shard_map/ppermute | solution.py:540
  94.2 1.6 %spread.2.refs_2_ = f32[4,8,16,1024]{3,2,1,0:T(8,128)} custom-call(s32[22]{0:T(128)S(1)} %pad_add_fusion.info, bf16[4,8,16,256]{3,2,1,0:T(8,128)(2,1)S(1)} %get-tuple-element.72.refs_0_, bf16[4,8,16,256]{3,2,1,0:T(8,128)(2,1)S(1)} %collective-permute-done.9.refs_1_), custom_call_target="tpu_custom_call" | custom-call | flops 4 | bytes 4 | tf_op jit(solution)/shard_map/spread/pallas_call | solution.py:451
  95.8 1.6 %spread.3 = f32[4,8,16,1024]{3,2,1,0:T(8,128)} custom-call(s32[22]{0:T(128)S(1)} %pad_add_fusion.info, bf16[4,8,16,256]{3,2,1,0:T(8,128)(2,1)S(1)} %collective-permute-done.7.refs_0_, bf16[4,8,16,256]{3,2,1,0:T(8,128)(2,1)S(1)} %collective-permute-done.8.refs_1_, f32[4,8,16,1024]{3,2,1,0:T(8,128)} %spread.2.refs_2_), custom_call_target="tpu_custom_call", output_to_operand_aliasing={{}: (3, {})} | custom-call | flops 4 | bytes 4 | tf_op jit(solution)/shard_map/spread/pallas_call | solution.py:451
  (1 shorter events, 0.0 us)
Async XLA Ops:
  0.6 14.3 %copy-start.4 = (s32[16]{0:T(128)S(1)}, s32[16]{0:T(128)}, u32[]{:S(2)}) copy-start(s32[16]{0:T(128)} %param.11) | copy-start | bytes 196
  0.6 14.3 %copy-start.5 = (s32[4]{0:T(128)S(1)}, s32[4]{0:T(128)}, u32[]{:S(2)}) copy-start(s32[4]{0:T(128)} %param.15) | copy-start | bytes 52
  0.7 18.7 %copy-start.1 = (f32[16,16]{1,0:T(8,128)S(1)}, f32[16,16]{1,0:T(8,128)}, u32[]{:S(2)}) copy-start(f32[16,16]{1,0:T(8,128)} %base_ref.1) | copy-start | bytes 3076
  0.7 18.7 %copy-start.2 = (f32[16,16]{1,0:T(8,128)S(1)}, f32[16,16]{1,0:T(8,128)}, u32[]{:S(2)}) copy-start(f32[16,16]{1,0:T(8,128)} %temp_ref.1) | copy-start | bytes 3076
  15.0 13.6 %copy-start.3 = (s32[640]{0:T(1024)S(1)}, s32[640]{0:T(1024)}, u32[]{:S(2)}) copy-start(s32[640]{0:T(1024)} %param.10) | copy-start | bytes 7684
  15.1 21.9 %all-to-all-start = ((bf16[8,8,16,512]{3,2,1,0:T(8,128)(2,1)}), bf16[8,8,16,512]{3,2,1,0:T(8,128)(2,1)S(1)}, u32[]{:S(2)}, u32[]{:S(2)}) async-start(bf16[8,8,16,512]{3,2,1,0:T(8,128)(2,1)} %legendre.1), calls=%async_computation | async-start | bytes 2097152 | tf_op jit(solution)/shard_map/all_to_all | solution.py:560
  24.1 10.2 %collective-permute-start = (bf16[32,16,256]{2,1,0:T(8,128)(2,1)S(1)}, bf16[32,16,256]{2,1,0:T(8,128)(2,1)S(1)}, u32[]{:S(2)}, u32[]{:S(2)}) collective-permute-start(bf16[32,16,256]{2,1,0:T(8,128)(2,1)S(1)} %get-tuple-element.45), channel_id=1, source_target_pairs={{0,4},{4,0},{8,12},{12,8},{16,20},{20,16},{24,28},{28,24},{1,5},{5... | collective-permute-start | bytes 786440 | tf_op jit(solution)/shard_map/ppermute | solution.py:540
  24.3 12.7 %collective-permute-start.1 = (bf16[32,16,256]{2,1,0:T(8,128)(2,1)S(1)}, bf16[32,16,256]{2,1,0:T(8,128)(2,1)S(1)}, u32[]{:S(2)}, u32[]{:S(2)}) collective-permute-start(bf16[32,16,256]{2,1,0:T(8,128)(2,1)S(1)} %get-tuple-element.46), channel_id=1, source_target_pairs={{4,8},{8,4},{12,16},{16,12},{20,24},{24,20},{5,9},{9,5},{13,17},{1... | collective-permute-start | bytes 786440 | tf_op jit(solution)/shard_map/ppermute | solution.py:540
  26.2 8.1 %collective-permute-start.2 = (bf16[256,128]{1,0:T(8,128)(2,1)S(1)}, bf16[256,128]{1,0:T(8,128)(2,1)S(1)}, u32[]{:S(2)}, u32[]{:S(2)}) collective-permute-start(bf16[256,128]{1,0:T(8,128)(2,1)S(1)} %get-tuple-element.47), channel_id=1, source_target_pairs={{0,1},{1,0},{2,3},{3,2},{4,5},{5,4},{6,7},{7,6},{8,9},{9,8},{10,11... | collective-permute-start | bytes 196616 | tf_op jit(solution)/shard_map/ppermute | solution.py:540
  27.9 6.4 %collective-permute-start.3 = (bf16[256,128]{1,0:T(8,128)(2,1)S(1)}, bf16[256,128]{1,0:T(8,128)(2,1)S(1)}, u32[]{:S(2)}, u32[]{:S(2)}) collective-permute-start(bf16[256,128]{1,0:T(8,128)(2,1)S(1)} %get-tuple-element.48), channel_id=1, source_target_pairs={{1,2},{2,1},{5,6},{6,5},{9,10},{10,9},{13,14},{14,13},{17,18},{18,... | collective-permute-start | bytes 196616 | tf_op jit(solution)/shard_map/ppermute | solution.py:540
  37.0 8.3 %copy-start = (bf16[16,32,16,256]{3,2,1,0:T(8,128)(2,1)S(1)}, bf16[16,32,16,256]{3,2,1,0:T(8,128)(2,1)}, u32[]{:S(2)}) copy-start(bf16[16,32,16,256]{3,2,1,0:T(8,128)(2,1)} %refs_0_.7) | copy-start | bytes 12582916
  42.6 12.2 %collective-permute-start.6 = (bf16[3,8,16,256]{3,2,1,0:T(8,128)(2,1)S(1)}, bf16[3,8,16,256]{3,2,1,0:T(8,128)(2,1)S(1)}, u32[]{:S(2)}, u32[]{:S(2)}) collective-permute-start(bf16[3,8,16,256]{3,2,1,0:T(8,128)(2,1)S(1)} %get-tuple-element.63), channel_id=1, source_target_pairs={{0,2},{2,0},{1,3},{3,1},{4,6},{6,4},{5,7},{7,5},{8,10},{10,8},{9,1... | collective-permute-start | bytes 589832 | tf_op jit(solution)/shard_map/ppermute | solution.py:540
  49.5 9.5 %collective-permute-start.5 = (bf16[3,8,16,256]{3,2,1,0:T(8,128)(2,1)S(1)}, bf16[3,8,16,256]{3,2,1,0:T(8,128)(2,1)S(1)}, u32[]{:S(2)}, u32[]{:S(2)}) collective-permute-start(bf16[3,8,16,256]{3,2,1,0:T(8,128)(2,1)S(1)} %get-tuple-element.62), channel_id=1, source_target_pairs={{0,3},{3,0},{1,2},{2,1},{4,7},{7,4},{5,6},{6,5},{8,11},{11,8},{9,1... | collective-permute-start | bytes 589832 | tf_op jit(solution)/shard_map/ppermute | solution.py:540
  51.1 20.7 %collective-permute-start.4 = (bf16[3,8,16,256]{3,2,1,0:T(8,128)(2,1)S(1)}, bf16[3,8,16,256]{3,2,1,0:T(8,128)(2,1)S(1)}, u32[]{:S(2)}, u32[]{:S(2)}) collective-permute-start(bf16[3,8,16,256]{3,2,1,0:T(8,128)(2,1)S(1)} %get-tuple-element.61), channel_id=1, source_target_pairs={{0,1},{1,0},{2,3},{3,2},{4,5},{5,4},{6,7},{7,6},{8,9},{9,8},{10,11... | collective-permute-start | bytes 589832 | tf_op jit(solution)/shard_map/ppermute | solution.py:540
  63.3 15.8 %collective-permute-start.7 = (bf16[4,8,16,256]{3,2,1,0:T(8,128)(2,1)S(1)}, bf16[4,8,16,256]{3,2,1,0:T(8,128)(2,1)S(1)}, u32[]{:S(2)}, u32[]{:S(2)}) collective-permute-start(bf16[4,8,16,256]{3,2,1,0:T(8,128)(2,1)S(1)} %get-tuple-element.68), channel_id=1, source_target_pairs={{0,3},{3,0},{1,2},{2,1},{4,7},{7,4},{5,6},{6,5},{8,11},{11,8},{9,1... | collective-permute-start | bytes 786440 | tf_op jit(solution)/shard_map/ppermute | solution.py:540
  76.1 10.1 %collective-permute-start.8 = (bf16[4,8,16,256]{3,2,1,0:T(8,128)(2,1)S(1)}, bf16[4,8,16,256]{3,2,1,0:T(8,128)(2,1)S(1)}, u32[]{:S(2)}, u32[]{:S(2)}) collective-permute-start(bf16[4,8,16,256]{3,2,1,0:T(8,128)(2,1)S(1)} %get-tuple-element.69), channel_id=1, source_target_pairs={{0,1},{1,0},{2,3},{3,2},{4,5},{5,4},{6,7},{7,6},{8,9},{9,8},{10,11... | collective-permute-start | bytes 786440 | tf_op jit(solution)/shard_map/ppermute | solution.py:540
  76.1 18.2 %collective-permute-start.9 = (bf16[4,8,16,256]{3,2,1,0:T(8,128)(2,1)S(1)}, bf16[4,8,16,256]{3,2,1,0:T(8,128)(2,1)S(1)}, u32[]{:S(2)}, u32[]{:S(2)}) collective-permute-start(bf16[4,8,16,256]{3,2,1,0:T(8,128)(2,1)S(1)} %get-tuple-element.73), channel_id=1, source_target_pairs={{0,2},{2,0},{1,3},{3,1},{4,6},{6,4},{5,7},{7,5},{8,10},{10,8},{9,1... | collective-permute-start | bytes 786440 | tf_op jit(solution)/shard_map/ppermute | solution.py:540
